TPU v7x, 32 devices: a whole 2x2x4 slice. The times are simulated.
32 devices in a mesh: dp: 8 (over y, x, core), fsdp: 4 (over z).
Axes of the slice: x: 2, y: 2, z: 4, core: 2. Of those that a mesh axis runs over, the one named last changes fastest.
Arguments:
- acts: bfloat16 [4096, 4096], P(('dp', 'fsdp')), may hold values from -6 to 6
- cotangent: bfloat16 [4096, 512], P(('dp', 'fsdp')), may hold values from -6 to 6
- tenant: int32 [4096], P(('dp', 'fsdp')), may hold values from 0 to 63, as said below
- advantage: int32 [4096], P(('dp', 'fsdp')), may hold values from -8 to 8
- base_weight: bfloat16 [4096, 512], P('fsdp'), may hold values from -0.25 to 0.25
- a_param: float32 [4096, 2048], P('fsdp', 'dp'), may hold values from -6 to 6
- a_moment: float32 [4096, 2048], P('fsdp', 'dp'), may hold values from -6 to 6
- a_second: float32 [4096, 2048], P('fsdp', 'dp'), may hold values from 0.1 to 10
- b_param: float32 [2048, 512], P(('dp', 'fsdp')), may hold values from -6 to 6
- b_moment: float32 [2048, 512], P(('dp', 'fsdp')), may hold values from -6 to 6
- b_second: float32 [2048, 512], P(('dp', 'fsdp')), may hold values from 0.1 to 10
Outputs:
- grad_input: bfloat16 [4096, 4096], P(('dp', 'fsdp'))
- new_a_param: float32 [4096, 2048], P('fsdp', 'dp')
- new_a_moment: float32 [4096, 2048], P('fsdp', 'dp')
- new_a_second: float32 [4096, 2048], P('fsdp', 'dp')
- new_b_param: float32 [2048, 512], P(('dp', 'fsdp'))
- new_b_moment: float32 [2048, 512], P(('dp', 'fsdp'))
- new_b_second: float32 [2048, 512], P(('dp', 'fsdp'))
Inputs may be any that keep to these rules, and one draw needn't show every extreme that they name: `tenant`: tenant t belongs to owner group t // 8. Among the 128 rows of each device, at most 38 belong to the tenants of one owner group; in every draw one owner group has exactly 38 rows on every device.
All inputs are finite; a program needn't handle non-finite values.
Results may differ from a plain program's by a relative error of at most 0.014.
Values may be sent and summed in bfloat16 or wider, within the bound.
No kernel may reach another device: no remote copies, remote signals or barrier semaphores. Data moves between devices by JAX's collectives and lax.ppermute only.
A program may use at most 64 MiB of HBM per device.

v0:
```python
import jax
import jax.numpy as jnp
from jax import lax
from jax.sharding import PartitionSpec as P

MODEL_WIDTH = 4096
ADAPTER_RANK = 32
TEN_DEV = 8


adapter_scale = 2.0
learn_rate = 0.02
beta_one = 0.9
beta_two = 0.999
adam_eps = 1e-08
bias_one = 1.0 - 0.9**10
bias_two = 1.0 - 0.999**10


def adam_step(param, moment, second, gradient):
    moment = beta_one * moment + (1.0 - beta_one) * gradient
    second = beta_two * second + (1.0 - beta_two) * gradient * gradient
    param = param - learn_rate * (moment / bias_one) / (jnp.sqrt(second / bias_two) + adam_eps)
    return (param, moment, second)


def contract_rows(left, right):
    return lax.dot_general(
        left, right, (((0,), (0,)), ((), ())), preferred_element_type=jnp.float32
    )


def contracted_columns(left, right):
    return lax.dot_general(
        left, right, (((1,), (1,)), ((), ())), preferred_element_type=jnp.float32
    )


def per_device(
    acts,
    cotangent,
    tenant,
    advantage,
    base_weight,
    a_param,
    a_moment,
    a_second,
    b_param,
    b_moment,
    b_second,
):
    owners = lax.axis_size("dp")
    row_count = acts.shape[0]
    capacity = 12 * row_count // (5 * owners)
    slot_count = owners * capacity
    columns = a_param.shape[1]
    scaled = (
        cotangent.astype(jnp.float32) * (advantage.astype(jnp.float32) * 0.25)[:, None]
    ).astype(jnp.bfloat16)
    a_low = (a_param * MODEL_WIDTH ** (-0.5)).astype(jnp.bfloat16)
    b_low = (b_param * ADAPTER_RANK ** (-0.5)).astype(jnp.bfloat16)
    owner_of = tenant // TEN_DEV
    member = (owner_of[:, None] == jnp.arange(owners, dtype=jnp.int32)[None, :]).astype(jnp.int32)
    before = jnp.cumsum(member, axis=0) - member
    placed = jnp.sum(before * member, axis=1)
    slot_of = owner_of * capacity + placed
    source = (
        jnp.zeros((slot_count,), jnp.int32).at[slot_of].set(jnp.arange(row_count, dtype=jnp.int32))
    )
    filled = jnp.zeros((slot_count,), jnp.bool_).at[slot_of].set(True)
    send_x = jnp.where(filled[:, None], acts[source], jnp.zeros((), jnp.bfloat16))
    send_g = jnp.where(filled[:, None], scaled[source], jnp.zeros((), jnp.bfloat16))
    send_t = jnp.where(filled, tenant[source] % TEN_DEV, TEN_DEV)
    down_coefficient = adapter_scale * MODEL_WIDTH ** (-0.5)
    up_coefficient = adapter_scale * ADAPTER_RANK ** (-0.5)
    down_factor_whole, b_full = (
        lax.all_gather(a_low, "fsdp", axis=0, tiled=True),
        lax.all_gather(b_low, "fsdp", axis=0, tiled=True),
    )
    recv_x, recv_g, recv_t = (
        lax.all_to_all(send_x, "dp", split_axis=0, concat_axis=0, tiled=True),
        lax.all_to_all(send_g, "dp", split_axis=0, concat_axis=0, tiled=True),
        lax.all_to_all(send_t, "dp", split_axis=0, concat_axis=0, tiled=True),
    )
    column = jnp.arange(columns, dtype=jnp.int32) // ADAPTER_RANK
    tenant_mask = (recv_t[:, None] == column[None, :]).astype(jnp.float32)
    mid_proj = (
        jnp.dot(recv_x, down_factor_whole, preferred_element_type=jnp.float32) * tenant_mask
    ).astype(jnp.bfloat16)
    backward_projection = (contracted_columns(recv_g, b_full) * tenant_mask).astype(jnp.bfloat16)
    adapter_branch_term = (
        adapter_scale * contracted_columns(backward_projection, down_factor_whole)
    ).astype(jnp.bfloat16)
    returned = lax.all_to_all(adapter_branch_term, "dp", split_axis=0, concat_axis=0, tiled=True)
    down_factor_gradient = lax.psum_scatter(
        (down_coefficient * contract_rows(recv_x, backward_projection)).astype(jnp.bfloat16),
        "fsdp",
        scatter_dimension=0,
        tiled=True,
    ).astype(jnp.float32)
    term_b = up_coefficient * contract_rows(mid_proj, recv_g)
    total_b = lax.psum(term_b.astype(jnp.bfloat16), "fsdp").astype(jnp.float32)
    own_rows = b_param.shape[0]
    up_factor_gradient = lax.dynamic_slice_in_dim(
        total_b, lax.axis_index("fsdp") * own_rows, own_rows, 0
    )
    side_rows = returned[slot_of]
    all_cots = lax.all_gather(scaled, "fsdp", axis=0, tiled=True)
    local_part = contracted_columns(all_cots, base_weight).astype(jnp.bfloat16)
    base_term = lax.all_to_all(local_part, "fsdp", split_axis=0, concat_axis=1, tiled=True)
    grad_input = (base_term.astype(jnp.float32) + side_rows.astype(jnp.float32)).astype(
        jnp.bfloat16
    )
    new_a = adam_step(a_param, a_moment, a_second, down_factor_gradient)
    new_b = adam_step(b_param, b_moment, b_second, up_factor_gradient)
    return (grad_input, new_a[0], new_a[1], new_a[2], new_b[0], new_b[1], new_b[2])


def solution(mesh):
    in_specs = (
        P(("dp", "fsdp"), None),
        P(("dp", "fsdp"), None),
        P(("dp", "fsdp")),
        P(("dp", "fsdp")),
        P("fsdp", None),
        P("fsdp", "dp"),
        P("fsdp", "dp"),
        P("fsdp", "dp"),
        P(("dp", "fsdp"), None),
        P(("dp", "fsdp"), None),
        P(("dp", "fsdp"), None),
    )
    out_specs = (
        P(("dp", "fsdp"), None),
        P("fsdp", "dp"),
        P("fsdp", "dp"),
        P("fsdp", "dp"),
        P(("dp", "fsdp"), None),
        P(("dp", "fsdp"), None),
        P(("dp", "fsdp"), None),
    )
    return jax.shard_map(
        per_device, mesh=mesh, in_specs=in_specs, out_specs=out_specs, check_vma=False
    )
```

profile of v0, /device:TPU:0, one launch (start us, length us, event | category | flops | bytes accessed | tf_op | source)
XLA Modules:
  0.0 265.7 jit_solution(12482594312867034171)
XLA Ops:
  7.2 0.0 copy-start
  7.2 0.8 and_select_fusion.1
  8.0 0.1 fusion.13
  8.1 0.2 reduce_window_sum.11
  8.2 0.2 select_reduce_fusion
  8.4 0.7 compare_select_fusion.1
  9.1 1.0 scatter_custom_fusion.1
  10.1 3.4 %gather_fusion = s32[304]{0:T(512)S(1)} fusion(s32[128]{0:T(128)} %param.13, s32[1024]{0:T(1024)S(1)} %pad_clamp_fusion.1), kind=kCustom, calls=%fused_computation | custom fusion | bytes 3648 | tf_op jit(solution)/shard_map/gather | solution.py:73
  13.6 1.0 scatter_custom_fusion
  14.6 0.7 all_to_all.38
  15.3 5.2 %all-to-all-start.1 = ((s32[8,38,1]{1,2,0:T(1,128)}), s32[8,38,1]{1,2,0:T(1,128)S(1)}, u32[]{:S(2)}, u32[]{:S(2)}) async-start(s32[8,38,1]{1,2,0:T(1,128)} %bitcast.2), calls=%async_computation.1 | async-start | bytes 8192 | tf_op jit(solution)/shard_map/all_to_all | solution.py:83
  20.4 0.1 broadcast_in_dim.55
  20.5 0.7 convert_multiply_fusion.2
  21.2 0.0 copy-done.8
  21.2 0.1 multiply_convert_fusion.1
  21.3 2.0 gather_fusion.1
  23.3 0.1 gather.18
  23.4 0.8 broadcast_select_fusion.1
  24.2 0.0 copy-done
  24.2 3.8 %gather_fusion.3 = bf16[304,4096]{1,0:T(8,128)(2,1)} fusion(bf16[128,4096]{1,0:T(8,128)(2,1)S(1)} %copy-done, s32[1024]{0:T(1024)S(1)} %pad_clamp_fusion.1), kind=kCustom, calls=%fused_computation.3 | custom fusion | bytes 4981952 | tf_op jit(solution)/shard_map/gather | solution.py:71
  28.0 3.2 %gather.21 = bf16[8,38,4096]{2,1,0:T(8,128)(2,1)} reshape(bf16[304,4096]{1,0:T(8,128)(2,1)} %gather_fusion.3) | data formatting | bytes 4980736 | tf_op jit(solution)/shard_map/gather | solution.py:71
  31.2 0.0 all-to-all-done.1
  31.2 4.2 %all-to-all-start.2 = ((bf16[8,38,512]{2,1,0:T(8,128)(2,1)}), bf16[8,38,512]{2,1,0:T(8,128)(2,1)S(1)}, u32[]{:S(2)}, u32[]{:S(2)}) async-start(bf16[8,38,512]{2,1,0:T(8,128)(2,1)} %broadcast_select_fusion.1), calls=%async_computation.2 | async-start | bytes 655360 | tf_op jit(solution)/shard_map/all_to_all | solution.py:82
  35.4 3.5 %broadcast_select_fusion = bf16[8,38,4096]{2,1,0:T(8,128)(2,1)} fusion(bf16[8,38,4096]{2,1,0:T(8,128)(2,1)} %gather.21, pred[8,38]{1,0:T(8,128)(4,1)S(1)} %broadcast_in_dim.55), kind=kLoop, calls=%fused_computation.10 | loop fusion | flops 1245184 | bytes 4981040 | tf_op jit(solution)/shard_map/jit(_where)/select_n | solution.py:71
  38.9 4.1 %all-to-all-done.2 = bf16[8,38,512]{2,1,0:T(8,128)(2,1)S(1)} async-done(((bf16[8,38,512]{2,1,0:T(8,128)(2,1)}), bf16[8,38,512]{2,1,0:T(8,128)(2,1)S(1)}, u32[]{:S(2)}, u32[]{:S(2)}) %all-to-all-start.2) | async-done | bytes 311328 | tf_op jit(solution)/shard_map/all_to_all | solution.py:82
  43.0 4.4 %all-to-all-start.4 = ((bf16[8,38,4096]{2,1,0:T(8,128)(2,1)}), bf16[8,38,4096]{2,1,0:T(8,128)(2,1)}, u32[]{:S(2)}, u32[]{:S(2)}) async-start(bf16[8,38,4096]{2,1,0:T(8,128)(2,1)} %broadcast_select_fusion), calls=%async_computation.4 | async-start | bytes 5242880 | tf_op jit(solution)/shard_map/all_to_all | solution.py:81
  47.4 0.0 reduce-scatter.2.cloned.1.call-start
  47.5 14.1 %all_gather.10 = bf16[256,512]{1,0:T(8,128)(2,1)S(1)} all-gather(bf16[64,512]{1,0:T(8,128)(2,1)S(1)} %multiply_convert_fusion.2), channel_id=1, replica_groups=mesh['dp'=8,'fsdp'=4] {'fsdp'}, dimensions={0}, use_global_device_ids=true | all-gather | bytes 327680 | tf_op jit(solution)/shard_map/all_gather | solution.py:78
  61.6 0.5 broadcast.107
  62.1 0.7 reduce.3
  62.8 0.1 eq.33
  62.9 0.1 all_to_all.41
  63.0 0.0 copy-start.7
  63.0 0.3 fusion.3
  63.3 16.4 %all-to-all-done.4 = bf16[8,38,4096]{2,1,0:T(8,128)(2,1)} async-done(((bf16[8,38,4096]{2,1,0:T(8,128)(2,1)}), bf16[8,38,4096]{2,1,0:T(8,128)(2,1)}, u32[]{:S(2)}, u32[]{:S(2)}) %all-to-all-start.4) | async-done | bytes 2490400 | tf_op jit(solution)/shard_map/all_to_all | solution.py:81
  79.7 3.1 %all_to_all.46 = bf16[304,4096]{1,0:T(8,128)(2,1)} reshape(bf16[8,38,4096]{2,1,0:T(8,128)(2,1)} %all-to-all-done.4) | data formatting | bytes 4980736 | tf_op jit(solution)/shard_map/all_to_all | solution.py:81
  82.9 4.3 %fusion.1 = bf16[4096,256]{1,0:T(8,128)(2,1)} fusion(bf16[304,4096]{1,0:T(8,128)(2,1)} %all_to_all.46, bf16[304,256]{1,0:T(8,128)(2,1)S(1)} %fusion.3), kind=kOutput, calls=%fused_computation.9 | convolution fusion | flops 639631360 | bytes 4743168 | tf_op jit(solution)/shard_map/dot_general | solution.py:28
  87.2 0.0 reduce-scatter.2.cloned.1.call-update
  87.2 0.0 all-gather.2.cloned.1.call-start
  87.2 43.4 %reduce-scatter.2.cloned.1.call-done = bf16[1024,256]{1,0:T(8,128)(2,1)} async-done(((bf16[4096,256]{1,0:T(8,128)(2,1)}), bf16[1024,256]{1,0:T(8,128)(2,1)}) %reduce-scatter.2.cloned.1.call-update) | async-done | bytes 524304 | tf_op jit(solution)/shard_map/reduce_scatter | solution.py:95
  130.6 3.8 %divide_subtract_fusion = (f32[1024,256]{1,0:T(8,128)}, f32[1024,256]{1,0:T(8,128)}, f32[1024,256]{1,0:T(8,128)}, bf16[1024,256]{1,0:T(8,128)(2,1)}) fusion(f32[1024,256]{1,0:T(8,128)S(1)} %copy-done.2, bf16[1024,256]{1,0:T(8,128)(2,1)} %reduce-scatter.2.cloned.1.call-done, f32[1024,256]{1,0:T(8,128)S(1)} %copy-done.3, f32[1024,256]{1,0:T(8,128)} %param.18), kind=kLoop, calls=%fused_computation.24 | loop fusion | flops 3932160 | bytes 7340032 | tf_op jit(solution)/shard_map/sub | solution.py:23
  134.4 0.0 all-gather.2.cloned.1.call-update
  134.4 18.4 %all_gather.9 = bf16[512,512]{1,0:T(8,128)(2,1)S(1)} all-gather(bf16[128,512]{1,0:T(8,128)(2,1)S(1)} %multiply_convert_fusion.1), channel_id=1, replica_groups=mesh['dp'=8,'fsdp'=4] {'fsdp'}, dimensions={0}, use_global_device_ids=true | all-gather | bytes 655360 | tf_op jit(solution)/shard_map/all_gather | solution.py:108
  152.8 3.0 %convolution_convert_fusion = bf16[512,1024]{1,0:T(8,128)(2,1)} fusion(bf16[512,512]{1,0:T(8,128)(2,1)S(1)} %all_gather.9, bf16[1024,512]{1,0:T(8,128)(2,1)} %param.15), kind=kOutput, calls=%fused_computation.14 | convolution fusion | flops 537395200 | bytes 2621440 | tf_op jit(solution)/shard_map/dot_general | solution.py:34
  155.8 4.3 %all-to-all-start = ((bf16[4,128,1024]{2,1,0:T(8,128)(2,1)}), bf16[4,128,1024]{2,1,0:T(8,128)(2,1)}, u32[]{:S(2)}, u32[]{:S(2)}) async-start(bf16[4,128,1024]{2,1,0:T(8,128)(2,1)} %bitcast), calls=%async_computation | async-start | bytes 2097152 | tf_op jit(solution)/shard_map/all_to_all | solution.py:110
  160.1 43.1 %all-gather.2.cloned.1.call-done = bf16[4096,256]{1,0:T(8,128)(2,1)} async-done(((bf16[1024,256]{1,0:T(8,128)(2,1)}), bf16[4096,256]{1,0:T(8,128)(2,1)}) %all-gather.2.cloned.1.call-update) | async-done | bytes 2097168 | tf_op jit(solution)/shard_map/all_gather | solution.py:77
  203.2 2.5 fusion
  205.7 1.8 all_to_all.42
  207.6 0.0 all-to-all-done
  207.6 4.6 %all-to-all-start.3 = ((bf16[8,38,4096]{2,1,0:T(8,128)(2,1)}), bf16[8,38,4096]{2,1,0:T(8,128)(2,1)}, u32[]{:S(2)}, u32[]{:S(2)}) async-start(bf16[8,38,4096]{2,1,0:T(8,128)(2,1)} %all_to_all.42), calls=%async_computation.3 | async-start | bytes 5242880 | tf_op jit(solution)/shard_map/all_to_all | solution.py:94
  212.1 0.2 all-reduce.2.cloned.1.call-start
  212.4 3.6 %fusion.2 = bf16[256,512]{1,0:T(8,128)(2,1)} fusion(bf16[304,512]{1,0:T(8,128)(2,1)} %copy-done.7, bf16[304,4096]{1,0:T(8,128)(2,1)S(1)} %copy-done.1, bf16[4096,256]{1,0:T(8,128)(2,1)} %all-gather.2.cloned.1.call-done, s32[256]{0:T(256)S(1)} %and_select_fusion, s32[304]{0:T(512)S(1)} %eq.33), kind=kOutput, calls=%fused_computation.17 | convolution fusion | flops 717721600 | bytes 5163200 | tf_op jit(solution)/shard_map/dot_general | solution.py:28
  216.0 0.0 all-reduce.2.cloned.1.call-update
  216.1 1.5 convert_bitcast_fusion
  217.5 0.0 copy-start.5
  217.5 0.0 copy-start.9
  217.6 0.0 copy-start.10
  217.6 1.5 copy.22
  219.0 31.3 %all-reduce.2.cloned.1.call-done = bf16[256,512]{1,0:T(8,128)(2,1)} async-done(((bf16[256,512]{1,0:T(8,128)(2,1)}), bf16[256,512]{1,0:T(8,128)(2,1)}) %all-reduce.2.cloned.1.call-update) | async-done | bytes 262160 | tf_op jit(solution)/shard_map/psum | solution.py:102
  250.3 1.6 divide_subtract_fusion.1
  251.9 0.0 all-to-all-done.3
  251.9 2.1 all_to_all.44
  254.0 2.2 gather_fusion.2
  256.2 3.0 %add_convert_fusion = bf16[128,4096]{1,0:T(8,128)(2,1)} fusion(f32[128,4096]{1,0:T(8,128)} %bitcast.18, bf16[128,4096]{1,0:T(8,128)(2,1)} %gather_fusion.2), kind=kLoop, calls=%fused_computation.12 | loop fusion | flops 1572864 | bytes 4194304 | tf_op jit(solution)/shard_map/convert_element_type | solution.py:111
  (23 shorter events, 0.1 us)
Async XLA Ops:
  7.2 17.1 %copy-start = (bf16[128,4096]{1,0:T(8,128)(2,1)S(1)}, bf16[128,4096]{1,0:T(8,128)(2,1)}, u32[]{:S(2)}) copy-start(bf16[128,4096]{1,0:T(8,128)(2,1)} %param.11) | copy-start | bytes 3145732
  7.2 14.0 %copy-start.8 = (bf16[128,512]{1,0:T(8,128)(2,1)S(1)}, bf16[128,512]{1,0:T(8,128)(2,1)}, u32[]{:S(2)}) copy-start(bf16[128,512]{1,0:T(8,128)(2,1)} %param.12) | copy-start | bytes 393220
  15.3 15.9 %all-to-all-start.1 = ((s32[8,38,1]{1,2,0:T(1,128)}), s32[8,38,1]{1,2,0:T(1,128)S(1)}, u32[]{:S(2)}, u32[]{:S(2)}) async-start(s32[8,38,1]{1,2,0:T(1,128)} %bitcast.2), calls=%async_computation.1 | async-start | bytes 8192 | tf_op jit(solution)/shard_map/all_to_all | solution.py:83
  31.2 11.8 %all-to-all-start.2 = ((bf16[8,38,512]{2,1,0:T(8,128)(2,1)}), bf16[8,38,512]{2,1,0:T(8,128)(2,1)S(1)}, u32[]{:S(2)}, u32[]{:S(2)}) async-start(bf16[8,38,512]{2,1,0:T(8,128)(2,1)} %broadcast_select_fusion.1), calls=%async_computation.2 | async-start | bytes 655360 | tf_op jit(solution)/shard_map/all_to_all | solution.py:82
  38.9 8.6 %copy-start.4 = (f32[64,512]{1,0:T(8,128)S(1)}, f32[64,512]{1,0:T(8,128)}, u32[]{:S(2)}) copy-start(f32[64,512]{1,0:T(8,128)} %param.19) | copy-start | bytes 393220
  43.0 36.7 %all-to-all-start.4 = ((bf16[8,38,4096]{2,1,0:T(8,128)(2,1)}), bf16[8,38,4096]{2,1,0:T(8,128)(2,1)}, u32[]{:S(2)}, u32[]{:S(2)}) async-start(bf16[8,38,4096]{2,1,0:T(8,128)(2,1)} %broadcast_select_fusion), calls=%async_computation.4 | async-start | bytes 5242880 | tf_op jit(solution)/shard_map/all_to_all | solution.py:81
  47.4 83.2 %reduce-scatter.2.cloned.1.call-start = ((), (), s32[]{:S(2)}) async-start(), calls=%async_computation.7 | async-start | bytes 2621440 | tf_op jit(solution)/shard_map/reduce_scatter | solution.py:95
  63.0 19.9 %copy-start.7 = (bf16[304,512]{1,0:T(8,128)(2,1)}, bf16[304,512]{1,0:T(8,128)(2,1)S(1)}, u32[]{:S(2)}) copy-start(bf16[304,512]{1,0:T(8,128)(2,1)S(1)} %all_to_all.41) | copy-start | bytes 933892
  63.3 19.6 %copy-start.6 = (bf16[304,256]{1,0:T(8,128)(2,1)}, bf16[304,256]{1,0:T(8,128)(2,1)S(1)}, u32[]{:S(2)}) copy-start(bf16[304,256]{1,0:T(8,128)(2,1)S(1)} %fusion.3) | copy-start | bytes 466948
  87.2 43.5 %copy-start.2 = (f32[1024,256]{1,0:T(8,128)S(1)}, f32[1024,256]{1,0:T(8,128)}, u32[]{:S(2)}) copy-start(f32[1024,256]{1,0:T(8,128)} %param.16) | copy-start | bytes 3145732
  87.2 43.5 %copy-start.3 = (f32[1024,256]{1,0:T(8,128)S(1)}, f32[1024,256]{1,0:T(8,128)}, u32[]{:S(2)}) copy-start(f32[1024,256]{1,0:T(8,128)} %param.17) | copy-start | bytes 3145732
  87.2 116.0 %all-gather.2.cloned.1.call-start = ((), (), s32[]{:S(2)}) async-start(), calls=%async_computation.6 | async-start | bytes 2621440 | tf_op jit(solution)/shard_map/all_gather | solution.py:77
  155.8 51.8 %all-to-all-start = ((bf16[4,128,1024]{2,1,0:T(8,128)(2,1)}), bf16[4,128,1024]{2,1,0:T(8,128)(2,1)}, u32[]{:S(2)}, u32[]{:S(2)}) async-start(bf16[4,128,1024]{2,1,0:T(8,128)(2,1)} %bitcast), calls=%async_computation | async-start | bytes 2097152 | tf_op jit(solution)/shard_map/all_to_all | solution.py:110
  207.6 4.8 %copy-start.1 = (bf16[304,4096]{1,0:T(8,128)(2,1)S(1)}, bf16[304,4096]{1,0:T(8,128)(2,1)}, u32[]{:S(2)}) copy-start(bf16[304,4096]{1,0:T(8,128)(2,1)} %all_to_all.46) | copy-start | bytes 7471108
  207.6 44.4 %all-to-all-start.3 = ((bf16[8,38,4096]{2,1,0:T(8,128)(2,1)}), bf16[8,38,4096]{2,1,0:T(8,128)(2,1)}, u32[]{:S(2)}, u32[]{:S(2)}) async-start(bf16[8,38,4096]{2,1,0:T(8,128)(2,1)} %all_to_all.42), calls=%async_computation.3 | async-start | bytes 5242880 | tf_op jit(solution)/shard_map/all_to_all | solution.py:94
  212.1 38.2 %all-reduce.2.cloned.1.call-start = ((), (), s32[]{:S(2)}) async-start(), calls=%async_computation.8 | async-start | bytes 524288 | tf_op jit(solution)/shard_map/psum | solution.py:102
  217.5 32.8 %copy-start.5 = (f32[64,512]{1,0:T(8,128)S(1)}, f32[64,512]{1,0:T(8,128)}, u32[]{:S(2)}) copy-start(f32[64,512]{1,0:T(8,128)} %param.19) | copy-start | bytes 393220
  217.5 32.8 %copy-start.9 = (f32[64,512]{1,0:T(8,128)S(1)}, f32[64,512]{1,0:T(8,128)}, u32[]{:S(2)}) copy-start(f32[64,512]{1,0:T(8,128)} %param.20) | copy-start | bytes 393220
  217.6 32.7 %copy-start.10 = (f32[64,512]{1,0:T(8,128)S(1)}, f32[64,512]{1,0:T(8,128)}, u32[]{:S(2)}) copy-start(f32[64,512]{1,0:T(8,128)} %param.21) | copy-start | bytes 393220
Sparse Core Ops, SparseCore 0:
  87.3 43.2 reduce-scatter.1
  134.5 68.5 all-gather.1
  216.2 34.0 all-reduce.1
where the time goes:
time: 267 us; the launch traced here: 266 us
  waiting for transfers between devices  138 us (52%)
  blocking collectives  32.5 us (12%)
  local copies, waits for them, and re-layouts  26.7 us (10%)
  starting transfers between devices  22.9 us (9%)
  other arithmetic  17.6 us (7%)
  between operations  14 us (5%)
  matrix products  13.7 us (5%)
    reduce_scatter x1, waiting for transfers between devices, per_device(): lax.psum_scatter((down_coefficient * contract_rows(recv_x, backward_proje...  43.4 us
    all_gather x1, waiting for transfers between devices, per_device(): lax.all_gather(a_low, 'fsdp', axis=0, tiled=True)  43.1 us
    psum x1, waiting for transfers between devices, per_device(): total_b = lax.psum(term_b.astype(jnp.bfloat16), 'fsdp').astype(jnp.float32)  31.3 us
    all_gather x1, blocking collectives, per_device(): all_cots = lax.all_gather(scaled, 'fsdp', axis=0, tiled=True)  18.4 us
    all_to_all x1, waiting for transfers between devices, per_device(): lax.all_to_all(send_x, 'dp', split_axis=0, concat_axis=0, tiled=True)  16.4 us
    all_gather x1, blocking collectives, per_device(): lax.all_gather(b_low, 'fsdp', axis=0, tiled=True)  14.1 us
    dot_general x2, matrix products, contract_rows(): lax.dot_general(left, right, (((0,), (0,)), ((), ())), preferred_element_...  7.96 us
    gather x2, local copies, waits for them, and re-layouts, per_device(): acts[source]  6.97 us
  transfers between devices with their start and end apart: 8, of which 5 were waited for; matrix products, arithmetic and copies ran while one was open for 11% of the time, Pallas kernels for 0%

commit v1 on v0

v1 whole, which is shorter than its diff:
```python
import jax
import jax.numpy as jnp
from jax import lax
from jax.sharding import PartitionSpec as P

MODEL_WIDTH = 4096
ADAPTER_RANK = 32
TEN_DEV = 8
GROUP_ELEMENTS = 1 << 20


adapter_scale = 2.0
learn_rate = 0.02
beta_one = 0.9
beta_two = 0.999
adam_eps = 1e-08
bias_one = 1.0 - 0.9**10
bias_two = 1.0 - 0.999**10


def adam_step(param, moment, second, gradient):
    moment = beta_one * moment + (1.0 - beta_one) * gradient
    second = beta_two * second + (1.0 - beta_two) * gradient * gradient
    param = param - learn_rate * (moment / bias_one) / (jnp.sqrt(second / bias_two) + adam_eps)
    return (param, moment, second)


def contract(left, right, left_dim, right_dim):
    return lax.dot_general(
        left, right, (((left_dim,), (right_dim,)), ((), ())), preferred_element_type=jnp.float32
    )


def swap(block, bit):
    size = lax.axis_size("dp")
    return lax.ppermute(block, "dp", [(i, i ^ bit) for i in range(size)])


def cube_gather(block, order):
    held = {0: block}
    for bit in order:
        held.update({k ^ bit: swap(v, bit) for k, v in list(held.items())})
    return held


def sum_scatter(blocks, order):
    for bit in order:
        after = {}
        for k in [k for k in blocks if not k & bit]:
            after[k] = blocks[k].astype(jnp.float32) + swap(blocks[k ^ bit], bit).astype(
                jnp.float32
            )
        if len(after) > 1:
            after = {k: v.astype(jnp.bfloat16) for k, v in after.items()}
        blocks = after
    return blocks[0]


def per_device(
    acts,
    cotangent,
    tenant,
    advantage,
    base_weight,
    a_param,
    a_moment,
    a_second,
    b_param,
    b_moment,
    b_second,
):
    owners = lax.axis_size("dp")
    shards = lax.axis_size("fsdp")
    me = lax.axis_index("dp")
    row_count, keys = cotangent.shape
    features, columns = a_param.shape
    own_rows = b_param.shape[0]
    rows = row_count * shards
    group = min(max(GROUP_ELEMENTS // (rows * columns), 1), owners)
    wires = [1 << i for i in range(1, owners.bit_length() - 1)]
    orders = (wires + [1], wires[::-1] + [1])
    back_orders = ([1] + wires, [1] + wires[::-1])

    scaled = (
        cotangent.astype(jnp.float32) * (advantage.astype(jnp.float32) * 0.25)[:, None]
    ).astype(jnp.bfloat16)
    a_low = (a_param * MODEL_WIDTH ** (-0.5)).astype(jnp.bfloat16)
    b_low = (b_param * ADAPTER_RANK ** (-0.5)).astype(jnp.bfloat16)

    labels = jnp.stack([tenant // TEN_DEV, tenant % TEN_DEV]).astype(jnp.bfloat16)
    labels = jnp.pad(labels, ((0, 14), (0, keys - row_count)))
    packed = jnp.concatenate([scaled, b_low, labels], axis=0)
    shared = lax.all_to_all(
        jnp.broadcast_to(packed[None], (shards,) + packed.shape), "fsdp", 0, 0, tiled=True
    )
    scaled_all = shared[:, :row_count].reshape(rows, keys)
    b_owner = shared[:, row_count : row_count + own_rows].reshape(columns, keys)
    labels = shared[:, row_count + own_rows :, :row_count].astype(jnp.int32)
    label = ((labels[:, 0] ^ me) * TEN_DEV + labels[:, 1]).reshape(rows)

    acts_part = lax.all_to_all(acts, "fsdp", split_axis=1, concat_axis=0, tiled=True)

    half = features // 2
    a_blocks = [
        cube_gather(a_low[i * half : (i + 1) * half], orders[i]) for i in range(2)
    ]
    b_blocks = cube_gather(b_owner, orders[0])

    base_term = contract(scaled_all, base_weight, 1, 1).astype(jnp.bfloat16)

    width = group * columns
    column = jnp.arange(width, dtype=jnp.int32) // ADAPTER_RANK
    fold = (
        jnp.arange(width, dtype=jnp.int32)[:, None] % ADAPTER_RANK
        == jnp.arange(ADAPTER_RANK, dtype=jnp.int32)[None, :]
    ).astype(jnp.bfloat16)
    down_coefficient = adapter_scale * MODEL_WIDTH ** (-0.5)
    up_coefficient = adapter_scale * ADAPTER_RANK ** (-0.5)

    grad_a_blocks = ({}, {})
    side = [None, None]
    mid = None
    for first in range(0, owners, group):
        members = range(first, first + group)
        mask = label[:, None] == (column + first * TEN_DEV)[None, :]
        b_group = jnp.concatenate([b_blocks[k] for k in members], axis=0)
        back = jnp.where(mask, contract(scaled_all, b_group, 1, 1), 0.0).astype(jnp.bfloat16)
        grad_a = (down_coefficient * contract(acts_part, back, 0, 0)).astype(jnp.bfloat16)
        for n, k in enumerate(members):
            for i in range(2):
                grad_a_blocks[i][k] = grad_a[
                    i * half : (i + 1) * half, n * columns : (n + 1) * columns
                ]
        mid_wide = None
        for i in range(2):
            a_group = jnp.concatenate([a_blocks[i][k] for k in members], axis=1)
            term = contract(back, a_group, 1, 1)
            side[i] = term if side[i] is None else side[i] + term
            term = contract(acts_part[:, i * half : (i + 1) * half], a_group, 1, 0)
            mid_wide = term if mid_wide is None else mid_wide + term
        mid_wide = jnp.where(mask, mid_wide, 0.0).astype(jnp.bfloat16)
        term = contract(fold, mid_wide, 0, 1)
        mid = term if mid is None else mid + term

    side_term = (adapter_scale * jnp.concatenate(side, axis=1)).astype(jnp.bfloat16)
    grad_part = (base_term.astype(jnp.float32) + side_term.astype(jnp.float32)).astype(
        jnp.bfloat16
    )
    grad_input = lax.all_to_all(grad_part, "fsdp", split_axis=0, concat_axis=1, tiled=True)

    mid_parts = lax.all_to_all(
        jnp.broadcast_to(mid.astype(jnp.bfloat16)[None], (shards,) + mid.shape),
        "fsdp",
        0,
        0,
        tiled=True,
    )
    mid = jnp.sum(mid_parts.astype(jnp.float32), axis=0).astype(jnp.bfloat16)
    start = lax.axis_index("fsdp") * own_rows
    mid_rows = lax.dynamic_slice_in_dim(jnp.tile(mid, (TEN_DEV, 1)), start, own_rows, 0)
    local = (start + jnp.arange(own_rows, dtype=jnp.int32)) // ADAPTER_RANK
    wanted = jnp.arange(owners, dtype=jnp.int32)[:, None] * TEN_DEV + local[None, :]
    mid_spread = jnp.where(
        wanted[:, :, None] == label[None, None, :], mid_rows[None], jnp.zeros((), jnp.bfloat16)
    ).reshape(owners * own_rows, rows)
    grad_b = (up_coefficient * contract(mid_spread, scaled_all, 1, 0)).astype(jnp.bfloat16)
    grad_b = sum_scatter(
        {k: grad_b[k * own_rows : (k + 1) * own_rows] for k in range(owners)}, back_orders[0]
    )
    grad_a = jnp.concatenate(
        [sum_scatter(grad_a_blocks[i], back_orders[i]) for i in range(2)], axis=0
    )

    new_a = adam_step(a_param, a_moment, a_second, grad_a)
    new_b = adam_step(b_param, b_moment, b_second, grad_b)
    return (grad_input, new_a[0], new_a[1], new_a[2], new_b[0], new_b[1], new_b[2])


def solution(mesh):
    rows = P(("dp", "fsdp"), None)
    labels = P(("dp", "fsdp"))
    first = P("fsdp", "dp")
    return jax.shard_map(
        per_device,
        mesh=mesh,
        in_specs=(rows, rows, labels, labels, P("fsdp", None), first, first, first, rows, rows, rows),
        out_specs=(rows, first, first, first, rows, rows, rows),
        check_vma=False,
    )
```

time: 267 us -> 199 us (0.75)
  waiting for transfers between devices: 138 us -> 92.6 us
  blocking collectives: 32.5 us -> 0 us
  starting transfers between devices: 22.9 us -> 44.5 us
  between operations: 14 us -> 1.15 us
  matrix products: 13.7 us -> 23.4 us
  other arithmetic: 17.6 us -> 10.6 us
    ppermute x0 -> x42, waiting for transfers between devices: none -> 45.2 us  [swap(): return lax.ppermute(block, 'dp', [(i, i ^ bit) for i in range(size)])]
    reduce_scatter x1 -> x0, waiting for transfers between devices: 43.4 us -> none  [per_device(): lax.psum_scatter((down_coefficient * contract_rows(recv_x, backward_proje...]
    all_gather x1 -> x0, waiting for transfers between devices: 43.1 us -> none  [per_device(): lax.all_gather(a_low, 'fsdp', axis=0, tiled=True)]
    all_gather x2 -> x0, blocking collectives: 32.5 us -> none  [the longest x1 18.4 us: per_device(): all_cots = lax.all_gather(scaled, 'fsdp', axis=0, tiled=True)]
    psum x1 -> x0, waiting for transfers between devices: 31.3 us -> none  [per_device(): total_b = lax.psum(term_b.astype(jnp.bfloat16), 'fsdp').astype(jnp.float32)]
    ppermute x0 -> x42, starting transfers between devices: none -> 27.8 us  [swap(): return lax.ppermute(block, 'dp', [(i, i ^ bit) for i in range(size)])]
    all_to_all x5 -> x4, waiting for transfers between devices: 20.6 us -> 47.4 us  [the longest x1 20.2 us: per_device(): lax.all_to_all(jnp.broadcast_to(packed[None], (shards,) + packed.shape),...]
    unnamed x22 -> x50, local copies, waits for them, and re-layouts: 0.06 us -> 19.2 us
  transfers between devices with their start and end apart: 8 -> 46, of which waited for: 5 -> 20; matrix products, arithmetic and copies ran while one was open for 11% -> 16% of each run, Pallas kernels for 0% -> 0%
where the time goes in v1:
time: 199 us; the launch traced here: 198 us
  waiting for transfers between devices  92.6 us (47%)
  starting transfers between devices  44.5 us (22%)
  local copies, waits for them, and re-layouts  25.9 us (13%)
  matrix products  23.4 us (12%)
  other arithmetic  10.6 us (5%)
    ppermute x42, waiting for transfers between devices, swap(): return lax.ppermute(block, 'dp', [(i, i ^ bit) for i in range(size)])  45.2 us
    ppermute x42, starting transfers between devices, swap(): return lax.ppermute(block, 'dp', [(i, i ^ bit) for i in range(size)])  27.8 us
    dot_general x8, matrix products, contract(): lax.dot_general(left, right, (((left_dim,), (right_dim,)), ((), ())), pre...  23.4 us
    all_to_all x1, waiting for transfers between devices, per_device(): lax.all_to_all(jnp.broadcast_to(packed[None], (shards,) + packed.shape),...  20.2 us
    unnamed x50, local copies, waits for them, and re-layouts  19.2 us
    all_to_all x1, waiting for transfers between devices, per_device(): lax.all_to_all(grad_part, 'fsdp', split_axis=0, concat_axis=1, tiled=True)  13.5 us
    all_to_all x1, waiting for transfers between devices, per_device(): lax.all_to_all(acts, 'fsdp', split_axis=1, concat_axis=0, tiled=True)  10.5 us
    all_to_all x1, starting transfers between devices, per_device(): lax.all_to_all(jnp.broadcast_to(packed[None], (shards,) + packed.shape),...  6.32 us
  transfers between devices with their start and end apart: 46, of which 20 were waited for; matrix products, arithmetic and copies ran while one was open for 16% of the time, Pallas kernels for 0%

profile of v1, /device:TPU:0, one launch (start us, length us, event | category | flops | bytes accessed | tf_op | source)
XLA Modules:
  0.0 198.2 jit_solution(13528217125545671655)
XLA Ops:
  0.7 0.8 convert_bitcast_fusion
  1.5 0.9 multiply_convert_fusion.3
  3.1 1.0 multiply_convert_fusion.2
  4.1 1.0 broadcast_in_dim.17
  5.1 6.3 %all-to-all-start = ((bf16[4,208,512]{2,1,0:T(8,128)(2,1)}), bf16[4,208,512]{2,1,0:T(8,128)(2,1)S(1)}, u32[]{:S(2)}, u32[]{:S(2)}) async-start(bf16[4,208,512]{2,1,0:T(8,128)(2,1)} %broadcast_in_dim.17), calls=%async_computation | async-start | bytes 1703936 | tf_op jit(solution)/shard_map/all_to_all | solution.py:93
  11.4 1.3 copy.34
  12.7 20.2 %all-to-all-done = bf16[4,208,512]{2,1,0:T(8,128)(2,1)S(1)} async-done(((bf16[4,208,512]{2,1,0:T(8,128)(2,1)}), bf16[4,208,512]{2,1,0:T(8,128)(2,1)S(1)}, u32[]{:S(2)}, u32[]{:S(2)}) %all-to-all-start) | async-done | bytes 852000 | tf_op jit(solution)/shard_map/all_to_all | solution.py:93
  32.9 3.5 %all-to-all-start.2 = ((bf16[128,4,1024]{0,2,1:T(8,128)(2,1)}), bf16[128,4,1024]{0,2,1:T(8,128)(2,1)S(1)}, u32[]{:S(2)}, u32[]{:S(2)}) async-start(bf16[128,4,1024]{0,2,1:T(8,128)(2,1)} %bitcast.7), calls=%async_computation.2 | async-start | bytes 2097152 | tf_op jit(solution)/shard_map/all_to_all | solution.py:101
  36.5 1.6 collective-permute-start.1
  38.1 1.5 collective-permute-start.3
  39.6 5.7 %collective-permute-done.1 = bf16[256,512]{1,0:T(8,128)(2,1)} collective-permute-done((bf16[256,512]{1,0:T(8,128)(2,1)S(1)}, bf16[256,512]{1,0:T(8,128)(2,1)}, u32[]{:S(2)}, u32[]{:S(2)}) %collective-permute-start.1) | collective-permute-done | bytes 262176 | tf_op jit(solution)/shard_map/ppermute | solution.py:36
  45.4 1.5 collective-permute-start.5
  47.6 0.9 slice.132
  49.4 1.7 constant_dynamic-update-slice_fusion.5
  51.1 10.5 %all-to-all-done.2 = bf16[128,4,1024]{0,2,1:T(8,128)(2,1)S(1)} async-done(((bf16[128,4,1024]{0,2,1:T(8,128)(2,1)}), bf16[128,4,1024]{0,2,1:T(8,128)(2,1)S(1)}, u32[]{:S(2)}, u32[]{:S(2)}) %all-to-all-start.2) | async-done | bytes 1048608 | tf_op jit(solution)/shard_map/all_to_all | solution.py:101
  62.3 2.1 %constant_dynamic-update-slice_fusion.4 = bf16[2048,512]{1,0:T(8,128)(2,1)} fusion(bf16[2048,512]{1,0:T(8,128)(2,1)} %constant_dynamic-update-slice_fusion.5, bf16[256,512]{1,0:T(8,128)(2,1)} %collective-permute-done.2), kind=kLoop, calls=%fused_computation.59 | loop fusion | bytes 524288
  65.1 1.7 constant_dynamic-update-slice_fusion.2
  66.7 1.7 constant_dynamic-update-slice_fusion.1
  69.1 2.9 %fusion = bf16[512,2048]{1,0:T(8,128)(2,1)S(1)} fusion(bf16[512,512]{1,0:T(8,128)(2,1)S(1)} %bitcast.49, bf16[2048,512]{1,0:T(8,128)(2,1)} %constant_dynamic-update-slice_fusion, s32[2048]{0:T(1024)S(1)} %add_select_fusion, s32[512]{0:T(512)S(1)} %bitcast.53), kind=kOutput, calls=%fused_computation.3 | convolution fusion | flops 1076887552 | bytes 4728832 | tf_op jit(solution)/shard_map/dot_general | solution.py:29
  72.1 2.4 %fusion.2 = bf16[1024,2048]{1,0:T(8,128)(2,1)S(1)} fusion(bf16[512,2048]{1,0:T(8,128)(2,1)S(1)} %fusion, bf16[512,1024]{1,0:T(8,128)(2,1)S(1)} %bitcast.40), kind=kOutput, calls=%fused_computation.5 | convolution fusion | flops 2151677952 | bytes 7340032 | tf_op jit(solution)/shard_map/dot_general | solution.py:29
  75.3 0.9 collective-permute-done.22
  76.8 1.6 collective-permute-start.26
  79.4 6.6 %collective-permute-done.26 = bf16[512,256]{1,0:T(8,128)(2,1)S(1)} collective-permute-done((bf16[512,256]{1,0:T(8,128)(2,1)S(1)}, bf16[512,256]{1,0:T(8,128)(2,1)S(1)}, u32[]{:S(2)}, u32[]{:S(2)}) %collective-permute-start.26) | collective-permute-done | bytes 262176 | tf_op jit(solution)/shard_map/ppermute | solution.py:36
  86.1 1.6 collective-permute-start.27
  87.7 3.1 %collective-permute-done.23 = bf16[512,256]{1,0:T(8,128)(2,1)S(1)} collective-permute-done((bf16[512,256]{1,0:T(8,128)(2,1)S(1)}, bf16[512,256]{1,0:T(8,128)(2,1)S(1)}, u32[]{:S(2)}, u32[]{:S(2)}) %collective-permute-start.23) | collective-permute-done | bytes 262176 | tf_op jit(solution)/shard_map/ppermute | solution.py:36
  90.8 2.1 %collective-permute-done.27 = bf16[512,256]{1,0:T(8,128)(2,1)S(1)} collective-permute-done((bf16[512,256]{1,0:T(8,128)(2,1)S(1)}, bf16[512,256]{1,0:T(8,128)(2,1)S(1)}, u32[]{:S(2)}, u32[]{:S(2)}) %collective-permute-start.27) | collective-permute-done | bytes 262176 | tf_op jit(solution)/shard_map/ppermute | solution.py:36
  93.2 1.6 collective-permute-start.33
  95.3 6.2 %collective-permute-done.33 = bf16[512,256]{1,0:T(8,128)(2,1)S(1)} collective-permute-done((bf16[512,256]{1,0:T(8,128)(2,1)S(1)}, bf16[512,256]{1,0:T(8,128)(2,1)S(1)}, u32[]{:S(2)}, u32[]{:S(2)}) %collective-permute-start.33) | collective-permute-done | bytes 262176 | tf_op jit(solution)/shard_map/ppermute | solution.py:36
  101.4 0.8 add_convert_fusion.1
  102.2 1.5 collective-permute-start.34
  103.7 1.6 collective-permute-done.30
  105.3 3.6 %collective-permute-done.34 = bf16[512,256]{1,0:T(8,128)(2,1)} collective-permute-done((bf16[512,256]{1,0:T(8,128)(2,1)}, bf16[512,256]{1,0:T(8,128)(2,1)}, u32[]{:S(2)}, u32[]{:S(2)}) %collective-permute-start.34) | collective-permute-done | bytes 262176 | tf_op jit(solution)/shard_map/ppermute | solution.py:36
  108.9 1.2 convert_add_fusion
  110.2 3.4 %divide_subtract_fusion = (f32[1024,256]{1,0:T(8,128)}, f32[1024,256]{1,0:T(8,128)}, f32[1024,256]{1,0:T(8,128)}, bf16[1024,256]{1,0:T(8,128)(2,1)S(1)}) fusion(f32[1024,256]{1,0:T(8,128)S(1)} %copy-done.5, f32[512,256]{1,0:T(8,128)S(1)} %convert_add_fusion, f32[512,256]{1,0:T(8,128)S(1)} %get-tuple-element.13, f32[1024,256]{1,0:T(8,128)S(1)} %copy-done.6, ...), kind=kLoop, calls=%fused_computation.18 | loop fusion | flops 3932160 | bytes 7864320 | tf_op jit(solution)/shard_map/sub | solution.py:24
  113.6 0.9 fusion.37
  114.5 1.5 collective-permute-start.15
  116.0 2.5 %collective-permute-start.17 = (bf16[512,256]{1,0:T(8,128)(2,1)}, bf16[512,256]{1,0:T(8,128)(2,1)}, u32[]{:S(2)}, u32[]{:S(2)}) collective-permute-start(bf16[512,256]{1,0:T(8,128)(2,1)} %get-tuple-element.36), channel_id=1, source_target_pairs={{0,16},{4,20},{8,24},{12,28},{16,0},{20,4},{24,8},{28,12},{1,17},{... | collective-permute-start | bytes 786440 | tf_op jit(solution)/shard_map/ppermute | solution.py:36
  119.3 4.6 %collective-permute-done.15 = bf16[512,256]{1,0:T(8,128)(2,1)} collective-permute-done((bf16[512,256]{1,0:T(8,128)(2,1)}, bf16[512,256]{1,0:T(8,128)(2,1)}, u32[]{:S(2)}, u32[]{:S(2)}) %collective-permute-start.15) | collective-permute-done | bytes 262176 | tf_op jit(solution)/shard_map/ppermute | solution.py:36
  123.9 1.0 constant_dynamic-update-slice_fusion.22
  124.9 1.0 constant_dynamic-update-slice_fusion.21
  126.5 1.5 collective-permute-start.19
  127.9 1.1 collective-permute-done.8
  129.0 1.7 constant_dynamic-update-slice_fusion.14
  131.5 2.5 %collective-permute-start.12 = (bf16[512,256]{1,0:T(8,128)(2,1)S(1)}, bf16[512,256]{1,0:T(8,128)(2,1)S(1)}, u32[]{:S(2)}, u32[]{:S(2)}) collective-permute-start(bf16[512,256]{1,0:T(8,128)(2,1)S(1)} %collective-permute-done.8), channel_id=1, source_target_pairs={{0,16},{4,20},{8,24},{12,28},{16,0},{20,4},{24,8},{28,12},{1,17},{... | collective-permute-start | bytes 786440 | tf_op jit(solution)/shard_map/ppermute | solution.py:36
  134.2 1.1 constant_dynamic-update-slice_fusion.19
  135.8 0.8 constant_dynamic-update-slice_fusion.12
  136.6 0.8 constant_dynamic-update-slice_fusion.11
  137.3 3.6 %collective-permute-done.12 = bf16[512,256]{1,0:T(8,128)(2,1)S(1)} collective-permute-done((bf16[512,256]{1,0:T(8,128)(2,1)S(1)}, bf16[512,256]{1,0:T(8,128)(2,1)S(1)}, u32[]{:S(2)}, u32[]{:S(2)}) %collective-permute-start.12) | collective-permute-done | bytes 262176 | tf_op jit(solution)/shard_map/ppermute | solution.py:36
  140.9 0.8 constant_dynamic-update-slice_fusion.10
  142.5 2.3 %fusion.39 = f32[512,512]{1,0:T(8,128)} fusion(bf16[512,2048]{1,0:T(8,128)(2,1)S(1)} %copy-done.14, bf16[512,2048]{1,0:T(8,128)(2,1)S(1)} %constant_dynamic-update-slice_fusion.16), kind=kOutput, calls=%fused_computation.123 | convolution fusion | flops 1073741824 | bytes 5242880 | tf_op jit(solution)/shard_map/dot_general | solution.py:29
  144.8 3.3 %fusion.10 = f32[2048,512]{0,1:T(8,128)} fusion(bf16[512,2048]{1,0:T(8,128)(2,1)S(1)} %constant_dynamic-update-slice_fusion.16, bf16[512,1024]{1,0:T(8,128)(2,1)S(1)} %bitcast.41), kind=kOutput, calls=%fused_computation.23 | convolution fusion | flops 1073741824 | bytes 6815744 | tf_op jit(solution)/shard_map/dot_general | solution.py:29
  148.8 4.0 %fusion.38 = f32[512,512]{1,0:T(8,128)} fusion(bf16[512,2048]{1,0:T(8,128)(2,1)S(1)} %copy-done.14, bf16[512,2048]{1,0:T(8,128)(2,1)} %constant_dynamic-update-slice_fusion.8), kind=kOutput, calls=%fused_computation.122 | convolution fusion | flops 1073741824 | bytes 5242880 | tf_op jit(solution)/shard_map/dot_general | solution.py:29
  152.8 4.9 %fusion.6 = bf16[32,512]{1,0:T(8,128)(2,1)S(1)} fusion(f32[2048,512]{0,1:T(8,128)} %fusion.10, bf16[512,2048]{1,0:T(8,128)(2,1)} %constant_dynamic-update-slice_fusion.8, s32[2048]{0:T(1024)S(1)} %add_select_fusion, s32[512]{0:T(512)S(1)} %bitcast.54, bf16[512,1024]{1,0:T(8,128)(2,1)S(1)} %bitcast.42, s32[2048]{0:T(1024)S(1)} %fusion.22), kind=kOutput, calls=%fused_computation.14 | convolution fusion | flops 1145192448 | bytes 6866944 | tf_op jit(solution)/shard_map/dot_general | solution.py:29
  158.3 3.3 %all-to-all-start.3 = ((bf16[4,32,512]{2,1,0:T(8,128)(2,1)}), bf16[4,32,512]{2,1,0:T(8,128)(2,1)S(1)}, u32[]{:S(2)}, u32[]{:S(2)}) async-start(bf16[4,32,512]{2,1,0:T(8,128)(2,1)} %broadcast_in_dim.19), calls=%async_computation.3 | async-start | bytes 262144 | tf_op jit(solution)/shard_map/all_to_all | solution.py:151
  161.7 3.3 %add_convert_fusion = bf16[512,1024]{1,0:T(8,128)(2,1)} fusion(f32[512,512]{1,0:T(8,128)} %fusion.39, f32[512,512]{1,0:T(8,128)} %fusion.38, bf16[512,512]{1,0:T(8,128)(2,1)S(1)} %bitcast.50, bf16[1024,512]{1,0:T(8,128)(2,1)S(1)} %copy-done), kind=kOutput, calls=%fused_computation.8 | convolution fusion | flops 541065216 | bytes 4718592 | tf_op jit(solution)/shard_map/dot_general | solution.py:29
  165.0 3.1 %all-to-all-done.3 = bf16[4,32,512]{2,1,0:T(8,128)(2,1)S(1)} async-done(((bf16[4,32,512]{2,1,0:T(8,128)(2,1)}), bf16[4,32,512]{2,1,0:T(8,128)(2,1)S(1)}, u32[]{:S(2)}, u32[]{:S(2)}) %all-to-all-start.3) | async-done | bytes 131104 | tf_op jit(solution)/shard_map/all_to_all | solution.py:151
  168.1 3.5 %all-to-all-start.1 = ((bf16[4,128,1024]{2,1,0:T(8,128)(2,1)}), bf16[4,128,1024]{2,1,0:T(8,128)(2,1)S(1)}, u32[]{:S(2)}, u32[]{:S(2)}) async-start(bf16[4,128,1024]{2,1,0:T(8,128)(2,1)} %bitcast.5), calls=%async_computation.1 | async-start | bytes 2097152 | tf_op jit(solution)/shard_map/all_to_all | solution.py:149
  173.9 1.5 collective-permute-start.40
  176.1 2.2 %collective-permute-done.40 = bf16[64,512]{1,0:T(8,128)(2,1)S(1)} collective-permute-done((bf16[64,512]{1,0:T(8,128)(2,1)S(1)}, bf16[64,512]{1,0:T(8,128)(2,1)S(1)}, u32[]{:S(2)}, u32[]{:S(2)}) %collective-permute-start.40) | collective-permute-done | bytes 65568 | tf_op jit(solution)/shard_map/ppermute | solution.py:36
  178.4 1.8 collective-permute-start.41
  180.2 2.5 %collective-permute-done.41 = bf16[64,512]{1,0:T(8,128)(2,1)S(1)} collective-permute-done((bf16[64,512]{1,0:T(8,128)(2,1)S(1)}, bf16[64,512]{1,0:T(8,128)(2,1)S(1)}, u32[]{:S(2)}, u32[]{:S(2)}) %collective-permute-start.41) | collective-permute-done | bytes 65568 | tf_op jit(solution)/shard_map/ppermute | solution.py:36
  182.7 0.8 divide_subtract_fusion.1
  183.5 13.5 %all-to-all-done.1 = bf16[4,128,1024]{2,1,0:T(8,128)(2,1)S(1)} async-done(((bf16[4,128,1024]{2,1,0:T(8,128)(2,1)}), bf16[4,128,1024]{2,1,0:T(8,128)(2,1)S(1)}, u32[]{:S(2)}, u32[]{:S(2)}) %all-to-all-start.1) | async-done | bytes 1048608 | tf_op jit(solution)/shard_map/all_to_all | solution.py:149
  197.1 1.1 copy.42
  (124 shorter events, 15.7 us)
Async XLA Ops:
  0.6 161.0 %copy-start = (bf16[1024,512]{1,0:T(8,128)(2,1)S(1)}, bf16[1024,512]{1,0:T(8,128)(2,1)}, u32[]{:S(2)}) copy-start(bf16[1024,512]{1,0:T(8,128)(2,1)} %param.15) | copy-start | bytes 3145732
  0.6 10.7 %copy-start.7 = (bf16[128,4096]{1,0:T(8,128)(2,1)S(1)}, bf16[128,4096]{1,0:T(8,128)(2,1)}, u32[]{:S(2)}) copy-start(bf16[128,4096]{1,0:T(8,128)(2,1)} %param.11) | copy-start | bytes 3145732
  5.1 27.8 %all-to-all-start = ((bf16[4,208,512]{2,1,0:T(8,128)(2,1)}), bf16[4,208,512]{2,1,0:T(8,128)(2,1)S(1)}, u32[]{:S(2)}, u32[]{:S(2)}) async-start(bf16[4,208,512]{2,1,0:T(8,128)(2,1)} %broadcast_in_dim.17), calls=%async_computation | async-start | bytes 1703936 | tf_op jit(solution)/shard_map/all_to_all | solution.py:93
  32.9 28.7 %all-to-all-start.2 = ((bf16[128,4,1024]{0,2,1:T(8,128)(2,1)}), bf16[128,4,1024]{0,2,1:T(8,128)(2,1)S(1)}, u32[]{:S(2)}, u32[]{:S(2)}) async-start(bf16[128,4,1024]{0,2,1:T(8,128)(2,1)} %bitcast.7), calls=%async_computation.2 | async-start | bytes 2097152 | tf_op jit(solution)/shard_map/all_to_all | solution.py:101
  36.5 12.3 %collective-permute-start = (bf16[256,512]{1,0:T(8,128)(2,1)S(1)}, bf16[256,512]{1,0:T(8,128)(2,1)S(1)}, u32[]{:S(2)}, u32[]{:S(2)}) collective-permute-start(bf16[256,512]{1,0:T(8,128)(2,1)S(1)} %bitcast.44), channel_id=1, source_target_pairs={{0,4},{4,0},{8,12},{12,8},{16,20},{20,16},{24,28},{28,24},{1,5},{5... | collective-permute-start | bytes 786440 | tf_op jit(solution)/shard_map/ppermute | solution.py:36
  36.5 8.8 %collective-permute-start.1 = (bf16[256,512]{1,0:T(8,128)(2,1)S(1)}, bf16[256,512]{1,0:T(8,128)(2,1)}, u32[]{:S(2)}, u32[]{:S(2)}) collective-permute-start(bf16[256,512]{1,0:T(8,128)(2,1)S(1)} %bitcast.45), channel_id=1, source_target_pairs={{0,8},{4,12},{8,0},{12,4},{16,24},{20,28},{24,16},{28,20},{1,9},{5... | collective-permute-start | bytes 786440 | tf_op jit(solution)/shard_map/ppermute | solution.py:36
  38.1 10.4 %collective-permute-start.3 = (bf16[256,512]{1,0:T(8,128)(2,1)S(1)}, bf16[256,512]{1,0:T(8,128)(2,1)S(1)}, u32[]{:S(2)}, u32[]{:S(2)}) collective-permute-start(bf16[256,512]{1,0:T(8,128)(2,1)S(1)} %bitcast.46), channel_id=1, source_target_pairs={{0,16},{4,20},{8,24},{12,28},{16,0},{20,4},{24,8},{28,12},{1,17},{... | collective-permute-start | bytes 786440 | tf_op jit(solution)/shard_map/ppermute | solution.py:36
  45.4 16.9 %collective-permute-start.2 = (bf16[256,512]{1,0:T(8,128)(2,1)}, bf16[256,512]{1,0:T(8,128)(2,1)}, u32[]{:S(2)}, u32[]{:S(2)}) collective-permute-start(bf16[256,512]{1,0:T(8,128)(2,1)} %collective-permute-done.1), channel_id=1, source_target_pairs={{0,4},{4,0},{8,12},{12,8},{16,20},{20,16},{24,28},{28,24},{1,5},{5... | collective-permute-start | bytes 786440 | tf_op jit(solution)/shard_map/ppermute | solution.py:36
  45.4 16.8 %collective-permute-start.5 = (bf16[256,512]{1,0:T(8,128)(2,1)}, bf16[256,512]{1,0:T(8,128)(2,1)}, u32[]{:S(2)}, u32[]{:S(2)}) collective-permute-start(bf16[256,512]{1,0:T(8,128)(2,1)} %collective-permute-done.1), channel_id=1, source_target_pairs={{0,16},{4,20},{8,24},{12,28},{16,0},{20,4},{24,8},{28,12},{1,17},{... | collective-permute-start | bytes 786440 | tf_op jit(solution)/shard_map/ppermute | solution.py:36
  48.5 16.6 %collective-permute-start.4 = (bf16[256,512]{1,0:T(8,128)(2,1)S(1)}, bf16[256,512]{1,0:T(8,128)(2,1)}, u32[]{:S(2)}, u32[]{:S(2)}) collective-permute-start(bf16[256,512]{1,0:T(8,128)(2,1)S(1)} %collective-permute-done.3), channel_id=1, source_target_pairs={{0,4},{4,0},{8,12},{12,8},{16,20},{20,16},{24,28},{28,24},{1,5},{5... | collective-permute-start | bytes 786440 | tf_op jit(solution)/shard_map/ppermute | solution.py:36
  62.1 9.9 %copy-start.2 = (bf16[4,128,1024]{2,1,0:T(8,128)(2,1)}, bf16[4,128,1024]{2,1,0:T(8,128)(2,1)S(1)}, u32[]{:S(2)}) copy-start(bf16[4,128,1024]{2,1,0:T(8,128)(2,1)S(1)} %copy.35) | copy-start | bytes 3145732
  62.1 7.0 %copy-start.8 = (bf16[4,128,512]{2,1,0:T(8,128)(2,1)S(1)}, bf16[4,128,512]{2,1,0:T(8,128)(2,1)}, u32[]{:S(2)}) copy-start(bf16[4,128,512]{2,1,0:T(8,128)(2,1)} %slice.132) | copy-start | bytes 1572868
  62.2 6.2 %collective-permute-start.6 = (bf16[256,512]{1,0:T(8,128)(2,1)}, bf16[256,512]{1,0:T(8,128)(2,1)S(1)}, u32[]{:S(2)}, u32[]{:S(2)}) collective-permute-start(bf16[256,512]{1,0:T(8,128)(2,1)} %collective-permute-done.5), channel_id=1, source_target_pairs={{0,4},{4,0},{8,12},{12,8},{16,20},{20,16},{24,28},{28,24},{1,5},{5... | collective-permute-start | bytes 786440 | tf_op jit(solution)/shard_map/ppermute | solution.py:36
  72.1 2.4 %copy-start.13 = (bf16[512,2048]{1,0:T(8,128)(2,1)}, bf16[512,2048]{1,0:T(8,128)(2,1)S(1)}, u32[]{:S(2)}) copy-start(bf16[512,2048]{1,0:T(8,128)(2,1)S(1)} %fusion) | copy-start | bytes 6291460
  74.5 27.0 %copy-start.1 = (bf16[1024,2048]{1,0:T(8,128)(2,1)}, bf16[1024,2048]{1,0:T(8,128)(2,1)S(1)}, u32[]{:S(2)}) copy-start(bf16[1024,2048]{1,0:T(8,128)(2,1)S(1)} %fusion.2) | copy-start | bytes 12582916
  74.6 1.6 collective-permute-start.22
  74.8 1.8 collective-permute-start.25
  75.2 3.7 %collective-permute-start.24 = (bf16[512,256]{1,0:T(8,128)(2,1)S(1)}, bf16[512,256]{1,0:T(8,128)(2,1)S(1)}, u32[]{:S(2)}, u32[]{:S(2)}) collective-permute-start(bf16[512,256]{1,0:T(8,128)(2,1)S(1)} %get-tuple-element.22), channel_id=1, source_target_pairs={{0,4},{4,0},{8,12},{12,8},{16,20},{20,16},{24,28},{28,24},{1,5},{5... | collective-permute-start | bytes 786440 | tf_op jit(solution)/shard_map/ppermute | solution.py:36
  76.8 9.2 %collective-permute-start.26 = (bf16[512,256]{1,0:T(8,128)(2,1)S(1)}, bf16[512,256]{1,0:T(8,128)(2,1)S(1)}, u32[]{:S(2)}, u32[]{:S(2)}) collective-permute-start(bf16[512,256]{1,0:T(8,128)(2,1)S(1)} %get-tuple-element.25), channel_id=1, source_target_pairs={{0,8},{4,12},{8,0},{12,4},{16,24},{20,28},{24,16},{28,20},{1,9},{5... | collective-permute-start | bytes 786440 | tf_op jit(solution)/shard_map/ppermute | solution.py:36
  78.4 9.4 %collective-permute-start.21 = (bf16[512,256]{1,0:T(8,128)(2,1)S(1)}, bf16[512,256]{1,0:T(8,128)(2,1)S(1)}, u32[]{:S(2)}, u32[]{:S(2)}) collective-permute-start(bf16[512,256]{1,0:T(8,128)(2,1)S(1)} %get-tuple-element.16), channel_id=1, source_target_pairs={{0,4},{4,0},{8,12},{12,8},{16,20},{20,16},{24,28},{28,24},{1,5},{5... | collective-permute-start | bytes 786440 | tf_op jit(solution)/shard_map/ppermute | solution.py:36
  78.4 9.4 %collective-permute-start.32 = (bf16[512,256]{1,0:T(8,128)(2,1)S(1)}, bf16[512,256]{1,0:T(8,128)(2,1)S(1)}, u32[]{:S(2)}, u32[]{:S(2)}) collective-permute-start(bf16[512,256]{1,0:T(8,128)(2,1)S(1)} %get-tuple-element.17), channel_id=1, source_target_pairs={{0,4},{4,0},{8,12},{12,8},{16,20},{20,16},{24,28},{28,24},{1,5},{5... | collective-permute-start | bytes 786440 | tf_op jit(solution)/shard_map/ppermute | solution.py:36
  78.9 8.9 %collective-permute-start.29 = (bf16[512,256]{1,0:T(8,128)(2,1)S(1)}, bf16[512,256]{1,0:T(8,128)(2,1)S(1)}, u32[]{:S(2)}, u32[]{:S(2)}) collective-permute-start(bf16[512,256]{1,0:T(8,128)(2,1)S(1)} %get-tuple-element.19), channel_id=1, source_target_pairs={{0,4},{4,0},{8,12},{12,8},{16,20},{20,16},{24,28},{28,24},{1,5},{5... | collective-permute-start | bytes 786440 | tf_op jit(solution)/shard_map/ppermute | solution.py:36
  78.9 12.0 %collective-permute-start.23 = (bf16[512,256]{1,0:T(8,128)(2,1)S(1)}, bf16[512,256]{1,0:T(8,128)(2,1)S(1)}, u32[]{:S(2)}, u32[]{:S(2)}) collective-permute-start(bf16[512,256]{1,0:T(8,128)(2,1)S(1)} %get-tuple-element.24), channel_id=1, source_target_pairs={{0,8},{4,12},{8,0},{12,4},{16,24},{20,28},{24,16},{28,20},{1,9},{5... | collective-permute-start | bytes 786440 | tf_op jit(solution)/shard_map/ppermute | solution.py:36
  86.1 6.8 %collective-permute-start.27 = (bf16[512,256]{1,0:T(8,128)(2,1)S(1)}, bf16[512,256]{1,0:T(8,128)(2,1)S(1)}, u32[]{:S(2)}, u32[]{:S(2)}) collective-permute-start(bf16[512,256]{1,0:T(8,128)(2,1)S(1)} %add_convert_fusion.7), channel_id=1, source_target_pairs={{0,16},{4,20},{8,24},{12,28},{16,0},{20,4},{24,8},{28,12},{1,17},{... | collective-permute-start | bytes 786440 | tf_op jit(solution)/shard_map/ppermute | solution.py:36
  87.7 7.5 %collective-permute-start.31 = (bf16[512,256]{1,0:T(8,128)(2,1)S(1)}, bf16[512,256]{1,0:T(8,128)(2,1)S(1)}, u32[]{:S(2)}, u32[]{:S(2)}) collective-permute-start(bf16[512,256]{1,0:T(8,128)(2,1)S(1)} %get-tuple-element.18), channel_id=1, source_target_pairs={{0,4},{4,0},{8,12},{12,8},{16,20},{20,16},{24,28},{28,24},{1,5},{5... | collective-permute-start | bytes 786440 | tf_op jit(solution)/shard_map/ppermute | solution.py:36
  93.2 17.0 %copy-start.5 = (f32[1024,256]{1,0:T(8,128)S(1)}, f32[1024,256]{1,0:T(8,128)}, u32[]{:S(2)}) copy-start(f32[1024,256]{1,0:T(8,128)} %param.16) | copy-start | bytes 3145732
  93.2 8.2 %collective-permute-start.33 = (bf16[512,256]{1,0:T(8,128)(2,1)S(1)}, bf16[512,256]{1,0:T(8,128)(2,1)S(1)}, u32[]{:S(2)}, u32[]{:S(2)}) collective-permute-start(bf16[512,256]{1,0:T(8,128)(2,1)S(1)} %get-tuple-element.14), channel_id=1, source_target_pairs={{0,16},{4,20},{8,24},{12,28},{16,0},{20,4},{24,8},{28,12},{1,17},{... | collective-permute-start | bytes 786440 | tf_op jit(solution)/shard_map/ppermute | solution.py:36
  94.8 9.0 %collective-permute-start.28 = (bf16[512,256]{1,0:T(8,128)(2,1)S(1)}, bf16[512,256]{1,0:T(8,128)(2,1)S(1)}, u32[]{:S(2)}, u32[]{:S(2)}) collective-permute-start(bf16[512,256]{1,0:T(8,128)(2,1)S(1)} %get-tuple-element.20), channel_id=1, source_target_pairs={{0,4},{4,0},{8,12},{12,8},{16,20},{20,16},{24,28},{28,24},{1,5},{5... | collective-permute-start | bytes 786440 | tf_op jit(solution)/shard_map/ppermute | solution.py:36
  94.8 10.6 %collective-permute-start.30 = (bf16[512,256]{1,0:T(8,128)(2,1)S(1)}, bf16[512,256]{1,0:T(8,128)(2,1)}, u32[]{:S(2)}, u32[]{:S(2)}) collective-permute-start(bf16[512,256]{1,0:T(8,128)(2,1)S(1)} %get-tuple-element.15), channel_id=1, source_target_pairs={{0,16},{4,20},{8,24},{12,28},{16,0},{20,4},{24,8},{28,12},{1,17},{... | collective-permute-start | bytes 786440 | tf_op jit(solution)/shard_map/ppermute | solution.py:36
  102.2 6.7 %collective-permute-start.34 = (bf16[512,256]{1,0:T(8,128)(2,1)}, bf16[512,256]{1,0:T(8,128)(2,1)}, u32[]{:S(2)}, u32[]{:S(2)}) collective-permute-start(bf16[512,256]{1,0:T(8,128)(2,1)} %add_convert_fusion.1), channel_id=1, source_target_pairs={{0,8},{4,12},{8,0},{12,4},{16,24},{20,28},{24,16},{28,20},{1,9},{5... | collective-permute-start | bytes 786440 | tf_op jit(solution)/shard_map/ppermute | solution.py:36
  103.7 6.5 %copy-start.6 = (f32[1024,256]{1,0:T(8,128)S(1)}, f32[1024,256]{1,0:T(8,128)}, u32[]{:S(2)}) copy-start(f32[1024,256]{1,0:T(8,128)} %param.17) | copy-start | bytes 3145732
  114.5 4.6 %collective-permute-start.14 = (bf16[512,256]{1,0:T(8,128)(2,1)}, bf16[512,256]{1,0:T(8,128)(2,1)}, u32[]{:S(2)}, u32[]{:S(2)}) collective-permute-start(bf16[512,256]{1,0:T(8,128)(2,1)} %get-tuple-element.36), channel_id=1, source_target_pairs={{0,4},{4,0},{8,12},{12,8},{16,20},{20,16},{24,28},{28,24},{1,5},{5... | collective-permute-start | bytes 786440 | tf_op jit(solution)/shard_map/ppermute | solution.py:36
  114.5 9.4 %collective-permute-start.15 = (bf16[512,256]{1,0:T(8,128)(2,1)}, bf16[512,256]{1,0:T(8,128)(2,1)}, u32[]{:S(2)}, u32[]{:S(2)}) collective-permute-start(bf16[512,256]{1,0:T(8,128)(2,1)} %get-tuple-element.36), channel_id=1, source_target_pairs={{0,8},{4,12},{8,0},{12,4},{16,24},{20,28},{24,16},{28,20},{1,9},{5... | collective-permute-start | bytes 786440 | tf_op jit(solution)/shard_map/ppermute | solution.py:36
  116.0 9.9 %collective-permute-start.17 = (bf16[512,256]{1,0:T(8,128)(2,1)}, bf16[512,256]{1,0:T(8,128)(2,1)}, u32[]{:S(2)}, u32[]{:S(2)}) collective-permute-start(bf16[512,256]{1,0:T(8,128)(2,1)} %get-tuple-element.36), channel_id=1, source_target_pairs={{0,16},{4,20},{8,24},{12,28},{16,0},{20,4},{24,8},{28,12},{1,17},{... | collective-permute-start | bytes 786440 | tf_op jit(solution)/shard_map/ppermute | solution.py:36
  118.5 7.9 %collective-permute-start.7 = (bf16[512,256]{1,0:T(8,128)(2,1)}, bf16[512,256]{1,0:T(8,128)(2,1)}, u32[]{:S(2)}, u32[]{:S(2)}) collective-permute-start(bf16[512,256]{1,0:T(8,128)(2,1)} %get-tuple-element.33), channel_id=1, source_target_pairs={{0,4},{4,0},{8,12},{12,8},{16,20},{20,16},{24,28},{28,24},{1,5},{5... | collective-permute-start | bytes 786440 | tf_op jit(solution)/shard_map/ppermute | solution.py:36
  118.5 10.5 %collective-permute-start.8 = (bf16[512,256]{1,0:T(8,128)(2,1)}, bf16[512,256]{1,0:T(8,128)(2,1)S(1)}, u32[]{:S(2)}, u32[]{:S(2)}) collective-permute-start(bf16[512,256]{1,0:T(8,128)(2,1)} %get-tuple-element.33), channel_id=1, source_target_pairs={{0,8},{4,12},{8,0},{12,4},{16,24},{20,28},{24,16},{28,20},{1,9},{5... | collective-permute-start | bytes 786440 | tf_op jit(solution)/shard_map/ppermute | solution.py:36
  119.1 12.4 %collective-permute-start.10 = (bf16[512,256]{1,0:T(8,128)(2,1)}, bf16[512,256]{1,0:T(8,128)(2,1)S(1)}, u32[]{:S(2)}, u32[]{:S(2)}) collective-permute-start(bf16[512,256]{1,0:T(8,128)(2,1)} %get-tuple-element.33), channel_id=1, source_target_pairs={{0,16},{4,20},{8,24},{12,28},{16,0},{20,4},{24,8},{28,12},{1,17},{... | collective-permute-start | bytes 786440 | tf_op jit(solution)/shard_map/ppermute | solution.py:36
  123.9 10.1 %collective-permute-start.16 = (bf16[512,256]{1,0:T(8,128)(2,1)}, bf16[512,256]{1,0:T(8,128)(2,1)S(1)}, u32[]{:S(2)}, u32[]{:S(2)}) collective-permute-start(bf16[512,256]{1,0:T(8,128)(2,1)} %collective-permute-done.15), channel_id=1, source_target_pairs={{0,4},{4,0},{8,12},{12,8},{16,20},{20,16},{24,28},{28,24},{1,5},{5... | collective-permute-start | bytes 786440 | tf_op jit(solution)/shard_map/ppermute | solution.py:36
  125.9 9.8 %collective-permute-start.18 = (bf16[512,256]{1,0:T(8,128)(2,1)}, bf16[512,256]{1,0:T(8,128)(2,1)S(1)}, u32[]{:S(2)}, u32[]{:S(2)}) collective-permute-start(bf16[512,256]{1,0:T(8,128)(2,1)} %collective-permute-done.17), channel_id=1, source_target_pairs={{0,4},{4,0},{8,12},{12,8},{16,20},{20,16},{24,28},{28,24},{1,5},{5... | collective-permute-start | bytes 786440 | tf_op jit(solution)/shard_map/ppermute | solution.py:36
  126.5 8.9 %collective-permute-start.19 = (bf16[512,256]{1,0:T(8,128)(2,1)}, bf16[512,256]{1,0:T(8,128)(2,1)S(1)}, u32[]{:S(2)}, u32[]{:S(2)}) collective-permute-start(bf16[512,256]{1,0:T(8,128)(2,1)} %collective-permute-done.17), channel_id=1, source_target_pairs={{0,8},{4,12},{8,0},{12,4},{16,24},{20,28},{24,16},{28,20},{1,9},{5... | collective-permute-start | bytes 786440 | tf_op jit(solution)/shard_map/ppermute | solution.py:36
  129.0 6.8 %collective-permute-start.9 = (bf16[512,256]{1,0:T(8,128)(2,1)S(1)}, bf16[512,256]{1,0:T(8,128)(2,1)S(1)}, u32[]{:S(2)}, u32[]{:S(2)}) collective-permute-start(bf16[512,256]{1,0:T(8,128)(2,1)S(1)} %collective-permute-done.8), channel_id=1, source_target_pairs={{0,4},{4,0},{8,12},{12,8},{16,20},{20,16},{24,28},{28,24},{1,5},{5... | collective-permute-start | bytes 786440 | tf_op jit(solution)/shard_map/ppermute | solution.py:36
  131.5 9.5 %collective-permute-start.12 = (bf16[512,256]{1,0:T(8,128)(2,1)S(1)}, bf16[512,256]{1,0:T(8,128)(2,1)S(1)}, u32[]{:S(2)}, u32[]{:S(2)}) collective-permute-start(bf16[512,256]{1,0:T(8,128)(2,1)S(1)} %collective-permute-done.8), channel_id=1, source_target_pairs={{0,16},{4,20},{8,24},{12,28},{16,0},{20,4},{24,8},{28,12},{1,17},{... | collective-permute-start | bytes 786440 | tf_op jit(solution)/shard_map/ppermute | solution.py:36
  134.0 7.0 %collective-permute-start.11 = (bf16[512,256]{1,0:T(8,128)(2,1)S(1)}, bf16[512,256]{1,0:T(8,128)(2,1)S(1)}, u32[]{:S(2)}, u32[]{:S(2)}) collective-permute-start(bf16[512,256]{1,0:T(8,128)(2,1)S(1)} %collective-permute-done.10), channel_id=1, source_target_pairs={{0,4},{4,0},{8,12},{12,8},{16,20},{20,16},{24,28},{28,24},{1,5},{5... | collective-permute-start | bytes 786440 | tf_op jit(solution)/shard_map/ppermute | solution.py:36
  134.2 8.3 %copy-start.14 = (bf16[512,2048]{1,0:T(8,128)(2,1)S(1)}, bf16[512,2048]{1,0:T(8,128)(2,1)}, u32[]{:S(2)}) copy-start(bf16[512,2048]{1,0:T(8,128)(2,1)} %copy-done.13) | copy-start | bytes 6291460
  135.4 7.1 %collective-permute-start.20 = (bf16[512,256]{1,0:T(8,128)(2,1)S(1)}, bf16[512,256]{1,0:T(8,128)(2,1)S(1)}, u32[]{:S(2)}, u32[]{:S(2)}) collective-permute-start(bf16[512,256]{1,0:T(8,128)(2,1)S(1)} %collective-permute-done.19), channel_id=1, source_target_pairs={{0,4},{4,0},{8,12},{12,8},{16,20},{20,16},{24,28},{28,24},{1,5},{5... | collective-permute-start | bytes 786440 | tf_op jit(solution)/shard_map/ppermute | solution.py:36
  140.9 7.1 %collective-permute-start.13 = (bf16[512,256]{1,0:T(8,128)(2,1)S(1)}, bf16[512,256]{1,0:T(8,128)(2,1)S(1)}, u32[]{:S(2)}, u32[]{:S(2)}) collective-permute-start(bf16[512,256]{1,0:T(8,128)(2,1)S(1)} %collective-permute-done.12), channel_id=1, source_target_pairs={{0,4},{4,0},{8,12},{12,8},{16,20},{20,16},{24,28},{28,24},{1,5},{5... | collective-permute-start | bytes 786440 | tf_op jit(solution)/shard_map/ppermute | solution.py:36
  142.5 2.3 %copy-start.3 = (bf16[4,128,1024]{2,1,0:T(8,128)(2,1)S(1)}, bf16[4,128,1024]{2,1,0:T(8,128)(2,1)}, u32[]{:S(2)}) copy-start(bf16[4,128,1024]{2,1,0:T(8,128)(2,1)} %copy-done.2) | copy-start | bytes 3145732
  148.8 4.0 %copy-start.4 = (bf16[4,128,1024]{2,1,0:T(8,128)(2,1)S(1)}, bf16[4,128,1024]{2,1,0:T(8,128)(2,1)}, u32[]{:S(2)}) copy-start(bf16[4,128,1024]{2,1,0:T(8,128)(2,1)} %copy-done.2) | copy-start | bytes 3145732
  152.8 8.9 %copy-start.9 = (bf16[4,128,512]{2,1,0:T(8,128)(2,1)S(1)}, bf16[4,128,512]{2,1,0:T(8,128)(2,1)}, u32[]{:S(2)}) copy-start(bf16[4,128,512]{2,1,0:T(8,128)(2,1)} %slice.132) | copy-start | bytes 1572868
  158.3 9.8 %all-to-all-start.3 = ((bf16[4,32,512]{2,1,0:T(8,128)(2,1)}), bf16[4,32,512]{2,1,0:T(8,128)(2,1)S(1)}, u32[]{:S(2)}, u32[]{:S(2)}) async-start(bf16[4,32,512]{2,1,0:T(8,128)(2,1)} %broadcast_in_dim.19), calls=%async_computation.3 | async-start | bytes 262144 | tf_op jit(solution)/shard_map/all_to_all | solution.py:151
  168.1 29.0 %all-to-all-start.1 = ((bf16[4,128,1024]{2,1,0:T(8,128)(2,1)}), bf16[4,128,1024]{2,1,0:T(8,128)(2,1)S(1)}, u32[]{:S(2)}, u32[]{:S(2)}) async-start(bf16[4,128,1024]{2,1,0:T(8,128)(2,1)} %bitcast.5), calls=%async_computation.1 | async-start | bytes 2097152 | tf_op jit(solution)/shard_map/all_to_all | solution.py:149
  171.6 11.1 %copy-start.10 = (f32[64,512]{1,0:T(8,128)S(1)}, f32[64,512]{1,0:T(8,128)}, u32[]{:S(2)}) copy-start(f32[64,512]{1,0:T(8,128)} %param.19) | copy-start | bytes 393220
  171.7 11.1 %copy-start.11 = (f32[64,512]{1,0:T(8,128)S(1)}, f32[64,512]{1,0:T(8,128)}, u32[]{:S(2)}) copy-start(f32[64,512]{1,0:T(8,128)} %param.20) | copy-start | bytes 393220
  171.7 11.1 %copy-start.12 = (f32[64,512]{1,0:T(8,128)S(1)}, f32[64,512]{1,0:T(8,128)}, u32[]{:S(2)}) copy-start(f32[64,512]{1,0:T(8,128)} %param.21) | copy-start | bytes 393220
  172.4 1.3 collective-permute-start.36
  172.5 1.4 collective-permute-start.39
  173.0 3.1 %collective-permute-start.38 = (bf16[64,512]{1,0:T(8,128)(2,1)S(1)}, bf16[64,512]{1,0:T(8,128)(2,1)S(1)}, u32[]{:S(2)}, u32[]{:S(2)}) collective-permute-start(bf16[64,512]{1,0:T(8,128)(2,1)S(1)} %get-tuple-element.29), channel_id=1, source_target_pairs={{0,4},{4,0},{8,12},{12,8},{16,20},{20,16},{24,28},{28,24},{1,5},{5... | collective-permute-start | bytes 196616 | tf_op jit(solution)/shard_map/ppermute | solution.py:36
  173.9 4.4 %collective-permute-start.40 = (bf16[64,512]{1,0:T(8,128)(2,1)S(1)}, bf16[64,512]{1,0:T(8,128)(2,1)S(1)}, u32[]{:S(2)}, u32[]{:S(2)}) collective-permute-start(bf16[64,512]{1,0:T(8,128)(2,1)S(1)} %get-tuple-element.32), channel_id=1, source_target_pairs={{0,8},{4,12},{8,0},{12,4},{16,24},{20,28},{24,16},{28,20},{1,9},{5... | collective-permute-start | bytes 196616 | tf_op jit(solution)/shard_map/ppermute | solution.py:36
  175.5 4.7 %collective-permute-start.35 = (bf16[64,512]{1,0:T(8,128)(2,1)S(1)}, bf16[64,512]{1,0:T(8,128)(2,1)S(1)}, u32[]{:S(2)}, u32[]{:S(2)}) collective-permute-start(bf16[64,512]{1,0:T(8,128)(2,1)S(1)} %get-tuple-element.27), channel_id=1, source_target_pairs={{0,4},{4,0},{8,12},{12,8},{16,20},{20,16},{24,28},{28,24},{1,5},{5... | collective-permute-start | bytes 196616 | tf_op jit(solution)/shard_map/ppermute | solution.py:36
  175.6 4.6 %collective-permute-start.37 = (bf16[64,512]{1,0:T(8,128)(2,1)S(1)}, bf16[64,512]{1,0:T(8,128)(2,1)S(1)}, u32[]{:S(2)}, u32[]{:S(2)}) collective-permute-start(bf16[64,512]{1,0:T(8,128)(2,1)S(1)} %get-tuple-element.31), channel_id=1, source_target_pairs={{0,8},{4,12},{8,0},{12,4},{16,24},{20,28},{24,16},{28,20},{1,9},{5... | collective-permute-start | bytes 196616 | tf_op jit(solution)/shard_map/ppermute | solution.py:36
  178.4 4.3 %collective-permute-start.41 = (bf16[64,512]{1,0:T(8,128)(2,1)S(1)}, bf16[64,512]{1,0:T(8,128)(2,1)S(1)}, u32[]{:S(2)}, u32[]{:S(2)}) collective-permute-start(bf16[64,512]{1,0:T(8,128)(2,1)S(1)} %add_convert_fusion.13), channel_id=1, source_target_pairs={{0,16},{4,20},{8,24},{12,28},{16,0},{20,4},{24,8},{28,12},{1,17},{... | collective-permute-start | bytes 196616 | tf_op jit(solution)/shard_map/ppermute | solution.py:36

commit v2 on v0

v2 whole, which is shorter than its diff:
```python
import functools

import jax
import jax.numpy as jnp
from jax import lax
from jax.experimental import pallas as pl
from jax.experimental.pallas import tpu as pltpu
from jax.sharding import PartitionSpec as P

MODEL_WIDTH = 4096
ADAPTER_RANK = 32
TEN_DEV = 8
LANES = 128
ROW_STEP = 512
LABEL_ROWS = 16

adapter_scale = 2.0
learn_rate = 0.02
beta_one = 0.9
beta_two = 0.999
adam_eps = 1e-08
bias_one = 1.0 - 0.9**10
bias_two = 1.0 - 0.999**10

f32 = jnp.float32
bf16 = jnp.bfloat16
ANY = pl.BlockSpec(memory_space=pl.ANY)
VMEM = pl.BlockSpec(memory_space=pltpu.VMEM)


def shape(dims, kind=bf16):
    return jax.ShapeDtypeStruct(tuple(dims), kind)


def call(body, outs, ins, scratch=(), in_specs=None, cost=0):
    return pl.pallas_call(
        body,
        out_shape=outs,
        in_specs=in_specs or [VMEM] * len(ins),
        out_specs=jax.tree.map(lambda _: VMEM, outs),
        scratch_shapes=list(scratch),
        compiler_params=pltpu.CompilerParams(vmem_limit_bytes=48 << 20),
        cost_estimate=pl.CostEstimate(flops=cost, bytes_accessed=cost, transcendentals=0),
    )(*ins)


def adam_step(param, moment, second, gradient):
    moment = beta_one * moment + (1.0 - beta_one) * gradient
    second = beta_two * second + (1.0 - beta_two) * gradient * gradient
    param = param - learn_rate * (moment / bias_one) / (jnp.sqrt(second / bias_two) + adam_eps)
    return (param, moment, second)


def dot(left, right, left_dim=1, right_dim=0):
    return lax.dot_general(
        left, right, (((left_dim,), (right_dim,)), ((), ())), preferred_element_type=f32
    )


def iota(dims, axis):
    return lax.broadcasted_iota(jnp.int32, dims, axis)


def column_of(row, lanes=LANES):
    n = row.shape[1]
    wide = jnp.broadcast_to(row.astype(f32), (lanes, n))
    return jnp.transpose(wide)


def prep_kernel(cot, tenant, advantage, a_param, b_param, share, a_low, b_low):
    rows, keys = cot.shape
    factor = column_of(advantage[...]) * 0.25
    factor = jnp.concatenate([factor] * (keys // LANES), axis=1)
    share[:rows] = (cot[...].astype(f32) * factor).astype(bf16)
    t = tenant[...]
    line = iota((LABEL_ROWS, rows), 0)
    owner = jnp.broadcast_to(lax.div(t, TEN_DEV), (LABEL_ROWS, rows))
    local = jnp.broadcast_to(lax.rem(t, TEN_DEV), (LABEL_ROWS, rows))
    labels = jnp.where(line == 0, owner, jnp.where(line == 1, local, 0)).astype(f32)
    share[rows:, :rows] = labels.astype(bf16)
    share[rows:, rows:] = jnp.zeros((LABEL_ROWS, keys - rows), bf16)
    a_low[...] = (a_param[...] * MODEL_WIDTH ** (-0.5)).astype(bf16)
    b_low[...] = (b_param[...] * ADAPTER_RANK ** (-0.5)).astype(bf16)


def second_ids(owners, own_rows, rows):
    line = iota((owners * own_rows, rows), 0)
    inner = lax.rem(line, own_rows) + lax.axis_index("fsdp") * own_rows
    return lax.div(line, own_rows) * TEN_DEV + lax.div(inner, ADAPTER_RANK)


def back_kernel(shards, owners, *refs):
    shares, b_blocks = refs[:shards], refs[shards : shards + owners]
    scaled, label, back, b_all = refs[shards + owners :]
    rd = shares[0].shape[0] - LABEL_ROWS
    own_rows = b_blocks[0].shape[0]
    me, place = lax.axis_index("dp"), lax.axis_index("fsdp")
    for j in range(shards):
        at = pl.ds(pl.multiple_of((place ^ j) * rd, rd), rd)
        scaled[at] = shares[j][:rd]
        ids = shares[j][rd:, :rd].astype(f32).astype(jnp.int32)
        tid = (ids[0:1] ^ me) * TEN_DEV + ids[1:2]
        label[:, at] = jnp.broadcast_to(tid, (8, rd))
    for k in range(owners):
        b_all[k * own_rows : (k + 1) * own_rows] = b_blocks[k][...]
    rows = scaled.shape[0]
    step = min(ROW_STEP, rows)
    ids = second_ids(owners, own_rows, step)
    for r in range(0, rows, step):
        wide = dot(b_all[...], scaled[r : r + step], 1, 1)
        wide = jnp.where(ids == label[0:1, r : r + step], wide, 0.0)
        if own_rows >= ADAPTER_RANK:
            low = jnp.sum(wide.reshape(-1, ADAPTER_RANK, step), axis=0)
        else:
            low = jnp.sum(wide.reshape(-1, own_rows, step), axis=0)
            low = jnp.concatenate([low] * (ADAPTER_RANK // own_rows), axis=0)
            part = lax.div(iota(low.shape, 0), own_rows)
            low = jnp.where(part == lax.rem(place, ADAPTER_RANK // own_rows), low, 0.0)
        back[:, r : r + step] = low.astype(bf16)


def total(parts, at):
    value = parts[0][:, at].astype(f32)
    for part in parts[1:]:
        value = value + part[:, at].astype(f32)
    return value


def load_factors(a_blocks, a_all, sems):
    columns = a_blocks[0].shape[1]
    copies = [
        pltpu.make_async_copy(
            block, a_all.at[:, k * columns : (k + 1) * columns], sems.at[k]
        )
        for k, block in enumerate(a_blocks)
    ]
    for copy in copies:
        copy.start()
    return copies


def side_kernel(shards, owners, *refs):
    backs, a_blocks = refs[:shards], refs[shards : shards + owners]
    label, scaled, weight, out, a_all, back_wide, sems = refs[shards + owners :]
    copies = load_factors(a_blocks, a_all, sems)
    rows, features = out.shape
    step = min(ROW_STEP, rows)
    width = a_all.shape[1]
    for r in range(0, rows, step):
        at = slice(r, r + step)
        low = adapter_scale * jnp.transpose(total(backs, at))
        low = jnp.concatenate([low] * (LANES // ADAPTER_RANK), axis=1)
        where = column_of(label[0:1, at]).astype(jnp.int32) - lax.div(
            iota((step, LANES), 1), ADAPTER_RANK
        )
        for q in range(width // LANES):
            hit = where == q * (LANES // ADAPTER_RANK)
            back_wide[:, q * LANES : (q + 1) * LANES] = jnp.where(hit, low, 0.0).astype(bf16)
        if r == 0:
            for copy in copies:
                copy.wait()
        chunk = min(256, features)
        for c in range(0, features, chunk):
            base = dot(scaled[at], weight[c : c + chunk], 1, 1).astype(bf16)
            side = dot(back_wide[...], a_all[c : c + chunk], 1, 1).astype(bf16)
            out[at, c : c + chunk] = (base.astype(f32) + side.astype(f32)).astype(bf16)


def spread(low, label, k, columns):
    rows = low.shape[1]
    ids = lax.div(iota((columns, rows), 0), ADAPTER_RANK) + k * TEN_DEV
    tall = jnp.concatenate([low] * (columns // ADAPTER_RANK), axis=0)
    return jnp.where(ids == label, tall, 0.0).astype(bf16)


def first_kernel(shards, owners, parity, *refs):
    backs = refs[:shards]
    label, acts = refs[shards : shards + 2]
    arrived = refs[shards + 2] if parity == 0 else None
    outs = refs[shards + 2 + (parity == 0) :]
    coefficient = adapter_scale * MODEL_WIDTH ** (-0.5)
    low = total(backs, slice(None))
    for n in range(owners // 2):
        k = 2 * n + parity
        columns = outs[0].shape[-2]
        grad = coefficient * dot(spread(low, label[0:1], k, columns), acts[...])
        if parity:
            outs[0][n] = grad.astype(bf16)
        else:
            outs[n][...] = (grad + arrived[n].astype(f32)).astype(bf16)


def mid_kernel(owners, *refs):
    a_blocks = refs[:owners]
    label, acts, out, a_all, sems = refs[owners:]
    copies = load_factors(a_blocks, a_all, sems)
    rows = acts.shape[0]
    columns = a_blocks[0].shape[1]
    step = min(ROW_STEP, rows)
    for r in range(0, rows, step):
        at = slice(r, r + step)
        where = column_of(label[0:1, at]).astype(jnp.int32) - lax.div(
            iota((step, LANES), 1), ADAPTER_RANK
        )
        low = jnp.zeros((step, LANES), f32)
        for k in range(owners):
            if r == 0:
                copies[k].wait()
            wide = dot(acts[at], a_all[:, k * columns : (k + 1) * columns])
            for q in range(columns // LANES):
                hit = where == k * TEN_DEV + q * (LANES // ADAPTER_RANK)
                low = low + jnp.where(hit, wide[:, q * LANES : (q + 1) * LANES], 0.0)
        low = jnp.transpose(low).reshape(LANES // ADAPTER_RANK, ADAPTER_RANK, step)
        out[:, at] = jnp.sum(low, axis=0).astype(bf16)


def second_kernel(shards, owners, *refs):
    mids = refs[:shards]
    label, scaled, out, held = refs[shards:]
    own_rows, keys = out.shape[1:]
    rows = scaled.shape[0]
    step = min(ROW_STEP, rows)
    coefficient = adapter_scale * ADAPTER_RANK ** (-0.5)
    ids = second_ids(owners, own_rows, step)
    grad = jnp.zeros((owners * own_rows, keys), f32)
    for r in range(0, rows, step):
        at = slice(r, r + step)
        held[...] = total(mids, at)
        if own_rows >= ADAPTER_RANK:
            low = jnp.concatenate([held[...]] * (owners * own_rows // ADAPTER_RANK), axis=0)
        else:
            first = lax.rem(lax.axis_index("fsdp") * own_rows, ADAPTER_RANK)
            low = held[pl.ds(pl.multiple_of(first, own_rows), own_rows)]
            low = jnp.concatenate([low] * owners, axis=0)
        low = jnp.where(ids == label[0:1, at], low, 0.0).astype(bf16)
        grad = grad + dot(low, scaled[at])
    grad = (coefficient * grad).astype(bf16)
    for k in range(owners):
        out[k] = grad[k * own_rows : (k + 1) * own_rows]


def adam_a_kernel(count, *refs):
    grads, (param, moment, second), outs = refs[:count], refs[count : count + 3], refs[count + 3 :]
    grad = grads[0][...].astype(f32)
    for part in grads[1:]:
        grad = grad + part[...].astype(f32)
    new = adam_step(param[...], moment[...], second[...], jnp.transpose(grad))
    for out, value in zip(outs, new):
        out[...] = value


def adam_b_kernel(count, *refs):
    grads, (param, moment, second), outs = refs[:count], refs[count : count + 3], refs[count + 3 :]
    grad = grads[0][...].astype(f32)
    for part in grads[1:]:
        grad = grad + part[...].astype(f32)
    for out, value in zip(outs, adam_step(param[...], moment[...], second[...], grad)):
        out[...] = value


def swap(block, axis, bits):
    size = lax.axis_size(axis)
    return lax.ppermute(block, axis, [(i, i ^ bits) for i in range(size)])


def per_device(
    acts,
    cotangent,
    tenant,
    advantage,
    base_weight,
    a_param,
    a_moment,
    a_second,
    b_param,
    b_moment,
    b_second,
):
    owners = lax.axis_size("dp")
    shards = lax.axis_size("fsdp")
    row_count, keys = cotangent.shape
    features, columns = a_param.shape
    own_rows = b_param.shape[0]
    rows = row_count * shards

    share, a_low, b_low = call(
        prep_kernel,
        (shape((row_count + LABEL_ROWS, keys)), shape((features, columns)), shape((own_rows, keys))),
        (cotangent, tenant[None], advantage[None], a_param, b_param),
    )
    b_blocks = [b_low] + [swap(b_low, "dp", k) for k in range(1, owners)]
    shares = [share] + [swap(share, "fsdp", j) for j in range(1, shards)]
    chips = [a_low] + [swap(a_low, "dp", k) for k in range(2, owners, 2)]
    acts_part = lax.all_to_all(acts, "fsdp", split_axis=1, concat_axis=0, tiled=True)
    a_blocks = []
    for block in chips:
        a_blocks += [block, swap(block, "dp", 1)]

    scaled, label, back = call(
        functools.partial(back_kernel, shards, owners),
        (shape((rows, keys)), shape((8, rows), jnp.int32), shape((ADAPTER_RANK, rows))),
        (*shares, *b_blocks),
        [pltpu.VMEM((owners * own_rows, keys), bf16)],
    )
    backs = [back] + [swap(back, "fsdp", j) for j in range(1, shards)]

    step = min(ROW_STEP, rows)
    factor_scratch = [pltpu.VMEM((features, owners * columns), bf16)]
    sems = [pltpu.SemaphoreType.DMA((owners,))]
    grad_part = call(
        functools.partial(side_kernel, shards, owners),
        shape((rows, features)),
        (*backs, *a_blocks, label, scaled, base_weight),
        factor_scratch + [pltpu.VMEM((step, owners * columns), bf16)] + sems,
        [VMEM] * shards + [ANY] * owners + [VMEM] * 3,
    )
    grad_input = lax.all_to_all(grad_part, "fsdp", split_axis=0, concat_axis=1, tiled=True)

    odd = call(
        functools.partial(first_kernel, shards, owners, 1),
        shape((owners // 2, columns, features)),
        (*backs, label, acts_part),
    )
    even = call(
        functools.partial(first_kernel, shards, owners, 0),
        [shape((columns, features))] * (owners // 2),
        (*backs, label, acts_part, swap(odd, "dp", 1)),
    )
    grad_a = [even[0]] + [swap(even[n], "dp", 2 * n) for n in range(1, owners // 2)]

    mid = call(
        functools.partial(mid_kernel, owners),
        shape((ADAPTER_RANK, rows)),
        (*a_blocks, label, acts_part),
        factor_scratch + sems,
        [ANY] * owners + [VMEM] * 2,
    )
    mids = [mid] + [swap(mid, "fsdp", j) for j in range(1, shards)]
    grad_b = call(
        functools.partial(second_kernel, shards, owners),
        shape((owners, own_rows, keys)),
        (*mids, label, scaled),
        [pltpu.VMEM((ADAPTER_RANK, step), f32)],
    )
    grad_b = [grad_b[0]] + [swap(grad_b[k], "dp", k) for k in range(1, owners)]

    new_b = call(
        functools.partial(adam_b_kernel, owners),
        [shape(b_param.shape, f32)] * 3,
        (*grad_b, b_param, b_moment, b_second),
    )
    block = min(256, features)
    wide = pl.BlockSpec((columns, block), lambda i: (0, i))
    tall = pl.BlockSpec((block, columns), lambda i: (i, 0))
    new_a = pl.pallas_call(
        functools.partial(adam_a_kernel, owners // 2),
        grid=(features // block,),
        out_shape=[shape(a_param.shape, f32)] * 3,
        in_specs=[wide] * (owners // 2) + [tall] * 3,
        out_specs=[tall] * 3,
        compiler_params=pltpu.CompilerParams(vmem_limit_bytes=48 << 20),
    )(*grad_a, a_param, a_moment, a_second)
    return (grad_input, new_a[0], new_a[1], new_a[2], new_b[0], new_b[1], new_b[2])


def solution(mesh):
    rows = P(("dp", "fsdp"), None)
    labels = P(("dp", "fsdp"))
    first = P("fsdp", "dp")
    return jax.shard_map(
        per_device,
        mesh=mesh,
        in_specs=(rows, rows, labels, labels, P("fsdp", None), first, first, first, rows, rows, rows),
        out_specs=(rows, first, first, first, rows, rows, rows),
        check_vma=False,
    )
```

time: 267 us -> 156 us (0.58)
  waiting for transfers between devices: 138 us -> 71.3 us
  blocking collectives: 32.5 us -> 0 us
  Pallas kernels: 0 us -> 25.8 us
  starting transfers between devices: 22.9 us -> 47.4 us
  other arithmetic: 17.6 us -> 0 us
  local copies, waits for them, and re-layouts: 26.7 us -> 9.79 us
  matrix products: 13.7 us -> 0 us
  between operations: 14 us -> 0.94 us
    ppermute x0 -> x34, waiting for transfers between devices: none -> 71.3 us  [swap(): return lax.ppermute(block, axis, [(i, i ^ bits) for i in range(size)])]
    reduce_scatter x1 -> x0, waiting for transfers between devices: 43.4 us -> none  [per_device(): lax.psum_scatter((down_coefficient * contract_rows(recv_x, backward_proje...]
    all_gather x1 -> x0, waiting for transfers between devices: 43.1 us -> none  [per_device(): lax.all_gather(a_low, 'fsdp', axis=0, tiled=True)]
    ppermute x0 -> x34, starting transfers between devices: none -> 36.6 us  [swap(): return lax.ppermute(block, axis, [(i, i ^ bits) for i in range(size)])]
    all_gather x2 -> x0, blocking collectives: 32.5 us -> none  [the longest x1 18.4 us: per_device(): all_cots = lax.all_gather(scaled, 'fsdp', axis=0, tiled=True)]
    psum x1 -> x0, waiting for transfers between devices: 31.3 us -> none  [per_device(): total_b = lax.psum(term_b.astype(jnp.bfloat16), 'fsdp').astype(jnp.float32)]
    pallas_call x0 -> x9, Pallas kernels: none -> 25.8 us  [the longest x8 21.4 us: call(): pl.pallas_call(body, out_shape=outs, in_specs=in_specs or [VMEM] * len(in...]
    all_to_all x5 -> x2, waiting for transfers between devices: 20.6 us -> 0.01 us  [the longest x1 0.01 us: per_device(): lax.all_to_all(acts, 'fsdp', split_axis=1, concat_axis=0, tiled=True)]
  transfers between devices with their start and end apart: 8 -> 36, of which waited for: 5 -> 17; matrix products, arithmetic and copies ran while one was open for 11% -> 2% of each run, Pallas kernels for 0% -> 14%
where the time goes in v2:
time: 156 us; the launch traced here: 155 us
  waiting for transfers between devices  71.3 us (46%)
  starting transfers between devices  47.4 us (30%)
  Pallas kernels  25.8 us (17%)
  local copies, waits for them, and re-layouts  9.79 us (6%)
    ppermute x34, waiting for transfers between devices, swap(): return lax.ppermute(block, axis, [(i, i ^ bits) for i in range(size)])  71.3 us
    ppermute x34, starting transfers between devices, swap(): return lax.ppermute(block, axis, [(i, i ^ bits) for i in range(size)])  36.6 us
    pallas_call x8, Pallas kernels, call(): pl.pallas_call(body, out_shape=outs, in_specs=in_specs or [VMEM] * len(in...  21.4 us
    all_to_all x1, starting transfers between devices, per_device(): lax.all_to_all(acts, 'fsdp', split_axis=1, concat_axis=0, tiled=True)  6.32 us
    unnamed x44, local copies, waits for them, and re-layouts  5.03 us
    all_to_all x1, starting transfers between devices, per_device(): lax.all_to_all(grad_part, 'fsdp', split_axis=0, concat_axis=1, tiled=True)  4.44 us
    pallas_call x1, Pallas kernels, per_device(): pl.pallas_call(functools.partial(adam_a_kernel, owners // 2), grid=(featu...  4.4 us
  transfers between devices with their start and end apart: 36, of which 17 were waited for; matrix products, arithmetic and copies ran while one was open for 2% of the time, Pallas kernels for 14%

profile of v2, /device:TPU:0, one launch (start us, length us, event | category | flops | bytes accessed | tf_op | source)
XLA Modules:
  0.0 155.2 jit_solution(18347607218950102168)
XLA Ops:
  0.7 2.4 %copy.23 = bf16[16,4,8,1024]{3,2,0,1:T(8,128)(2,1)} copy(bf16[16,4,8,1024]{3,2,1,0:T(8,128)(2,1)} %bitcast.35) | data formatting | bytes 2097152 | tf_op jit(solution)/shard_map/all_to_all | solution.py:294
  3.1 6.3 %all-to-all-start.1 = ((bf16[128,4,1024]{2,0,1:T(8,128)(2,1)}), bf16[128,4,1024]{2,0,1:T(8,128)(2,1)S(1)}, u32[]{:S(2)}, u32[]{:S(2)}) async-start(bf16[128,4,1024]{2,0,1:T(8,128)(2,1)} %bitcast.34), calls=%async_computation.1 | async-start | bytes 2097152 | tf_op jit(solution)/shard_map/all_to_all | solution.py:294
  9.4 0.2 shard_map.162
  9.6 1.7 %collective-permute-start.9 = (bf16[64,512]{1,0:T(8,128)(2,1)S(1)}, bf16[64,512]{1,0:T(8,128)(2,1)S(1)}, u32[]{:S(2)}, u32[]{:S(2)}) collective-permute-start(bf16[64,512]{1,0:T(8,128)(2,1)S(1)} %get-tuple-element.24.refs_4_), channel_id=1, source_target_pairs={{0,28},{4,24},{8,20},{12,16},{16,12},{20,8},{24,4},{28,0},{1,29},{... | collective-permute-start | bytes 196616 | tf_op jit(solution)/shard_map/ppermute | solution.py:263
  11.2 0.9 collective-permute-start.8
  12.2 1.4 collective-permute-start.7
  13.5 3.8 %collective-permute-start.2 = (bf16[144,512]{1,0:T(8,128)(2,1)S(1)}, bf16[144,512]{1,0:T(8,128)(2,1)S(1)}, u32[]{:S(2)}, u32[]{:S(2)}) collective-permute-start(bf16[144,512]{1,0:T(8,128)(2,1)S(1)} %get-tuple-element.23.refs_0_), channel_id=1, source_target_pairs={{0,3},{1,2},{2,1},{3,0},{4,7},{5,6},{6,5},{7,4},{8,11},{9,10},{10,... | collective-permute-start | bytes 442376 | tf_op jit(solution)/shard_map/ppermute | solution.py:263
  17.4 0.6 collective-permute-start
  17.9 0.5 collective-permute-start.6
  18.4 0.3 collective-permute-start.5
  18.8 3.4 %collective-permute-done.6.refs_8_ = bf16[64,512]{1,0:T(8,128)(2,1)S(1)} collective-permute-done((bf16[64,512]{1,0:T(8,128)(2,1)S(1)}, bf16[64,512]{1,0:T(8,128)(2,1)S(1)}, u32[]{:S(2)}, u32[]{:S(2)}) %collective-permute-start.6) | collective-permute-done | bytes 65568 | tf_op jit(solution)/shard_map/ppermute | solution.py:263
  22.2 1.5 collective-permute-start.4
  23.7 2.8 %collective-permute-done.4.refs_6_ = bf16[64,512]{1,0:T(8,128)(2,1)S(1)} collective-permute-done((bf16[64,512]{1,0:T(8,128)(2,1)S(1)}, bf16[64,512]{1,0:T(8,128)(2,1)S(1)}, u32[]{:S(2)}, u32[]{:S(2)}) %collective-permute-start.4) | collective-permute-done | bytes 65568 | tf_op jit(solution)/shard_map/ppermute | solution.py:263
  26.5 8.7 %collective-permute-done.2.refs_3_ = bf16[144,512]{1,0:T(8,128)(2,1)S(1)} collective-permute-done((bf16[144,512]{1,0:T(8,128)(2,1)S(1)}, bf16[144,512]{1,0:T(8,128)(2,1)S(1)}, u32[]{:S(2)}, u32[]{:S(2)}) %collective-permute-start.2) | collective-permute-done | bytes 147488 | tf_op jit(solution)/shard_map/ppermute | solution.py:263
  35.1 12.6 %collective-permute-done.1.refs_2_ = bf16[144,512]{1,0:T(8,128)(2,1)S(1)} collective-permute-done((bf16[144,512]{1,0:T(8,128)(2,1)S(1)}, bf16[144,512]{1,0:T(8,128)(2,1)S(1)}, u32[]{:S(2)}, u32[]{:S(2)}) %collective-permute-start.1) | collective-permute-done | bytes 147488 | tf_op jit(solution)/shard_map/ppermute | solution.py:263
  47.8 0.5 shard_map.163
  48.3 0.0 copy-start.9
  48.3 0.8 copy-done.9
  49.1 1.5 collective-permute-start.12
  50.6 2.9 %collective-permute-start.10 = (bf16[32,512]{1,0:T(8,128)(2,1)S(1)}, bf16[32,512]{1,0:T(8,128)(2,1)S(1)}, u32[]{:S(2)}, u32[]{:S(2)}) collective-permute-start(bf16[32,512]{1,0:T(8,128)(2,1)S(1)} %get-tuple-element.25.refs_0_), channel_id=1, source_target_pairs={{0,1},{1,0},{2,3},{3,2},{4,5},{5,4},{6,7},{7,6},{8,9},{9,8},{10,11... | collective-permute-start | bytes 98312 | tf_op jit(solution)/shard_map/ppermute | solution.py:263
  53.5 2.4 %collective-permute-start.18 = (bf16[1024,256]{1,0:T(8,128)(2,1)S(1)}, bf16[1024,256]{1,0:T(8,128)(2,1)S(1)}, u32[]{:S(2)}, u32[]{:S(2)}) collective-permute-start(bf16[1024,256]{1,0:T(8,128)(2,1)S(1)} %get-tuple-element.26.refs_4_.refs_0_), channel_id=1, source_target_pairs={{0,24},{4,28},{8,16},{12,20},{16,8},{20,12},{24,0},{28,4},{1,25},{... | collective-permute-start | bytes 1572872 | tf_op jit(solution)/shard_map/ppermute | solution.py:263
  55.9 0.5 collective-permute-start.16
  56.4 0.5 collective-permute-start.14
  57.0 2.6 %shard_map.165 = bf16[4,256,1024]{2,1,0:T(8,128)(2,1)} custom-call(bf16[32,512]{1,0:T(8,128)(2,1)S(1)} %get-tuple-element.25.refs_0_, bf16[32,512]{1,0:T(8,128)(2,1)S(1)} %collective-permute-done.10.refs_1_, bf16[32,512]{1,0:T(8,128)(2,1)S(1)} %collective-permute-done.11.refs_2_, bf16[32,512]{1,0:T(8,128)(2,1)S(1)} %collective-permute-done.12.refs_3_, ...), custom_call_target="tpu_custom_call" | custom-call | tf_op jit(solution)/shard_map/pallas_call | solution.py:36
  59.6 0.5 collective-permute-start.13
  60.2 9.1 %collective-permute-done.18.refs_10_.refs_6_ = bf16[1024,256]{1,0:T(8,128)(2,1)S(1)} collective-permute-done((bf16[1024,256]{1,0:T(8,128)(2,1)S(1)}, bf16[1024,256]{1,0:T(8,128)(2,1)S(1)}, u32[]{:S(2)}, u32[]{:S(2)}) %collective-permute-start.18) | collective-permute-done | bytes 524320 | tf_op jit(solution)/shard_map/ppermute | solution.py:263
  69.3 8.5 %collective-permute-done.16.refs_8_.refs_4_ = bf16[1024,256]{1,0:T(8,128)(2,1)} collective-permute-done((bf16[1024,256]{1,0:T(8,128)(2,1)S(1)}, bf16[1024,256]{1,0:T(8,128)(2,1)}, u32[]{:S(2)}, u32[]{:S(2)}) %collective-permute-start.16) | collective-permute-done | bytes 524320 | tf_op jit(solution)/shard_map/ppermute | solution.py:263
  77.8 0.0 collective-permute-start.17
  77.8 0.1 collective-permute-done.14.refs_6_.refs_2_
  77.9 0.4 collective-permute-start.15
  78.3 1.6 %collective-permute-done.17.refs_9_.refs_5_ = bf16[1024,256]{1,0:T(8,128)(2,1)S(1)} collective-permute-done((bf16[1024,256]{1,0:T(8,128)(2,1)}, bf16[1024,256]{1,0:T(8,128)(2,1)S(1)}, u32[]{:S(2)}, u32[]{:S(2)}) %collective-permute-start.17) | collective-permute-done | bytes 524320 | tf_op jit(solution)/shard_map/ppermute | solution.py:263
  79.9 0.7 collective-permute-done.15.refs_7_.refs_3_
  80.7 6.7 %shard_map.164 = bf16[512,1024]{1,0:T(8,128)(2,1)} custom-call(bf16[32,512]{1,0:T(8,128)(2,1)S(1)} %get-tuple-element.25.refs_0_, bf16[32,512]{1,0:T(8,128)(2,1)S(1)} %collective-permute-done.10.refs_1_, bf16[32,512]{1,0:T(8,128)(2,1)S(1)} %collective-permute-done.11.refs_2_, bf16[32,512]{1,0:T(8,128)(2,1)S(1)} %collective-permute-done.12.refs_3_, ...), custom_call_target="tpu_custom_call" | custom-call | tf_op jit(solution)/shard_map/pallas_call | solution.py:36
  87.4 4.4 %all-to-all-start = ((bf16[4,128,1024]{2,1,0:T(8,128)(2,1)}), bf16[4,128,1024]{2,1,0:T(8,128)(2,1)}, u32[]{:S(2)}, u32[]{:S(2)}) async-start(bf16[4,128,1024]{2,1,0:T(8,128)(2,1)} %bitcast.2), calls=%async_computation | async-start | bytes 2097152 | tf_op jit(solution)/shard_map/all_to_all | solution.py:317
  91.9 1.0 copy-done.2
  92.9 1.0 copy-done.4
  94.0 1.0 copy-done.6
  95.0 1.0 copy-done.8
  96.1 6.3 %shard_map.168.refs_0_ = bf16[32,512]{1,0:T(8,128)(2,1)S(1)} custom-call(bf16[1024,256]{1,0:T(8,128)(2,1)S(1)} %get-tuple-element.26.refs_4_.refs_0_, bf16[1024,256]{1,0:T(8,128)(2,1)S(1)} %copy-done.2, bf16[1024,256]{1,0:T(8,128)(2,1)} %collective-permute-done.14.refs_6_.refs_2_, bf16[1024,256]{1,0:T(8,128)(2,1)S(1)} %copy-done.8, ...), custom_call_target="tpu_custom_call" | custom-call | tf_op jit(solution)/shard_map/pallas_call | solution.py:36
  102.4 3.7 %collective-permute-start.26 = (bf16[32,512]{1,0:T(8,128)(2,1)S(1)}, bf16[32,512]{1,0:T(8,128)(2,1)S(1)}, u32[]{:S(2)}, u32[]{:S(2)}) collective-permute-start(bf16[32,512]{1,0:T(8,128)(2,1)S(1)} %shard_map.168.refs_0_), channel_id=1, source_target_pairs={{0,3},{1,2},{2,1},{3,0},{4,7},{5,6},{6,5},{7,4},{8,11},{9,10},{10,... | collective-permute-start | bytes 98312 | tf_op jit(solution)/shard_map/ppermute | solution.py:263
  106.0 0.8 collective-permute-start.24
  106.8 3.7 %shard_map.166 = (bf16[256,1024]{1,0:T(8,128)(2,1)S(1)}, bf16[256,1024]{1,0:T(8,128)(2,1)}, bf16[256,1024]{1,0:T(8,128)(2,1)}, bf16[256,1024]{1,0:T(8,128)(2,1)}) custom-call(bf16[32,512]{1,0:T(8,128)(2,1)S(1)} %get-tuple-element.25.refs_0_, bf16[32,512]{1,0:T(8,128)(2,1)S(1)} %collective-permute-done.10.refs_1_, ...), custom_call_target="tpu_custom_call" | custom-call | tf_op jit(solution)/shard_map/pallas_call | solution.py:36
  110.6 1.5 collective-permute-start.21
  112.1 0.8 collective-permute-start.22
  112.9 1.9 %collective-permute-done.26.refs_3_ = bf16[32,512]{1,0:T(8,128)(2,1)S(1)} collective-permute-done((bf16[32,512]{1,0:T(8,128)(2,1)S(1)}, bf16[32,512]{1,0:T(8,128)(2,1)S(1)}, u32[]{:S(2)}, u32[]{:S(2)}) %collective-permute-start.26) | collective-permute-done | bytes 32800 | tf_op jit(solution)/shard_map/ppermute | solution.py:263
  114.7 1.7 %collective-permute-start.23 = (bf16[256,1024]{1,0:T(8,128)(2,1)}, bf16[256,1024]{1,0:T(8,128)(2,1)}, u32[]{:S(2)}, u32[]{:S(2)}) collective-permute-start(bf16[256,1024]{1,0:T(8,128)(2,1)} %get-tuple-element.32), channel_id=1, source_target_pairs={{0,24},{4,28},{8,16},{12,20},{16,8},{20,12},{24,0},{28,4},{1,25},{... | collective-permute-start | bytes 1572872 | tf_op jit(solution)/shard_map/ppermute | solution.py:263
  116.5 4.3 %collective-permute-done.25.refs_2_ = bf16[32,512]{1,0:T(8,128)(2,1)S(1)} collective-permute-done((bf16[32,512]{1,0:T(8,128)(2,1)S(1)}, bf16[32,512]{1,0:T(8,128)(2,1)S(1)}, u32[]{:S(2)}, u32[]{:S(2)}) %collective-permute-start.25) | collective-permute-done | bytes 32800 | tf_op jit(solution)/shard_map/ppermute | solution.py:263
  120.8 0.5 shard_map.169
  121.3 0.8 collective-permute-start.33
  122.2 1.2 collective-permute-start.32
  123.3 13.0 %collective-permute-done.33.refs_7_ = bf16[64,512]{1,0:T(8,128)(2,1)S(1)} collective-permute-done((bf16[64,512]{1,0:T(8,128)(2,1)S(1)}, bf16[64,512]{1,0:T(8,128)(2,1)S(1)}, u32[]{:S(2)}, u32[]{:S(2)}) %collective-permute-start.33) | collective-permute-done | bytes 65568 | tf_op jit(solution)/shard_map/ppermute | solution.py:263
  136.3 1.9 %collective-permute-start.31 = (bf16[64,512]{1,0:T(8,128)(2,1)S(1)}, bf16[64,512]{1,0:T(8,128)(2,1)S(1)}, u32[]{:S(2)}, u32[]{:S(2)}) collective-permute-start(bf16[64,512]{1,0:T(8,128)(2,1)S(1)} %get-tuple-element.41), channel_id=1, source_target_pairs={{0,20},{4,16},{8,28},{12,24},{16,4},{20,0},{24,12},{28,8},{1,21},{... | collective-permute-start | bytes 196616 | tf_op jit(solution)/shard_map/ppermute | solution.py:263
  138.2 0.8 collective-permute-done.32.refs_6_
  139.0 0.7 collective-permute-start.30
  139.8 0.9 collective-permute-done.31.refs_5_
  140.6 1.9 %collective-permute-start.29 = (bf16[64,512]{1,0:T(8,128)(2,1)S(1)}, bf16[64,512]{1,0:T(8,128)(2,1)S(1)}, u32[]{:S(2)}, u32[]{:S(2)}) collective-permute-start(bf16[64,512]{1,0:T(8,128)(2,1)S(1)} %get-tuple-element.43), channel_id=1, source_target_pairs={{0,12},{4,8},{8,4},{12,0},{16,28},{20,24},{24,20},{28,16},{1,13},{... | collective-permute-start | bytes 196616 | tf_op jit(solution)/shard_map/ppermute | solution.py:263
  142.5 0.8 collective-permute-done.30.refs_4_
  143.3 0.7 collective-permute-start.28
  144.0 0.5 collective-permute-done.29.refs_3_
  144.5 1.4 collective-permute-start.27
  145.8 1.7 %collective-permute-done.28.refs_2_ = bf16[64,512]{1,0:T(8,128)(2,1)S(1)} collective-permute-done((bf16[64,512]{1,0:T(8,128)(2,1)S(1)}, bf16[64,512]{1,0:T(8,128)(2,1)S(1)}, u32[]{:S(2)}, u32[]{:S(2)}) %collective-permute-start.28) | collective-permute-done | bytes 65568 | tf_op jit(solution)/shard_map/ppermute | solution.py:263
  147.6 0.8 shard_map.170
  148.4 2.3 %copy.21 = bf16[4,16,8,1024]{3,2,0,1:T(8,128)(2,1)} copy(bf16[4,16,8,1024]{3,2,1,0:T(8,128)(2,1)} %bitcast.17) | data formatting | bytes 2097152 | tf_op jit(solution)/shard_map/all_to_all | solution.py:317
  150.8 4.4 %shard_map.167 = (f32[1024,256]{1,0:T(8,128)}, f32[1024,256]{1,0:T(8,128)}, f32[1024,256]{1,0:T(8,128)}) custom-call(bf16[256,1024]{1,0:T(8,128)(2,1)S(1)} %copy-done.15, bf16[256,1024]{1,0:T(8,128)(2,1)} %collective-permute-done.21.refs_1_, bf16[256,1024]{1,0:T(8,128)(2,1)} %collective-permute-done.22.refs_2_, ...), custom_call_target="tpu_custom_call" | custom-call | tf_op jit(solution)/shard_map/pallas_call | solution.py:355
  (64 shorter events, 0.2 us)
Async XLA Ops:
  0.6 8.8 %copy-start = (f32[1024,256]{1,0:T(8,128)S(1)}, f32[1024,256]{1,0:T(8,128)}, u32[]{:S(2)}) copy-start(f32[1024,256]{1,0:T(8,128)} %refs_4_.1) | copy-start | bytes 3145732
  0.6 8.7 %copy-start.16 = (f32[64,512]{1,0:T(8,128)S(1)}, f32[64,512]{1,0:T(8,128)}, u32[]{:S(2)}) copy-start(f32[64,512]{1,0:T(8,128)} %refs_8_.1) | copy-start | bytes 393220
  0.7 8.7 %copy-start.17 = (bf16[128,512]{1,0:T(8,128)(2,1)S(1)}, bf16[128,512]{1,0:T(8,128)(2,1)}, u32[]{:S(2)}) copy-start(bf16[128,512]{1,0:T(8,128)(2,1)} %cot.1) | copy-start | bytes 393220
  0.7 8.7 %copy-start.20 = (s32[128]{0:T(128)S(1)}, s32[128]{0:T(128)}, u32[]{:S(2)}) copy-start(s32[128]{0:T(128)} %param.13) | copy-start | bytes 1540
  0.7 8.7 %copy-start.21 = (s32[128]{0:T(128)S(1)}, s32[128]{0:T(128)}, u32[]{:S(2)}) copy-start(s32[128]{0:T(128)} %param.14) | copy-start | bytes 1540
  3.1 53.9 %all-to-all-start.1 = ((bf16[128,4,1024]{2,0,1:T(8,128)(2,1)}), bf16[128,4,1024]{2,0,1:T(8,128)(2,1)S(1)}, u32[]{:S(2)}, u32[]{:S(2)}) async-start(bf16[128,4,1024]{2,0,1:T(8,128)(2,1)} %bitcast.34), calls=%async_computation.1 | async-start | bytes 2097152 | tf_op jit(solution)/shard_map/all_to_all | solution.py:294
  9.6 7.8 %collective-permute-start.9 = (bf16[64,512]{1,0:T(8,128)(2,1)S(1)}, bf16[64,512]{1,0:T(8,128)(2,1)S(1)}, u32[]{:S(2)}, u32[]{:S(2)}) collective-permute-start(bf16[64,512]{1,0:T(8,128)(2,1)S(1)} %get-tuple-element.24.refs_4_), channel_id=1, source_target_pairs={{0,28},{4,24},{8,20},{12,16},{16,12},{20,8},{24,4},{28,0},{1,29},{... | collective-permute-start | bytes 196616 | tf_op jit(solution)/shard_map/ppermute | solution.py:263
  11.2 6.7 %collective-permute-start.8 = (bf16[64,512]{1,0:T(8,128)(2,1)S(1)}, bf16[64,512]{1,0:T(8,128)(2,1)S(1)}, u32[]{:S(2)}, u32[]{:S(2)}) collective-permute-start(bf16[64,512]{1,0:T(8,128)(2,1)S(1)} %get-tuple-element.24.refs_4_), channel_id=1, source_target_pairs={{0,24},{4,28},{8,16},{12,20},{16,8},{20,12},{24,0},{28,4},{1,25},{... | collective-permute-start | bytes 196616 | tf_op jit(solution)/shard_map/ppermute | solution.py:263
  12.2 6.3 %collective-permute-start.7 = (bf16[64,512]{1,0:T(8,128)(2,1)S(1)}, bf16[64,512]{1,0:T(8,128)(2,1)S(1)}, u32[]{:S(2)}, u32[]{:S(2)}) collective-permute-start(bf16[64,512]{1,0:T(8,128)(2,1)S(1)} %get-tuple-element.24.refs_4_), channel_id=1, source_target_pairs={{0,20},{4,16},{8,28},{12,24},{16,4},{20,0},{24,12},{28,8},{1,21},{... | collective-permute-start | bytes 196616 | tf_op jit(solution)/shard_map/ppermute | solution.py:263
  13.5 21.6 %collective-permute-start.2 = (bf16[144,512]{1,0:T(8,128)(2,1)S(1)}, bf16[144,512]{1,0:T(8,128)(2,1)S(1)}, u32[]{:S(2)}, u32[]{:S(2)}) collective-permute-start(bf16[144,512]{1,0:T(8,128)(2,1)S(1)} %get-tuple-element.23.refs_0_), channel_id=1, source_target_pairs={{0,3},{1,2},{2,1},{3,0},{4,7},{5,6},{6,5},{7,4},{8,11},{9,10},{10,... | collective-permute-start | bytes 442376 | tf_op jit(solution)/shard_map/ppermute | solution.py:263
  17.3 30.4 %collective-permute-start.1 = (bf16[144,512]{1,0:T(8,128)(2,1)S(1)}, bf16[144,512]{1,0:T(8,128)(2,1)S(1)}, u32[]{:S(2)}, u32[]{:S(2)}) collective-permute-start(bf16[144,512]{1,0:T(8,128)(2,1)S(1)} %get-tuple-element.23.refs_0_), channel_id=1, source_target_pairs={{0,2},{1,3},{2,0},{3,1},{4,6},{5,7},{6,4},{7,5},{8,10},{9,11},{10,... | collective-permute-start | bytes 442376 | tf_op jit(solution)/shard_map/ppermute | solution.py:263
  17.4 30.4 %collective-permute-start = (bf16[144,512]{1,0:T(8,128)(2,1)S(1)}, bf16[144,512]{1,0:T(8,128)(2,1)S(1)}, u32[]{:S(2)}, u32[]{:S(2)}) collective-permute-start(bf16[144,512]{1,0:T(8,128)(2,1)S(1)} %get-tuple-element.23.refs_0_), channel_id=1, source_target_pairs={{0,1},{1,0},{2,3},{3,2},{4,5},{5,4},{6,7},{7,6},{8,9},{9,8},{10,11... | collective-permute-start | bytes 442376 | tf_op jit(solution)/shard_map/ppermute | solution.py:263
  17.9 4.3 %collective-permute-start.6 = (bf16[64,512]{1,0:T(8,128)(2,1)S(1)}, bf16[64,512]{1,0:T(8,128)(2,1)S(1)}, u32[]{:S(2)}, u32[]{:S(2)}) collective-permute-start(bf16[64,512]{1,0:T(8,128)(2,1)S(1)} %get-tuple-element.24.refs_4_), channel_id=1, source_target_pairs={{0,16},{4,20},{8,24},{12,28},{16,0},{20,4},{24,8},{28,12},{1,17},{... | collective-permute-start | bytes 196616 | tf_op jit(solution)/shard_map/ppermute | solution.py:263
  18.4 5.3 %collective-permute-start.5 = (bf16[64,512]{1,0:T(8,128)(2,1)S(1)}, bf16[64,512]{1,0:T(8,128)(2,1)S(1)}, u32[]{:S(2)}, u32[]{:S(2)}) collective-permute-start(bf16[64,512]{1,0:T(8,128)(2,1)S(1)} %get-tuple-element.24.refs_4_), channel_id=1, source_target_pairs={{0,12},{4,8},{8,4},{12,0},{16,28},{20,24},{24,20},{28,16},{1,13},{... | collective-permute-start | bytes 196616 | tf_op jit(solution)/shard_map/ppermute | solution.py:263
  22.2 4.3 %collective-permute-start.4 = (bf16[64,512]{1,0:T(8,128)(2,1)S(1)}, bf16[64,512]{1,0:T(8,128)(2,1)S(1)}, u32[]{:S(2)}, u32[]{:S(2)}) collective-permute-start(bf16[64,512]{1,0:T(8,128)(2,1)S(1)} %get-tuple-element.24.refs_4_), channel_id=1, source_target_pairs={{0,8},{4,12},{8,0},{12,4},{16,24},{20,28},{24,16},{28,20},{1,9},{5... | collective-permute-start | bytes 196616 | tf_op jit(solution)/shard_map/ppermute | solution.py:263
  23.7 2.8 %collective-permute-start.3 = (bf16[64,512]{1,0:T(8,128)(2,1)S(1)}, bf16[64,512]{1,0:T(8,128)(2,1)S(1)}, u32[]{:S(2)}, u32[]{:S(2)}) collective-permute-start(bf16[64,512]{1,0:T(8,128)(2,1)S(1)} %get-tuple-element.24.refs_4_), channel_id=1, source_target_pairs={{0,4},{4,0},{8,12},{12,8},{16,20},{20,16},{24,28},{28,24},{1,5},{5... | collective-permute-start | bytes 196616 | tf_op jit(solution)/shard_map/ppermute | solution.py:263
  48.3 0.8 copy-start.9
  49.1 7.3 %collective-permute-start.12 = (bf16[32,512]{1,0:T(8,128)(2,1)S(1)}, bf16[32,512]{1,0:T(8,128)(2,1)S(1)}, u32[]{:S(2)}, u32[]{:S(2)}) collective-permute-start(bf16[32,512]{1,0:T(8,128)(2,1)S(1)} %get-tuple-element.25.refs_0_), channel_id=1, source_target_pairs={{0,3},{1,2},{2,1},{3,0},{4,7},{5,6},{6,5},{7,4},{8,11},{9,10},{10,... | collective-permute-start | bytes 98312 | tf_op jit(solution)/shard_map/ppermute | solution.py:263
  50.6 6.4 %collective-permute-start.11 = (bf16[32,512]{1,0:T(8,128)(2,1)S(1)}, bf16[32,512]{1,0:T(8,128)(2,1)S(1)}, u32[]{:S(2)}, u32[]{:S(2)}) collective-permute-start(bf16[32,512]{1,0:T(8,128)(2,1)S(1)} %get-tuple-element.25.refs_0_), channel_id=1, source_target_pairs={{0,2},{1,3},{2,0},{3,1},{4,6},{5,7},{6,4},{7,5},{8,10},{9,11},{10,... | collective-permute-start | bytes 98312 | tf_op jit(solution)/shard_map/ppermute | solution.py:263
  50.6 6.4 %collective-permute-start.10 = (bf16[32,512]{1,0:T(8,128)(2,1)S(1)}, bf16[32,512]{1,0:T(8,128)(2,1)S(1)}, u32[]{:S(2)}, u32[]{:S(2)}) collective-permute-start(bf16[32,512]{1,0:T(8,128)(2,1)S(1)} %get-tuple-element.25.refs_0_), channel_id=1, source_target_pairs={{0,1},{1,0},{2,3},{3,2},{4,5},{5,4},{6,7},{7,6},{8,9},{9,8},{10,11... | collective-permute-start | bytes 98312 | tf_op jit(solution)/shard_map/ppermute | solution.py:263
  53.5 15.8 %collective-permute-start.18 = (bf16[1024,256]{1,0:T(8,128)(2,1)S(1)}, bf16[1024,256]{1,0:T(8,128)(2,1)S(1)}, u32[]{:S(2)}, u32[]{:S(2)}) collective-permute-start(bf16[1024,256]{1,0:T(8,128)(2,1)S(1)} %get-tuple-element.26.refs_4_.refs_0_), channel_id=1, source_target_pairs={{0,24},{4,28},{8,16},{12,20},{16,8},{20,12},{24,0},{28,4},{1,25},{... | collective-permute-start | bytes 1572872 | tf_op jit(solution)/shard_map/ppermute | solution.py:263
  55.9 21.8 %collective-permute-start.16 = (bf16[1024,256]{1,0:T(8,128)(2,1)S(1)}, bf16[1024,256]{1,0:T(8,128)(2,1)}, u32[]{:S(2)}, u32[]{:S(2)}) collective-permute-start(bf16[1024,256]{1,0:T(8,128)(2,1)S(1)} %get-tuple-element.26.refs_4_.refs_0_), channel_id=1, source_target_pairs={{0,16},{4,20},{8,24},{12,28},{16,0},{20,4},{24,8},{28,12},{1,17},{... | collective-permute-start | bytes 1572872 | tf_op jit(solution)/shard_map/ppermute | solution.py:263
  56.4 21.4 %collective-permute-start.14 = (bf16[1024,256]{1,0:T(8,128)(2,1)S(1)}, bf16[1024,256]{1,0:T(8,128)(2,1)}, u32[]{:S(2)}, u32[]{:S(2)}) collective-permute-start(bf16[1024,256]{1,0:T(8,128)(2,1)S(1)} %get-tuple-element.26.refs_4_.refs_0_), channel_id=1, source_target_pairs={{0,8},{4,12},{8,0},{12,4},{16,24},{20,28},{24,16},{28,20},{1,9},{5... | collective-permute-start | bytes 1572872 | tf_op jit(solution)/shard_map/ppermute | solution.py:263
  57.0 23.7 %copy-start.10 = (bf16[512,512]{1,0:T(8,128)(2,1)S(1)}, bf16[512,512]{1,0:T(8,128)(2,1)}, u32[]{:S(2)}) copy-start(bf16[512,512]{1,0:T(8,128)(2,1)} %copy-done.9) | copy-start | bytes 1572868
  59.6 47.2 %collective-permute-start.20 = (bf16[4,256,1024]{2,1,0:T(8,128)(2,1)}, bf16[4,256,1024]{2,1,0:T(8,128)(2,1)}, u32[]{:S(2)}, u32[]{:S(2)}) collective-permute-start(bf16[4,256,1024]{2,1,0:T(8,128)(2,1)} %shard_map.165), channel_id=1, source_target_pairs={{0,4},{4,0},{8,12},{12,8},{16,20},{20,16},{24,28},{28,24},{1,5},{5... | collective-permute-start | bytes 6291464 | tf_op jit(solution)/shard_map/ppermute | solution.py:263
  59.6 18.7 %collective-permute-start.13 = (bf16[1024,256]{1,0:T(8,128)(2,1)S(1)}, bf16[1024,256]{1,0:T(8,128)(2,1)S(1)}, u32[]{:S(2)}, u32[]{:S(2)}) collective-permute-start(bf16[1024,256]{1,0:T(8,128)(2,1)S(1)} %get-tuple-element.26.refs_4_.refs_0_), channel_id=1, source_target_pairs={{0,4},{4,0},{8,12},{12,8},{16,20},{20,16},{24,28},{28,24},{1,5},{5... | collective-permute-start | bytes 1572872 | tf_op jit(solution)/shard_map/ppermute | solution.py:263
  69.3 9.0 %collective-permute-start.19 = (bf16[1024,256]{1,0:T(8,128)(2,1)S(1)}, bf16[1024,256]{1,0:T(8,128)(2,1)S(1)}, u32[]{:S(2)}, u32[]{:S(2)}) collective-permute-start(bf16[1024,256]{1,0:T(8,128)(2,1)S(1)} %collective-permute-done.18.refs_10_.refs_6_), channel_id=1, source_target_pairs={{0,4},{4,0},{8,12},{12,8},{16,20},{20,16},{24,28},{28,24},{1,5},{5... | collective-permute-start | bytes 1572872 | tf_op jit(solution)/shard_map/ppermute | solution.py:263
  77.8 2.1 %collective-permute-start.17 = (bf16[1024,256]{1,0:T(8,128)(2,1)}, bf16[1024,256]{1,0:T(8,128)(2,1)S(1)}, u32[]{:S(2)}, u32[]{:S(2)}) collective-permute-start(bf16[1024,256]{1,0:T(8,128)(2,1)} %collective-permute-done.16.refs_8_.refs_4_), channel_id=1, source_target_pairs={{0,4},{4,0},{8,12},{12,8},{16,20},{20,16},{24,28},{28,24},{1,5},{5... | collective-permute-start | bytes 1572872 | tf_op jit(solution)/shard_map/ppermute | solution.py:263
  77.9 2.8 %collective-permute-start.15 = (bf16[1024,256]{1,0:T(8,128)(2,1)}, bf16[1024,256]{1,0:T(8,128)(2,1)S(1)}, u32[]{:S(2)}, u32[]{:S(2)}) collective-permute-start(bf16[1024,256]{1,0:T(8,128)(2,1)} %collective-permute-done.14.refs_6_.refs_2_), channel_id=1, source_target_pairs={{0,4},{4,0},{8,12},{12,8},{16,20},{20,16},{24,28},{28,24},{1,5},{5... | collective-permute-start | bytes 1572872 | tf_op jit(solution)/shard_map/ppermute | solution.py:263
  78.3 9.1 %copy-start.1 = (bf16[1024,256]{1,0:T(8,128)(2,1)}, bf16[1024,256]{1,0:T(8,128)(2,1)S(1)}, u32[]{:S(2)}) copy-start(bf16[1024,256]{1,0:T(8,128)(2,1)S(1)} %collective-permute-done.13.refs_5_.refs_1_) | copy-start | bytes 1572868
  78.3 9.1 %copy-start.3 = (bf16[1024,256]{1,0:T(8,128)(2,1)}, bf16[1024,256]{1,0:T(8,128)(2,1)S(1)}, u32[]{:S(2)}) copy-start(bf16[1024,256]{1,0:T(8,128)(2,1)S(1)} %collective-permute-done.19.refs_11_.refs_7_) | copy-start | bytes 1572868
  79.9 7.5 %copy-start.5 = (bf16[1024,256]{1,0:T(8,128)(2,1)}, bf16[1024,256]{1,0:T(8,128)(2,1)S(1)}, u32[]{:S(2)}) copy-start(bf16[1024,256]{1,0:T(8,128)(2,1)S(1)} %collective-permute-done.17.refs_9_.refs_5_) | copy-start | bytes 1572868
  80.7 6.8 %copy-start.7 = (bf16[1024,256]{1,0:T(8,128)(2,1)}, bf16[1024,256]{1,0:T(8,128)(2,1)S(1)}, u32[]{:S(2)}) copy-start(bf16[1024,256]{1,0:T(8,128)(2,1)S(1)} %collective-permute-done.15.refs_7_.refs_3_) | copy-start | bytes 1572868
  87.4 61.0 %all-to-all-start = ((bf16[4,128,1024]{2,1,0:T(8,128)(2,1)}), bf16[4,128,1024]{2,1,0:T(8,128)(2,1)}, u32[]{:S(2)}, u32[]{:S(2)}) async-start(bf16[4,128,1024]{2,1,0:T(8,128)(2,1)} %bitcast.2), calls=%async_computation | async-start | bytes 2097152 | tf_op jit(solution)/shard_map/all_to_all | solution.py:317
  91.9 1.0 copy-start.2
  92.9 1.0 copy-start.4
  94.0 1.0 copy-start.6
  95.0 1.0 copy-start.8
  102.3 18.4 %copy-start.11 = (bf16[512,512]{1,0:T(8,128)(2,1)S(1)}, bf16[512,512]{1,0:T(8,128)(2,1)}, u32[]{:S(2)}) copy-start(bf16[512,512]{1,0:T(8,128)(2,1)} %copy-done.9) | copy-start | bytes 1572868
  102.4 45.2 %copy-start.18 = (f32[64,512]{1,0:T(8,128)S(1)}, f32[64,512]{1,0:T(8,128)}, u32[]{:S(2)}) copy-start(f32[64,512]{1,0:T(8,128)} %refs_9_.1) | copy-start | bytes 393220
  102.4 45.2 %copy-start.19 = (f32[64,512]{1,0:T(8,128)S(1)}, f32[64,512]{1,0:T(8,128)}, u32[]{:S(2)}) copy-start(f32[64,512]{1,0:T(8,128)} %refs_10_.1) | copy-start | bytes 393220
  102.4 12.4 %collective-permute-start.26 = (bf16[32,512]{1,0:T(8,128)(2,1)S(1)}, bf16[32,512]{1,0:T(8,128)(2,1)S(1)}, u32[]{:S(2)}, u32[]{:S(2)}) collective-permute-start(bf16[32,512]{1,0:T(8,128)(2,1)S(1)} %shard_map.168.refs_0_), channel_id=1, source_target_pairs={{0,3},{1,2},{2,1},{3,0},{4,7},{5,6},{6,5},{7,4},{8,11},{9,10},{10,... | collective-permute-start | bytes 98312 | tf_op jit(solution)/shard_map/ppermute | solution.py:263
  106.0 14.7 %collective-permute-start.25 = (bf16[32,512]{1,0:T(8,128)(2,1)S(1)}, bf16[32,512]{1,0:T(8,128)(2,1)S(1)}, u32[]{:S(2)}, u32[]{:S(2)}) collective-permute-start(bf16[32,512]{1,0:T(8,128)(2,1)S(1)} %shard_map.168.refs_0_), channel_id=1, source_target_pairs={{0,2},{1,3},{2,0},{3,1},{4,6},{5,7},{6,4},{7,5},{8,10},{9,11},{10,... | collective-permute-start | bytes 98312 | tf_op jit(solution)/shard_map/ppermute | solution.py:263
  106.0 14.7 %collective-permute-start.24 = (bf16[32,512]{1,0:T(8,128)(2,1)S(1)}, bf16[32,512]{1,0:T(8,128)(2,1)S(1)}, u32[]{:S(2)}, u32[]{:S(2)}) collective-permute-start(bf16[32,512]{1,0:T(8,128)(2,1)S(1)} %shard_map.168.refs_0_), channel_id=1, source_target_pairs={{0,1},{1,0},{2,3},{3,2},{4,5},{5,4},{6,7},{7,6},{8,9},{9,8},{10,11... | collective-permute-start | bytes 98312 | tf_op jit(solution)/shard_map/ppermute | solution.py:263
  110.6 10.7 %copy-start.14 = (bf16[256,1024]{1,0:T(8,128)(2,1)}, bf16[256,1024]{1,0:T(8,128)(2,1)S(1)}, u32[]{:S(2)}) copy-start(bf16[256,1024]{1,0:T(8,128)(2,1)S(1)} %get-tuple-element.29.refs_0_) | copy-start | bytes 1572868
  110.6 40.2 %collective-permute-start.21 = (bf16[256,1024]{1,0:T(8,128)(2,1)}, bf16[256,1024]{1,0:T(8,128)(2,1)}, u32[]{:S(2)}, u32[]{:S(2)}) collective-permute-start(bf16[256,1024]{1,0:T(8,128)(2,1)} %get-tuple-element.30), channel_id=1, source_target_pairs={{0,8},{4,12},{8,0},{12,4},{16,24},{20,28},{24,16},{28,20},{1,9},{5... | collective-permute-start | bytes 1572872 | tf_op jit(solution)/shard_map/ppermute | solution.py:263
  112.1 38.7 %collective-permute-start.22 = (bf16[256,1024]{1,0:T(8,128)(2,1)}, bf16[256,1024]{1,0:T(8,128)(2,1)}, u32[]{:S(2)}, u32[]{:S(2)}) collective-permute-start(bf16[256,1024]{1,0:T(8,128)(2,1)} %get-tuple-element.31), channel_id=1, source_target_pairs={{0,16},{4,20},{8,24},{12,28},{16,0},{20,4},{24,8},{28,12},{1,17},{... | collective-permute-start | bytes 1572872 | tf_op jit(solution)/shard_map/ppermute | solution.py:263
  114.7 36.0 %collective-permute-start.23 = (bf16[256,1024]{1,0:T(8,128)(2,1)}, bf16[256,1024]{1,0:T(8,128)(2,1)}, u32[]{:S(2)}, u32[]{:S(2)}) collective-permute-start(bf16[256,1024]{1,0:T(8,128)(2,1)} %get-tuple-element.32), channel_id=1, source_target_pairs={{0,24},{4,28},{8,16},{12,20},{16,8},{20,12},{24,0},{28,4},{1,25},{... | collective-permute-start | bytes 1572872 | tf_op jit(solution)/shard_map/ppermute | solution.py:263
  121.2 29.5 %copy-start.12 = (f32[1024,256]{1,0:T(8,128)S(1)}, f32[1024,256]{1,0:T(8,128)}, u32[]{:S(2)}) copy-start(f32[1024,256]{1,0:T(8,128)} %refs_5_.1) | copy-start | bytes 3145732
  121.3 29.5 %copy-start.13 = (f32[1024,256]{1,0:T(8,128)S(1)}, f32[1024,256]{1,0:T(8,128)}, u32[]{:S(2)}) copy-start(f32[1024,256]{1,0:T(8,128)} %refs_6_.1) | copy-start | bytes 3145732
  121.3 15.0 %collective-permute-start.33 = (bf16[64,512]{1,0:T(8,128)(2,1)S(1)}, bf16[64,512]{1,0:T(8,128)(2,1)S(1)}, u32[]{:S(2)}, u32[]{:S(2)}) collective-permute-start(bf16[64,512]{1,0:T(8,128)(2,1)S(1)} %get-tuple-element.39), channel_id=1, source_target_pairs={{0,28},{4,24},{8,20},{12,16},{16,12},{20,8},{24,4},{28,0},{1,29},{... | collective-permute-start | bytes 196616 | tf_op jit(solution)/shard_map/ppermute | solution.py:263
  122.2 16.9 %collective-permute-start.32 = (bf16[64,512]{1,0:T(8,128)(2,1)S(1)}, bf16[64,512]{1,0:T(8,128)(2,1)S(1)}, u32[]{:S(2)}, u32[]{:S(2)}) collective-permute-start(bf16[64,512]{1,0:T(8,128)(2,1)S(1)} %get-tuple-element.40), channel_id=1, source_target_pairs={{0,24},{4,28},{8,16},{12,20},{16,8},{20,12},{24,0},{28,4},{1,25},{... | collective-permute-start | bytes 196616 | tf_op jit(solution)/shard_map/ppermute | solution.py:263
  136.3 4.3 %collective-permute-start.31 = (bf16[64,512]{1,0:T(8,128)(2,1)S(1)}, bf16[64,512]{1,0:T(8,128)(2,1)S(1)}, u32[]{:S(2)}, u32[]{:S(2)}) collective-permute-start(bf16[64,512]{1,0:T(8,128)(2,1)S(1)} %get-tuple-element.41), channel_id=1, source_target_pairs={{0,20},{4,16},{8,28},{12,24},{16,4},{20,0},{24,12},{28,8},{1,21},{... | collective-permute-start | bytes 196616 | tf_op jit(solution)/shard_map/ppermute | solution.py:263
  139.0 4.3 %collective-permute-start.30 = (bf16[64,512]{1,0:T(8,128)(2,1)S(1)}, bf16[64,512]{1,0:T(8,128)(2,1)S(1)}, u32[]{:S(2)}, u32[]{:S(2)}) collective-permute-start(bf16[64,512]{1,0:T(8,128)(2,1)S(1)} %get-tuple-element.42), channel_id=1, source_target_pairs={{0,16},{4,20},{8,24},{12,28},{16,0},{20,4},{24,8},{28,12},{1,17},{... | collective-permute-start | bytes 196616 | tf_op jit(solution)/shard_map/ppermute | solution.py:263
  140.6 3.8 %collective-permute-start.29 = (bf16[64,512]{1,0:T(8,128)(2,1)S(1)}, bf16[64,512]{1,0:T(8,128)(2,1)S(1)}, u32[]{:S(2)}, u32[]{:S(2)}) collective-permute-start(bf16[64,512]{1,0:T(8,128)(2,1)S(1)} %get-tuple-element.43), channel_id=1, source_target_pairs={{0,12},{4,8},{8,4},{12,0},{16,28},{20,24},{24,20},{28,16},{1,13},{... | collective-permute-start | bytes 196616 | tf_op jit(solution)/shard_map/ppermute | solution.py:263
  143.3 4.3 %collective-permute-start.28 = (bf16[64,512]{1,0:T(8,128)(2,1)S(1)}, bf16[64,512]{1,0:T(8,128)(2,1)S(1)}, u32[]{:S(2)}, u32[]{:S(2)}) collective-permute-start(bf16[64,512]{1,0:T(8,128)(2,1)S(1)} %get-tuple-element.44), channel_id=1, source_target_pairs={{0,8},{4,12},{8,0},{12,4},{16,24},{20,28},{24,16},{28,20},{1,9},{5... | collective-permute-start | bytes 196616 | tf_op jit(solution)/shard_map/ppermute | solution.py:263
  144.5 3.1 %collective-permute-start.27 = (bf16[64,512]{1,0:T(8,128)(2,1)S(1)}, bf16[64,512]{1,0:T(8,128)(2,1)S(1)}, u32[]{:S(2)}, u32[]{:S(2)}) collective-permute-start(bf16[64,512]{1,0:T(8,128)(2,1)S(1)} %get-tuple-element.45), channel_id=1, source_target_pairs={{0,4},{4,0},{8,12},{12,8},{16,20},{20,16},{24,28},{28,24},{1,5},{5... | collective-permute-start | bytes 196616 | tf_op jit(solution)/shard_map/ppermute | solution.py:263
  148.4 2.4 %copy-start.15 = (bf16[256,1024]{1,0:T(8,128)(2,1)S(1)}, bf16[256,1024]{1,0:T(8,128)(2,1)}, u32[]{:S(2)}) copy-start(bf16[256,1024]{1,0:T(8,128)(2,1)} %copy-done.14) | copy-start | bytes 1572868

commit v3 on v2

--- a/solution.py
+++ b/solution.py
@@ -13,6 +13,7 @@
 LANES = 128
 ROW_STEP = 512
 LABEL_ROWS = 16
+PARTS = 1
 
 adapter_scale = 2.0
 learn_rate = 0.02
@@ -32,22 +33,23 @@
     return jax.ShapeDtypeStruct(tuple(dims), kind)
 
 
-def call(body, outs, ins, scratch=(), in_specs=None, cost=0):
+def call(body, outs, ins, scratch=(), in_specs=None, out_specs=None, vmem=16):
     return pl.pallas_call(
         body,
         out_shape=outs,
         in_specs=in_specs or [VMEM] * len(ins),
-        out_specs=jax.tree.map(lambda _: VMEM, outs),
+        out_specs=out_specs or jax.tree.map(lambda _: VMEM, outs),
         scratch_shapes=list(scratch),
-        compiler_params=pltpu.CompilerParams(vmem_limit_bytes=48 << 20),
-        cost_estimate=pl.CostEstimate(flops=cost, bytes_accessed=cost, transcendentals=0),
+        compiler_params=pltpu.CompilerParams(vmem_limit_bytes=vmem << 20),
+        cost_estimate=pl.CostEstimate(flops=0, bytes_accessed=0, transcendentals=0),
     )(*ins)
 
 
 def adam_step(param, moment, second, gradient):
     moment = beta_one * moment + (1.0 - beta_one) * gradient
     second = beta_two * second + (1.0 - beta_two) * gradient * gradient
-    param = param - learn_rate * (moment / bias_one) / (jnp.sqrt(second / bias_two) + adam_eps)
+    step = (learn_rate / bias_one) * moment
+    param = param - step / (jnp.sqrt((1.0 / bias_two) * second) + adam_eps)
     return (param, moment, second)
 
 
@@ -67,7 +69,19 @@
     return jnp.transpose(wide)
 
 
-def prep_kernel(cot, tenant, advantage, a_param, b_param, share, a_low, b_low):
+def prep_kernel(parts, *refs):
+    acts, cot, tenant, advantage, a_param, b_param, share, low = refs[:8]
+    cuts, sems = refs[8 : 8 + parts], refs[-1]
+    shards, _, width = cuts[0].shape
+    copies = []
+    for h in range(parts):
+        for j in range(shards):
+            at = pl.ds((j * parts + h) * width, width)
+            copies.append(
+                pltpu.make_async_copy(acts.at[:, at], cuts[h].at[j], sems.at[h * shards + j])
+            )
+    for copy in copies:
+        copy.start()
     rows, keys = cot.shape
     factor = column_of(advantage[...]) * 0.25
     factor = jnp.concatenate([factor] * (keys // LANES), axis=1)
@@ -79,8 +93,14 @@
     labels = jnp.where(line == 0, owner, jnp.where(line == 1, local, 0)).astype(f32)
     share[rows:, :rows] = labels.astype(bf16)
     share[rows:, rows:] = jnp.zeros((LABEL_ROWS, keys - rows), bf16)
-    a_low[...] = (a_param[...] * MODEL_WIDTH ** (-0.5)).astype(bf16)
-    b_low[...] = (b_param[...] * ADAPTER_RANK ** (-0.5)).astype(bf16)
+    features, columns = a_param.shape
+    low[:features] = (a_param[...] * MODEL_WIDTH ** (-0.5)).astype(bf16)
+    own_rows = b_param.shape[0]
+    for q in range(keys // columns):
+        part = b_param[:, q * columns : (q + 1) * columns] * ADAPTER_RANK ** (-0.5)
+        low[features + q * own_rows : features + (q + 1) * own_rows] = part.astype(bf16)
+    for copy in copies:
+        copy.wait()
 
 
 def second_ids(owners, own_rows, rows):
@@ -89,11 +109,10 @@
     return lax.div(line, own_rows) * TEN_DEV + lax.div(inner, ADAPTER_RANK)
 
 
-def back_kernel(shards, owners, *refs):
-    shares, b_blocks = refs[:shards], refs[shards : shards + owners]
-    scaled, label, back, b_all = refs[shards + owners :]
+def base_kernel(shards, *refs):
+    shares, weight = refs[:shards], refs[shards]
+    scaled, label, base = refs[shards + 1 :]
     rd = shares[0].shape[0] - LABEL_ROWS
-    own_rows = b_blocks[0].shape[0]
     me, place = lax.axis_index("dp"), lax.axis_index("fsdp")
     for j in range(shards):
         at = pl.ds(pl.multiple_of((place ^ j) * rd, rd), rd)
@@ -101,11 +120,34 @@
         ids = shares[j][rd:, :rd].astype(f32).astype(jnp.int32)
         tid = (ids[0:1] ^ me) * TEN_DEV + ids[1:2]
         label[:, at] = jnp.broadcast_to(tid, (8, rd))
+    rows = scaled.shape[0]
+    step = min(ROW_STEP, rows)
+    for r in range(0, rows, step):
+        base[r : r + step] = dot(scaled[r : r + step], weight[...], 1, 1).astype(bf16)
+
+
+def back_kernel(owners, own_rows, *refs):
+    blocks = refs[:owners]
+    scaled, label, back, b_all, sems = refs[owners:]
+    features = blocks[0].shape[0] - own_rows * scaled.shape[1] // blocks[0].shape[1]
+    columns = blocks[0].shape[1]
+    rows, keys = scaled.shape
+    copies = []
     for k in range(owners):
-        b_all[k * own_rows : (k + 1) * own_rows] = b_blocks[k][...]
-    rows = scaled.shape[0]
+        for q in range(keys // columns):
+            copies.append(
+                pltpu.make_async_copy(
+                    blocks[k].at[pl.ds(features + q * own_rows, own_rows)],
+                    b_all.at[pl.ds(k * own_rows, own_rows), pl.ds(q * columns, columns)],
+                    sems.at[k, q],
+                )
+            )
+    for copy in copies:
+        copy.start()
     step = min(ROW_STEP, rows)
     ids = second_ids(owners, own_rows, step)
+    for copy in copies:
+        copy.wait()
     for r in range(0, rows, step):
         wide = dot(b_all[...], scaled[r : r + step], 1, 1)
         wide = jnp.where(ids == label[0:1, r : r + step], wide, 0.0)
@@ -115,7 +157,8 @@
             low = jnp.sum(wide.reshape(-1, own_rows, step), axis=0)
             low = jnp.concatenate([low] * (ADAPTER_RANK // own_rows), axis=0)
             part = lax.div(iota(low.shape, 0), own_rows)
-            low = jnp.where(part == lax.rem(place, ADAPTER_RANK // own_rows), low, 0.0)
+            place = lax.rem(lax.axis_index("fsdp"), ADAPTER_RANK // own_rows)
+            low = jnp.where(part == place, low, 0.0)
         back[:, r : r + step] = low.astype(bf16)
 
 
@@ -130,7 +173,9 @@
     columns = a_blocks[0].shape[1]
     copies = [
         pltpu.make_async_copy(
-            block, a_all.at[:, k * columns : (k + 1) * columns], sems.at[k]
+            block.at[pl.ds(0, a_all.shape[0])],
+            a_all.at[:, pl.ds(k * columns, columns)],
+            sems.at[k],
         )
         for k, block in enumerate(a_blocks)
     ]
@@ -141,7 +186,7 @@
 
 def side_kernel(shards, owners, *refs):
     backs, a_blocks = refs[:shards], refs[shards : shards + owners]
-    label, scaled, weight, out, a_all, back_wide, sems = refs[shards + owners :]
+    label, base, out, a_all, back_wide, sems = refs[shards + owners :]
     copies = load_factors(a_blocks, a_all, sems)
     rows, features = out.shape
     step = min(ROW_STEP, rows)
@@ -161,9 +206,9 @@
                 copy.wait()
         chunk = min(256, features)
         for c in range(0, features, chunk):
-            base = dot(scaled[at], weight[c : c + chunk], 1, 1).astype(bf16)
             side = dot(back_wide[...], a_all[c : c + chunk], 1, 1).astype(bf16)
-            out[at, c : c + chunk] = (base.astype(f32) + side.astype(f32)).astype(bf16)
+            whole = base[at, c : c + chunk].astype(f32) + side.astype(f32)
+            out[at, c : c + chunk] = whole.astype(bf16)
 
 
 def spread(low, label, k, columns):
@@ -190,11 +235,12 @@
             outs[n][...] = (grad + arrived[n].astype(f32)).astype(bf16)
 
 
-def mid_kernel(owners, *refs):
+def mid_kernel(owners, parts, *refs):
     a_blocks = refs[:owners]
-    label, acts, out, a_all, sems = refs[owners:]
+    label, acts = refs[owners], refs[owners + 1 : owners + 1 + parts]
+    out, a_all, sems = refs[owners + 1 + parts :]
     copies = load_factors(a_blocks, a_all, sems)
-    rows = acts.shape[0]
+    rows, width = acts[0].shape
     columns = a_blocks[0].shape[1]
     step = min(ROW_STEP, rows)
     for r in range(0, rows, step):
@@ -206,7 +252,11 @@
         for k in range(owners):
             if r == 0:
                 copies[k].wait()
-            wide = dot(acts[at], a_all[:, k * columns : (k + 1) * columns])
+            wide = None
+            for h in range(parts):
+                factor = a_all[h * width : (h + 1) * width, k * columns : (k + 1) * columns]
+                term = dot(acts[h][at], factor)
+                wide = term if wide is None else wide + term
             for q in range(columns // LANES):
                 hit = where == k * TEN_DEV + q * (LANES // ADAPTER_RANK)
                 low = low + jnp.where(hit, wide[:, q * LANES : (q + 1) * LANES], 0.0)
@@ -235,8 +285,9 @@
         low = jnp.where(ids == label[0:1, at], low, 0.0).astype(bf16)
         grad = grad + dot(low, scaled[at])
     grad = (coefficient * grad).astype(bf16)
+    me = lax.axis_index("dp")
     for k in range(owners):
-        out[k] = grad[k * own_rows : (k + 1) * own_rows]
+        out[me ^ k] = grad[k * own_rows : (k + 1) * own_rows]
 
 
 def adam_a_kernel(count, *refs):
@@ -249,13 +300,26 @@
         out[...] = value
 
 
-def adam_b_kernel(count, *refs):
-    grads, (param, moment, second), outs = refs[:count], refs[count : count + 3], refs[count + 3 :]
-    grad = grads[0][...].astype(f32)
-    for part in grads[1:]:
-        grad = grad + part[...].astype(f32)
+def adam_b_kernel(grads, param, moment, second, *outs):
+    grad = jnp.sum(grads[...].astype(f32), axis=0)
     for out, value in zip(outs, adam_step(param[...], moment[...], second[...], grad)):
         out[...] = value
+
+
+def lay_kernel(*refs):
+    parts, out, sems = refs[:-2], refs[-2], refs[-1]
+    shards, _, width = parts[0].shape
+    copies = []
+    for h, part in enumerate(parts):
+        for j in range(shards):
+            at = pl.ds((j * len(parts) + h) * width, width)
+            copies.append(
+                pltpu.make_async_copy(part.at[j], out.at[:, at], sems.at[h * shards + j])
+            )
+    for copy in copies:
+        copy.start()
+    for copy in copies:
+        copy.wait()
 
 
 def swap(block, axis, bits):
@@ -283,57 +347,83 @@
     own_rows = b_param.shape[0]
     rows = row_count * shards
 
-    share, a_low, b_low = call(
-        prep_kernel,
-        (shape((row_count + LABEL_ROWS, keys)), shape((features, columns)), shape((own_rows, keys))),
-        (cotangent, tenant[None], advantage[None], a_param, b_param),
-    )
-    b_blocks = [b_low] + [swap(b_low, "dp", k) for k in range(1, owners)]
+    parts = PARTS
+    width = features // parts
+    b_lines = own_rows * keys // columns
+    cut = shape((shards, row_count, width))
+    dma = pltpu.SemaphoreType.DMA
+
+    share, low, *cuts = call(
+        functools.partial(prep_kernel, parts),
+        [shape((row_count + LABEL_ROWS, keys)), shape((features + b_lines, columns))] + [cut] * parts,
+        (acts, cotangent, tenant[None], advantage[None], a_param, b_param),
+        [dma((parts * shards,))],
+        [ANY] + [VMEM] * 5,
+        [VMEM] * 2 + [ANY] * parts,
+    )
     shares = [share] + [swap(share, "fsdp", j) for j in range(1, shards)]
-    chips = [a_low] + [swap(a_low, "dp", k) for k in range(2, owners, 2)]
-    acts_part = lax.all_to_all(acts, "fsdp", split_axis=1, concat_axis=0, tiled=True)
-    a_blocks = []
+    chips = [low] + [swap(low, "dp", k) for k in range(2, owners, 2)]
+    blocks = []
     for block in chips:
-        a_blocks += [block, swap(block, "dp", 1)]
-
-    scaled, label, back = call(
-        functools.partial(back_kernel, shards, owners),
-        (shape((rows, keys)), shape((8, rows), jnp.int32), shape((ADAPTER_RANK, rows))),
-        (*shares, *b_blocks),
-        [pltpu.VMEM((owners * own_rows, keys), bf16)],
+        blocks += [block, swap(block, "dp", 1)]
+    shares[1], *cuts = lax.optimization_barrier((shares[1], *cuts))
+    acts_parts = [
+        lax.all_to_all(c, "fsdp", split_axis=0, concat_axis=0, tiled=True).reshape(rows, width)
+        for c in cuts
+    ]
+
+    scaled, label, base = call(
+        functools.partial(base_kernel, shards),
+        (shape((rows, keys)), shape((8, rows), jnp.int32), shape((rows, features))),
+        (*shares, base_weight),
+    )
+    back = call(
+        functools.partial(back_kernel, owners, own_rows),
+        shape((ADAPTER_RANK, rows)),
+        (*blocks, scaled, label),
+        [pltpu.VMEM((owners * own_rows, keys), bf16), dma((owners, keys // columns))],
+        [ANY] * owners + [VMEM] * 2,
     )
     backs = [back] + [swap(back, "fsdp", j) for j in range(1, shards)]
 
     step = min(ROW_STEP, rows)
     factor_scratch = [pltpu.VMEM((features, owners * columns), bf16)]
-    sems = [pltpu.SemaphoreType.DMA((owners,))]
+    sems = [dma((owners,))]
     grad_part = call(
         functools.partial(side_kernel, shards, owners),
         shape((rows, features)),
-        (*backs, *a_blocks, label, scaled, base_weight),
+        (*backs, *blocks, label, base),
         factor_scratch + [pltpu.VMEM((step, owners * columns), bf16)] + sems,
-        [VMEM] * shards + [ANY] * owners + [VMEM] * 3,
-    )
-    grad_input = lax.all_to_all(grad_part, "fsdp", split_axis=0, concat_axis=1, tiled=True)
-
-    odd = call(
-        functools.partial(first_kernel, shards, owners, 1),
-        shape((owners // 2, columns, features)),
-        (*backs, label, acts_part),
-    )
-    even = call(
-        functools.partial(first_kernel, shards, owners, 0),
-        [shape((columns, features))] * (owners // 2),
-        (*backs, label, acts_part, swap(odd, "dp", 1)),
-    )
-    grad_a = [even[0]] + [swap(even[n], "dp", 2 * n) for n in range(1, owners // 2)]
+        [VMEM] * shards + [ANY] * owners + [VMEM] * 2,
+        vmem=24,
+    )
+    returned = lax.all_to_all(
+        grad_part.reshape(shards, row_count, features), "fsdp", 0, 0, tiled=True
+    )
+    grad_input = call(
+        lay_kernel, shape((row_count, shards * features)), (returned,), [dma((shards,))], [ANY], ANY
+    )
+
+    grad_a = []
+    for acts_part in acts_parts:
+        odd = call(
+            functools.partial(first_kernel, shards, owners, 1),
+            shape((owners // 2, columns, width)),
+            (*backs, label, acts_part),
+        )
+        even = call(
+            functools.partial(first_kernel, shards, owners, 0),
+            [shape((columns, width))] * (owners // 2),
+            (*backs, label, acts_part, swap(odd, "dp", 1)),
+        )
+        grad_a.append([even[0]] + [swap(even[n], "dp", 2 * n) for n in range(1, owners // 2)])
 
     mid = call(
-        functools.partial(mid_kernel, owners),
+        functools.partial(mid_kernel, owners, parts),
         shape((ADAPTER_RANK, rows)),
-        (*a_blocks, label, acts_part),
+        (*blocks, label, *acts_parts),
         factor_scratch + sems,
-        [ANY] * owners + [VMEM] * 2,
+        [ANY] * owners + [VMEM] * (1 + parts),
     )
     mids = [mid] + [swap(mid, "fsdp", j) for j in range(1, shards)]
     grad_b = call(
@@ -342,24 +432,25 @@
         (*mids, label, scaled),
         [pltpu.VMEM((ADAPTER_RANK, step), f32)],
     )
-    grad_b = [grad_b[0]] + [swap(grad_b[k], "dp", k) for k in range(1, owners)]
-
     new_b = call(
-        functools.partial(adam_b_kernel, owners),
+        adam_b_kernel,
         [shape(b_param.shape, f32)] * 3,
-        (*grad_b, b_param, b_moment, b_second),
-    )
-    block = min(256, features)
+        (lax.all_to_all(grad_b, "dp", 0, 0, tiled=True), b_param, b_moment, b_second),
+    )
+    block = min(256, width)
+    steps = width // block
     wide = pl.BlockSpec((columns, block), lambda i: (0, i))
-    tall = pl.BlockSpec((block, columns), lambda i: (i, 0))
-    new_a = pl.pallas_call(
-        functools.partial(adam_a_kernel, owners // 2),
-        grid=(features // block,),
-        out_shape=[shape(a_param.shape, f32)] * 3,
-        in_specs=[wide] * (owners // 2) + [tall] * 3,
-        out_specs=[tall] * 3,
-        compiler_params=pltpu.CompilerParams(vmem_limit_bytes=48 << 20),
-    )(*grad_a, a_param, a_moment, a_second)
+    new_a = (a_param, a_moment, a_second)
+    for h in range(parts):
+        tall = pl.BlockSpec((block, columns), lambda i, h=h: (h * steps + i, 0))
+        new_a = pl.pallas_call(
+            functools.partial(adam_a_kernel, owners // 2),
+            grid=(steps,),
+            out_shape=[shape(a_param.shape, f32)] * 3,
+            in_specs=[wide] * (owners // 2) + [tall] * 3,
+            out_specs=[tall] * 3,
+            compiler_params=pltpu.CompilerParams(vmem_limit_bytes=16 << 20),
+        )(*grad_a[h], *new_a)
     return (grad_input, new_a[0], new_a[1], new_a[2], new_b[0], new_b[1], new_b[2])
 
 

time: 156 us -> 154 us (0.987)
  local copies, waits for them, and re-layouts: 9.79 us -> 20.8 us
  starting transfers between devices: 47.4 us -> 39.5 us
  waiting for transfers between devices: 71.3 us -> 64.7 us
    ppermute x34 -> x20, waiting for transfers between devices: 71.3 us -> 48.2 us  [swap(): return lax.ppermute(block, axis, [(i, i ^ bits) for i in range(size)])]
    all_to_all x2 -> x3, waiting for transfers between devices: 0.01 us -> 16.5 us  [the longest x1 16.5 us: per_device(): lax.all_to_all(grad_part.reshape(shards, row_count, features), 'fsdp', 0,...]
    unnamed x44 -> x74, local copies, waits for them, and re-layouts: 5.03 us -> 20.8 us
    ppermute x34 -> x20, starting transfers between devices: 36.6 us -> 26.8 us  [swap(): return lax.ppermute(block, axis, [(i, i ^ bits) for i in range(size)])]
    all_to_all x2 -> x0, local copies, waits for them, and re-layouts: 4.72 us -> none  [the longest x1 2.38 us: per_device(): lax.all_to_all(acts, 'fsdp', split_axis=1, concat_axis=0, tiled=True)]
    all_to_all x2 -> x3, starting transfers between devices: 10.8 us -> 12.7 us  [the longest x1 5.03 us: per_device(): lax.all_to_all(c, 'fsdp', split_axis=0, concat_axis=0, tiled=True)]
    pallas_call x8 -> x10, Pallas kernels: 21.4 us -> 22.7 us  [call(): pl.pallas_call(body, out_shape=outs, in_specs=in_specs or [VMEM] * len(in...]
  transfers between devices with their start and end apart: 36 -> 23, of which waited for: 17 -> 12; matrix products, arithmetic and copies ran while one was open for 2% -> 0% of each run, Pallas kernels for 14% -> 12%
where the time goes in v3:
time: 154 us; the launch traced here: 153 us
  waiting for transfers between devices  64.7 us (42%)
  starting transfers between devices  39.5 us (26%)
  Pallas kernels  27 us (18%)
  local copies, waits for them, and re-layouts  20.8 us (14%)
    ppermute x20, waiting for transfers between devices, swap(): return lax.ppermute(block, axis, [(i, i ^ bits) for i in range(size)])  48.2 us
    ppermute x20, starting transfers between devices, swap(): return lax.ppermute(block, axis, [(i, i ^ bits) for i in range(size)])  26.8 us
    pallas_call x10, Pallas kernels, call(): pl.pallas_call(body, out_shape=outs, in_specs=in_specs or [VMEM] * len(in...  22.7 us
    unnamed x74, local copies, waits for them, and re-layouts  20.8 us
    all_to_all x1, waiting for transfers between devices, per_device(): lax.all_to_all(grad_part.reshape(shards, row_count, features), 'fsdp', 0,...  16.5 us
    all_to_all x1, starting transfers between devices, per_device(): lax.all_to_all(c, 'fsdp', split_axis=0, concat_axis=0, tiled=True)  5.03 us
    pallas_call x1, Pallas kernels, per_device(): pl.pallas_call(functools.partial(adam_a_kernel, owners // 2), grid=(steps...  4.36 us
    all_to_all x1, starting transfers between devices, per_device(): lax.all_to_all(grad_b, 'dp', 0, 0, tiled=True)  4.14 us
  transfers between devices with their start and end apart: 23, of which 12 were waited for; matrix products, arithmetic and copies ran while one was open for 0% of the time, Pallas kernels for 12%

profile of v3, /device:TPU:0, one launch (start us, length us, event | category | flops | bytes accessed | tf_op | source)
XLA Modules:
  0.0 152.9 jit_solution(10241877989138316189)
XLA Ops:
  0.6 1.2 copy-done.12
  1.9 1.2 copy-done.20
  3.1 0.9 copy-done.26
  4.0 0.9 copy-done.32
  4.9 0.7 copy-done.35
  5.6 0.7 copy-done.36
  6.2 1.0 shard_map.162
  7.2 3.1 %collective-permute-start.7 = (bf16[144,512]{1,0:T(8,128)(2,1)S(1)}, bf16[144,512]{1,0:T(8,128)(2,1)S(1)}, u32[]{:S(2)}, u32[]{:S(2)}) collective-permute-start(bf16[144,512]{1,0:T(8,128)(2,1)S(1)} %get-tuple-element.26.refs_0_), channel_id=1, source_target_pairs={{0,1},{1,0},{2,3},{3,2},{4,5},{5,4},{6,7},{7,6},{8,9},{9,8},{10,11... | collective-permute-start | bytes 442376 | tf_op jit(solution)/shard_map/ppermute | solution.py:327
  10.3 3.8 %collective-permute-done.7.refs_1_ = bf16[144,512]{1,0:T(8,128)(2,1)S(1)} collective-permute-done((bf16[144,512]{1,0:T(8,128)(2,1)S(1)}, bf16[144,512]{1,0:T(8,128)(2,1)S(1)}, u32[]{:S(2)}, u32[]{:S(2)}) %collective-permute-start.7) | collective-permute-done | bytes 147488 | tf_op jit(solution)/shard_map/ppermute | solution.py:327
  14.2 0.7 copy-done.30
  14.8 5.0 %all-to-all-start.1 = ((bf16[4,128,1024]{2,1,0:T(8,128)(2,1)}), bf16[4,128,1024]{2,1,0:T(8,128)(2,1)S(1)}, u32[]{:S(2)}, u32[]{:S(2)}) async-start(bf16[4,128,1024]{2,1,0:T(8,128)(2,1)} %get-tuple-element.32), calls=%async_computation.1 | async-start | bytes 2097152 | tf_op jit(solution)/shard_map/all_to_all | solution.py:371
  19.9 2.4 %collective-permute-start.5 = (bf16[1152,256]{1,0:T(8,128)(2,1)S(1)}, bf16[1152,256]{1,0:T(8,128)(2,1)S(1)}, u32[]{:S(2)}, u32[]{:S(2)}) collective-permute-start(bf16[1152,256]{1,0:T(8,128)(2,1)S(1)} %get-tuple-element.25.refs_0_.refs_4_), channel_id=1, source_target_pairs={{0,24},{4,28},{8,16},{12,20},{16,8},{20,12},{24,0},{28,4},{1,25},{... | collective-permute-start | bytes 1769480 | tf_op jit(solution)/shard_map/ppermute | solution.py:327
  22.3 0.5 collective-permute-start.3
  22.8 0.5 collective-permute-start.1
  23.4 13.7 %collective-permute-done.5.refs_6_.refs_10_ = bf16[1152,256]{1,0:T(8,128)(2,1)S(1)} collective-permute-done((bf16[1152,256]{1,0:T(8,128)(2,1)S(1)}, bf16[1152,256]{1,0:T(8,128)(2,1)S(1)}, u32[]{:S(2)}, u32[]{:S(2)}) %collective-permute-start.5) | collective-permute-done | bytes 589856 | tf_op jit(solution)/shard_map/ppermute | solution.py:327
  37.1 10.2 %collective-permute-done.3.refs_4_.refs_8_ = bf16[1152,256]{1,0:T(8,128)(2,1)S(1)} collective-permute-done((bf16[1152,256]{1,0:T(8,128)(2,1)S(1)}, bf16[1152,256]{1,0:T(8,128)(2,1)S(1)}, u32[]{:S(2)}, u32[]{:S(2)}) %collective-permute-start.3) | collective-permute-done | bytes 589856 | tf_op jit(solution)/shard_map/ppermute | solution.py:327
  47.4 0.4 collective-permute-start.2
  47.8 3.5 %collective-permute-start.9 = (bf16[144,512]{1,0:T(8,128)(2,1)S(1)}, bf16[144,512]{1,0:T(8,128)(2,1)S(1)}, u32[]{:S(2)}, u32[]{:S(2)}) collective-permute-start(bf16[144,512]{1,0:T(8,128)(2,1)S(1)} %get-tuple-element.26.refs_0_), channel_id=1, source_target_pairs={{0,3},{1,2},{2,1},{3,0},{4,7},{5,6},{6,5},{7,4},{8,11},{9,10},{10,... | collective-permute-start | bytes 442376 | tf_op jit(solution)/shard_map/ppermute | solution.py:327
  51.4 4.2 %collective-permute-done.9.refs_3_ = bf16[144,512]{1,0:T(8,128)(2,1)S(1)} collective-permute-done((bf16[144,512]{1,0:T(8,128)(2,1)S(1)}, bf16[144,512]{1,0:T(8,128)(2,1)S(1)}, u32[]{:S(2)}, u32[]{:S(2)}) %collective-permute-start.9) | collective-permute-done | bytes 147488 | tf_op jit(solution)/shard_map/ppermute | solution.py:327
  55.6 3.9 %collective-permute-start.8 = (bf16[144,512]{1,0:T(8,128)(2,1)S(1)}, bf16[144,512]{1,0:T(8,128)(2,1)S(1)}, u32[]{:S(2)}, u32[]{:S(2)}) collective-permute-start(bf16[144,512]{1,0:T(8,128)(2,1)S(1)} %get-tuple-element.26.refs_0_), channel_id=1, source_target_pairs={{0,2},{1,3},{2,0},{3,1},{4,6},{5,7},{6,4},{7,5},{8,10},{9,11},{10,... | collective-permute-start | bytes 442376 | tf_op jit(solution)/shard_map/ppermute | solution.py:327
  59.5 6.4 %collective-permute-done.8.refs_2_ = bf16[144,512]{1,0:T(8,128)(2,1)S(1)} collective-permute-done((bf16[144,512]{1,0:T(8,128)(2,1)S(1)}, bf16[144,512]{1,0:T(8,128)(2,1)S(1)}, u32[]{:S(2)}, u32[]{:S(2)}) %collective-permute-start.8) | collective-permute-done | bytes 147488 | tf_op jit(solution)/shard_map/ppermute | solution.py:327
  65.9 1.2 copy-done.21
  67.1 0.9 copy-done.29
  68.1 0.9 copy-done.31
  69.0 0.7 shard_map.163
  69.8 0.8 shard_map.164.refs_0_
  70.7 0.2 copy-done.22
  70.9 0.2 copy-done
  71.0 0.2 copy-done.3
  71.2 0.2 copy-done.6
  71.5 0.2 copy-done.9
  71.6 2.2 %collective-permute-start.12 = (bf16[32,512]{1,0:T(8,128)(2,1)S(1)}, bf16[32,512]{1,0:T(8,128)(2,1)S(1)}, u32[]{:S(2)}, u32[]{:S(2)}) collective-permute-start(bf16[32,512]{1,0:T(8,128)(2,1)S(1)} %shard_map.164.refs_0_), channel_id=1, source_target_pairs={{0,3},{1,2},{2,1},{3,0},{4,7},{5,6},{6,5},{7,4},{8,11},{9,10},{10,... | collective-permute-start | bytes 98312 | tf_op jit(solution)/shard_map/ppermute | solution.py:327
  73.9 2.2 %collective-permute-start.10 = (bf16[32,512]{1,0:T(8,128)(2,1)S(1)}, bf16[32,512]{1,0:T(8,128)(2,1)S(1)}, u32[]{:S(2)}, u32[]{:S(2)}) collective-permute-start(bf16[32,512]{1,0:T(8,128)(2,1)S(1)} %shard_map.164.refs_0_), channel_id=1, source_target_pairs={{0,1},{1,0},{2,3},{3,2},{4,5},{5,4},{6,7},{7,6},{8,9},{9,8},{10,11... | collective-permute-start | bytes 98312 | tf_op jit(solution)/shard_map/ppermute | solution.py:327
  76.0 1.6 %collective-permute-done.12.refs_3_ = bf16[32,512]{1,0:T(8,128)(2,1)S(1)} collective-permute-done((bf16[32,512]{1,0:T(8,128)(2,1)S(1)}, bf16[32,512]{1,0:T(8,128)(2,1)S(1)}, u32[]{:S(2)}, u32[]{:S(2)}) %collective-permute-start.12) | collective-permute-done | bytes 32800 | tf_op jit(solution)/shard_map/ppermute | solution.py:327
  77.6 1.1 collective-permute-done.11.refs_2_
  78.7 2.6 %shard_map.167 = bf16[4,256,1024]{2,1,0:T(8,128)(2,1)} custom-call(bf16[32,512]{1,0:T(8,128)(2,1)S(1)} %shard_map.164.refs_0_, bf16[32,512]{1,0:T(8,128)(2,1)S(1)} %collective-permute-done.10.refs_1_, bf16[32,512]{1,0:T(8,128)(2,1)S(1)} %collective-permute-done.11.refs_2_, bf16[32,512]{1,0:T(8,128)(2,1)S(1)} %collective-permute-done.12.refs_3_, ...), custom_call_target="tpu_custom_call" | custom-call | tf_op jit(solution)/shard_map/pallas_call | solution.py:37
  81.4 6.4 %shard_map.170.refs_0_ = bf16[32,512]{1,0:T(8,128)(2,1)S(1)} custom-call(bf16[1152,256]{1,0:T(8,128)(2,1)S(1)} %get-tuple-element.25.refs_0_.refs_4_, bf16[1152,256]{1,0:T(8,128)(2,1)S(1)} %copy-done.1, bf16[1152,256]{1,0:T(8,128)(2,1)S(1)} %collective-permute-done.1.refs_2_.refs_6_, bf16[1152,256]{1,0:T(8,128)(2,1)S(1)} %copy-done.10, ...), custom_call_target="tpu_custom_call" | custom-call | tf_op jit(solution)/shard_map/pallas_call | solution.py:37
  87.8 1.9 %collective-permute-start.19 = (bf16[32,512]{1,0:T(8,128)(2,1)S(1)}, bf16[32,512]{1,0:T(8,128)(2,1)S(1)}, u32[]{:S(2)}, u32[]{:S(2)}) collective-permute-start(bf16[32,512]{1,0:T(8,128)(2,1)S(1)} %shard_map.170.refs_0_), channel_id=1, source_target_pairs={{0,3},{1,2},{2,1},{3,0},{4,7},{5,6},{6,5},{7,4},{8,11},{9,10},{10,... | collective-permute-start | bytes 98312 | tf_op jit(solution)/shard_map/ppermute | solution.py:327
  89.6 0.9 collective-permute-start.18
  90.6 1.7 %collective-permute-start.17 = (bf16[32,512]{1,0:T(8,128)(2,1)S(1)}, bf16[32,512]{1,0:T(8,128)(2,1)S(1)}, u32[]{:S(2)}, u32[]{:S(2)}) collective-permute-start(bf16[32,512]{1,0:T(8,128)(2,1)S(1)} %shard_map.170.refs_0_), channel_id=1, source_target_pairs={{0,1},{1,0},{2,3},{3,2},{4,5},{5,4},{6,7},{7,6},{8,9},{9,8},{10,11... | collective-permute-start | bytes 98312 | tf_op jit(solution)/shard_map/ppermute | solution.py:327
  92.2 1.4 collective-permute-done.19.refs_3_
  93.7 1.3 collective-permute-done.18.refs_2_
  95.0 0.5 shard_map.171
  95.4 0.8 copy-done.17
  96.2 4.1 %all-to-all-start.2 = ((bf16[8,64,512]{2,1,0:T(8,128)(2,1)}), bf16[8,64,512]{2,1,0:T(8,128)(2,1)}, u32[]{:S(2)}, u32[]{:S(2)}) async-start(bf16[8,64,512]{2,1,0:T(8,128)(2,1)} %copy-done.17), calls=%async_computation.2 | async-start | bytes 1048576 | tf_op jit(solution)/shard_map/all_to_all | solution.py:438
  100.4 1.1 copy-done.2
  101.5 1.1 copy-done.5
  102.5 1.1 copy-done.8
  103.6 1.1 copy-done.11
  104.6 1.2 copy-done.23
  105.9 3.9 %shard_map.165 = bf16[512,1024]{1,0:T(8,128)(2,1)S(1)} custom-call(bf16[32,512]{1,0:T(8,128)(2,1)S(1)} %shard_map.164.refs_0_, bf16[32,512]{1,0:T(8,128)(2,1)S(1)} %collective-permute-done.10.refs_1_, bf16[32,512]{1,0:T(8,128)(2,1)S(1)} %collective-permute-done.11.refs_2_, bf16[32,512]{1,0:T(8,128)(2,1)S(1)} %collective-permute-done.12.refs_3_, ...), custom_call_target="tpu_custom_call" | custom-call | tf_op jit(solution)/shard_map/pallas_call | solution.py:37
  109.8 1.0 copy-done.14
  110.7 3.5 %all-to-all-start = ((bf16[4,128,1024]{2,1,0:T(8,128)(2,1)}), bf16[4,128,1024]{2,1,0:T(8,128)(2,1)S(1)}, u32[]{:S(2)}, u32[]{:S(2)}) async-start(bf16[4,128,1024]{2,1,0:T(8,128)(2,1)} %bitcast.7), calls=%async_computation | async-start | bytes 2097152 | tf_op jit(solution)/shard_map/all_to_all | solution.py:400
  114.3 3.8 %shard_map.168 = (bf16[256,1024]{1,0:T(8,128)(2,1)S(1)}, bf16[256,1024]{1,0:T(8,128)(2,1)S(1)}, bf16[256,1024]{1,0:T(8,128)(2,1)}, bf16[256,1024]{1,0:T(8,128)(2,1)}) custom-call(bf16[32,512]{1,0:T(8,128)(2,1)S(1)} %shard_map.164.refs_0_, bf16[32,512]{1,0:T(8,128)(2,1)S(1)} %collective-permute-done.10.refs_1_, ...), custom_call_target="tpu_custom_call" | custom-call | tf_op jit(solution)/shard_map/pallas_call | solution.py:37
  118.1 0.8 copy-done.24
  118.9 1.9 %collective-permute-start.14 = (bf16[256,1024]{1,0:T(8,128)(2,1)S(1)}, bf16[256,1024]{1,0:T(8,128)(2,1)}, u32[]{:S(2)}, u32[]{:S(2)}) collective-permute-start(bf16[256,1024]{1,0:T(8,128)(2,1)S(1)} %get-tuple-element.34), channel_id=1, source_target_pairs={{0,8},{4,12},{8,0},{12,4},{16,24},{20,28},{24,16},{28,20},{1,9},{5... | collective-permute-start | bytes 1572872 | tf_op jit(solution)/shard_map/ppermute | solution.py:327
  120.8 1.5 collective-permute-start.15
  122.4 1.9 %shard_map.172 = (f32[64,512]{1,0:T(8,128)}, f32[64,512]{1,0:T(8,128)}, f32[64,512]{1,0:T(8,128)}) custom-call(bf16[8,64,512]{2,1,0:T(8,128)(2,1)} %all-to-all-done.2.grads, f32[64,512]{1,0:T(8,128)S(1)} %copy-done.27, f32[64,512]{1,0:T(8,128)S(1)} %copy-done.33, f32[64,512]{1,0:T(8,128)S(1)} %copy-done.34), custom_call_target="tpu_custom_call" | custom-call | tf_op jit(solution)/shard_map/pallas_call | solution.py:37
  124.3 16.5 %all-to-all-done.refs_0_ = bf16[4,128,1024]{2,1,0:T(8,128)(2,1)S(1)} async-done(((bf16[4,128,1024]{2,1,0:T(8,128)(2,1)}), bf16[4,128,1024]{2,1,0:T(8,128)(2,1)S(1)}, u32[]{:S(2)}, u32[]{:S(2)}) %all-to-all-start) | async-done | bytes 1048608 | tf_op jit(solution)/shard_map/all_to_all | solution.py:400
  140.8 1.0 shard_map.166
  141.8 4.3 %collective-permute-done.15.refs_2_ = bf16[256,1024]{1,0:T(8,128)(2,1)} collective-permute-done((bf16[256,1024]{1,0:T(8,128)(2,1)}, bf16[256,1024]{1,0:T(8,128)(2,1)}, u32[]{:S(2)}, u32[]{:S(2)}) %collective-permute-start.15) | collective-permute-done | bytes 524320 | tf_op jit(solution)/shard_map/ppermute | solution.py:327
  146.1 1.2 copy-done.18
  147.3 1.2 copy-done.19
  148.5 4.4 %shard_map.169 = (f32[1024,256]{1,0:T(8,128)}, f32[1024,256]{1,0:T(8,128)}, f32[1024,256]{1,0:T(8,128)}) custom-call(bf16[256,1024]{1,0:T(8,128)(2,1)S(1)} %copy-done.25, bf16[256,1024]{1,0:T(8,128)(2,1)} %collective-permute-done.14.refs_1_, bf16[256,1024]{1,0:T(8,128)(2,1)} %collective-permute-done.15.refs_2_, ...), custom_call_target="tpu_custom_call" | custom-call | tf_op jit(solution)/shard_map/pallas_call | solution.py:446
  (67 shorter events, 0.4 us)
Async XLA Ops:
  0.6 1.2 copy-start.12
  1.9 1.2 copy-start.20
  3.1 0.9 copy-start.26
  4.0 0.9 copy-start.32
  4.9 0.7 copy-start.35
  5.6 0.7 copy-start.36
  7.2 52.3 %copy-start.28 = (bf16[144,512]{1,0:T(8,128)(2,1)}, bf16[144,512]{1,0:T(8,128)(2,1)S(1)}, u32[]{:S(2)}) copy-start(bf16[144,512]{1,0:T(8,128)(2,1)S(1)} %get-tuple-element.26.refs_0_) | copy-start | bytes 442372
  7.2 6.9 %collective-permute-start.7 = (bf16[144,512]{1,0:T(8,128)(2,1)S(1)}, bf16[144,512]{1,0:T(8,128)(2,1)S(1)}, u32[]{:S(2)}, u32[]{:S(2)}) collective-permute-start(bf16[144,512]{1,0:T(8,128)(2,1)S(1)} %get-tuple-element.26.refs_0_), channel_id=1, source_target_pairs={{0,1},{1,0},{2,3},{3,2},{4,5},{5,4},{6,7},{7,6},{8,9},{9,8},{10,11... | collective-permute-start | bytes 442376 | tf_op jit(solution)/shard_map/ppermute | solution.py:327
  14.2 0.7 copy-start.30
  14.8 63.8 %all-to-all-start.1 = ((bf16[4,128,1024]{2,1,0:T(8,128)(2,1)}), bf16[4,128,1024]{2,1,0:T(8,128)(2,1)S(1)}, u32[]{:S(2)}, u32[]{:S(2)}) async-start(bf16[4,128,1024]{2,1,0:T(8,128)(2,1)} %get-tuple-element.32), calls=%async_computation.1 | async-start | bytes 2097152 | tf_op jit(solution)/shard_map/all_to_all | solution.py:371
  19.9 17.2 %collective-permute-start.5 = (bf16[1152,256]{1,0:T(8,128)(2,1)S(1)}, bf16[1152,256]{1,0:T(8,128)(2,1)S(1)}, u32[]{:S(2)}, u32[]{:S(2)}) collective-permute-start(bf16[1152,256]{1,0:T(8,128)(2,1)S(1)} %get-tuple-element.25.refs_0_.refs_4_), channel_id=1, source_target_pairs={{0,24},{4,28},{8,16},{12,20},{16,8},{20,12},{24,0},{28,4},{1,25},{... | collective-permute-start | bytes 1769480 | tf_op jit(solution)/shard_map/ppermute | solution.py:327
  22.3 25.0 %collective-permute-start.3 = (bf16[1152,256]{1,0:T(8,128)(2,1)S(1)}, bf16[1152,256]{1,0:T(8,128)(2,1)S(1)}, u32[]{:S(2)}, u32[]{:S(2)}) collective-permute-start(bf16[1152,256]{1,0:T(8,128)(2,1)S(1)} %get-tuple-element.25.refs_0_.refs_4_), channel_id=1, source_target_pairs={{0,16},{4,20},{8,24},{12,28},{16,0},{20,4},{24,8},{28,12},{1,17},{... | collective-permute-start | bytes 1769480 | tf_op jit(solution)/shard_map/ppermute | solution.py:327
  22.8 24.6 %collective-permute-start.1 = (bf16[1152,256]{1,0:T(8,128)(2,1)S(1)}, bf16[1152,256]{1,0:T(8,128)(2,1)S(1)}, u32[]{:S(2)}, u32[]{:S(2)}) collective-permute-start(bf16[1152,256]{1,0:T(8,128)(2,1)S(1)} %get-tuple-element.25.refs_0_.refs_4_), channel_id=1, source_target_pairs={{0,8},{4,12},{8,0},{12,4},{16,24},{20,28},{24,16},{28,20},{1,9},{5... | collective-permute-start | bytes 1769480 | tf_op jit(solution)/shard_map/ppermute | solution.py:327
  23.4 46.4 %collective-permute-start = (bf16[1152,256]{1,0:T(8,128)(2,1)S(1)}, bf16[1152,256]{1,0:T(8,128)(2,1)S(1)}, u32[]{:S(2)}, u32[]{:S(2)}) collective-permute-start(bf16[1152,256]{1,0:T(8,128)(2,1)S(1)} %get-tuple-element.25.refs_0_.refs_4_), channel_id=1, source_target_pairs={{0,4},{4,0},{8,12},{12,8},{16,20},{20,16},{24,28},{28,24},{1,5},{5... | collective-permute-start | bytes 1769480 | tf_op jit(solution)/shard_map/ppermute | solution.py:327
  37.1 32.7 %collective-permute-start.6 = (bf16[1152,256]{1,0:T(8,128)(2,1)S(1)}, bf16[1152,256]{1,0:T(8,128)(2,1)S(1)}, u32[]{:S(2)}, u32[]{:S(2)}) collective-permute-start(bf16[1152,256]{1,0:T(8,128)(2,1)S(1)} %collective-permute-done.5.refs_6_.refs_10_), channel_id=1, source_target_pairs={{0,4},{4,0},{8,12},{12,8},{16,20},{20,16},{24,28},{28,24},{1,5},{5... | collective-permute-start | bytes 1769480 | tf_op jit(solution)/shard_map/ppermute | solution.py:327
  47.3 22.5 %collective-permute-start.4 = (bf16[1152,256]{1,0:T(8,128)(2,1)S(1)}, bf16[1152,256]{1,0:T(8,128)(2,1)S(1)}, u32[]{:S(2)}, u32[]{:S(2)}) collective-permute-start(bf16[1152,256]{1,0:T(8,128)(2,1)S(1)} %collective-permute-done.3.refs_4_.refs_8_), channel_id=1, source_target_pairs={{0,4},{4,0},{8,12},{12,8},{16,20},{20,16},{24,28},{28,24},{1,5},{5... | collective-permute-start | bytes 1769480 | tf_op jit(solution)/shard_map/ppermute | solution.py:327
  47.4 22.4 %collective-permute-start.2 = (bf16[1152,256]{1,0:T(8,128)(2,1)S(1)}, bf16[1152,256]{1,0:T(8,128)(2,1)S(1)}, u32[]{:S(2)}, u32[]{:S(2)}) collective-permute-start(bf16[1152,256]{1,0:T(8,128)(2,1)S(1)} %collective-permute-done.1.refs_2_.refs_6_), channel_id=1, source_target_pairs={{0,4},{4,0},{8,12},{12,8},{16,20},{20,16},{24,28},{28,24},{1,5},{5... | collective-permute-start | bytes 1769480 | tf_op jit(solution)/shard_map/ppermute | solution.py:327
  47.8 7.8 %collective-permute-start.9 = (bf16[144,512]{1,0:T(8,128)(2,1)S(1)}, bf16[144,512]{1,0:T(8,128)(2,1)S(1)}, u32[]{:S(2)}, u32[]{:S(2)}) collective-permute-start(bf16[144,512]{1,0:T(8,128)(2,1)S(1)} %get-tuple-element.26.refs_0_), channel_id=1, source_target_pairs={{0,3},{1,2},{2,1},{3,0},{4,7},{5,6},{6,5},{7,4},{8,11},{9,10},{10,... | collective-permute-start | bytes 442376 | tf_op jit(solution)/shard_map/ppermute | solution.py:327
  55.6 10.3 %collective-permute-start.8 = (bf16[144,512]{1,0:T(8,128)(2,1)S(1)}, bf16[144,512]{1,0:T(8,128)(2,1)S(1)}, u32[]{:S(2)}, u32[]{:S(2)}) collective-permute-start(bf16[144,512]{1,0:T(8,128)(2,1)S(1)} %get-tuple-element.26.refs_0_), channel_id=1, source_target_pairs={{0,2},{1,3},{2,0},{3,1},{4,6},{5,7},{6,4},{7,5},{8,10},{9,11},{10,... | collective-permute-start | bytes 442376 | tf_op jit(solution)/shard_map/ppermute | solution.py:327
  65.9 1.2 copy-start.21
  67.1 0.9 copy-start.29
  68.1 0.9 copy-start.31
  69.7 1.0 copy-start.15
  69.7 1.1 copy-start.22
  69.7 1.3 copy-start
  69.8 1.5 copy-start.3
  69.8 1.7 %copy-start.6 = (bf16[1152,256]{1,0:T(8,128)(2,1)}, bf16[1152,256]{1,0:T(8,128)(2,1)S(1)}, u32[]{:S(2)}) copy-start(bf16[1152,256]{1,0:T(8,128)(2,1)S(1)} %collective-permute-done.4.refs_5_.refs_9_) | copy-start | bytes 1769476
  69.8 1.8 %copy-start.9 = (bf16[1152,256]{1,0:T(8,128)(2,1)}, bf16[1152,256]{1,0:T(8,128)(2,1)S(1)}, u32[]{:S(2)}) copy-start(bf16[1152,256]{1,0:T(8,128)(2,1)S(1)} %collective-permute-done.2.refs_3_.refs_7_) | copy-start | bytes 1769476
  71.6 5.9 %collective-permute-start.12 = (bf16[32,512]{1,0:T(8,128)(2,1)S(1)}, bf16[32,512]{1,0:T(8,128)(2,1)S(1)}, u32[]{:S(2)}, u32[]{:S(2)}) collective-permute-start(bf16[32,512]{1,0:T(8,128)(2,1)S(1)} %shard_map.164.refs_0_), channel_id=1, source_target_pairs={{0,3},{1,2},{2,1},{3,0},{4,7},{5,6},{6,5},{7,4},{8,11},{9,10},{10,... | collective-permute-start | bytes 98312 | tf_op jit(solution)/shard_map/ppermute | solution.py:327
  73.8 4.8 %collective-permute-start.11 = (bf16[32,512]{1,0:T(8,128)(2,1)S(1)}, bf16[32,512]{1,0:T(8,128)(2,1)S(1)}, u32[]{:S(2)}, u32[]{:S(2)}) collective-permute-start(bf16[32,512]{1,0:T(8,128)(2,1)S(1)} %shard_map.164.refs_0_), channel_id=1, source_target_pairs={{0,2},{1,3},{2,0},{3,1},{4,6},{5,7},{6,4},{7,5},{8,10},{9,11},{10,... | collective-permute-start | bytes 98312 | tf_op jit(solution)/shard_map/ppermute | solution.py:327
  73.9 4.8 %collective-permute-start.10 = (bf16[32,512]{1,0:T(8,128)(2,1)S(1)}, bf16[32,512]{1,0:T(8,128)(2,1)S(1)}, u32[]{:S(2)}, u32[]{:S(2)}) collective-permute-start(bf16[32,512]{1,0:T(8,128)(2,1)S(1)} %shard_map.164.refs_0_), channel_id=1, source_target_pairs={{0,1},{1,0},{2,3},{3,2},{4,5},{5,4},{6,7},{7,6},{8,9},{9,8},{10,11... | collective-permute-start | bytes 98312 | tf_op jit(solution)/shard_map/ppermute | solution.py:327
  78.7 2.7 %copy-start.1 = (bf16[1152,256]{1,0:T(8,128)(2,1)S(1)}, bf16[1152,256]{1,0:T(8,128)(2,1)}, u32[]{:S(2)}) copy-start(bf16[1152,256]{1,0:T(8,128)(2,1)} %copy-done) | copy-start | bytes 1769476
  78.7 2.7 %copy-start.4 = (bf16[1152,256]{1,0:T(8,128)(2,1)S(1)}, bf16[1152,256]{1,0:T(8,128)(2,1)}, u32[]{:S(2)}) copy-start(bf16[1152,256]{1,0:T(8,128)(2,1)} %copy-done.3) | copy-start | bytes 1769476
  78.7 2.6 %copy-start.7 = (bf16[1152,256]{1,0:T(8,128)(2,1)S(1)}, bf16[1152,256]{1,0:T(8,128)(2,1)}, u32[]{:S(2)}) copy-start(bf16[1152,256]{1,0:T(8,128)(2,1)} %copy-done.6) | copy-start | bytes 1769476
  78.7 2.6 %copy-start.10 = (bf16[1152,256]{1,0:T(8,128)(2,1)S(1)}, bf16[1152,256]{1,0:T(8,128)(2,1)}, u32[]{:S(2)}) copy-start(bf16[1152,256]{1,0:T(8,128)(2,1)} %copy-done.9) | copy-start | bytes 1769476
  81.3 13.7 %copy-start.16 = (bf16[512,512]{1,0:T(8,128)(2,1)S(1)}, bf16[512,512]{1,0:T(8,128)(2,1)}, u32[]{:S(2)}) copy-start(bf16[512,512]{1,0:T(8,128)(2,1)} %copy-done.15) | copy-start | bytes 1572868
  81.3 33.0 %collective-permute-start.13 = (bf16[4,256,1024]{2,1,0:T(8,128)(2,1)}, bf16[4,256,1024]{2,1,0:T(8,128)(2,1)}, u32[]{:S(2)}, u32[]{:S(2)}) collective-permute-start(bf16[4,256,1024]{2,1,0:T(8,128)(2,1)} %shard_map.167), channel_id=1, source_target_pairs={{0,4},{4,0},{8,12},{12,8},{16,20},{20,16},{24,28},{28,24},{1,5},{5... | collective-permute-start | bytes 6291464 | tf_op jit(solution)/shard_map/ppermute | solution.py:327
  87.8 5.9 %collective-permute-start.19 = (bf16[32,512]{1,0:T(8,128)(2,1)S(1)}, bf16[32,512]{1,0:T(8,128)(2,1)S(1)}, u32[]{:S(2)}, u32[]{:S(2)}) collective-permute-start(bf16[32,512]{1,0:T(8,128)(2,1)S(1)} %shard_map.170.refs_0_), channel_id=1, source_target_pairs={{0,3},{1,2},{2,1},{3,0},{4,7},{5,6},{6,5},{7,4},{8,11},{9,10},{10,... | collective-permute-start | bytes 98312 | tf_op jit(solution)/shard_map/ppermute | solution.py:327
  89.6 5.3 %collective-permute-start.18 = (bf16[32,512]{1,0:T(8,128)(2,1)S(1)}, bf16[32,512]{1,0:T(8,128)(2,1)S(1)}, u32[]{:S(2)}, u32[]{:S(2)}) collective-permute-start(bf16[32,512]{1,0:T(8,128)(2,1)S(1)} %shard_map.170.refs_0_), channel_id=1, source_target_pairs={{0,2},{1,3},{2,0},{3,1},{4,6},{5,7},{6,4},{7,5},{8,10},{9,11},{10,... | collective-permute-start | bytes 98312 | tf_op jit(solution)/shard_map/ppermute | solution.py:327
  90.6 4.4 %collective-permute-start.17 = (bf16[32,512]{1,0:T(8,128)(2,1)S(1)}, bf16[32,512]{1,0:T(8,128)(2,1)S(1)}, u32[]{:S(2)}, u32[]{:S(2)}) collective-permute-start(bf16[32,512]{1,0:T(8,128)(2,1)S(1)} %shard_map.170.refs_0_), channel_id=1, source_target_pairs={{0,1},{1,0},{2,3},{3,2},{4,5},{5,4},{6,7},{7,6},{8,9},{9,8},{10,11... | collective-permute-start | bytes 98312 | tf_op jit(solution)/shard_map/ppermute | solution.py:327
  95.4 0.8 copy-start.17
  96.2 14.5 %all-to-all-start.2 = ((bf16[8,64,512]{2,1,0:T(8,128)(2,1)}), bf16[8,64,512]{2,1,0:T(8,128)(2,1)}, u32[]{:S(2)}, u32[]{:S(2)}) async-start(bf16[8,64,512]{2,1,0:T(8,128)(2,1)} %copy-done.17), calls=%async_computation.2 | async-start | bytes 1048576 | tf_op jit(solution)/shard_map/all_to_all | solution.py:438
  100.4 1.1 copy-start.2
  101.4 1.1 copy-start.5
  102.5 1.1 copy-start.8
  103.6 1.1 copy-start.11
  104.6 1.2 copy-start.23
  109.8 1.0 copy-start.14
  110.7 30.0 %all-to-all-start = ((bf16[4,128,1024]{2,1,0:T(8,128)(2,1)}), bf16[4,128,1024]{2,1,0:T(8,128)(2,1)S(1)}, u32[]{:S(2)}, u32[]{:S(2)}) async-start(bf16[4,128,1024]{2,1,0:T(8,128)(2,1)} %bitcast.7), calls=%async_computation | async-start | bytes 2097152 | tf_op jit(solution)/shard_map/all_to_all | solution.py:400
  114.3 8.2 %copy-start.27 = (f32[64,512]{1,0:T(8,128)S(1)}, f32[64,512]{1,0:T(8,128)}, u32[]{:S(2)}) copy-start(f32[64,512]{1,0:T(8,128)} %param.23) | copy-start | bytes 393220
  114.3 8.2 %copy-start.33 = (f32[64,512]{1,0:T(8,128)S(1)}, f32[64,512]{1,0:T(8,128)}, u32[]{:S(2)}) copy-start(f32[64,512]{1,0:T(8,128)} %moment.1) | copy-start | bytes 393220
  114.3 8.1 %copy-start.34 = (f32[64,512]{1,0:T(8,128)S(1)}, f32[64,512]{1,0:T(8,128)}, u32[]{:S(2)}) copy-start(f32[64,512]{1,0:T(8,128)} %second.1) | copy-start | bytes 393220
  118.1 0.8 copy-start.24
  118.9 27.1 %copy-start.13 = (f32[1024,256]{1,0:T(8,128)S(1)}, f32[1024,256]{1,0:T(8,128)}, u32[]{:S(2)}) copy-start(f32[1024,256]{1,0:T(8,128)} %refs_4_.5) | copy-start | bytes 3145732
  118.9 22.9 %collective-permute-start.14 = (bf16[256,1024]{1,0:T(8,128)(2,1)S(1)}, bf16[256,1024]{1,0:T(8,128)(2,1)}, u32[]{:S(2)}, u32[]{:S(2)}) collective-permute-start(bf16[256,1024]{1,0:T(8,128)(2,1)S(1)} %get-tuple-element.34), channel_id=1, source_target_pairs={{0,8},{4,12},{8,0},{12,4},{16,24},{20,28},{24,16},{28,20},{1,9},{5... | collective-permute-start | bytes 1572872 | tf_op jit(solution)/shard_map/ppermute | solution.py:327
  120.8 25.2 %collective-permute-start.15 = (bf16[256,1024]{1,0:T(8,128)(2,1)}, bf16[256,1024]{1,0:T(8,128)(2,1)}, u32[]{:S(2)}, u32[]{:S(2)}) collective-permute-start(bf16[256,1024]{1,0:T(8,128)(2,1)} %get-tuple-element.35), channel_id=1, source_target_pairs={{0,16},{4,20},{8,24},{12,28},{16,0},{20,4},{24,8},{28,12},{1,17},{... | collective-permute-start | bytes 1572872 | tf_op jit(solution)/shard_map/ppermute | solution.py:327
  122.3 23.8 %collective-permute-start.16 = (bf16[256,1024]{1,0:T(8,128)(2,1)}, bf16[256,1024]{1,0:T(8,128)(2,1)}, u32[]{:S(2)}, u32[]{:S(2)}) collective-permute-start(bf16[256,1024]{1,0:T(8,128)(2,1)} %get-tuple-element.36), channel_id=1, source_target_pairs={{0,24},{4,28},{8,16},{12,20},{16,8},{20,12},{24,0},{28,4},{1,25},{... | collective-permute-start | bytes 1572872 | tf_op jit(solution)/shard_map/ppermute | solution.py:327
  140.8 5.3 %copy-start.25 = (bf16[256,1024]{1,0:T(8,128)(2,1)S(1)}, bf16[256,1024]{1,0:T(8,128)(2,1)}, u32[]{:S(2)}) copy-start(bf16[256,1024]{1,0:T(8,128)(2,1)} %copy-done.24) | copy-start | bytes 1572868
  146.1 1.2 copy-start.18
  147.3 1.2 copy-start.19

commit v4 on v3

--- a/solution.py
+++ b/solution.py
@@ -13,6 +13,7 @@
 LANES = 128
 ROW_STEP = 512
 LABEL_ROWS = 16
+VMEM_BYTES = 62 << 20
 PARTS = 1
 
 adapter_scale = 2.0
@@ -25,25 +26,61 @@
 
 f32 = jnp.float32
 bf16 = jnp.bfloat16
-ANY = pl.BlockSpec(memory_space=pl.ANY)
 VMEM = pl.BlockSpec(memory_space=pltpu.VMEM)
-
+HBM = pl.BlockSpec(memory_space=pltpu.HBM)
+DMA = pltpu.SemaphoreType.DMA
 
 def shape(dims, kind=bf16):
     return jax.ShapeDtypeStruct(tuple(dims), kind)
 
-
-def call(body, outs, ins, scratch=(), in_specs=None, out_specs=None, vmem=16):
-    return pl.pallas_call(
-        body,
+def call(body, outs, ins, kinds, out_kinds, scratch=()):
+    single = not isinstance(outs, (list, tuple))
+    outs = [outs] if single else list(outs)
+    staged = [x for x, kind in zip(ins, kinds) if kind == "h"]
+    staged_outs = [x for x, kind in zip(outs, out_kinds) if kind == "h"]
+    count = len(staged) + len(staged_outs)
+    buffers = [pltpu.VMEM(x.shape, x.dtype) for x in staged + staged_outs]
+
+    def kernel(*refs):
+        refs = list(refs)
+        given, made = refs[: len(ins)], refs[len(ins) : len(ins) + len(outs)]
+        rest = refs[len(ins) + len(outs) :]
+        held, own = rest[:count], rest[count : len(rest) - bool(count)]
+        sems = rest[-1]
+        loads, stores = [], []
+        for n, kind in enumerate(kinds):
+            if kind == "h":
+                at = len(loads)
+                loads.append(pltpu.make_async_copy(given[n], held[at], sems.at[at]))
+                given[n] = held[at]
+        for n, kind in enumerate(out_kinds):
+            if kind == "h":
+                at = len(loads) + len(stores)
+                stores.append(pltpu.make_async_copy(held[at], made[n], sems.at[at]))
+                made[n] = held[at]
+        for copy in loads:
+            copy.start()
+
+        def ready():
+            for copy in loads:
+                copy.wait()
+
+        body(ready, *given, *made, *own)
+        for copy in stores:
+            copy.start()
+        for copy in stores:
+            copy.wait()
+
+    result = pl.pallas_call(
+        kernel,
         out_shape=outs,
-        in_specs=in_specs or [VMEM] * len(ins),
-        out_specs=out_specs or jax.tree.map(lambda _: VMEM, outs),
-        scratch_shapes=list(scratch),
-        compiler_params=pltpu.CompilerParams(vmem_limit_bytes=vmem << 20),
+        in_specs=[VMEM if kind == "v" else HBM for kind in kinds],
+        out_specs=[VMEM if kind == "v" else HBM for kind in out_kinds],
+        scratch_shapes=buffers + list(scratch) + ([DMA((count,))] if count else []),
+        compiler_params=pltpu.CompilerParams(vmem_limit_bytes=VMEM_BYTES),
         cost_estimate=pl.CostEstimate(flops=0, bytes_accessed=0, transcendentals=0),
     )(*ins)
-
+    return result[0] if single else result
 
 def adam_step(param, moment, second, gradient):
     moment = beta_one * moment + (1.0 - beta_one) * gradient
@@ -52,24 +89,20 @@
     param = param - step / (jnp.sqrt((1.0 / bias_two) * second) + adam_eps)
     return (param, moment, second)
 
-
 def dot(left, right, left_dim=1, right_dim=0):
     return lax.dot_general(
         left, right, (((left_dim,), (right_dim,)), ((), ())), preferred_element_type=f32
     )
 
-
 def iota(dims, axis):
     return lax.broadcasted_iota(jnp.int32, dims, axis)
-
 
 def column_of(row, lanes=LANES):
     n = row.shape[1]
     wide = jnp.broadcast_to(row.astype(f32), (lanes, n))
     return jnp.transpose(wide)
 
-
-def prep_kernel(parts, *refs):
+def prep_kernel(parts, ready, *refs):
     acts, cot, tenant, advantage, a_param, b_param, share, low = refs[:8]
     cuts, sems = refs[8 : 8 + parts], refs[-1]
     shards, _, width = cuts[0].shape
@@ -82,17 +115,21 @@
             )
     for copy in copies:
         copy.start()
+    ready()
     rows, keys = cot.shape
     factor = column_of(advantage[...]) * 0.25
     factor = jnp.concatenate([factor] * (keys // LANES), axis=1)
-    share[:rows] = (cot[...].astype(f32) * factor).astype(bf16)
+    scaled = (cot[...].astype(f32) * factor).astype(bf16)
     t = tenant[...]
     line = iota((LABEL_ROWS, rows), 0)
     owner = jnp.broadcast_to(lax.div(t, TEN_DEV), (LABEL_ROWS, rows))
     local = jnp.broadcast_to(lax.rem(t, TEN_DEV), (LABEL_ROWS, rows))
     labels = jnp.where(line == 0, owner, jnp.where(line == 1, local, 0)).astype(f32)
-    share[rows:, :rows] = labels.astype(bf16)
-    share[rows:, rows:] = jnp.zeros((LABEL_ROWS, keys - rows), bf16)
+    labels = labels.astype(bf16)
+    for j in range(shards):
+        share[j, :rows] = scaled
+        share[j, rows:, :rows] = labels
+        share[j, rows:, rows:] = jnp.zeros((LABEL_ROWS, keys - rows), bf16)
     features, columns = a_param.shape
     low[:features] = (a_param[...] * MODEL_WIDTH ** (-0.5)).astype(bf16)
     own_rows = b_param.shape[0]
@@ -102,31 +139,27 @@
     for copy in copies:
         copy.wait()
 
-
 def second_ids(owners, own_rows, rows):
     line = iota((owners * own_rows, rows), 0)
     inner = lax.rem(line, own_rows) + lax.axis_index("fsdp") * own_rows
     return lax.div(line, own_rows) * TEN_DEV + lax.div(inner, ADAPTER_RANK)
 
-
-def base_kernel(shards, *refs):
-    shares, weight = refs[:shards], refs[shards]
-    scaled, label, base = refs[shards + 1 :]
-    rd = shares[0].shape[0] - LABEL_ROWS
-    me, place = lax.axis_index("dp"), lax.axis_index("fsdp")
+def base_kernel(ready, shares, weight, scaled, label, base):
+    ready()
+    shards, lines, _ = shares.shape
+    rd = lines - LABEL_ROWS
+    me = lax.axis_index("dp")
     for j in range(shards):
-        at = pl.ds(pl.multiple_of((place ^ j) * rd, rd), rd)
-        scaled[at] = shares[j][:rd]
-        ids = shares[j][rd:, :rd].astype(f32).astype(jnp.int32)
+        scaled[j * rd : (j + 1) * rd] = shares[j, :rd]
+        ids = shares[j, rd:, :rd].astype(f32).astype(jnp.int32)
         tid = (ids[0:1] ^ me) * TEN_DEV + ids[1:2]
-        label[:, at] = jnp.broadcast_to(tid, (8, rd))
+        label[:, j * rd : (j + 1) * rd] = jnp.broadcast_to(tid, (8, rd))
     rows = scaled.shape[0]
     step = min(ROW_STEP, rows)
     for r in range(0, rows, step):
         base[r : r + step] = dot(scaled[r : r + step], weight[...], 1, 1).astype(bf16)
 
-
-def back_kernel(owners, own_rows, *refs):
+def back_kernel(owners, own_rows, ready, *refs):
     blocks = refs[:owners]
     scaled, label, back, b_all, sems = refs[owners:]
     features = blocks[0].shape[0] - own_rows * scaled.shape[1] // blocks[0].shape[1]
@@ -146,6 +179,7 @@
         copy.start()
     step = min(ROW_STEP, rows)
     ids = second_ids(owners, own_rows, step)
+    ready()
     for copy in copies:
         copy.wait()
     for r in range(0, rows, step):
@@ -159,15 +193,11 @@
             part = lax.div(iota(low.shape, 0), own_rows)
             place = lax.rem(lax.axis_index("fsdp"), ADAPTER_RANK // own_rows)
             low = jnp.where(part == place, low, 0.0)
-        back[:, r : r + step] = low.astype(bf16)
-
+        for j in range(back.shape[0]):
+            back[j, :, r : r + step] = low.astype(bf16)
 
 def total(parts, at):
-    value = parts[0][:, at].astype(f32)
-    for part in parts[1:]:
-        value = value + part[:, at].astype(f32)
-    return value
-
+    return jnp.sum(parts[:, :, at].astype(f32), axis=0)
 
 def load_factors(a_blocks, a_all, sems):
     columns = a_blocks[0].shape[1]
@@ -183,11 +213,11 @@
         copy.start()
     return copies
 
-
-def side_kernel(shards, owners, *refs):
-    backs, a_blocks = refs[:shards], refs[shards : shards + owners]
-    label, base, out, a_all, back_wide, sems = refs[shards + owners :]
+def side_kernel(owners, ready, *refs):
+    backs, a_blocks = refs[0], refs[1 : 1 + owners]
+    label, base, out, a_all, back_wide, sems = refs[1 + owners :]
     copies = load_factors(a_blocks, a_all, sems)
+    ready()
     rows, features = out.shape
     step = min(ROW_STEP, rows)
     width = a_all.shape[1]
@@ -210,19 +240,16 @@
             whole = base[at, c : c + chunk].astype(f32) + side.astype(f32)
             out[at, c : c + chunk] = whole.astype(bf16)
 
-
 def spread(low, label, k, columns):
     rows = low.shape[1]
     ids = lax.div(iota((columns, rows), 0), ADAPTER_RANK) + k * TEN_DEV
     tall = jnp.concatenate([low] * (columns // ADAPTER_RANK), axis=0)
     return jnp.where(ids == label, tall, 0.0).astype(bf16)
 
-
-def first_kernel(shards, owners, parity, *refs):
-    backs = refs[:shards]
-    label, acts = refs[shards : shards + 2]
-    arrived = refs[shards + 2] if parity == 0 else None
-    outs = refs[shards + 2 + (parity == 0) :]
+def first_kernel(owners, parity, ready, backs, label, acts, *refs):
+    arrived = refs[0] if parity == 0 else None
+    outs = refs[parity == 0 :]
+    ready()
     coefficient = adapter_scale * MODEL_WIDTH ** (-0.5)
     low = total(backs, slice(None))
     for n in range(owners // 2):
@@ -234,12 +261,12 @@
         else:
             outs[n][...] = (grad + arrived[n].astype(f32)).astype(bf16)
 
-
-def mid_kernel(owners, parts, *refs):
+def mid_kernel(owners, parts, ready, *refs):
     a_blocks = refs[:owners]
     label, acts = refs[owners], refs[owners + 1 : owners + 1 + parts]
     out, a_all, sems = refs[owners + 1 + parts :]
     copies = load_factors(a_blocks, a_all, sems)
+    ready()
     rows, width = acts[0].shape
     columns = a_blocks[0].shape[1]
     step = min(ROW_STEP, rows)
@@ -261,12 +288,11 @@
                 hit = where == k * TEN_DEV + q * (LANES // ADAPTER_RANK)
                 low = low + jnp.where(hit, wide[:, q * LANES : (q + 1) * LANES], 0.0)
         low = jnp.transpose(low).reshape(LANES // ADAPTER_RANK, ADAPTER_RANK, step)
-        out[:, at] = jnp.sum(low, axis=0).astype(bf16)
-
-
-def second_kernel(shards, owners, *refs):
-    mids = refs[:shards]
-    label, scaled, out, held = refs[shards:]
+        for j in range(out.shape[0]):
+            out[j, :, at] = jnp.sum(low, axis=0).astype(bf16)
+
+def second_kernel(owners, ready, mids, label, scaled, out, held):
+    ready()
     own_rows, keys = out.shape[1:]
     rows = scaled.shape[0]
     step = min(ROW_STEP, rows)
@@ -289,7 +315,6 @@
     for k in range(owners):
         out[me ^ k] = grad[k * own_rows : (k + 1) * own_rows]
 
-
 def adam_a_kernel(count, *refs):
     grads, (param, moment, second), outs = refs[:count], refs[count : count + 3], refs[count + 3 :]
     grad = grads[0][...].astype(f32)
@@ -299,14 +324,13 @@
     for out, value in zip(outs, new):
         out[...] = value
 
-
-def adam_b_kernel(grads, param, moment, second, *outs):
+def adam_b_kernel(ready, grads, param, moment, second, *outs):
+    ready()
     grad = jnp.sum(grads[...].astype(f32), axis=0)
     for out, value in zip(outs, adam_step(param[...], moment[...], second[...], grad)):
         out[...] = value
 
-
-def lay_kernel(*refs):
+def lay_kernel(ready, *refs):
     parts, out, sems = refs[:-2], refs[-2], refs[-1]
     shards, _, width = parts[0].shape
     copies = []
@@ -321,11 +345,12 @@
     for copy in copies:
         copy.wait()
 
-
 def swap(block, axis, bits):
     size = lax.axis_size(axis)
     return lax.ppermute(block, axis, [(i, i ^ bits) for i in range(size)])
 
+def exchange(blocks, axis):
+    return lax.all_to_all(blocks, axis, split_axis=0, concat_axis=0, tiled=True)
 
 def per_device(
     acts,
@@ -351,91 +376,109 @@
     width = features // parts
     b_lines = own_rows * keys // columns
     cut = shape((shards, row_count, width))
-    dma = pltpu.SemaphoreType.DMA
 
     share, low, *cuts = call(
         functools.partial(prep_kernel, parts),
-        [shape((row_count + LABEL_ROWS, keys)), shape((features + b_lines, columns))] + [cut] * parts,
+        [shape((shards, row_count + LABEL_ROWS, keys)), shape((features + b_lines, columns))]
+        + [cut] * parts,
         (acts, cotangent, tenant[None], advantage[None], a_param, b_param),
-        [dma((parts * shards,))],
-        [ANY] + [VMEM] * 5,
-        [VMEM] * 2 + [ANY] * parts,
-    )
-    shares = [share] + [swap(share, "fsdp", j) for j in range(1, shards)]
-    chips = [low] + [swap(low, "dp", k) for k in range(2, owners, 2)]
-    blocks = []
+        "rhhhhh",
+        "hh" + "r" * parts,
+        [DMA((parts * shards,))],
+    )
+    shares = exchange(share, "fsdp")
+    chips = [swap(low, "dp", k) for k in range(2, owners, 2)]
+    own = swap(low, "dp", 1)
+    shares, *rest = lax.optimization_barrier((shares, *chips, *cuts))
+    chips, cuts = rest[: len(chips)], rest[len(chips) :]
+    blocks = [low, own]
     for block in chips:
         blocks += [block, swap(block, "dp", 1)]
-    shares[1], *cuts = lax.optimization_barrier((shares[1], *cuts))
-    acts_parts = [
-        lax.all_to_all(c, "fsdp", split_axis=0, concat_axis=0, tiled=True).reshape(rows, width)
-        for c in cuts
-    ]
+    acts_parts = [exchange(c, "fsdp").reshape(rows, width) for c in cuts]
 
     scaled, label, base = call(
-        functools.partial(base_kernel, shards),
+        base_kernel,
         (shape((rows, keys)), shape((8, rows), jnp.int32), shape((rows, features))),
-        (*shares, base_weight),
-    )
-    back = call(
-        functools.partial(back_kernel, owners, own_rows),
-        shape((ADAPTER_RANK, rows)),
-        (*blocks, scaled, label),
-        [pltpu.VMEM((owners * own_rows, keys), bf16), dma((owners, keys // columns))],
-        [ANY] * owners + [VMEM] * 2,
-    )
-    backs = [back] + [swap(back, "fsdp", j) for j in range(1, shards)]
+        (shares, base_weight),
+        "hh",
+        "hvh",
+    )
+    backs = exchange(
+        call(
+            functools.partial(back_kernel, owners, own_rows),
+            shape((shards, ADAPTER_RANK, rows)),
+            (*blocks, scaled, label),
+            "r" * owners + "hv",
+            "h",
+            [pltpu.VMEM((owners * own_rows, keys), bf16), DMA((owners, keys // columns))],
+        ),
+        "fsdp",
+    )
 
     step = min(ROW_STEP, rows)
     factor_scratch = [pltpu.VMEM((features, owners * columns), bf16)]
-    sems = [dma((owners,))]
+    sems = [DMA((owners,))]
     grad_part = call(
-        functools.partial(side_kernel, shards, owners),
+        functools.partial(side_kernel, owners),
         shape((rows, features)),
-        (*backs, *blocks, label, base),
+        (backs, *blocks, label, base),
+        "h" + "r" * owners + "vh",
+        "h",
         factor_scratch + [pltpu.VMEM((step, owners * columns), bf16)] + sems,
-        [VMEM] * shards + [ANY] * owners + [VMEM] * 2,
-        vmem=24,
-    )
-    returned = lax.all_to_all(
-        grad_part.reshape(shards, row_count, features), "fsdp", 0, 0, tiled=True
-    )
+
+    )
+    grad_part, *acts_parts = lax.optimization_barrier((grad_part, *acts_parts))
+    returned = exchange(grad_part.reshape(shards, row_count, features), "fsdp")
     grad_input = call(
-        lay_kernel, shape((row_count, shards * features)), (returned,), [dma((shards,))], [ANY], ANY
+        lay_kernel, shape((row_count, shards * features)), (returned,), "r", "r", [DMA((shards,))]
     )
 
     grad_a = []
     for acts_part in acts_parts:
         odd = call(
-            functools.partial(first_kernel, shards, owners, 1),
+            functools.partial(first_kernel, owners, 1),
             shape((owners // 2, columns, width)),
-            (*backs, label, acts_part),
+            (backs, label, acts_part),
+            "hvh",
+            "h",
         )
         even = call(
-            functools.partial(first_kernel, shards, owners, 0),
+            functools.partial(first_kernel, owners, 0),
             [shape((columns, width))] * (owners // 2),
-            (*backs, label, acts_part, swap(odd, "dp", 1)),
+            (backs, label, acts_part, swap(odd, "dp", 1)),
+            "hvhh",
+            "h" * (owners // 2),
         )
-        grad_a.append([even[0]] + [swap(even[n], "dp", 2 * n) for n in range(1, owners // 2)])
-
-    mid = call(
-        functools.partial(mid_kernel, owners, parts),
-        shape((ADAPTER_RANK, rows)),
-        (*blocks, label, *acts_parts),
-        factor_scratch + sems,
-        [ANY] * owners + [VMEM] * (1 + parts),
-    )
-    mids = [mid] + [swap(mid, "fsdp", j) for j in range(1, shards)]
+        grad_a.append(list(even))
+    label, *grads = lax.optimization_barrier((label, *sum(grad_a, [])))
+    grad_a = [grads[h * (owners // 2) : (h + 1) * (owners // 2)] for h in range(parts)]
+    grad_a = [[g[0]] + [swap(g[n], "dp", 2 * n) for n in range(1, owners // 2)] for g in grad_a]
+
+    mids = exchange(
+        call(
+            functools.partial(mid_kernel, owners, parts),
+            shape((shards, ADAPTER_RANK, rows)),
+            (*blocks, label, *acts_parts),
+            "r" * owners + "v" + "h" * parts,
+            "h",
+            factor_scratch + sems,
+        ),
+        "fsdp",
+    )
     grad_b = call(
-        functools.partial(second_kernel, shards, owners),
+        functools.partial(second_kernel, owners),
         shape((owners, own_rows, keys)),
-        (*mids, label, scaled),
+        (mids, label, scaled),
+        "hvh",
+        "h",
         [pltpu.VMEM((ADAPTER_RANK, step), f32)],
     )
     new_b = call(
         adam_b_kernel,
         [shape(b_param.shape, f32)] * 3,
-        (lax.all_to_all(grad_b, "dp", 0, 0, tiled=True), b_param, b_moment, b_second),
+        (exchange(grad_b, "dp"), b_param, b_moment, b_second),
+        "hhhh",
+        "hhh",
     )
     block = min(256, width)
     steps = width // block
@@ -449,10 +492,9 @@
             out_shape=[shape(a_param.shape, f32)] * 3,
             in_specs=[wide] * (owners // 2) + [tall] * 3,
             out_specs=[tall] * 3,
-            compiler_params=pltpu.CompilerParams(vmem_limit_bytes=16 << 20),
+            compiler_params=pltpu.CompilerParams(vmem_limit_bytes=VMEM_BYTES),
         )(*grad_a[h], *new_a)
     return (grad_input, new_a[0], new_a[1], new_a[2], new_b[0], new_b[1], new_b[2])
-
 
 def solution(mesh):
     rows = P(("dp", "fsdp"), None)

time: 154 us -> 226 us (1.47)
  Pallas kernels: 27 us -> 111 us
  blocking collectives: 0 us -> 21.6 us
  local copies, waits for them, and re-layouts: 20.8 us -> 2.02 us
  starting transfers between devices: 39.5 us -> 24.6 us
    pallas_call x10, Pallas kernels: 22.7 us -> 106 us  [call(): pl.pallas_call(kernel, out_shape=outs, in_specs=[VMEM if kind == 'v' else...]
    all_to_all x0 -> x2, blocking collectives: none -> 21.6 us  [exchange(): return lax.all_to_all(blocks, axis, split_axis=0, concat_axis=0, tiled=True)]
    ppermute x20 -> x11, starting transfers between devices: 26.8 us -> 7.69 us  [swap(): return lax.ppermute(block, axis, [(i, i ^ bits) for i in range(size)])]
    all_to_all x3 -> x4, waiting for transfers between devices: 16.5 us -> 35.4 us  [exchange(): return lax.all_to_all(blocks, axis, split_axis=0, concat_axis=0, tiled=True)]
    unnamed x74 -> x12, local copies, waits for them, and re-layouts: 20.8 us -> 2.02 us
    ppermute x20 -> x11, waiting for transfers between devices: 48.2 us -> 29.8 us  [swap(): return lax.ppermute(block, axis, [(i, i ^ bits) for i in range(size)])]
    all_to_all x3 -> x4, starting transfers between devices: 12.7 us -> 16.9 us  [exchange(): return lax.all_to_all(blocks, axis, split_axis=0, concat_axis=0, tiled=True)]
  transfers between devices with their start and end apart: 23 -> 15, of which waited for: 12 -> 6; matrix products, arithmetic and copies ran while one was open for 0% -> 0% of each run, Pallas kernels for 12% -> 23%
where the time goes in v4:
time: 226 us; the launch traced here: 225 us
  Pallas kernels  111 us (49%)
  waiting for transfers between devices  65.2 us (29%)
  starting transfers between devices  24.6 us (11%)
  blocking collectives  21.6 us (10%)
    pallas_call x10, Pallas kernels, call(): pl.pallas_call(kernel, out_shape=outs, in_specs=[VMEM if kind == 'v' else...  106 us
    all_to_all x4, waiting for transfers between devices, exchange(): return lax.all_to_all(blocks, axis, split_axis=0, concat_axis=0, tiled=True)  35.4 us
    ppermute x11, waiting for transfers between devices, swap(): return lax.ppermute(block, axis, [(i, i ^ bits) for i in range(size)])  29.8 us
    all_to_all x2, blocking collectives, exchange(): return lax.all_to_all(blocks, axis, split_axis=0, concat_axis=0, tiled=True)  21.6 us
    all_to_all x4, starting transfers between devices, exchange(): return lax.all_to_all(blocks, axis, split_axis=0, concat_axis=0, tiled=True)  16.9 us
    ppermute x11, starting transfers between devices, swap(): return lax.ppermute(block, axis, [(i, i ^ bits) for i in range(size)])  7.69 us
    pallas_call x1, Pallas kernels, per_device(): pl.pallas_call(functools.partial(adam_a_kernel, owners // 2), grid=(steps...  5.03 us
  transfers between devices with their start and end apart: 15, of which 6 were waited for; matrix products, arithmetic and copies ran while one was open for 0% of the time, Pallas kernels for 23%

profile of v4, /device:TPU:0, one launch (start us, length us, event | category | flops | bytes accessed | tf_op | source)
XLA Modules:
  0.0 224.9 jit_solution(793310835898279045)
XLA Ops:
  0.6 34.0 %shard_map.162 = (bf16[4,144,512]{2,1,0:T(8,128)(2,1)}, bf16[1152,256]{1,0:T(8,128)(2,1)}, bf16[4,128,1024]{2,1,0:T(8,128)(2,1)}) custom-call(bf16[128,4096]{1,0:T(8,128)(2,1)} %refs_0_.1, bf16[128,512]{1,0:T(8,128)(2,1)} %refs_1_.3, s32[1,128]{1,0:T(1,128)} %bitcast.8, s32[1,128]{1,0:T(1,128)} %bitcast.9, f32[1024,256]{1,0:T(8,128)} %refs_4_.3, ...), custom_call_target="tpu_custom_call" | custom-call | tf_op jit(solution)/shard_map/pallas_call | solution.py:74
  34.6 6.3 %all-to-all-start = ((bf16[4,144,512]{2,1,0:T(8,128)(2,1)}), bf16[4,144,512]{2,1,0:T(8,128)(2,1)S(1)}, u32[]{:S(2)}, u32[]{:S(2)}) async-start(bf16[4,144,512]{2,1,0:T(8,128)(2,1)} %get-tuple-element.36), calls=%async_computation | async-start | bytes 1179648 | tf_op jit(solution)/shard_map/all_to_all | solution.py:353
  40.9 2.4 %collective-permute-start.3 = (bf16[1152,256]{1,0:T(8,128)(2,1)}, bf16[1152,256]{1,0:T(8,128)(2,1)S(1)}, u32[]{:S(2)}, u32[]{:S(2)}) collective-permute-start(bf16[1152,256]{1,0:T(8,128)(2,1)} %get-tuple-element.35.refs_0_.refs_1_), channel_id=1, source_target_pairs={{0,24},{4,28},{8,16},{12,20},{16,8},{20,12},{24,0},{28,4},{1,25},{... | collective-permute-start | bytes 1769480 | tf_op jit(solution)/shard_map/ppermute | solution.py:350
  43.4 0.5 collective-permute-start.2
  43.9 0.5 collective-permute-start.1
  44.4 0.0 collective-permute-start
  44.4 13.9 %collective-permute-done.3.refs_6_.refs_7_ = bf16[1152,256]{1,0:T(8,128)(2,1)S(1)} collective-permute-done((bf16[1152,256]{1,0:T(8,128)(2,1)}, bf16[1152,256]{1,0:T(8,128)(2,1)S(1)}, u32[]{:S(2)}, u32[]{:S(2)}) %collective-permute-start.3) | collective-permute-done | bytes 589856 | tf_op jit(solution)/shard_map/ppermute | solution.py:350
  58.4 0.0 copy-start.1
  58.4 11.1 %collective-permute-done.2.refs_4_.refs_5_ = bf16[1152,256]{1,0:T(8,128)(2,1)S(1)} collective-permute-done((bf16[1152,256]{1,0:T(8,128)(2,1)}, bf16[1152,256]{1,0:T(8,128)(2,1)S(1)}, u32[]{:S(2)}, u32[]{:S(2)}) %collective-permute-start.2) | collective-permute-done | bytes 589856 | tf_op jit(solution)/shard_map/ppermute | solution.py:350
  69.5 0.0 copy-start.2
  69.5 0.2 collective-permute-done.1.refs_2_.refs_3_
  69.7 0.0 all-to-all-done.refs_0_
  69.7 0.0 copy-start.4
  69.7 0.0 collective-permute-start.4
  69.7 0.5 collective-permute-start.5
  70.2 0.1 collective-permute-start.6
  70.3 0.2 copy-done.4
  70.5 3.8 %shard_map.163 = (bf16[512,512]{1,0:T(8,128)(2,1)}, s32[8,512]{1,0:T(8,128)}, bf16[512,1024]{1,0:T(8,128)(2,1)}) custom-call(bf16[4,144,512]{2,1,0:T(8,128)(2,1)} %copy-done.4, bf16[1024,512]{1,0:T(8,128)(2,1)} %refs_1_.4), custom_call_target="tpu_custom_call" | custom-call | tf_op jit(solution)/shard_map/pallas_call | solution.py:74
  74.3 0.0 collective-permute-done.refs_1_.refs_2_
  74.3 0.0 collective-permute-done.4.refs_3_.refs_4_
  74.3 0.0 collective-permute-done.5.refs_5_.refs_6_
  74.3 0.0 collective-permute-done.6.refs_7_.refs_8_
  74.3 0.0 copy-done.1
  74.3 0.0 copy-done.2
  74.3 3.4 %shard_map.164 = bf16[4,32,512]{2,1,0:T(8,128)(2,1)} custom-call(bf16[1152,256]{1,0:T(8,128)(2,1)} %get-tuple-element.35.refs_0_.refs_1_, bf16[1152,256]{1,0:T(8,128)(2,1)} %collective-permute-done.refs_1_.refs_2_, bf16[1152,256]{1,0:T(8,128)(2,1)} %collective-permute-done.1.refs_2_.refs_3_, bf16[1152,256]{1,0:T(8,128)(2,1)} %collective-permute-done.4.refs_3_.refs_4_, ...), custom_call_target="tpu_custom_call" | custom-call | tf_op jit(solution)/shard_map/pallas_call | solution.py:74
  77.7 11.2 %all_to_all.30.refs_0_ = bf16[4,32,512]{2,1,0:T(8,128)(2,1)} all-to-all(bf16[4,32,512]{2,1,0:T(8,128)(2,1)} %shard_map.164), channel_id=1, replica_groups=mesh['dp'=8,'fsdp'=4] {'fsdp'}, dimensions={0} | all-to-all | bytes 262144 | tf_op jit(solution)/shard_map/all_to_all | solution.py:353
  88.9 3.5 %all-to-all-start.2 = ((bf16[4,128,1024]{2,1,0:T(8,128)(2,1)}), bf16[4,128,1024]{2,1,0:T(8,128)(2,1)S(1)}, u32[]{:S(2)}, u32[]{:S(2)}) async-start(bf16[4,128,1024]{2,1,0:T(8,128)(2,1)} %get-tuple-element.45), calls=%async_computation.2 | async-start | bytes 2097152 | tf_op jit(solution)/shard_map/all_to_all | solution.py:353
  92.4 7.4 %shard_map.165 = bf16[512,1024]{1,0:T(8,128)(2,1)} custom-call(bf16[4,32,512]{2,1,0:T(8,128)(2,1)} %all_to_all.30.refs_0_, bf16[1152,256]{1,0:T(8,128)(2,1)} %get-tuple-element.35.refs_0_.refs_1_, bf16[1152,256]{1,0:T(8,128)(2,1)} %collective-permute-done.refs_1_.refs_2_, bf16[1152,256]{1,0:T(8,128)(2,1)} %collective-permute-done.1.refs_2_.refs_3_, ...), custom_call_target="tpu_custom_call" | custom-call | tf_op jit(solution)/shard_map/pallas_call | solution.py:74
  99.8 17.3 %all-to-all-done.2 = bf16[4,128,1024]{2,1,0:T(8,128)(2,1)S(1)} async-done(((bf16[4,128,1024]{2,1,0:T(8,128)(2,1)}), bf16[4,128,1024]{2,1,0:T(8,128)(2,1)S(1)}, u32[]{:S(2)}, u32[]{:S(2)}) %all-to-all-start.2) | async-done | bytes 1048608 | tf_op jit(solution)/shard_map/all_to_all | solution.py:353
  117.1 0.0 copy-start
  117.1 1.0 copy-done
  118.1 4.6 %shard_map.167 = bf16[4,256,1024]{2,1,0:T(8,128)(2,1)} custom-call(bf16[4,32,512]{2,1,0:T(8,128)(2,1)} %all_to_all.30.refs_0_, s32[8,512]{1,0:T(8,128)} %get-tuple-element.59.refs_9_.refs_1_.refs_8_, bf16[512,1024]{1,0:T(8,128)(2,1)} %bitcast.4), custom_call_target="tpu_custom_call" | custom-call | tf_op jit(solution)/shard_map/pallas_call | solution.py:74
  122.7 0.1 collective-permute-start.7
  122.8 4.5 %collective-permute-done.7.refs_3_ = bf16[4,256,1024]{2,1,0:T(8,128)(2,1)} collective-permute-done((bf16[4,256,1024]{2,1,0:T(8,128)(2,1)}, bf16[4,256,1024]{2,1,0:T(8,128)(2,1)}, u32[]{:S(2)}, u32[]{:S(2)}) %collective-permute-start.7) | collective-permute-done | bytes 2097184 | tf_op jit(solution)/shard_map/ppermute | solution.py:350
  127.3 4.9 %shard_map.168 = (bf16[256,1024]{1,0:T(8,128)(2,1)}, bf16[256,1024]{1,0:T(8,128)(2,1)}, bf16[256,1024]{1,0:T(8,128)(2,1)}, bf16[256,1024]{1,0:T(8,128)(2,1)}) custom-call(bf16[4,32,512]{2,1,0:T(8,128)(2,1)} %all_to_all.30.refs_0_, s32[8,512]{1,0:T(8,128)} %get-tuple-element.59.refs_9_.refs_1_.refs_8_, bf16[512,1024]{1,0:T(8,128)(2,1)} %bitcast.5, ...), custom_call_target="tpu_custom_call" | custom-call | tf_op jit(solution)/shard_map/pallas_call | solution.py:74
  132.2 9.6 %shard_map.170 = bf16[4,32,512]{2,1,0:T(8,128)(2,1)} custom-call(bf16[1152,256]{1,0:T(8,128)(2,1)} %get-tuple-element.35.refs_0_.refs_1_, bf16[1152,256]{1,0:T(8,128)(2,1)} %collective-permute-done.refs_1_.refs_2_, bf16[1152,256]{1,0:T(8,128)(2,1)} %collective-permute-done.1.refs_2_.refs_3_, bf16[1152,256]{1,0:T(8,128)(2,1)} %collective-permute-done.4.refs_3_.refs_4_, ...), custom_call_target="tpu_custom_call" | custom-call | tf_op jit(solution)/shard_map/pallas_call | solution.py:74
  141.8 10.4 %all_to_all.31.refs_0_ = bf16[4,32,512]{2,1,0:T(8,128)(2,1)} all-to-all(bf16[4,32,512]{2,1,0:T(8,128)(2,1)} %shard_map.170), channel_id=1, replica_groups=mesh['dp'=8,'fsdp'=4] {'fsdp'}, dimensions={0} | all-to-all | bytes 262144 | tf_op jit(solution)/shard_map/all_to_all | solution.py:353
  152.2 3.5 %all-to-all-start.3 = ((bf16[4,128,1024]{2,1,0:T(8,128)(2,1)}), bf16[4,128,1024]{2,1,0:T(8,128)(2,1)S(1)}, u32[]{:S(2)}, u32[]{:S(2)}) async-start(bf16[4,128,1024]{2,1,0:T(8,128)(2,1)} %bitcast.7), calls=%async_computation.3 | async-start | bytes 2097152 | tf_op jit(solution)/shard_map/all_to_all | solution.py:353
  155.7 1.6 collective-permute-start.8
  157.3 0.7 collective-permute-start.9
  158.0 1.3 collective-permute-start.10
  159.3 3.1 %shard_map.171 = bf16[8,64,512]{2,1,0:T(8,128)(2,1)} custom-call(bf16[4,32,512]{2,1,0:T(8,128)(2,1)} %all_to_all.31.refs_0_, s32[8,512]{1,0:T(8,128)} %get-tuple-element.59.refs_9_.refs_1_.refs_8_, bf16[512,512]{1,0:T(8,128)(2,1)} %get-tuple-element.42.refs_8_.refs_2_), custom_call_target="tpu_custom_call" | custom-call | tf_op jit(solution)/shard_map/pallas_call | solution.py:74
  162.4 18.1 %all-to-all-done.3.refs_0_ = bf16[4,128,1024]{2,1,0:T(8,128)(2,1)S(1)} async-done(((bf16[4,128,1024]{2,1,0:T(8,128)(2,1)}), bf16[4,128,1024]{2,1,0:T(8,128)(2,1)S(1)}, u32[]{:S(2)}, u32[]{:S(2)}) %all-to-all-start.3) | async-done | bytes 1048608 | tf_op jit(solution)/shard_map/all_to_all | solution.py:353
  180.5 0.0 copy-start.3
  180.5 3.5 %all-to-all-start.5 = ((bf16[8,64,512]{2,1,0:T(8,128)(2,1)}), bf16[8,64,512]{2,1,0:T(8,128)(2,1)S(1)}, u32[]{:S(2)}, u32[]{:S(2)}) async-start(bf16[8,64,512]{2,1,0:T(8,128)(2,1)} %shard_map.171), calls=%async_computation.5 | async-start | bytes 1048576 | tf_op jit(solution)/shard_map/all_to_all | solution.py:353
  184.0 0.0 copy-done.3
  184.0 32.9 %shard_map.166 = bf16[128,4096]{1,0:T(8,128)(2,1)} custom-call(bf16[4,128,1024]{2,1,0:T(8,128)(2,1)} %copy-done.3), custom_call_target="tpu_custom_call" | custom-call | tf_op jit(solution)/shard_map/pallas_call | solution.py:74
  216.9 0.0 collective-permute-done.8.refs_1_
  216.9 0.0 collective-permute-done.9.refs_2_
  217.0 0.0 collective-permute-done.10.refs_3_
  217.0 5.0 %shard_map.169 = (f32[1024,256]{1,0:T(8,128)}, f32[1024,256]{1,0:T(8,128)}, f32[1024,256]{1,0:T(8,128)}) custom-call(bf16[256,1024]{1,0:T(8,128)(2,1)} %get-tuple-element.52.refs_0_, bf16[256,1024]{1,0:T(8,128)(2,1)} %collective-permute-done.8.refs_1_, bf16[256,1024]{1,0:T(8,128)(2,1)} %collective-permute-done.9.refs_2_, ...), custom_call_target="tpu_custom_call" | custom-call | tf_op jit(solution)/shard_map/pallas_call | solution.py:489
  222.0 0.0 all-to-all-done.5.refs_0_
  222.0 0.0 copy-start.5
  222.0 0.8 copy-done.5
  222.8 2.1 shard_map.172
Async XLA Ops:
  34.6 35.1 %all-to-all-start = ((bf16[4,144,512]{2,1,0:T(8,128)(2,1)}), bf16[4,144,512]{2,1,0:T(8,128)(2,1)S(1)}, u32[]{:S(2)}, u32[]{:S(2)}) async-start(bf16[4,144,512]{2,1,0:T(8,128)(2,1)} %get-tuple-element.36), calls=%async_computation | async-start | bytes 1179648 | tf_op jit(solution)/shard_map/all_to_all | solution.py:353
  40.9 17.4 %collective-permute-start.3 = (bf16[1152,256]{1,0:T(8,128)(2,1)}, bf16[1152,256]{1,0:T(8,128)(2,1)S(1)}, u32[]{:S(2)}, u32[]{:S(2)}) collective-permute-start(bf16[1152,256]{1,0:T(8,128)(2,1)} %get-tuple-element.35.refs_0_.refs_1_), channel_id=1, source_target_pairs={{0,24},{4,28},{8,16},{12,20},{16,8},{20,12},{24,0},{28,4},{1,25},{... | collective-permute-start | bytes 1769480 | tf_op jit(solution)/shard_map/ppermute | solution.py:350
  43.4 26.1 %collective-permute-start.2 = (bf16[1152,256]{1,0:T(8,128)(2,1)}, bf16[1152,256]{1,0:T(8,128)(2,1)S(1)}, u32[]{:S(2)}, u32[]{:S(2)}) collective-permute-start(bf16[1152,256]{1,0:T(8,128)(2,1)} %get-tuple-element.35.refs_0_.refs_1_), channel_id=1, source_target_pairs={{0,16},{4,20},{8,24},{12,28},{16,0},{20,4},{24,8},{28,12},{1,17},{... | collective-permute-start | bytes 1769480 | tf_op jit(solution)/shard_map/ppermute | solution.py:350
  43.9 25.8 %collective-permute-start.1 = (bf16[1152,256]{1,0:T(8,128)(2,1)}, bf16[1152,256]{1,0:T(8,128)(2,1)}, u32[]{:S(2)}, u32[]{:S(2)}) collective-permute-start(bf16[1152,256]{1,0:T(8,128)(2,1)} %get-tuple-element.35.refs_0_.refs_1_), channel_id=1, source_target_pairs={{0,8},{4,12},{8,0},{12,4},{16,24},{20,28},{24,16},{28,20},{1,9},{5... | collective-permute-start | bytes 1769480 | tf_op jit(solution)/shard_map/ppermute | solution.py:350
  44.4 29.9 %collective-permute-start = (bf16[1152,256]{1,0:T(8,128)(2,1)}, bf16[1152,256]{1,0:T(8,128)(2,1)}, u32[]{:S(2)}, u32[]{:S(2)}) collective-permute-start(bf16[1152,256]{1,0:T(8,128)(2,1)} %get-tuple-element.35.refs_0_.refs_1_), channel_id=1, source_target_pairs={{0,4},{4,0},{8,12},{12,8},{16,20},{20,16},{24,28},{28,24},{1,5},{5... | collective-permute-start | bytes 1769480 | tf_op jit(solution)/shard_map/ppermute | solution.py:350
  58.4 16.0 %copy-start.1 = (bf16[1152,256]{1,0:T(8,128)(2,1)}, bf16[1152,256]{1,0:T(8,128)(2,1)S(1)}, u32[]{:S(2)}) copy-start(bf16[1152,256]{1,0:T(8,128)(2,1)S(1)} %collective-permute-done.3.refs_6_.refs_7_) | copy-start | bytes 1769476
  69.5 4.9 %copy-start.2 = (bf16[1152,256]{1,0:T(8,128)(2,1)}, bf16[1152,256]{1,0:T(8,128)(2,1)S(1)}, u32[]{:S(2)}) copy-start(bf16[1152,256]{1,0:T(8,128)(2,1)S(1)} %collective-permute-done.2.refs_4_.refs_5_) | copy-start | bytes 1769476
  69.7 0.8 copy-start.4
  69.7 4.6 %collective-permute-start.4 = (bf16[1152,256]{1,0:T(8,128)(2,1)}, bf16[1152,256]{1,0:T(8,128)(2,1)}, u32[]{:S(2)}, u32[]{:S(2)}) collective-permute-start(bf16[1152,256]{1,0:T(8,128)(2,1)} %collective-permute-done.1.refs_2_.refs_3_), channel_id=1, source_target_pairs={{0,4},{4,0},{8,12},{12,8},{16,20},{20,16},{24,28},{28,24},{1,5},{5... | collective-permute-start | bytes 1769480 | tf_op jit(solution)/shard_map/ppermute | solution.py:350
  69.7 4.6 %collective-permute-start.5 = (bf16[1152,256]{1,0:T(8,128)(2,1)S(1)}, bf16[1152,256]{1,0:T(8,128)(2,1)}, u32[]{:S(2)}, u32[]{:S(2)}) collective-permute-start(bf16[1152,256]{1,0:T(8,128)(2,1)S(1)} %collective-permute-done.2.refs_4_.refs_5_), channel_id=1, source_target_pairs={{0,4},{4,0},{8,12},{12,8},{16,20},{20,16},{24,28},{28,24},{1,5},{5... | collective-permute-start | bytes 1769480 | tf_op jit(solution)/shard_map/ppermute | solution.py:350
  70.2 4.1 %collective-permute-start.6 = (bf16[1152,256]{1,0:T(8,128)(2,1)S(1)}, bf16[1152,256]{1,0:T(8,128)(2,1)}, u32[]{:S(2)}, u32[]{:S(2)}) collective-permute-start(bf16[1152,256]{1,0:T(8,128)(2,1)S(1)} %collective-permute-done.3.refs_6_.refs_7_), channel_id=1, source_target_pairs={{0,4},{4,0},{8,12},{12,8},{16,20},{20,16},{24,28},{28,24},{1,5},{5... | collective-permute-start | bytes 1769480 | tf_op jit(solution)/shard_map/ppermute | solution.py:350
  88.9 28.2 %all-to-all-start.2 = ((bf16[4,128,1024]{2,1,0:T(8,128)(2,1)}), bf16[4,128,1024]{2,1,0:T(8,128)(2,1)S(1)}, u32[]{:S(2)}, u32[]{:S(2)}) async-start(bf16[4,128,1024]{2,1,0:T(8,128)(2,1)} %get-tuple-element.45), calls=%async_computation.2 | async-start | bytes 2097152 | tf_op jit(solution)/shard_map/all_to_all | solution.py:353
  117.1 1.0 copy-start
  122.7 4.6 %collective-permute-start.7 = (bf16[4,256,1024]{2,1,0:T(8,128)(2,1)}, bf16[4,256,1024]{2,1,0:T(8,128)(2,1)}, u32[]{:S(2)}, u32[]{:S(2)}) collective-permute-start(bf16[4,256,1024]{2,1,0:T(8,128)(2,1)} %shard_map.167), channel_id=1, source_target_pairs={{0,4},{4,0},{8,12},{12,8},{16,20},{20,16},{24,28},{28,24},{1,5},{5... | collective-permute-start | bytes 6291464 | tf_op jit(solution)/shard_map/ppermute | solution.py:350
  152.2 28.3 %all-to-all-start.3 = ((bf16[4,128,1024]{2,1,0:T(8,128)(2,1)}), bf16[4,128,1024]{2,1,0:T(8,128)(2,1)S(1)}, u32[]{:S(2)}, u32[]{:S(2)}) async-start(bf16[4,128,1024]{2,1,0:T(8,128)(2,1)} %bitcast.7), calls=%async_computation.3 | async-start | bytes 2097152 | tf_op jit(solution)/shard_map/all_to_all | solution.py:353
  155.7 61.2 %collective-permute-start.8 = (bf16[256,1024]{1,0:T(8,128)(2,1)}, bf16[256,1024]{1,0:T(8,128)(2,1)}, u32[]{:S(2)}, u32[]{:S(2)}) collective-permute-start(bf16[256,1024]{1,0:T(8,128)(2,1)} %get-tuple-element.53), channel_id=1, source_target_pairs={{0,8},{4,12},{8,0},{12,4},{16,24},{20,28},{24,16},{28,20},{1,9},{5... | collective-permute-start | bytes 1572872 | tf_op jit(solution)/shard_map/ppermute | solution.py:350
  157.3 59.7 %collective-permute-start.9 = (bf16[256,1024]{1,0:T(8,128)(2,1)}, bf16[256,1024]{1,0:T(8,128)(2,1)}, u32[]{:S(2)}, u32[]{:S(2)}) collective-permute-start(bf16[256,1024]{1,0:T(8,128)(2,1)} %get-tuple-element.54), channel_id=1, source_target_pairs={{0,16},{4,20},{8,24},{12,28},{16,0},{20,4},{24,8},{28,12},{1,17},{... | collective-permute-start | bytes 1572872 | tf_op jit(solution)/shard_map/ppermute | solution.py:350
  158.0 59.0 %collective-permute-start.10 = (bf16[256,1024]{1,0:T(8,128)(2,1)}, bf16[256,1024]{1,0:T(8,128)(2,1)}, u32[]{:S(2)}, u32[]{:S(2)}) collective-permute-start(bf16[256,1024]{1,0:T(8,128)(2,1)} %get-tuple-element.55), channel_id=1, source_target_pairs={{0,24},{4,28},{8,16},{12,20},{16,8},{20,12},{24,0},{28,4},{1,25},{... | collective-permute-start | bytes 1572872 | tf_op jit(solution)/shard_map/ppermute | solution.py:350
  180.5 3.5 %copy-start.3 = (bf16[4,128,1024]{2,1,0:T(8,128)(2,1)}, bf16[4,128,1024]{2,1,0:T(8,128)(2,1)S(1)}, u32[]{:S(2)}) copy-start(bf16[4,128,1024]{2,1,0:T(8,128)(2,1)S(1)} %all-to-all-done.3.refs_0_) | copy-start | bytes 3145732
  180.5 41.5 %all-to-all-start.5 = ((bf16[8,64,512]{2,1,0:T(8,128)(2,1)}), bf16[8,64,512]{2,1,0:T(8,128)(2,1)S(1)}, u32[]{:S(2)}, u32[]{:S(2)}) async-start(bf16[8,64,512]{2,1,0:T(8,128)(2,1)} %shard_map.171), calls=%async_computation.5 | async-start | bytes 1048576 | tf_op jit(solution)/shard_map/all_to_all | solution.py:353
  222.0 0.8 copy-start.5

commit v5 on v4

--- a/solution.py
+++ b/solution.py
@@ -13,7 +13,8 @@
 LANES = 128
 ROW_STEP = 512
 LABEL_ROWS = 16
-VMEM_BYTES = 62 << 20
+ROOMY = 48
+FULL = 62
 PARTS = 1
 
 adapter_scale = 2.0
@@ -33,7 +34,7 @@
 def shape(dims, kind=bf16):
     return jax.ShapeDtypeStruct(tuple(dims), kind)
 
-def call(body, outs, ins, kinds, out_kinds, scratch=()):
+def call(body, outs, ins, kinds, out_kinds, scratch=(), vmem=ROOMY):
     single = not isinstance(outs, (list, tuple))
     outs = [outs] if single else list(outs)
     staged = [x for x, kind in zip(ins, kinds) if kind == "h"]
@@ -46,7 +47,7 @@
         given, made = refs[: len(ins)], refs[len(ins) : len(ins) + len(outs)]
         rest = refs[len(ins) + len(outs) :]
         held, own = rest[:count], rest[count : len(rest) - bool(count)]
-        sems = rest[-1]
+        sems = rest[-1] if count else None
         loads, stores = [], []
         for n, kind in enumerate(kinds):
             if kind == "h":
@@ -77,7 +78,7 @@
         in_specs=[VMEM if kind == "v" else HBM for kind in kinds],
         out_specs=[VMEM if kind == "v" else HBM for kind in out_kinds],
         scratch_shapes=buffers + list(scratch) + ([DMA((count,))] if count else []),
-        compiler_params=pltpu.CompilerParams(vmem_limit_bytes=VMEM_BYTES),
+        compiler_params=pltpu.CompilerParams(vmem_limit_bytes=vmem << 20),
         cost_estimate=pl.CostEstimate(flops=0, bytes_accessed=0, transcendentals=0),
     )(*ins)
     return result[0] if single else result
@@ -104,18 +105,13 @@
 
 def prep_kernel(parts, ready, *refs):
     acts, cot, tenant, advantage, a_param, b_param, share, low = refs[:8]
-    cuts, sems = refs[8 : 8 + parts], refs[-1]
+    cuts = refs[8:]
     shards, _, width = cuts[0].shape
-    copies = []
+    ready()
     for h in range(parts):
         for j in range(shards):
-            at = pl.ds((j * parts + h) * width, width)
-            copies.append(
-                pltpu.make_async_copy(acts.at[:, at], cuts[h].at[j], sems.at[h * shards + j])
-            )
-    for copy in copies:
-        copy.start()
-    ready()
+            at = (j * parts + h) * width
+            cuts[h][j] = acts[:, at : at + width]
     rows, keys = cot.shape
     factor = column_of(advantage[...]) * 0.25
     factor = jnp.concatenate([factor] * (keys // LANES), axis=1)
@@ -136,8 +132,6 @@
     for q in range(keys // columns):
         part = b_param[:, q * columns : (q + 1) * columns] * ADAPTER_RANK ** (-0.5)
         low[features + q * own_rows : features + (q + 1) * own_rows] = part.astype(bf16)
-    for copy in copies:
-        copy.wait()
 
 def second_ids(owners, own_rows, rows):
     line = iota((owners * own_rows, rows), 0)
@@ -193,11 +187,13 @@
             part = lax.div(iota(low.shape, 0), own_rows)
             place = lax.rem(lax.axis_index("fsdp"), ADAPTER_RANK // own_rows)
             low = jnp.where(part == place, low, 0.0)
-        for j in range(back.shape[0]):
-            back[j, :, r : r + step] = low.astype(bf16)
+        back[:, r : r + step] = low.astype(bf16)
 
 def total(parts, at):
-    return jnp.sum(parts[:, :, at].astype(f32), axis=0)
+    value = parts[0][:, at].astype(f32)
+    for part in parts[1:]:
+        value = value + part[:, at].astype(f32)
+    return value
 
 def load_factors(a_blocks, a_all, sems):
     columns = a_blocks[0].shape[1]
@@ -213,9 +209,9 @@
         copy.start()
     return copies
 
-def side_kernel(owners, ready, *refs):
-    backs, a_blocks = refs[0], refs[1 : 1 + owners]
-    label, base, out, a_all, back_wide, sems = refs[1 + owners :]
+def side_kernel(shards, owners, ready, *refs):
+    backs, a_blocks = refs[:shards], refs[shards : shards + owners]
+    label, base, out, a_all, back_wide, sems = refs[shards + owners :]
     copies = load_factors(a_blocks, a_all, sems)
     ready()
     rows, features = out.shape
@@ -246,9 +242,10 @@
     tall = jnp.concatenate([low] * (columns // ADAPTER_RANK), axis=0)
     return jnp.where(ids == label, tall, 0.0).astype(bf16)
 
-def first_kernel(owners, parity, ready, backs, label, acts, *refs):
-    arrived = refs[0] if parity == 0 else None
-    outs = refs[parity == 0 :]
+def first_kernel(shards, owners, parity, ready, *refs):
+    backs, (label, acts) = refs[:shards], refs[shards : shards + 2]
+    arrived = refs[shards + 2] if parity == 0 else None
+    outs = refs[shards + 2 + (parity == 0) :]
     ready()
     coefficient = adapter_scale * MODEL_WIDTH ** (-0.5)
     low = total(backs, slice(None))
@@ -288,11 +285,10 @@
                 hit = where == k * TEN_DEV + q * (LANES // ADAPTER_RANK)
                 low = low + jnp.where(hit, wide[:, q * LANES : (q + 1) * LANES], 0.0)
         low = jnp.transpose(low).reshape(LANES // ADAPTER_RANK, ADAPTER_RANK, step)
-        for j in range(out.shape[0]):
-            out[j, :, at] = jnp.sum(low, axis=0).astype(bf16)
-
-def second_kernel(owners, ready, mids, label, scaled, out, held):
-    ready()
+        out[:, at] = jnp.sum(low, axis=0).astype(bf16)
+
+def second_kernel(shards, owners, ready, *refs):
+    mids, (label, scaled, out, held) = refs[:shards], refs[shards:]
     own_rows, keys = out.shape[1:]
     rows = scaled.shape[0]
     step = min(ROW_STEP, rows)
@@ -332,6 +328,7 @@
 
 def lay_kernel(ready, *refs):
     parts, out, sems = refs[:-2], refs[-2], refs[-1]
+    ready()
     shards, _, width = parts[0].shape
     copies = []
     for h, part in enumerate(parts):
@@ -382,9 +379,9 @@
         [shape((shards, row_count + LABEL_ROWS, keys)), shape((features + b_lines, columns))]
         + [cut] * parts,
         (acts, cotangent, tenant[None], advantage[None], a_param, b_param),
-        "rhhhhh",
-        "hh" + "r" * parts,
-        [DMA((parts * shards,))],
+        "h" * 6,
+        "hh" + "h" * parts,
+        vmem=FULL,
     )
     shares = exchange(share, "fsdp")
     chips = [swap(low, "dp", k) for k in range(2, owners, 2)]
@@ -400,85 +397,81 @@
         base_kernel,
         (shape((rows, keys)), shape((8, rows), jnp.int32), shape((rows, features))),
         (shares, base_weight),
-        "hh",
-        "hvh",
-    )
-    backs = exchange(
-        call(
-            functools.partial(back_kernel, owners, own_rows),
-            shape((shards, ADAPTER_RANK, rows)),
-            (*blocks, scaled, label),
-            "r" * owners + "hv",
-            "h",
-            [pltpu.VMEM((owners * own_rows, keys), bf16), DMA((owners, keys // columns))],
-        ),
-        "fsdp",
-    )
+        "vv",
+        "vvv",
+    )
+    back = call(
+        functools.partial(back_kernel, owners, own_rows),
+        shape((ADAPTER_RANK, rows)),
+        (*blocks, scaled, label),
+        "r" * owners + "vv",
+        "v",
+        [pltpu.VMEM((owners * own_rows, keys), bf16), DMA((owners, keys // columns))],
+    )
+    backs = [back] + [swap(back, "fsdp", j) for j in range(1, shards)]
 
     step = min(ROW_STEP, rows)
     factor_scratch = [pltpu.VMEM((features, owners * columns), bf16)]
     sems = [DMA((owners,))]
     grad_part = call(
-        functools.partial(side_kernel, owners),
+        functools.partial(side_kernel, shards, owners),
         shape((rows, features)),
-        (backs, *blocks, label, base),
-        "h" + "r" * owners + "vh",
-        "h",
+        (*backs, *blocks, label, base),
+        "v" * shards + "r" * owners + "vv",
+        "v",
         factor_scratch + [pltpu.VMEM((step, owners * columns), bf16)] + sems,
 
     )
     grad_part, *acts_parts = lax.optimization_barrier((grad_part, *acts_parts))
     returned = exchange(grad_part.reshape(shards, row_count, features), "fsdp")
     grad_input = call(
-        lay_kernel, shape((row_count, shards * features)), (returned,), "r", "r", [DMA((shards,))]
+        lay_kernel, shape((row_count, shards * features)), (returned,), "h", "r", [DMA((shards,))], FULL
     )
 
     grad_a = []
     for acts_part in acts_parts:
         odd = call(
-            functools.partial(first_kernel, owners, 1),
+            functools.partial(first_kernel, shards, owners, 1),
             shape((owners // 2, columns, width)),
-            (backs, label, acts_part),
-            "hvh",
-            "h",
+            (*backs, label, acts_part),
+            "v" * (shards + 2),
+            "v",
         )
         even = call(
-            functools.partial(first_kernel, owners, 0),
+            functools.partial(first_kernel, shards, owners, 0),
             [shape((columns, width))] * (owners // 2),
-            (backs, label, acts_part, swap(odd, "dp", 1)),
-            "hvhh",
-            "h" * (owners // 2),
+            (*backs, label, acts_part, swap(odd, "dp", 1)),
+            "v" * (shards + 3),
+            "v" * (owners // 2),
         )
         grad_a.append(list(even))
     label, *grads = lax.optimization_barrier((label, *sum(grad_a, [])))
     grad_a = [grads[h * (owners // 2) : (h + 1) * (owners // 2)] for h in range(parts)]
     grad_a = [[g[0]] + [swap(g[n], "dp", 2 * n) for n in range(1, owners // 2)] for g in grad_a]
 
-    mids = exchange(
-        call(
-            functools.partial(mid_kernel, owners, parts),
-            shape((shards, ADAPTER_RANK, rows)),
-            (*blocks, label, *acts_parts),
-            "r" * owners + "v" + "h" * parts,
-            "h",
-            factor_scratch + sems,
-        ),
-        "fsdp",
-    )
+    mid = call(
+        functools.partial(mid_kernel, owners, parts),
+        shape((ADAPTER_RANK, rows)),
+        (*blocks, label, *acts_parts),
+        "r" * owners + "v" * (1 + parts),
+        "v",
+        factor_scratch + sems,
+    )
+    mids = [mid] + [swap(mid, "fsdp", j) for j in range(1, shards)]
     grad_b = call(
-        functools.partial(second_kernel, owners),
+        functools.partial(second_kernel, shards, owners),
         shape((owners, own_rows, keys)),
-        (mids, label, scaled),
-        "hvh",
-        "h",
+        (*mids, label, scaled),
+        "v" * (shards + 2),
+        "v",
         [pltpu.VMEM((ADAPTER_RANK, step), f32)],
     )
     new_b = call(
         adam_b_kernel,
         [shape(b_param.shape, f32)] * 3,
         (exchange(grad_b, "dp"), b_param, b_moment, b_second),
-        "hhhh",
-        "hhh",
+        "vvvv",
+        "vvv",
     )
     block = min(256, width)
     steps = width // block
@@ -492,7 +485,7 @@
             out_shape=[shape(a_param.shape, f32)] * 3,
             in_specs=[wide] * (owners // 2) + [tall] * 3,
             out_specs=[tall] * 3,
-            compiler_params=pltpu.CompilerParams(vmem_limit_bytes=VMEM_BYTES),
+            compiler_params=pltpu.CompilerParams(vmem_limit_bytes=FULL << 20),
         )(*grad_a[h], *new_a)
     return (grad_input, new_a[0], new_a[1], new_a[2], new_b[0], new_b[1], new_b[2])
 

time: 226 us -> 140 us (0.62)
  Pallas kernels: 111 us -> 32.2 us
  blocking collectives: 21.6 us -> 0 us
  starting transfers between devices: 24.6 us -> 41.9 us
  waiting for transfers between devices: 65.2 us -> 59.3 us
  local copies, waits for them, and re-layouts: 2.02 us -> 4.94 us
    pallas_call x10, Pallas kernels: 106 us -> 27.2 us  [call(): pl.pallas_call(kernel, out_shape=outs, in_specs=[VMEM if kind == 'v' else...]
    all_to_all x4, waiting for transfers between devices: 35.4 us -> 7.78 us  [exchange(): return lax.all_to_all(blocks, axis, split_axis=0, concat_axis=0, tiled=True)]
    ppermute x11 -> x17, waiting for transfers between devices: 29.8 us -> 51.5 us  [swap(): return lax.ppermute(block, axis, [(i, i ^ bits) for i in range(size)])]
    all_to_all x2 -> x0, blocking collectives: 21.6 us -> none  [exchange(): return lax.all_to_all(blocks, axis, split_axis=0, concat_axis=0, tiled=True)]
    ppermute x11 -> x17, starting transfers between devices: 7.69 us -> 22.7 us  [swap(): return lax.ppermute(block, axis, [(i, i ^ bits) for i in range(size)])]
    unnamed x12 -> x42, local copies, waits for them, and re-layouts: 2.02 us -> 4.94 us
    all_to_all x4, starting transfers between devices: 16.9 us -> 19.2 us  [exchange(): return lax.all_to_all(blocks, axis, split_axis=0, concat_axis=0, tiled=True)]
  transfers between devices with their start and end apart: 15 -> 21, of which waited for: 6 -> 9; matrix products, arithmetic and copies ran while one was open for 0% -> 0% of each run, Pallas kernels for 23% -> 15%
where the time goes in v5:
time: 140 us; the launch traced here: 139 us
  waiting for transfers between devices  59.3 us (42%)
  starting transfers between devices  41.9 us (30%)
  Pallas kernels  32.2 us (23%)
  local copies, waits for them, and re-layouts  4.94 us (4%)
    ppermute x17, waiting for transfers between devices, swap(): return lax.ppermute(block, axis, [(i, i ^ bits) for i in range(size)])  51.5 us
    pallas_call x10, Pallas kernels, call(): pl.pallas_call(kernel, out_shape=outs, in_specs=[VMEM if kind == 'v' else...  27.2 us
    ppermute x17, starting transfers between devices, swap(): return lax.ppermute(block, axis, [(i, i ^ bits) for i in range(size)])  22.7 us
    all_to_all x4, starting transfers between devices, exchange(): return lax.all_to_all(blocks, axis, split_axis=0, concat_axis=0, tiled=True)  19.2 us
    all_to_all x4, waiting for transfers between devices, exchange(): return lax.all_to_all(blocks, axis, split_axis=0, concat_axis=0, tiled=True)  7.78 us
    pallas_call x1, Pallas kernels, per_device(): pl.pallas_call(functools.partial(adam_a_kernel, owners // 2), grid=(steps...  5.01 us
    unnamed x42, local copies, waits for them, and re-layouts  4.94 us
  transfers between devices with their start and end apart: 21, of which 9 were waited for; matrix products, arithmetic and copies ran while one was open for 0% of the time, Pallas kernels for 15%

profile of v5, /device:TPU:0, one launch (start us, length us, event | category | flops | bytes accessed | tf_op | source)
XLA Modules:
  0.0 139.3 jit_solution(6318701522373461598)
XLA Ops:
  0.6 3.2 %shard_map.162 = (bf16[4,144,512]{2,1,0:T(8,128)(2,1)}, bf16[1152,256]{1,0:T(8,128)(2,1)}, bf16[4,128,1024]{2,1,0:T(8,128)(2,1)}) custom-call(bf16[128,4096]{1,0:T(8,128)(2,1)} %refs_0_.1, bf16[128,512]{1,0:T(8,128)(2,1)} %refs_1_.3, s32[1,128]{1,0:T(1,128)} %bitcast.8, s32[1,128]{1,0:T(1,128)} %bitcast.9, f32[1024,256]{1,0:T(8,128)} %refs_4_.3, ...), custom_call_target="tpu_custom_call" | custom-call | tf_op jit(solution)/shard_map/pallas_call | solution.py:75
  3.9 0.0 copy-start
  3.9 6.5 %all-to-all-start = ((bf16[4,144,512]{2,1,0:T(8,128)(2,1)}), bf16[4,144,512]{2,1,0:T(8,128)(2,1)S(1)}, u32[]{:S(2)}, u32[]{:S(2)}) async-start(bf16[4,144,512]{2,1,0:T(8,128)(2,1)} %get-tuple-element.36), calls=%async_computation | async-start | bytes 1179648 | tf_op jit(solution)/shard_map/all_to_all | solution.py:350
  10.3 2.4 %collective-permute-start.3 = (bf16[1152,256]{1,0:T(8,128)(2,1)}, bf16[1152,256]{1,0:T(8,128)(2,1)S(1)}, u32[]{:S(2)}, u32[]{:S(2)}) collective-permute-start(bf16[1152,256]{1,0:T(8,128)(2,1)} %get-tuple-element.35.refs_0_.refs_4_), channel_id=1, source_target_pairs={{0,24},{4,28},{8,16},{12,20},{16,8},{20,12},{24,0},{28,4},{1,25},{... | collective-permute-start | bytes 1769480 | tf_op jit(solution)/shard_map/ppermute | solution.py:347
  12.8 0.5 collective-permute-start.2
  13.3 0.5 collective-permute-start.1
  13.8 13.9 %collective-permute-done.3.refs_6_.refs_10_ = bf16[1152,256]{1,0:T(8,128)(2,1)S(1)} collective-permute-done((bf16[1152,256]{1,0:T(8,128)(2,1)}, bf16[1152,256]{1,0:T(8,128)(2,1)S(1)}, u32[]{:S(2)}, u32[]{:S(2)}) %collective-permute-start.3) | collective-permute-done | bytes 589856 | tf_op jit(solution)/shard_map/ppermute | solution.py:347
  27.7 11.1 %collective-permute-done.2.refs_4_.refs_8_ = bf16[1152,256]{1,0:T(8,128)(2,1)S(1)} collective-permute-done((bf16[1152,256]{1,0:T(8,128)(2,1)}, bf16[1152,256]{1,0:T(8,128)(2,1)S(1)}, u32[]{:S(2)}, u32[]{:S(2)}) %collective-permute-start.2) | collective-permute-done | bytes 589856 | tf_op jit(solution)/shard_map/ppermute | solution.py:347
  38.9 0.1 collective-permute-done.1.refs_2_.refs_6_
  39.0 0.0 all-to-all-done.refs_0_
  39.0 0.8 copy-done.10
  39.8 4.8 %all-to-all-start.1 = ((bf16[4,128,1024]{2,1,0:T(8,128)(2,1)}), bf16[4,128,1024]{2,1,0:T(8,128)(2,1)S(1)}, u32[]{:S(2)}, u32[]{:S(2)}) async-start(bf16[4,128,1024]{2,1,0:T(8,128)(2,1)} %get-tuple-element.45), calls=%async_computation.1 | async-start | bytes 2097152 | tf_op jit(solution)/shard_map/all_to_all | solution.py:350
  44.6 0.0 collective-permute-start
  44.6 0.5 collective-permute-start.4
  45.1 0.1 collective-permute-start.5
  45.2 0.4 collective-permute-start.6
  45.6 1.1 copy-done.11
  46.7 1.2 copy-done.14
  47.9 0.7 shard_map.163
  48.7 0.0 copy-start.15
  48.7 0.0 collective-permute-done.refs_1_.refs_5_
  48.7 0.0 copy-start.1
  48.7 0.0 collective-permute-done.4.refs_3_.refs_7_
  48.7 0.0 copy-start.3
  48.7 0.4 collective-permute-done.6.refs_7_.refs_11_
  49.1 0.8 shard_map.164.refs_0_
  50.0 3.9 %collective-permute-start.9 = (bf16[32,512]{1,0:T(8,128)(2,1)S(1)}, bf16[32,512]{1,0:T(8,128)(2,1)S(1)}, u32[]{:S(2)}, u32[]{:S(2)}) collective-permute-start(bf16[32,512]{1,0:T(8,128)(2,1)S(1)} %shard_map.164.refs_0_), channel_id=1, source_target_pairs={{0,3},{1,2},{2,1},{3,0},{4,7},{5,6},{6,5},{7,4},{8,11},{9,10},{10,... | collective-permute-start | bytes 98312 | tf_op jit(solution)/shard_map/ppermute | solution.py:347
  53.9 0.0 collective-permute-start.8
  53.9 0.6 collective-permute-start.7
  54.5 12.6 %collective-permute-done.9.refs_3_ = bf16[32,512]{1,0:T(8,128)(2,1)S(1)} collective-permute-done((bf16[32,512]{1,0:T(8,128)(2,1)S(1)}, bf16[32,512]{1,0:T(8,128)(2,1)S(1)}, u32[]{:S(2)}, u32[]{:S(2)}) %collective-permute-start.9) | collective-permute-done | bytes 32800 | tf_op jit(solution)/shard_map/ppermute | solution.py:347
  67.2 6.0 %collective-permute-done.8.refs_2_ = bf16[32,512]{1,0:T(8,128)(2,1)S(1)} collective-permute-done((bf16[32,512]{1,0:T(8,128)(2,1)S(1)}, bf16[32,512]{1,0:T(8,128)(2,1)S(1)}, u32[]{:S(2)}, u32[]{:S(2)}) %collective-permute-start.8) | collective-permute-done | bytes 32800 | tf_op jit(solution)/shard_map/ppermute | solution.py:347
  73.2 0.0 collective-permute-done.7.refs_1_
  73.2 5.1 %shard_map.165 = bf16[512,1024]{1,0:T(8,128)(2,1)S(1)} custom-call(bf16[32,512]{1,0:T(8,128)(2,1)S(1)} %shard_map.164.refs_0_, bf16[32,512]{1,0:T(8,128)(2,1)S(1)} %collective-permute-done.7.refs_1_, bf16[32,512]{1,0:T(8,128)(2,1)S(1)} %collective-permute-done.8.refs_2_, bf16[32,512]{1,0:T(8,128)(2,1)S(1)} %collective-permute-done.9.refs_3_, ...), custom_call_target="tpu_custom_call" | custom-call | tf_op jit(solution)/shard_map/pallas_call | solution.py:75
  78.4 0.0 copy-start.9
  78.4 1.0 copy-done.9
  79.4 0.0 all-to-all-done.1
  79.4 2.6 %shard_map.167 = bf16[4,256,1024]{2,1,0:T(8,128)(2,1)} custom-call(bf16[32,512]{1,0:T(8,128)(2,1)S(1)} %shard_map.164.refs_0_, bf16[32,512]{1,0:T(8,128)(2,1)S(1)} %collective-permute-done.7.refs_1_, bf16[32,512]{1,0:T(8,128)(2,1)S(1)} %collective-permute-done.8.refs_2_, bf16[32,512]{1,0:T(8,128)(2,1)S(1)} %collective-permute-done.9.refs_3_, ...), custom_call_target="tpu_custom_call" | custom-call | tf_op jit(solution)/shard_map/pallas_call | solution.py:75
  82.0 0.0 collective-permute-start.10
  82.0 4.4 %all-to-all-start.2 = ((bf16[4,128,1024]{2,1,0:T(8,128)(2,1)}), bf16[4,128,1024]{2,1,0:T(8,128)(2,1)}, u32[]{:S(2)}, u32[]{:S(2)}) async-start(bf16[4,128,1024]{2,1,0:T(8,128)(2,1)} %bitcast.7), calls=%async_computation.2 | async-start | bytes 2097152 | tf_op jit(solution)/shard_map/all_to_all | solution.py:350
  86.4 0.0 copy-start.2
  86.4 0.0 copy-start.4
  86.4 0.0 collective-permute-done.10.refs_6_
  86.5 3.9 %shard_map.168 = (bf16[256,1024]{1,0:T(8,128)(2,1)S(1)}, bf16[256,1024]{1,0:T(8,128)(2,1)}, bf16[256,1024]{1,0:T(8,128)(2,1)}, bf16[256,1024]{1,0:T(8,128)(2,1)}) custom-call(bf16[32,512]{1,0:T(8,128)(2,1)S(1)} %shard_map.164.refs_0_, bf16[32,512]{1,0:T(8,128)(2,1)S(1)} %collective-permute-done.7.refs_1_, ...), custom_call_target="tpu_custom_call" | custom-call | tf_op jit(solution)/shard_map/pallas_call | solution.py:75
  90.4 6.4 %shard_map.170.refs_0_ = bf16[32,512]{1,0:T(8,128)(2,1)S(1)} custom-call(bf16[1152,256]{1,0:T(8,128)(2,1)S(1)} %copy-done, bf16[1152,256]{1,0:T(8,128)(2,1)S(1)} %copy-done.2, bf16[1152,256]{1,0:T(8,128)(2,1)S(1)} %collective-permute-done.1.refs_2_.refs_6_, bf16[1152,256]{1,0:T(8,128)(2,1)S(1)} %copy-done.4, ...), custom_call_target="tpu_custom_call" | custom-call | tf_op jit(solution)/shard_map/pallas_call | solution.py:75
  96.8 0.0 copy-start.17
  96.8 0.0 copy-start.18
  96.9 0.0 copy-start.19
  96.9 3.6 %collective-permute-start.16 = (bf16[32,512]{1,0:T(8,128)(2,1)S(1)}, bf16[32,512]{1,0:T(8,128)(2,1)S(1)}, u32[]{:S(2)}, u32[]{:S(2)}) collective-permute-start(bf16[32,512]{1,0:T(8,128)(2,1)S(1)} %shard_map.170.refs_0_), channel_id=1, source_target_pairs={{0,3},{1,2},{2,1},{3,0},{4,7},{5,6},{6,5},{7,4},{8,11},{9,10},{10,... | collective-permute-start | bytes 98312 | tf_op jit(solution)/shard_map/ppermute | solution.py:347
  100.5 1.5 %collective-permute-start.11 = (bf16[256,1024]{1,0:T(8,128)(2,1)}, bf16[256,1024]{1,0:T(8,128)(2,1)S(1)}, u32[]{:S(2)}, u32[]{:S(2)}) collective-permute-start(bf16[256,1024]{1,0:T(8,128)(2,1)} %get-tuple-element.53), channel_id=1, source_target_pairs={{0,8},{4,12},{8,0},{12,4},{16,24},{20,28},{24,16},{28,20},{1,9},{5... | collective-permute-start | bytes 1572872 | tf_op jit(solution)/shard_map/ppermute | solution.py:347
  102.0 0.1 collective-permute-start.12
  102.0 1.9 %collective-permute-start.13 = (bf16[256,1024]{1,0:T(8,128)(2,1)}, bf16[256,1024]{1,0:T(8,128)(2,1)}, u32[]{:S(2)}, u32[]{:S(2)}) collective-permute-start(bf16[256,1024]{1,0:T(8,128)(2,1)} %get-tuple-element.55), channel_id=1, source_target_pairs={{0,24},{4,28},{8,16},{12,20},{16,8},{20,12},{24,0},{28,4},{1,25},{... | collective-permute-start | bytes 1572872 | tf_op jit(solution)/shard_map/ppermute | solution.py:347
  104.0 5.3 %collective-permute-done.16.refs_3_ = bf16[32,512]{1,0:T(8,128)(2,1)S(1)} collective-permute-done((bf16[32,512]{1,0:T(8,128)(2,1)S(1)}, bf16[32,512]{1,0:T(8,128)(2,1)S(1)}, u32[]{:S(2)}, u32[]{:S(2)}) %collective-permute-start.16) | collective-permute-done | bytes 32800 | tf_op jit(solution)/shard_map/ppermute | solution.py:347
  109.3 6.5 %collective-permute-start.14 = (bf16[32,512]{1,0:T(8,128)(2,1)S(1)}, bf16[32,512]{1,0:T(8,128)(2,1)S(1)}, u32[]{:S(2)}, u32[]{:S(2)}) collective-permute-start(bf16[32,512]{1,0:T(8,128)(2,1)S(1)} %shard_map.170.refs_0_), channel_id=1, source_target_pairs={{0,1},{1,0},{2,3},{3,2},{4,5},{5,4},{6,7},{7,6},{8,9},{9,8},{10,11... | collective-permute-start | bytes 98312 | tf_op jit(solution)/shard_map/ppermute | solution.py:347
  115.9 1.9 %collective-permute-done.14.refs_1_ = bf16[32,512]{1,0:T(8,128)(2,1)S(1)} collective-permute-done((bf16[32,512]{1,0:T(8,128)(2,1)S(1)}, bf16[32,512]{1,0:T(8,128)(2,1)S(1)}, u32[]{:S(2)}, u32[]{:S(2)}) %collective-permute-start.14) | collective-permute-done | bytes 32800 | tf_op jit(solution)/shard_map/ppermute | solution.py:347
  117.8 1.3 shard_map.171
  119.0 3.5 %all-to-all-start.3 = ((bf16[8,64,512]{2,1,0:T(8,128)(2,1)}), bf16[8,64,512]{2,1,0:T(8,128)(2,1)S(1)}, u32[]{:S(2)}, u32[]{:S(2)}) async-start(bf16[8,64,512]{2,1,0:T(8,128)(2,1)} %shard_map.171), calls=%async_computation.3 | async-start | bytes 1048576 | tf_op jit(solution)/shard_map/all_to_all | solution.py:350
  122.5 2.2 %shard_map.166 = bf16[128,4096]{1,0:T(8,128)(2,1)} custom-call(bf16[4,128,1024]{2,1,0:T(8,128)(2,1)} %all-to-all-done.2.refs_0_), custom_call_target="tpu_custom_call" | custom-call | tf_op jit(solution)/shard_map/pallas_call | solution.py:75
  124.8 7.8 %all-to-all-done.3.refs_0_ = bf16[8,64,512]{2,1,0:T(8,128)(2,1)S(1)} async-done(((bf16[8,64,512]{2,1,0:T(8,128)(2,1)}), bf16[8,64,512]{2,1,0:T(8,128)(2,1)S(1)}, u32[]{:S(2)}, u32[]{:S(2)}) %all-to-all-start.3) | async-done | bytes 524320 | tf_op jit(solution)/shard_map/all_to_all | solution.py:350
  132.6 0.8 shard_map.172
  133.4 0.0 collective-permute-done.11.refs_1_
  133.4 0.0 collective-permute-done.12.refs_2_
  133.4 0.0 collective-permute-done.13.refs_3_
  133.4 0.8 copy-done.20
  134.2 5.0 %shard_map.169 = (f32[1024,256]{1,0:T(8,128)}, f32[1024,256]{1,0:T(8,128)}, f32[1024,256]{1,0:T(8,128)}) custom-call(bf16[256,1024]{1,0:T(8,128)(2,1)} %copy-done.16, bf16[256,1024]{1,0:T(8,128)(2,1)} %copy-done.20, bf16[256,1024]{1,0:T(8,128)(2,1)} %collective-permute-done.12.refs_2_, bf16[256,1024]{1,0:T(8,128)(2,1)} %collective-permute-done.13.refs_3_, ...), custom_call_target="tpu_custom_call" | custom-call | tf_op jit(solution)/shard_map/pallas_call | solution.py:482
  (31 shorter events, 0.1 us)
Async XLA Ops:
  3.9 40.7 %copy-start = (bf16[1152,256]{1,0:T(8,128)(2,1)S(1)}, bf16[1152,256]{1,0:T(8,128)(2,1)}, u32[]{:S(2)}) copy-start(bf16[1152,256]{1,0:T(8,128)(2,1)} %get-tuple-element.35.refs_0_.refs_4_) | copy-start | bytes 1769476
  3.9 35.1 %all-to-all-start = ((bf16[4,144,512]{2,1,0:T(8,128)(2,1)}), bf16[4,144,512]{2,1,0:T(8,128)(2,1)S(1)}, u32[]{:S(2)}, u32[]{:S(2)}) async-start(bf16[4,144,512]{2,1,0:T(8,128)(2,1)} %get-tuple-element.36), calls=%async_computation | async-start | bytes 1179648 | tf_op jit(solution)/shard_map/all_to_all | solution.py:350
  10.3 17.4 %collective-permute-start.3 = (bf16[1152,256]{1,0:T(8,128)(2,1)}, bf16[1152,256]{1,0:T(8,128)(2,1)S(1)}, u32[]{:S(2)}, u32[]{:S(2)}) collective-permute-start(bf16[1152,256]{1,0:T(8,128)(2,1)} %get-tuple-element.35.refs_0_.refs_4_), channel_id=1, source_target_pairs={{0,24},{4,28},{8,16},{12,20},{16,8},{20,12},{24,0},{28,4},{1,25},{... | collective-permute-start | bytes 1769480 | tf_op jit(solution)/shard_map/ppermute | solution.py:347
  12.8 26.1 %collective-permute-start.2 = (bf16[1152,256]{1,0:T(8,128)(2,1)}, bf16[1152,256]{1,0:T(8,128)(2,1)S(1)}, u32[]{:S(2)}, u32[]{:S(2)}) collective-permute-start(bf16[1152,256]{1,0:T(8,128)(2,1)} %get-tuple-element.35.refs_0_.refs_4_), channel_id=1, source_target_pairs={{0,16},{4,20},{8,24},{12,28},{16,0},{20,4},{24,8},{28,12},{1,17},{... | collective-permute-start | bytes 1769480 | tf_op jit(solution)/shard_map/ppermute | solution.py:347
  13.3 25.7 %collective-permute-start.1 = (bf16[1152,256]{1,0:T(8,128)(2,1)}, bf16[1152,256]{1,0:T(8,128)(2,1)S(1)}, u32[]{:S(2)}, u32[]{:S(2)}) collective-permute-start(bf16[1152,256]{1,0:T(8,128)(2,1)} %get-tuple-element.35.refs_0_.refs_4_), channel_id=1, source_target_pairs={{0,8},{4,12},{8,0},{12,4},{16,24},{20,28},{24,16},{28,20},{1,9},{5... | collective-permute-start | bytes 1769480 | tf_op jit(solution)/shard_map/ppermute | solution.py:347
  39.0 0.8 copy-start.10
  39.8 39.6 %all-to-all-start.1 = ((bf16[4,128,1024]{2,1,0:T(8,128)(2,1)}), bf16[4,128,1024]{2,1,0:T(8,128)(2,1)S(1)}, u32[]{:S(2)}, u32[]{:S(2)}) async-start(bf16[4,128,1024]{2,1,0:T(8,128)(2,1)} %get-tuple-element.45), calls=%async_computation.1 | async-start | bytes 2097152 | tf_op jit(solution)/shard_map/all_to_all | solution.py:350
  44.6 4.1 %collective-permute-start = (bf16[1152,256]{1,0:T(8,128)(2,1)S(1)}, bf16[1152,256]{1,0:T(8,128)(2,1)S(1)}, u32[]{:S(2)}, u32[]{:S(2)}) collective-permute-start(bf16[1152,256]{1,0:T(8,128)(2,1)S(1)} %copy-done), channel_id=1, source_target_pairs={{0,4},{4,0},{8,12},{12,8},{16,20},{20,16},{24,28},{28,24},{1,5},{5... | collective-permute-start | bytes 1769480 | tf_op jit(solution)/shard_map/ppermute | solution.py:347
  44.6 4.1 %collective-permute-start.4 = (bf16[1152,256]{1,0:T(8,128)(2,1)S(1)}, bf16[1152,256]{1,0:T(8,128)(2,1)S(1)}, u32[]{:S(2)}, u32[]{:S(2)}) collective-permute-start(bf16[1152,256]{1,0:T(8,128)(2,1)S(1)} %collective-permute-done.1.refs_2_.refs_6_), channel_id=1, source_target_pairs={{0,4},{4,0},{8,12},{12,8},{16,20},{20,16},{24,28},{28,24},{1,5},{5... | collective-permute-start | bytes 1769480 | tf_op jit(solution)/shard_map/ppermute | solution.py:347
  45.1 3.6 %collective-permute-start.5 = (bf16[1152,256]{1,0:T(8,128)(2,1)S(1)}, bf16[1152,256]{1,0:T(8,128)(2,1)S(1)}, u32[]{:S(2)}, u32[]{:S(2)}) collective-permute-start(bf16[1152,256]{1,0:T(8,128)(2,1)S(1)} %collective-permute-done.2.refs_4_.refs_8_), channel_id=1, source_target_pairs={{0,4},{4,0},{8,12},{12,8},{16,20},{20,16},{24,28},{28,24},{1,5},{5... | collective-permute-start | bytes 1769480 | tf_op jit(solution)/shard_map/ppermute | solution.py:347
  45.2 4.0 %collective-permute-start.6 = (bf16[1152,256]{1,0:T(8,128)(2,1)S(1)}, bf16[1152,256]{1,0:T(8,128)(2,1)S(1)}, u32[]{:S(2)}, u32[]{:S(2)}) collective-permute-start(bf16[1152,256]{1,0:T(8,128)(2,1)S(1)} %collective-permute-done.3.refs_6_.refs_10_), channel_id=1, source_target_pairs={{0,4},{4,0},{8,12},{12,8},{16,20},{20,16},{24,28},{28,24},{1,5},{5... | collective-permute-start | bytes 1769480 | tf_op jit(solution)/shard_map/ppermute | solution.py:347
  45.6 1.1 copy-start.11
  46.7 1.2 copy-start.14
  48.7 1.3 copy-start.12
  48.7 1.3 copy-start.15
  48.7 24.5 %copy-start.1 = (bf16[1152,256]{1,0:T(8,128)(2,1)}, bf16[1152,256]{1,0:T(8,128)(2,1)S(1)}, u32[]{:S(2)}) copy-start(bf16[1152,256]{1,0:T(8,128)(2,1)S(1)} %collective-permute-done.refs_1_.refs_5_) | copy-start | bytes 1769476
  48.7 24.5 %copy-start.3 = (bf16[1152,256]{1,0:T(8,128)(2,1)}, bf16[1152,256]{1,0:T(8,128)(2,1)S(1)}, u32[]{:S(2)}) copy-start(bf16[1152,256]{1,0:T(8,128)(2,1)S(1)} %collective-permute-done.4.refs_3_.refs_7_) | copy-start | bytes 1769476
  48.7 24.5 %copy-start.5 = (bf16[1152,256]{1,0:T(8,128)(2,1)}, bf16[1152,256]{1,0:T(8,128)(2,1)S(1)}, u32[]{:S(2)}) copy-start(bf16[1152,256]{1,0:T(8,128)(2,1)S(1)} %collective-permute-done.5.refs_5_.refs_9_) | copy-start | bytes 1769476
  49.1 24.1 %copy-start.7 = (bf16[1152,256]{1,0:T(8,128)(2,1)}, bf16[1152,256]{1,0:T(8,128)(2,1)S(1)}, u32[]{:S(2)}) copy-start(bf16[1152,256]{1,0:T(8,128)(2,1)S(1)} %collective-permute-done.6.refs_7_.refs_11_) | copy-start | bytes 1769476
  50.0 17.2 %collective-permute-start.9 = (bf16[32,512]{1,0:T(8,128)(2,1)S(1)}, bf16[32,512]{1,0:T(8,128)(2,1)S(1)}, u32[]{:S(2)}, u32[]{:S(2)}) collective-permute-start(bf16[32,512]{1,0:T(8,128)(2,1)S(1)} %shard_map.164.refs_0_), channel_id=1, source_target_pairs={{0,3},{1,2},{2,1},{3,0},{4,7},{5,6},{6,5},{7,4},{8,11},{9,10},{10,... | collective-permute-start | bytes 98312 | tf_op jit(solution)/shard_map/ppermute | solution.py:347
  53.9 19.3 %collective-permute-start.8 = (bf16[32,512]{1,0:T(8,128)(2,1)S(1)}, bf16[32,512]{1,0:T(8,128)(2,1)S(1)}, u32[]{:S(2)}, u32[]{:S(2)}) collective-permute-start(bf16[32,512]{1,0:T(8,128)(2,1)S(1)} %shard_map.164.refs_0_), channel_id=1, source_target_pairs={{0,2},{1,3},{2,0},{3,1},{4,6},{5,7},{6,4},{7,5},{8,10},{9,11},{10,... | collective-permute-start | bytes 98312 | tf_op jit(solution)/shard_map/ppermute | solution.py:347
  53.9 19.3 %collective-permute-start.7 = (bf16[32,512]{1,0:T(8,128)(2,1)S(1)}, bf16[32,512]{1,0:T(8,128)(2,1)S(1)}, u32[]{:S(2)}, u32[]{:S(2)}) collective-permute-start(bf16[32,512]{1,0:T(8,128)(2,1)S(1)} %shard_map.164.refs_0_), channel_id=1, source_target_pairs={{0,1},{1,0},{2,3},{3,2},{4,5},{5,4},{6,7},{7,6},{8,9},{9,8},{10,11... | collective-permute-start | bytes 98312 | tf_op jit(solution)/shard_map/ppermute | solution.py:347
  78.4 1.0 copy-start.9
  82.0 4.5 %collective-permute-start.10 = (bf16[4,256,1024]{2,1,0:T(8,128)(2,1)}, bf16[4,256,1024]{2,1,0:T(8,128)(2,1)}, u32[]{:S(2)}, u32[]{:S(2)}) collective-permute-start(bf16[4,256,1024]{2,1,0:T(8,128)(2,1)} %shard_map.167), channel_id=1, source_target_pairs={{0,4},{4,0},{8,12},{12,8},{16,20},{20,16},{24,28},{28,24},{1,5},{5... | collective-permute-start | bytes 6291464 | tf_op jit(solution)/shard_map/ppermute | solution.py:347
  82.0 37.1 %all-to-all-start.2 = ((bf16[4,128,1024]{2,1,0:T(8,128)(2,1)}), bf16[4,128,1024]{2,1,0:T(8,128)(2,1)}, u32[]{:S(2)}, u32[]{:S(2)}) async-start(bf16[4,128,1024]{2,1,0:T(8,128)(2,1)} %bitcast.7), calls=%async_computation.2 | async-start | bytes 2097152 | tf_op jit(solution)/shard_map/all_to_all | solution.py:350
  86.4 4.0 %copy-start.2 = (bf16[1152,256]{1,0:T(8,128)(2,1)S(1)}, bf16[1152,256]{1,0:T(8,128)(2,1)}, u32[]{:S(2)}) copy-start(bf16[1152,256]{1,0:T(8,128)(2,1)} %copy-done.1) | copy-start | bytes 1769476
  86.4 3.9 %copy-start.4 = (bf16[1152,256]{1,0:T(8,128)(2,1)S(1)}, bf16[1152,256]{1,0:T(8,128)(2,1)}, u32[]{:S(2)}) copy-start(bf16[1152,256]{1,0:T(8,128)(2,1)} %copy-done.3) | copy-start | bytes 1769476
  86.4 3.9 %copy-start.6 = (bf16[1152,256]{1,0:T(8,128)(2,1)S(1)}, bf16[1152,256]{1,0:T(8,128)(2,1)}, u32[]{:S(2)}) copy-start(bf16[1152,256]{1,0:T(8,128)(2,1)} %copy-done.5) | copy-start | bytes 1769476
  86.4 3.9 %copy-start.8 = (bf16[1152,256]{1,0:T(8,128)(2,1)S(1)}, bf16[1152,256]{1,0:T(8,128)(2,1)}, u32[]{:S(2)}) copy-start(bf16[1152,256]{1,0:T(8,128)(2,1)} %copy-done.7) | copy-start | bytes 1769476
  90.4 6.5 %copy-start.16 = (bf16[256,1024]{1,0:T(8,128)(2,1)}, bf16[256,1024]{1,0:T(8,128)(2,1)S(1)}, u32[]{:S(2)}) copy-start(bf16[256,1024]{1,0:T(8,128)(2,1)S(1)} %get-tuple-element.52.refs_0_) | copy-start | bytes 1572868
  90.4 27.4 %copy-start.13 = (bf16[512,512]{1,0:T(8,128)(2,1)S(1)}, bf16[512,512]{1,0:T(8,128)(2,1)}, u32[]{:S(2)}) copy-start(bf16[512,512]{1,0:T(8,128)(2,1)} %copy-done.12) | copy-start | bytes 1572868
  96.8 35.7 %copy-start.17 = (f32[64,512]{1,0:T(8,128)S(1)}, f32[64,512]{1,0:T(8,128)}, u32[]{:S(2)}) copy-start(f32[64,512]{1,0:T(8,128)} %refs_1_.5) | copy-start | bytes 393220
  96.8 35.7 %copy-start.18 = (f32[64,512]{1,0:T(8,128)S(1)}, f32[64,512]{1,0:T(8,128)}, u32[]{:S(2)}) copy-start(f32[64,512]{1,0:T(8,128)} %refs_2_.1) | copy-start | bytes 393220
  96.9 35.7 %copy-start.19 = (f32[64,512]{1,0:T(8,128)S(1)}, f32[64,512]{1,0:T(8,128)}, u32[]{:S(2)}) copy-start(f32[64,512]{1,0:T(8,128)} %refs_3_.1) | copy-start | bytes 393220
  96.9 12.5 %collective-permute-start.16 = (bf16[32,512]{1,0:T(8,128)(2,1)S(1)}, bf16[32,512]{1,0:T(8,128)(2,1)S(1)}, u32[]{:S(2)}, u32[]{:S(2)}) collective-permute-start(bf16[32,512]{1,0:T(8,128)(2,1)S(1)} %shard_map.170.refs_0_), channel_id=1, source_target_pairs={{0,3},{1,2},{2,1},{3,0},{4,7},{5,6},{6,5},{7,4},{8,11},{9,10},{10,... | collective-permute-start | bytes 98312 | tf_op jit(solution)/shard_map/ppermute | solution.py:347
  100.5 32.9 %collective-permute-start.11 = (bf16[256,1024]{1,0:T(8,128)(2,1)}, bf16[256,1024]{1,0:T(8,128)(2,1)S(1)}, u32[]{:S(2)}, u32[]{:S(2)}) collective-permute-start(bf16[256,1024]{1,0:T(8,128)(2,1)} %get-tuple-element.53), channel_id=1, source_target_pairs={{0,8},{4,12},{8,0},{12,4},{16,24},{20,28},{24,16},{28,20},{1,9},{5... | collective-permute-start | bytes 1572872 | tf_op jit(solution)/shard_map/ppermute | solution.py:347
  102.0 31.4 %collective-permute-start.12 = (bf16[256,1024]{1,0:T(8,128)(2,1)}, bf16[256,1024]{1,0:T(8,128)(2,1)}, u32[]{:S(2)}, u32[]{:S(2)}) collective-permute-start(bf16[256,1024]{1,0:T(8,128)(2,1)} %get-tuple-element.54), channel_id=1, source_target_pairs={{0,16},{4,20},{8,24},{12,28},{16,0},{20,4},{24,8},{28,12},{1,17},{... | collective-permute-start | bytes 1572872 | tf_op jit(solution)/shard_map/ppermute | solution.py:347
  102.0 31.4 %collective-permute-start.13 = (bf16[256,1024]{1,0:T(8,128)(2,1)}, bf16[256,1024]{1,0:T(8,128)(2,1)}, u32[]{:S(2)}, u32[]{:S(2)}) collective-permute-start(bf16[256,1024]{1,0:T(8,128)(2,1)} %get-tuple-element.55), channel_id=1, source_target_pairs={{0,24},{4,28},{8,16},{12,20},{16,8},{20,12},{24,0},{28,4},{1,25},{... | collective-permute-start | bytes 1572872 | tf_op jit(solution)/shard_map/ppermute | solution.py:347
  104.0 11.9 %collective-permute-start.15 = (bf16[32,512]{1,0:T(8,128)(2,1)S(1)}, bf16[32,512]{1,0:T(8,128)(2,1)S(1)}, u32[]{:S(2)}, u32[]{:S(2)}) collective-permute-start(bf16[32,512]{1,0:T(8,128)(2,1)S(1)} %shard_map.170.refs_0_), channel_id=1, source_target_pairs={{0,2},{1,3},{2,0},{3,1},{4,6},{5,7},{6,4},{7,5},{8,10},{9,11},{10,... | collective-permute-start | bytes 98312 | tf_op jit(solution)/shard_map/ppermute | solution.py:347
  109.3 8.4 %collective-permute-start.14 = (bf16[32,512]{1,0:T(8,128)(2,1)S(1)}, bf16[32,512]{1,0:T(8,128)(2,1)S(1)}, u32[]{:S(2)}, u32[]{:S(2)}) collective-permute-start(bf16[32,512]{1,0:T(8,128)(2,1)S(1)} %shard_map.170.refs_0_), channel_id=1, source_target_pairs={{0,1},{1,0},{2,3},{3,2},{4,5},{5,4},{6,7},{7,6},{8,9},{9,8},{10,11... | collective-permute-start | bytes 98312 | tf_op jit(solution)/shard_map/ppermute | solution.py:347
  119.0 13.5 %all-to-all-start.3 = ((bf16[8,64,512]{2,1,0:T(8,128)(2,1)}), bf16[8,64,512]{2,1,0:T(8,128)(2,1)S(1)}, u32[]{:S(2)}, u32[]{:S(2)}) async-start(bf16[8,64,512]{2,1,0:T(8,128)(2,1)} %shard_map.171), calls=%async_computation.3 | async-start | bytes 1048576 | tf_op jit(solution)/shard_map/all_to_all | solution.py:350
  133.4 0.8 copy-start.20

commit v6 on v5

--- a/solution.py
+++ b/solution.py
@@ -34,7 +34,7 @@
 def shape(dims, kind=bf16):
     return jax.ShapeDtypeStruct(tuple(dims), kind)
 
-def call(body, outs, ins, kinds, out_kinds, scratch=(), vmem=ROOMY):
+def call(body, outs, ins, kinds, out_kinds, scratch=(), vmem=ROOMY, work=0):
     single = not isinstance(outs, (list, tuple))
     outs = [outs] if single else list(outs)
     staged = [x for x, kind in zip(ins, kinds) if kind == "h"]
@@ -79,7 +79,7 @@
         out_specs=[VMEM if kind == "v" else HBM for kind in out_kinds],
         scratch_shapes=buffers + list(scratch) + ([DMA((count,))] if count else []),
         compiler_params=pltpu.CompilerParams(vmem_limit_bytes=vmem << 20),
-        cost_estimate=pl.CostEstimate(flops=0, bytes_accessed=0, transcendentals=0),
+        cost_estimate=pl.CostEstimate(flops=work, bytes_accessed=0, transcendentals=0),
     )(*ins)
     return result[0] if single else result
 
@@ -245,18 +245,18 @@
 def first_kernel(shards, owners, parity, ready, *refs):
     backs, (label, acts) = refs[:shards], refs[shards : shards + 2]
     arrived = refs[shards + 2] if parity == 0 else None
-    outs = refs[shards + 2 + (parity == 0) :]
-    ready()
+    out = refs[-1]
+    chip = lax.div(lax.axis_index("dp"), 2)
     coefficient = adapter_scale * MODEL_WIDTH ** (-0.5)
     low = total(backs, slice(None))
     for n in range(owners // 2):
         k = 2 * n + parity
-        columns = outs[0].shape[-2]
+        columns = out.shape[1]
         grad = coefficient * dot(spread(low, label[0:1], k, columns), acts[...])
         if parity:
-            outs[0][n] = grad.astype(bf16)
+            out[n] = grad.astype(bf16)
         else:
-            outs[n][...] = (grad + arrived[n].astype(f32)).astype(bf16)
+            out[chip ^ n] = (grad + arrived[n].astype(f32)).astype(bf16)
 
 def mid_kernel(owners, parts, ready, *refs):
     a_blocks = refs[:owners]
@@ -311,14 +311,12 @@
     for k in range(owners):
         out[me ^ k] = grad[k * own_rows : (k + 1) * own_rows]
 
-def adam_a_kernel(count, *refs):
-    grads, (param, moment, second), outs = refs[:count], refs[count : count + 3], refs[count + 3 :]
-    grad = grads[0][...].astype(f32)
-    for part in grads[1:]:
-        grad = grad + part[...].astype(f32)
+def adam_a_kernel(grads, param, moment, second, *outs):
+    grad = jnp.sum(grads[...].astype(f32), axis=0)
     new = adam_step(param[...], moment[...], second[...], jnp.transpose(grad))
     for out, value in zip(outs, new):
         out[...] = value
+
 
 def adam_b_kernel(ready, grads, param, moment, second, *outs):
     ready()
@@ -346,8 +344,10 @@
     size = lax.axis_size(axis)
     return lax.ppermute(block, axis, [(i, i ^ bits) for i in range(size)])
 
-def exchange(blocks, axis):
-    return lax.all_to_all(blocks, axis, split_axis=0, concat_axis=0, tiled=True)
+def exchange(blocks, axis, groups=None):
+    return lax.all_to_all(
+        blocks, axis, split_axis=0, concat_axis=0, tiled=True, axis_index_groups=groups
+    )
 
 def per_device(
     acts,
@@ -386,8 +386,8 @@
     shares = exchange(share, "fsdp")
     chips = [swap(low, "dp", k) for k in range(2, owners, 2)]
     own = swap(low, "dp", 1)
-    shares, *rest = lax.optimization_barrier((shares, *chips, *cuts))
-    chips, cuts = rest[: len(chips)], rest[len(chips) :]
+    shares, *cuts = lax.optimization_barrier((shares, *cuts))
+    shares, *chips = lax.optimization_barrier((shares, *chips))
     blocks = [low, own]
     for block in chips:
         blocks += [block, swap(block, "dp", 1)]
@@ -413,6 +413,17 @@
     step = min(ROW_STEP, rows)
     factor_scratch = [pltpu.VMEM((features, owners * columns), bf16)]
     sems = [DMA((owners,))]
+    odds = [
+        call(
+            functools.partial(first_kernel, shards, owners, 1),
+            shape((owners // 2, columns, width)),
+            (*backs, label, acts_part),
+            "v" * (shards + 2),
+            "v",
+        )
+        for acts_part in acts_parts
+    ]
+    base, *odds = lax.optimization_barrier((base, *odds))
     grad_part = call(
         functools.partial(side_kernel, shards, owners),
         shape((rows, features)),
@@ -422,32 +433,24 @@
         factor_scratch + [pltpu.VMEM((step, owners * columns), bf16)] + sems,
 
     )
-    grad_part, *acts_parts = lax.optimization_barrier((grad_part, *acts_parts))
     returned = exchange(grad_part.reshape(shards, row_count, features), "fsdp")
     grad_input = call(
         lay_kernel, shape((row_count, shards * features)), (returned,), "h", "r", [DMA((shards,))], FULL
     )
 
-    grad_a = []
-    for acts_part in acts_parts:
-        odd = call(
-            functools.partial(first_kernel, shards, owners, 1),
+    evens = [
+        call(
+            functools.partial(first_kernel, shards, owners, 0),
             shape((owners // 2, columns, width)),
-            (*backs, label, acts_part),
-            "v" * (shards + 2),
+            (*backs, label, acts_part, swap(odd, "dp", 1)),
+            "v" * (shards + 3),
             "v",
         )
-        even = call(
-            functools.partial(first_kernel, shards, owners, 0),
-            [shape((columns, width))] * (owners // 2),
-            (*backs, label, acts_part, swap(odd, "dp", 1)),
-            "v" * (shards + 3),
-            "v" * (owners // 2),
-        )
-        grad_a.append(list(even))
-    label, *grads = lax.optimization_barrier((label, *sum(grad_a, [])))
-    grad_a = [grads[h * (owners // 2) : (h + 1) * (owners // 2)] for h in range(parts)]
-    grad_a = [[g[0]] + [swap(g[n], "dp", 2 * n) for n in range(1, owners // 2)] for g in grad_a]
+        for odd, acts_part in zip(odds, acts_parts)
+    ]
+    label, *evens = lax.optimization_barrier((label, *evens))
+    chips = [list(range(core, owners, 2)) for core in range(2)]
+    grad_a = [exchange(even, "dp", chips) for even in evens]
 
     mid = call(
         functools.partial(mid_kernel, owners, parts),
@@ -456,6 +459,7 @@
         "r" * owners + "v" * (1 + parts),
         "v",
         factor_scratch + sems,
+        work=12 * rows * features * owners * columns,
     )
     mids = [mid] + [swap(mid, "fsdp", j) for j in range(1, shards)]
     grad_b = call(
@@ -475,18 +479,16 @@
     )
     block = min(256, width)
     steps = width // block
-    wide = pl.BlockSpec((columns, block), lambda i: (0, i))
-    new_a = (a_param, a_moment, a_second)
-    for h in range(parts):
-        tall = pl.BlockSpec((block, columns), lambda i, h=h: (h * steps + i, 0))
-        new_a = pl.pallas_call(
-            functools.partial(adam_a_kernel, owners // 2),
-            grid=(steps,),
-            out_shape=[shape(a_param.shape, f32)] * 3,
-            in_specs=[wide] * (owners // 2) + [tall] * 3,
-            out_specs=[tall] * 3,
-            compiler_params=pltpu.CompilerParams(vmem_limit_bytes=FULL << 20),
-        )(*grad_a[h], *new_a)
+    wide = pl.BlockSpec((owners // 2, columns, block), lambda i: (0, 0, i))
+    tall = pl.BlockSpec((block, columns), lambda i: (i, 0))
+    new_a = pl.pallas_call(
+        adam_a_kernel,
+        grid=(steps,),
+        out_shape=[shape(a_param.shape, f32)] * 3,
+        in_specs=[wide] + [tall] * 3,
+        out_specs=[tall] * 3,
+        compiler_params=pltpu.CompilerParams(vmem_limit_bytes=FULL << 20),
+    )(grad_a[0], a_param, a_moment, a_second)
     return (grad_input, new_a[0], new_a[1], new_a[2], new_b[0], new_b[1], new_b[2])
 
 def solution(mesh):

time: 140 us -> 162 us (1.16)
  blocking collectives: 0 us -> 34.9 us
  starting transfers between devices: 41.9 us -> 25.4 us
  waiting for transfers between devices: 59.3 us -> 63.5 us
  local copies, waits for them, and re-layouts: 4.94 us -> 3.29 us
    all_to_all x0 -> x2, blocking collectives: none -> 34.9 us  [exchange(): lax.all_to_all(blocks, axis, split_axis=0, concat_axis=0, tiled=True, axi...]
    all_to_all x4 -> x3, waiting for transfers between devices: 7.78 us -> 21.4 us  [exchange(): lax.all_to_all(blocks, axis, split_axis=0, concat_axis=0, tiled=True, axi...]
    ppermute x17 -> x14, starting transfers between devices: 22.7 us -> 12.9 us  [swap(): return lax.ppermute(block, axis, [(i, i ^ bits) for i in range(size)])]
    ppermute x17 -> x14, waiting for transfers between devices: 51.5 us -> 42.1 us  [swap(): return lax.ppermute(block, axis, [(i, i ^ bits) for i in range(size)])]
    all_to_all x4 -> x3, starting transfers between devices: 19.2 us -> 12.4 us  [exchange(): lax.all_to_all(blocks, axis, split_axis=0, concat_axis=0, tiled=True, axi...]
    unnamed x42, local copies, waits for them, and re-layouts: 4.94 us -> 3.29 us
  transfers between devices with their start and end apart: 21 -> 17, of which waited for: 9 -> 8; matrix products, arithmetic and copies ran while one was open for 0% -> 0% of each run, Pallas kernels for 15% -> 14%
where the time goes in v6:
time: 162 us; the launch traced here: 161 us
  waiting for transfers between devices  63.5 us (39%)
  blocking collectives  34.9 us (22%)
  Pallas kernels  32.9 us (20%)
  starting transfers between devices  25.4 us (16%)
  local copies, waits for them, and re-layouts  3.29 us (2%)
    ppermute x14, waiting for transfers between devices, swap(): return lax.ppermute(block, axis, [(i, i ^ bits) for i in range(size)])  42.1 us
    all_to_all x2, blocking collectives, exchange(): lax.all_to_all(blocks, axis, split_axis=0, concat_axis=0, tiled=True, axi...  34.9 us
    pallas_call x10, Pallas kernels, call(): pl.pallas_call(kernel, out_shape=outs, in_specs=[VMEM if kind == 'v' else...  28 us
    all_to_all x3, waiting for transfers between devices, exchange(): lax.all_to_all(blocks, axis, split_axis=0, concat_axis=0, tiled=True, axi...  21.4 us
    ppermute x14, starting transfers between devices, swap(): return lax.ppermute(block, axis, [(i, i ^ bits) for i in range(size)])  12.9 us
    all_to_all x3, starting transfers between devices, exchange(): lax.all_to_all(blocks, axis, split_axis=0, concat_axis=0, tiled=True, axi...  12.4 us
    pallas_call x1, Pallas kernels, per_device(): pl.pallas_call(adam_a_kernel, grid=(steps,), out_shape=[shape(a_param.sha...  4.96 us
    unnamed x42, local copies, waits for them, and re-layouts  3.29 us
  transfers between devices with their start and end apart: 17, of which 8 were waited for; matrix products, arithmetic and copies ran while one was open for 0% of the time, Pallas kernels for 14%

profile of v6, /device:TPU:0, one launch (start us, length us, event | category | flops | bytes accessed | tf_op | source)
XLA Modules:
  0.0 161.0 jit_solution(12124972634955337817)
XLA Ops:
  0.6 3.2 %shard_map.162 = (bf16[4,144,512]{2,1,0:T(8,128)(2,1)}, bf16[1152,256]{1,0:T(8,128)(2,1)}, bf16[4,128,1024]{2,1,0:T(8,128)(2,1)}) custom-call(bf16[128,4096]{1,0:T(8,128)(2,1)} %refs_0_.1, bf16[128,512]{1,0:T(8,128)(2,1)} %refs_1_.3, s32[1,128]{1,0:T(1,128)} %bitcast.7, s32[1,128]{1,0:T(1,128)} %bitcast.8, f32[1024,256]{1,0:T(8,128)} %param.23, ...), custom_call_target="tpu_custom_call" | custom-call | tf_op jit(solution)/shard_map/pallas_call | solution.py:75
  3.9 0.0 copy-start
  3.9 22.5 %all_to_all.25.refs_0_ = bf16[4,144,512]{2,1,0:T(8,128)(2,1)} all-to-all(bf16[4,144,512]{2,1,0:T(8,128)(2,1)} %get-tuple-element.30), channel_id=1, replica_groups=mesh['dp'=8,'fsdp'=4] {'fsdp'}, dimensions={0} | all-to-all | bytes 1179648 | tf_op jit(solution)/shard_map/all_to_all | solution.py:348
  26.3 3.5 %all-to-all-start.1 = ((bf16[4,128,1024]{2,1,0:T(8,128)(2,1)}), bf16[4,128,1024]{2,1,0:T(8,128)(2,1)S(1)}, u32[]{:S(2)}, u32[]{:S(2)}) async-start(bf16[4,128,1024]{2,1,0:T(8,128)(2,1)} %get-tuple-element.40), calls=%async_computation.1 | async-start | bytes 2097152 | tf_op jit(solution)/shard_map/all_to_all | solution.py:348
  29.9 2.5 %collective-permute-start.3 = (bf16[1152,256]{1,0:T(8,128)(2,1)S(1)}, bf16[1152,256]{1,0:T(8,128)(2,1)S(1)}, u32[]{:S(2)}, u32[]{:S(2)}) collective-permute-start(bf16[1152,256]{1,0:T(8,128)(2,1)S(1)} %copy-done), channel_id=1, source_target_pairs={{0,24},{4,28},{8,16},{12,20},{16,8},{20,12},{24,0},{28,4},{1,25},{... | collective-permute-start | bytes 1769480 | tf_op jit(solution)/shard_map/ppermute | solution.py:345
  32.4 0.5 collective-permute-start.2
  32.9 0.5 collective-permute-start.1
  33.4 0.0 collective-permute-start
  33.4 13.7 %collective-permute-done.3.refs_6_.refs_10_ = bf16[1152,256]{1,0:T(8,128)(2,1)S(1)} collective-permute-done((bf16[1152,256]{1,0:T(8,128)(2,1)S(1)}, bf16[1152,256]{1,0:T(8,128)(2,1)S(1)}, u32[]{:S(2)}, u32[]{:S(2)}) %collective-permute-start.3) | collective-permute-done | bytes 589856 | tf_op jit(solution)/shard_map/ppermute | solution.py:345
  47.1 10.6 %collective-permute-done.2.refs_4_.refs_8_ = bf16[1152,256]{1,0:T(8,128)(2,1)S(1)} collective-permute-done((bf16[1152,256]{1,0:T(8,128)(2,1)S(1)}, bf16[1152,256]{1,0:T(8,128)(2,1)S(1)}, u32[]{:S(2)}, u32[]{:S(2)}) %collective-permute-start.2) | collective-permute-done | bytes 589856 | tf_op jit(solution)/shard_map/ppermute | solution.py:345
  57.7 0.1 collective-permute-done.1.refs_2_.refs_6_
  57.8 0.0 collective-permute-start.4
  57.8 0.5 collective-permute-start.5
  58.3 0.0 collective-permute-start.6
  58.3 1.1 copy-done.13
  59.4 1.2 copy-done.16
  60.6 0.7 shard_map.163
  61.4 0.0 copy-start.17
  61.4 0.0 collective-permute-done.refs_1_.refs_5_
  61.4 0.0 copy-start.1
  61.4 0.0 collective-permute-done.4.refs_3_.refs_7_
  61.4 0.0 copy-start.4
  61.4 0.0 collective-permute-done.5.refs_5_.refs_9_
  61.4 0.1 collective-permute-done.6.refs_7_.refs_11_
  61.5 0.8 shard_map.164.refs_0_
  62.3 0.1 copy-done.17
  62.5 0.2 copy-done.1
  62.7 0.2 copy-done.4
  62.9 0.2 copy-done.7
  63.1 0.2 copy-done.10
  63.3 3.4 %collective-permute-start.9 = (bf16[32,512]{1,0:T(8,128)(2,1)S(1)}, bf16[32,512]{1,0:T(8,128)(2,1)S(1)}, u32[]{:S(2)}, u32[]{:S(2)}) collective-permute-start(bf16[32,512]{1,0:T(8,128)(2,1)S(1)} %shard_map.164.refs_0_), channel_id=1, source_target_pairs={{0,3},{1,2},{2,1},{3,0},{4,7},{5,6},{6,5},{7,4},{8,11},{9,10},{10,... | collective-permute-start | bytes 98312 | tf_op jit(solution)/shard_map/ppermute | solution.py:345
  66.7 0.0 collective-permute-start.8
  66.7 0.9 collective-permute-start.7
  67.7 1.3 collective-permute-done.9.refs_3_
  69.0 2.5 %collective-permute-done.8.refs_2_ = bf16[32,512]{1,0:T(8,128)(2,1)S(1)} collective-permute-done((bf16[32,512]{1,0:T(8,128)(2,1)S(1)}, bf16[32,512]{1,0:T(8,128)(2,1)S(1)}, u32[]{:S(2)}, u32[]{:S(2)}) %collective-permute-start.8) | collective-permute-done | bytes 32800 | tf_op jit(solution)/shard_map/ppermute | solution.py:345
  71.5 0.0 collective-permute-done.7.refs_1_
  71.5 0.0 all-to-all-done.1
  71.5 0.0 copy-start.5
  71.6 2.6 %shard_map.165 = bf16[4,256,1024]{2,1,0:T(8,128)(2,1)} custom-call(bf16[32,512]{1,0:T(8,128)(2,1)S(1)} %shard_map.164.refs_0_, bf16[32,512]{1,0:T(8,128)(2,1)S(1)} %collective-permute-done.7.refs_1_, bf16[32,512]{1,0:T(8,128)(2,1)S(1)} %collective-permute-done.8.refs_2_, bf16[32,512]{1,0:T(8,128)(2,1)S(1)} %collective-permute-done.9.refs_3_, ...), custom_call_target="tpu_custom_call" | custom-call | tf_op jit(solution)/shard_map/pallas_call | solution.py:75
  74.2 0.0 collective-permute-start.10
  74.2 6.1 %shard_map.166 = bf16[512,1024]{1,0:T(8,128)(2,1)} custom-call(bf16[32,512]{1,0:T(8,128)(2,1)S(1)} %shard_map.164.refs_0_, bf16[32,512]{1,0:T(8,128)(2,1)S(1)} %collective-permute-done.7.refs_1_, bf16[32,512]{1,0:T(8,128)(2,1)S(1)} %collective-permute-done.8.refs_2_, bf16[32,512]{1,0:T(8,128)(2,1)S(1)} %collective-permute-done.9.refs_3_, ...), custom_call_target="tpu_custom_call" | custom-call | tf_op jit(solution)/shard_map/pallas_call | solution.py:75
  80.3 4.5 %all-to-all-start.2 = ((bf16[4,128,1024]{2,1,0:T(8,128)(2,1)}), bf16[4,128,1024]{2,1,0:T(8,128)(2,1)}, u32[]{:S(2)}, u32[]{:S(2)}) async-start(bf16[4,128,1024]{2,1,0:T(8,128)(2,1)} %bitcast.3), calls=%async_computation.2 | async-start | bytes 2097152 | tf_op jit(solution)/shard_map/all_to_all | solution.py:348
  84.8 0.0 copy-start.3
  84.8 0.0 copy-start.6
  84.8 0.0 collective-permute-done.10.refs_6_
  84.8 4.4 %shard_map.168 = bf16[4,256,1024]{2,1,0:T(8,128)(2,1)} custom-call(bf16[32,512]{1,0:T(8,128)(2,1)S(1)} %shard_map.164.refs_0_, bf16[32,512]{1,0:T(8,128)(2,1)S(1)} %collective-permute-done.7.refs_1_, bf16[32,512]{1,0:T(8,128)(2,1)S(1)} %collective-permute-done.8.refs_2_, bf16[32,512]{1,0:T(8,128)(2,1)S(1)} %collective-permute-done.9.refs_3_, ...), custom_call_target="tpu_custom_call" | custom-call | tf_op jit(solution)/shard_map/pallas_call | solution.py:75
  89.3 6.4 %shard_map.170.refs_0_ = bf16[32,512]{1,0:T(8,128)(2,1)S(1)} custom-call(bf16[1152,256]{1,0:T(8,128)(2,1)S(1)} %copy-done, bf16[1152,256]{1,0:T(8,128)(2,1)S(1)} %copy-done.3, bf16[1152,256]{1,0:T(8,128)(2,1)S(1)} %collective-permute-done.1.refs_2_.refs_6_, bf16[1152,256]{1,0:T(8,128)(2,1)S(1)} %copy-done.6, ...), custom_call_target="tpu_custom_call" | custom-call | flops 12884901888 | tf_op jit(solution)/shard_map/pallas_call | solution.py:75
  95.8 3.6 %collective-permute-start.13 = (bf16[32,512]{1,0:T(8,128)(2,1)S(1)}, bf16[32,512]{1,0:T(8,128)(2,1)S(1)}, u32[]{:S(2)}, u32[]{:S(2)}) collective-permute-start(bf16[32,512]{1,0:T(8,128)(2,1)S(1)} %shard_map.170.refs_0_), channel_id=1, source_target_pairs={{0,3},{1,2},{2,1},{3,0},{4,7},{5,6},{6,5},{7,4},{8,11},{9,10},{10,... | collective-permute-start | bytes 98312 | tf_op jit(solution)/shard_map/ppermute | solution.py:345
  99.4 0.0 collective-permute-start.12
  99.4 0.8 collective-permute-start.11
  100.2 7.5 %collective-permute-done.13.refs_3_ = bf16[32,512]{1,0:T(8,128)(2,1)S(1)} collective-permute-done((bf16[32,512]{1,0:T(8,128)(2,1)S(1)}, bf16[32,512]{1,0:T(8,128)(2,1)S(1)}, u32[]{:S(2)}, u32[]{:S(2)}) %collective-permute-start.13) | collective-permute-done | bytes 32800 | tf_op jit(solution)/shard_map/ppermute | solution.py:345
  107.7 6.3 %collective-permute-done.12.refs_2_ = bf16[32,512]{1,0:T(8,128)(2,1)S(1)} collective-permute-done((bf16[32,512]{1,0:T(8,128)(2,1)S(1)}, bf16[32,512]{1,0:T(8,128)(2,1)S(1)}, u32[]{:S(2)}, u32[]{:S(2)}) %collective-permute-start.12) | collective-permute-done | bytes 32800 | tf_op jit(solution)/shard_map/ppermute | solution.py:345
  114.0 0.0 collective-permute-done.11.refs_1_
  114.0 0.5 shard_map.171
  114.5 0.0 all-to-all-done.2.refs_0_
  114.5 12.5 %all_to_all.26.refs_0_ = bf16[8,64,512]{2,1,0:T(8,128)(2,1)S(1)} all-to-all(bf16[8,64,512]{2,1,0:T(8,128)(2,1)S(1)} %shard_map.171), channel_id=1, replica_groups=mesh['dp'=8,'fsdp'=4] {'dp'}, dimensions={0} | all-to-all | bytes 1048576 | tf_op jit(solution)/shard_map/all_to_all | solution.py:348
  127.0 4.5 %all-to-all-start.3 = ((bf16[4,256,1024]{2,1,0:T(8,128)(2,1)}), bf16[4,256,1024]{2,1,0:T(8,128)(2,1)}, u32[]{:S(2)}, u32[]{:S(2)}) async-start(bf16[4,256,1024]{2,1,0:T(8,128)(2,1)} %shard_map.168), calls=%async_computation.3 | async-start | bytes 4194304 | tf_op jit(solution)/shard_map/all_to_all | solution.py:348
  131.4 0.0 copy-start.18
  131.5 0.0 copy-start.19
  131.5 0.0 copy-start.20
  131.5 2.3 %shard_map.167 = bf16[128,4096]{1,0:T(8,128)(2,1)} custom-call(bf16[4,128,1024]{2,1,0:T(8,128)(2,1)} %all-to-all-done.2.refs_0_), custom_call_target="tpu_custom_call" | custom-call | tf_op jit(solution)/shard_map/pallas_call | solution.py:75
  133.8 0.8 shard_map.172
  134.6 21.4 %all-to-all-done.3.grads = bf16[4,256,1024]{2,1,0:T(8,128)(2,1)} async-done(((bf16[4,256,1024]{2,1,0:T(8,128)(2,1)}), bf16[4,256,1024]{2,1,0:T(8,128)(2,1)}, u32[]{:S(2)}, u32[]{:S(2)}) %all-to-all-start.3) | async-done | bytes 2097184 | tf_op jit(solution)/shard_map/all_to_all | solution.py:348
  156.0 5.0 %shard_map.169 = (f32[1024,256]{1,0:T(8,128)}, f32[1024,256]{1,0:T(8,128)}, f32[1024,256]{1,0:T(8,128)}) custom-call(bf16[4,256,1024]{2,1,0:T(8,128)(2,1)} %all-to-all-done.3.grads, f32[1024,256]{1,0:T(8,128)} %param.23, f32[1024,256]{1,0:T(8,128)} %moment.1, f32[1024,256]{1,0:T(8,128)} %second.1), custom_call_target="tpu_custom_call" | custom-call | tf_op jit(solution)/shard_map/pallas_call | solution.py:484
  (25 shorter events, 0.1 us)
Async XLA Ops:
  3.9 26.0 %copy-start = (bf16[1152,256]{1,0:T(8,128)(2,1)S(1)}, bf16[1152,256]{1,0:T(8,128)(2,1)}, u32[]{:S(2)}) copy-start(bf16[1152,256]{1,0:T(8,128)(2,1)} %get-tuple-element.29.refs_0_.refs_4_) | copy-start | bytes 1769476
  26.3 45.2 %all-to-all-start.1 = ((bf16[4,128,1024]{2,1,0:T(8,128)(2,1)}), bf16[4,128,1024]{2,1,0:T(8,128)(2,1)S(1)}, u32[]{:S(2)}, u32[]{:S(2)}) async-start(bf16[4,128,1024]{2,1,0:T(8,128)(2,1)} %get-tuple-element.40), calls=%async_computation.1 | async-start | bytes 2097152 | tf_op jit(solution)/shard_map/all_to_all | solution.py:348
  29.9 17.3 %collective-permute-start.3 = (bf16[1152,256]{1,0:T(8,128)(2,1)S(1)}, bf16[1152,256]{1,0:T(8,128)(2,1)S(1)}, u32[]{:S(2)}, u32[]{:S(2)}) collective-permute-start(bf16[1152,256]{1,0:T(8,128)(2,1)S(1)} %copy-done), channel_id=1, source_target_pairs={{0,24},{4,28},{8,16},{12,20},{16,8},{20,12},{24,0},{28,4},{1,25},{... | collective-permute-start | bytes 1769480 | tf_op jit(solution)/shard_map/ppermute | solution.py:345
  32.4 25.3 %collective-permute-start.2 = (bf16[1152,256]{1,0:T(8,128)(2,1)S(1)}, bf16[1152,256]{1,0:T(8,128)(2,1)S(1)}, u32[]{:S(2)}, u32[]{:S(2)}) collective-permute-start(bf16[1152,256]{1,0:T(8,128)(2,1)S(1)} %copy-done), channel_id=1, source_target_pairs={{0,16},{4,20},{8,24},{12,28},{16,0},{20,4},{24,8},{28,12},{1,17},{... | collective-permute-start | bytes 1769480 | tf_op jit(solution)/shard_map/ppermute | solution.py:345
  32.9 24.9 %collective-permute-start.1 = (bf16[1152,256]{1,0:T(8,128)(2,1)S(1)}, bf16[1152,256]{1,0:T(8,128)(2,1)S(1)}, u32[]{:S(2)}, u32[]{:S(2)}) collective-permute-start(bf16[1152,256]{1,0:T(8,128)(2,1)S(1)} %copy-done), channel_id=1, source_target_pairs={{0,8},{4,12},{8,0},{12,4},{16,24},{20,28},{24,16},{28,20},{1,9},{5... | collective-permute-start | bytes 1769480 | tf_op jit(solution)/shard_map/ppermute | solution.py:345
  33.4 28.0 %collective-permute-start = (bf16[1152,256]{1,0:T(8,128)(2,1)S(1)}, bf16[1152,256]{1,0:T(8,128)(2,1)S(1)}, u32[]{:S(2)}, u32[]{:S(2)}) collective-permute-start(bf16[1152,256]{1,0:T(8,128)(2,1)S(1)} %copy-done), channel_id=1, source_target_pairs={{0,4},{4,0},{8,12},{12,8},{16,20},{20,16},{24,28},{28,24},{1,5},{5... | collective-permute-start | bytes 1769480 | tf_op jit(solution)/shard_map/ppermute | solution.py:345
  57.8 3.6 %collective-permute-start.4 = (bf16[1152,256]{1,0:T(8,128)(2,1)S(1)}, bf16[1152,256]{1,0:T(8,128)(2,1)S(1)}, u32[]{:S(2)}, u32[]{:S(2)}) collective-permute-start(bf16[1152,256]{1,0:T(8,128)(2,1)S(1)} %collective-permute-done.1.refs_2_.refs_6_), channel_id=1, source_target_pairs={{0,4},{4,0},{8,12},{12,8},{16,20},{20,16},{24,28},{28,24},{1,5},{5... | collective-permute-start | bytes 1769480 | tf_op jit(solution)/shard_map/ppermute | solution.py:345
  57.8 3.6 %collective-permute-start.5 = (bf16[1152,256]{1,0:T(8,128)(2,1)S(1)}, bf16[1152,256]{1,0:T(8,128)(2,1)S(1)}, u32[]{:S(2)}, u32[]{:S(2)}) collective-permute-start(bf16[1152,256]{1,0:T(8,128)(2,1)S(1)} %collective-permute-done.2.refs_4_.refs_8_), channel_id=1, source_target_pairs={{0,4},{4,0},{8,12},{12,8},{16,20},{20,16},{24,28},{28,24},{1,5},{5... | collective-permute-start | bytes 1769480 | tf_op jit(solution)/shard_map/ppermute | solution.py:345
  58.3 3.2 %collective-permute-start.6 = (bf16[1152,256]{1,0:T(8,128)(2,1)S(1)}, bf16[1152,256]{1,0:T(8,128)(2,1)S(1)}, u32[]{:S(2)}, u32[]{:S(2)}) collective-permute-start(bf16[1152,256]{1,0:T(8,128)(2,1)S(1)} %collective-permute-done.3.refs_6_.refs_10_), channel_id=1, source_target_pairs={{0,4},{4,0},{8,12},{12,8},{16,20},{20,16},{24,28},{28,24},{1,5},{5... | collective-permute-start | bytes 1769480 | tf_op jit(solution)/shard_map/ppermute | solution.py:345
  58.3 1.1 copy-start.13
  59.4 1.2 copy-start.16
  61.4 1.0 copy-start.14
  61.4 1.1 copy-start.17
  61.4 1.3 copy-start.1
  61.4 1.5 copy-start.4
  61.4 1.7 %copy-start.7 = (bf16[1152,256]{1,0:T(8,128)(2,1)}, bf16[1152,256]{1,0:T(8,128)(2,1)S(1)}, u32[]{:S(2)}) copy-start(bf16[1152,256]{1,0:T(8,128)(2,1)S(1)} %collective-permute-done.5.refs_5_.refs_9_) | copy-start | bytes 1769476
  61.5 1.8 %copy-start.10 = (bf16[1152,256]{1,0:T(8,128)(2,1)}, bf16[1152,256]{1,0:T(8,128)(2,1)S(1)}, u32[]{:S(2)}) copy-start(bf16[1152,256]{1,0:T(8,128)(2,1)S(1)} %collective-permute-done.6.refs_7_.refs_11_) | copy-start | bytes 1769476
  63.3 5.7 %collective-permute-start.9 = (bf16[32,512]{1,0:T(8,128)(2,1)S(1)}, bf16[32,512]{1,0:T(8,128)(2,1)S(1)}, u32[]{:S(2)}, u32[]{:S(2)}) collective-permute-start(bf16[32,512]{1,0:T(8,128)(2,1)S(1)} %shard_map.164.refs_0_), channel_id=1, source_target_pairs={{0,3},{1,2},{2,1},{3,0},{4,7},{5,6},{6,5},{7,4},{8,11},{9,10},{10,... | collective-permute-start | bytes 98312 | tf_op jit(solution)/shard_map/ppermute | solution.py:345
  66.7 4.8 %collective-permute-start.8 = (bf16[32,512]{1,0:T(8,128)(2,1)S(1)}, bf16[32,512]{1,0:T(8,128)(2,1)S(1)}, u32[]{:S(2)}, u32[]{:S(2)}) collective-permute-start(bf16[32,512]{1,0:T(8,128)(2,1)S(1)} %shard_map.164.refs_0_), channel_id=1, source_target_pairs={{0,2},{1,3},{2,0},{3,1},{4,6},{5,7},{6,4},{7,5},{8,10},{9,11},{10,... | collective-permute-start | bytes 98312 | tf_op jit(solution)/shard_map/ppermute | solution.py:345
  66.7 4.8 %collective-permute-start.7 = (bf16[32,512]{1,0:T(8,128)(2,1)S(1)}, bf16[32,512]{1,0:T(8,128)(2,1)S(1)}, u32[]{:S(2)}, u32[]{:S(2)}) collective-permute-start(bf16[32,512]{1,0:T(8,128)(2,1)S(1)} %shard_map.164.refs_0_), channel_id=1, source_target_pairs={{0,1},{1,0},{2,3},{3,2},{4,5},{5,4},{6,7},{7,6},{8,9},{9,8},{10,11... | collective-permute-start | bytes 98312 | tf_op jit(solution)/shard_map/ppermute | solution.py:345
  71.5 2.7 %copy-start.2 = (bf16[1152,256]{1,0:T(8,128)(2,1)S(1)}, bf16[1152,256]{1,0:T(8,128)(2,1)}, u32[]{:S(2)}) copy-start(bf16[1152,256]{1,0:T(8,128)(2,1)} %copy-done.1) | copy-start | bytes 1769476
  71.5 2.7 %copy-start.5 = (bf16[1152,256]{1,0:T(8,128)(2,1)S(1)}, bf16[1152,256]{1,0:T(8,128)(2,1)}, u32[]{:S(2)}) copy-start(bf16[1152,256]{1,0:T(8,128)(2,1)} %copy-done.4) | copy-start | bytes 1769476
  71.5 2.7 %copy-start.8 = (bf16[1152,256]{1,0:T(8,128)(2,1)S(1)}, bf16[1152,256]{1,0:T(8,128)(2,1)}, u32[]{:S(2)}) copy-start(bf16[1152,256]{1,0:T(8,128)(2,1)} %copy-done.7) | copy-start | bytes 1769476
  71.5 2.7 %copy-start.11 = (bf16[1152,256]{1,0:T(8,128)(2,1)S(1)}, bf16[1152,256]{1,0:T(8,128)(2,1)}, u32[]{:S(2)}) copy-start(bf16[1152,256]{1,0:T(8,128)(2,1)} %copy-done.10) | copy-start | bytes 1769476
  74.2 10.6 %collective-permute-start.10 = (bf16[4,256,1024]{2,1,0:T(8,128)(2,1)}, bf16[4,256,1024]{2,1,0:T(8,128)(2,1)}, u32[]{:S(2)}, u32[]{:S(2)}) collective-permute-start(bf16[4,256,1024]{2,1,0:T(8,128)(2,1)} %shard_map.165), channel_id=1, source_target_pairs={{0,4},{4,0},{8,12},{12,8},{16,20},{20,16},{24,28},{28,24},{1,5},{5... | collective-permute-start | bytes 6291464 | tf_op jit(solution)/shard_map/ppermute | solution.py:345
  80.3 34.2 %all-to-all-start.2 = ((bf16[4,128,1024]{2,1,0:T(8,128)(2,1)}), bf16[4,128,1024]{2,1,0:T(8,128)(2,1)}, u32[]{:S(2)}, u32[]{:S(2)}) async-start(bf16[4,128,1024]{2,1,0:T(8,128)(2,1)} %bitcast.3), calls=%async_computation.2 | async-start | bytes 2097152 | tf_op jit(solution)/shard_map/all_to_all | solution.py:348
  84.8 4.5 %copy-start.3 = (bf16[1152,256]{1,0:T(8,128)(2,1)S(1)}, bf16[1152,256]{1,0:T(8,128)(2,1)}, u32[]{:S(2)}) copy-start(bf16[1152,256]{1,0:T(8,128)(2,1)} %copy-done.1) | copy-start | bytes 1769476
  84.8 4.5 %copy-start.6 = (bf16[1152,256]{1,0:T(8,128)(2,1)S(1)}, bf16[1152,256]{1,0:T(8,128)(2,1)}, u32[]{:S(2)}) copy-start(bf16[1152,256]{1,0:T(8,128)(2,1)} %copy-done.4) | copy-start | bytes 1769476
  84.8 4.5 %copy-start.9 = (bf16[1152,256]{1,0:T(8,128)(2,1)S(1)}, bf16[1152,256]{1,0:T(8,128)(2,1)}, u32[]{:S(2)}) copy-start(bf16[1152,256]{1,0:T(8,128)(2,1)} %copy-done.7) | copy-start | bytes 1769476
  84.8 4.5 %copy-start.12 = (bf16[1152,256]{1,0:T(8,128)(2,1)S(1)}, bf16[1152,256]{1,0:T(8,128)(2,1)}, u32[]{:S(2)}) copy-start(bf16[1152,256]{1,0:T(8,128)(2,1)} %copy-done.10) | copy-start | bytes 1769476
  89.3 24.7 %copy-start.15 = (bf16[512,512]{1,0:T(8,128)(2,1)S(1)}, bf16[512,512]{1,0:T(8,128)(2,1)}, u32[]{:S(2)}) copy-start(bf16[512,512]{1,0:T(8,128)(2,1)} %copy-done.14) | copy-start | bytes 1572868
  95.8 11.9 %collective-permute-start.13 = (bf16[32,512]{1,0:T(8,128)(2,1)S(1)}, bf16[32,512]{1,0:T(8,128)(2,1)S(1)}, u32[]{:S(2)}, u32[]{:S(2)}) collective-permute-start(bf16[32,512]{1,0:T(8,128)(2,1)S(1)} %shard_map.170.refs_0_), channel_id=1, source_target_pairs={{0,3},{1,2},{2,1},{3,0},{4,7},{5,6},{6,5},{7,4},{8,11},{9,10},{10,... | collective-permute-start | bytes 98312 | tf_op jit(solution)/shard_map/ppermute | solution.py:345
  99.4 14.6 %collective-permute-start.12 = (bf16[32,512]{1,0:T(8,128)(2,1)S(1)}, bf16[32,512]{1,0:T(8,128)(2,1)S(1)}, u32[]{:S(2)}, u32[]{:S(2)}) collective-permute-start(bf16[32,512]{1,0:T(8,128)(2,1)S(1)} %shard_map.170.refs_0_), channel_id=1, source_target_pairs={{0,2},{1,3},{2,0},{3,1},{4,6},{5,7},{6,4},{7,5},{8,10},{9,11},{10,... | collective-permute-start | bytes 98312 | tf_op jit(solution)/shard_map/ppermute | solution.py:345
  99.4 14.6 %collective-permute-start.11 = (bf16[32,512]{1,0:T(8,128)(2,1)S(1)}, bf16[32,512]{1,0:T(8,128)(2,1)S(1)}, u32[]{:S(2)}, u32[]{:S(2)}) collective-permute-start(bf16[32,512]{1,0:T(8,128)(2,1)S(1)} %shard_map.170.refs_0_), channel_id=1, source_target_pairs={{0,1},{1,0},{2,3},{3,2},{4,5},{5,4},{6,7},{7,6},{8,9},{9,8},{10,11... | collective-permute-start | bytes 98312 | tf_op jit(solution)/shard_map/ppermute | solution.py:345
  127.0 29.0 %all-to-all-start.3 = ((bf16[4,256,1024]{2,1,0:T(8,128)(2,1)}), bf16[4,256,1024]{2,1,0:T(8,128)(2,1)}, u32[]{:S(2)}, u32[]{:S(2)}) async-start(bf16[4,256,1024]{2,1,0:T(8,128)(2,1)} %shard_map.168), calls=%async_computation.3 | async-start | bytes 4194304 | tf_op jit(solution)/shard_map/all_to_all | solution.py:348
  131.4 2.3 %copy-start.18 = (f32[64,512]{1,0:T(8,128)S(1)}, f32[64,512]{1,0:T(8,128)}, u32[]{:S(2)}) copy-start(f32[64,512]{1,0:T(8,128)} %refs_1_.5) | copy-start | bytes 393220
  131.5 2.3 %copy-start.19 = (f32[64,512]{1,0:T(8,128)S(1)}, f32[64,512]{1,0:T(8,128)}, u32[]{:S(2)}) copy-start(f32[64,512]{1,0:T(8,128)} %refs_2_.1) | copy-start | bytes 393220
  131.5 2.3 %copy-start.20 = (f32[64,512]{1,0:T(8,128)S(1)}, f32[64,512]{1,0:T(8,128)}, u32[]{:S(2)}) copy-start(f32[64,512]{1,0:T(8,128)} %refs_3_.1) | copy-start | bytes 393220

commit v7 on v6

v7 whole, which is shorter than its diff:
```python
import functools

import jax
import jax.numpy as jnp
from jax import lax
from jax.experimental import pallas as pl
from jax.experimental.pallas import tpu as pltpu
from jax.sharding import PartitionSpec as P

MODEL_WIDTH = 4096
ADAPTER_RANK = 32
TEN_DEV = 8
LANES = 128
ROW_STEP = 512
LABEL_ROWS = 16
ROOMY = 48
FULL = 62

adapter_scale = 2.0
learn_rate = 0.02
beta_one = 0.9
beta_two = 0.999
adam_eps = 1e-08
bias_one = 1.0 - 0.9**10
bias_two = 1.0 - 0.999**10

f32 = jnp.float32
bf16 = jnp.bfloat16
VMEM = pl.BlockSpec(memory_space=pltpu.VMEM)
HBM = pl.BlockSpec(memory_space=pltpu.HBM)
DMA = pltpu.SemaphoreType.DMA

def shape(dims, kind=bf16):
    return jax.ShapeDtypeStruct(tuple(dims), kind)

def call(body, outs, ins, kinds, out_kinds, scratch=(), vmem=ROOMY, work=0):
    single = not isinstance(outs, (list, tuple))
    outs = [outs] if single else list(outs)
    staged = [x for x, kind in zip(ins, kinds) if kind == "h"]
    staged_outs = [x for x, kind in zip(outs, out_kinds) if kind == "h"]
    count = len(staged) + len(staged_outs)
    buffers = [pltpu.VMEM(x.shape, x.dtype) for x in staged + staged_outs]

    def kernel(*refs):
        refs = list(refs)
        given, made = refs[: len(ins)], refs[len(ins) : len(ins) + len(outs)]
        rest = refs[len(ins) + len(outs) :]
        held, own = rest[:count], rest[count : len(rest) - bool(count)]
        sems = rest[-1] if count else None
        loads, stores = [], []
        for n, kind in enumerate(kinds):
            if kind == "h":
                at = len(loads)
                loads.append(pltpu.make_async_copy(given[n], held[at], sems.at[at]))
                given[n] = held[at]
        for n, kind in enumerate(out_kinds):
            if kind == "h":
                at = len(loads) + len(stores)
                stores.append(pltpu.make_async_copy(held[at], made[n], sems.at[at]))
                made[n] = held[at]
        for copy in loads:
            copy.start()

        def ready():
            for copy in loads:
                copy.wait()

        body(ready, *given, *made, *own)
        for copy in stores:
            copy.start()
        for copy in stores:
            copy.wait()

    result = pl.pallas_call(
        kernel,
        out_shape=outs,
        in_specs=[VMEM if kind == "v" else HBM for kind in kinds],
        out_specs=[VMEM if kind == "v" else HBM for kind in out_kinds],
        scratch_shapes=buffers + list(scratch) + ([DMA((count,))] if count else []),
        compiler_params=pltpu.CompilerParams(vmem_limit_bytes=vmem << 20),
        cost_estimate=pl.CostEstimate(flops=work, bytes_accessed=0, transcendentals=0),
    )(*ins)
    return result[0] if single else result

def adam_step(param, moment, second, gradient):
    moment = beta_one * moment + (1.0 - beta_one) * gradient
    second = beta_two * second + (1.0 - beta_two) * gradient * gradient
    step = (learn_rate / bias_one) * moment
    param = param - step / (jnp.sqrt((1.0 / bias_two) * second) + adam_eps)
    return (param, moment, second)

def dot(left, right, left_dim=1, right_dim=0):
    return lax.dot_general(
        left, right, (((left_dim,), (right_dim,)), ((), ())), preferred_element_type=f32
    )

def iota(dims, axis):
    return lax.broadcasted_iota(jnp.int32, dims, axis)

def column_of(row, lanes=LANES):
    n = row.shape[1]
    wide = jnp.broadcast_to(row.astype(f32), (lanes, n))
    return jnp.transpose(wide)

def prep_kernel(ready, acts, cot, tenant, advantage, a_param, b_param, packed, low):
    ready()
    rows, keys = cot.shape
    shards, _, unit = packed.shape
    features, columns = a_param.shape
    factor = column_of(advantage[...]) * 0.25
    factor = jnp.concatenate([factor] * (keys // LANES), axis=1)
    scaled = (cot[...].astype(f32) * factor).astype(bf16)
    t = tenant[...]
    line = iota((LABEL_ROWS, rows), 0)
    owner = jnp.broadcast_to(lax.div(t, TEN_DEV), (LABEL_ROWS, rows))
    local = jnp.broadcast_to(lax.rem(t, TEN_DEV), (LABEL_ROWS, rows))
    labels = jnp.where(line == 0, owner, jnp.where(line == 1, local, 0)).astype(f32)
    labels = labels.astype(bf16)
    for j in range(shards):
        for q in range(features // unit):
            at = j * features + q * unit
            packed[j, q * rows : (q + 1) * rows] = acts[:, at : at + unit]
        first = features // unit * rows
        for q in range(keys // unit):
            packed[j, first + q * rows : first + (q + 1) * rows] = scaled[:, q * unit : (q + 1) * unit]
        first += keys // unit * rows
        packed[j, first:, :rows] = labels
        packed[j, first:, rows:] = jnp.zeros((LABEL_ROWS, unit - rows), bf16)
    low[:features] = (a_param[...] * MODEL_WIDTH ** (-0.5)).astype(bf16)
    own_rows = b_param.shape[0]
    for q in range(keys // columns):
        part = b_param[:, q * columns : (q + 1) * columns] * ADAPTER_RANK ** (-0.5)
        low[features + q * own_rows : features + (q + 1) * own_rows] = part.astype(bf16)


def second_ids(count, own_rows, rows):
    line = iota((count * own_rows, rows), 0)
    inner = lax.rem(line, own_rows) + lax.axis_index("fsdp") * own_rows
    return lax.div(line, own_rows) * TEN_DEV + lax.div(inner, ADAPTER_RANK)


def base_kernel(ready, scaled, weight, base):
    rows = scaled.shape[0]
    step = min(ROW_STEP, rows)
    for r in range(0, rows, step):
        base[r : r + step] = dot(scaled[r : r + step], weight[...], 1, 1).astype(bf16)


def load_factors(a_blocks, a_all, sems):
    columns = a_blocks[0].shape[1]
    copies = [
        pltpu.make_async_copy(
            block.at[pl.ds(0, a_all.shape[0])],
            a_all.at[:, pl.ds(k * columns, columns)],
            sems.at[k],
        )
        for k, block in enumerate(a_blocks)
    ]
    for copy in copies:
        copy.start()
    return copies


def open_kernel(owners, own_rows, ready, packed, *refs):
    blocks = refs[:owners]
    acts, scaled, label, both, b_all, a_all, b_sems, sems = refs[owners:]
    rows, features = acts.shape
    keys = scaled.shape[1]
    columns = blocks[0].shape[1]
    shards, _, unit = packed.shape
    rd = rows // shards
    b_copies = []
    for k in range(owners):
        for q in range(keys // columns):
            b_copies.append(
                pltpu.make_async_copy(
                    blocks[k].at[pl.ds(features + q * own_rows, own_rows)],
                    b_all.at[pl.ds(k * own_rows, own_rows), pl.ds(q * columns, columns)],
                    b_sems.at[k, q],
                )
            )
    for copy in b_copies:
        copy.start()
    copies = load_factors(blocks, a_all, sems)
    me = lax.axis_index("dp")
    for j in range(shards):
        at = slice(j * rd, (j + 1) * rd)
        for q in range(features // unit):
            acts[at, q * unit : (q + 1) * unit] = packed[j, q * rd : (q + 1) * rd]
        first = features // unit * rd
        for q in range(keys // unit):
            part = packed[j, first + q * rd : first + (q + 1) * rd]
            scaled[at, q * unit : (q + 1) * unit] = part
        first += keys // unit * rd
        ids = packed[j, first:, :rd].astype(f32).astype(jnp.int32)
        tid = (ids[0:1] ^ me) * TEN_DEV + ids[1:2]
        label[:, at] = jnp.broadcast_to(tid, (8, rd))
    step = min(ROW_STEP, rows)
    ids = second_ids(owners, own_rows, step)
    for copy in b_copies:
        copy.wait()
    for r in range(0, rows, step):
        at = slice(r, r + step)
        wide = dot(b_all[...], scaled[at], 1, 1)
        wide = jnp.where(ids == label[0:1, at], wide, 0.0)
        if own_rows >= ADAPTER_RANK:
            low = jnp.sum(wide.reshape(-1, ADAPTER_RANK, step), axis=0)
        else:
            low = jnp.sum(wide.reshape(-1, own_rows, step), axis=0)
            low = jnp.concatenate([low] * (ADAPTER_RANK // own_rows), axis=0)
            part = lax.div(iota(low.shape, 0), own_rows)
            place = lax.rem(lax.axis_index("fsdp"), ADAPTER_RANK // own_rows)
            low = jnp.where(part == place, low, 0.0)
        both[:ADAPTER_RANK, at] = low.astype(bf16)
        where = column_of(label[0:1, at]).astype(jnp.int32) - lax.div(
            iota((step, LANES), 1), ADAPTER_RANK
        )
        low = jnp.zeros((step, LANES), f32)
        for k in range(owners):
            if r == 0:
                copies[k].wait()
            wide = dot(acts[at], a_all[:, k * columns : (k + 1) * columns])
            for q in range(columns // LANES):
                hit = where == k * TEN_DEV + q * (LANES // ADAPTER_RANK)
                low = low + jnp.where(hit, wide[:, q * LANES : (q + 1) * LANES], 0.0)
        low = jnp.transpose(low).reshape(LANES // ADAPTER_RANK, ADAPTER_RANK, step)
        both[ADAPTER_RANK:, at] = jnp.sum(low, axis=0).astype(bf16)


def total(parts, lines, at):
    value = parts[0][lines, at].astype(f32)
    for part in parts[1:]:
        value = value + part[lines, at].astype(f32)
    return value


BACK = slice(0, ADAPTER_RANK)
MID = slice(ADAPTER_RANK, 2 * ADAPTER_RANK)


def side_kernel(shards, owners, ready, *refs):
    backs, a_blocks = refs[:shards], refs[shards : shards + owners]
    label, base, out, a_all, back_wide, sems = refs[shards + owners :]
    copies = load_factors(a_blocks, a_all, sems)
    ready()
    rows, features = out.shape
    step = min(ROW_STEP, rows)
    width = a_all.shape[1]
    for r in range(0, rows, step):
        at = slice(r, r + step)
        low = adapter_scale * jnp.transpose(total(backs, BACK, at))
        low = jnp.concatenate([low] * (LANES // ADAPTER_RANK), axis=1)
        where = column_of(label[0:1, at]).astype(jnp.int32) - lax.div(
            iota((step, LANES), 1), ADAPTER_RANK
        )
        for q in range(width // LANES):
            hit = where == q * (LANES // ADAPTER_RANK)
            back_wide[:, q * LANES : (q + 1) * LANES] = jnp.where(hit, low, 0.0).astype(bf16)
        if r == 0:
            for copy in copies:
                copy.wait()
        chunk = min(256, features)
        for c in range(0, features, chunk):
            side = dot(back_wide[...], a_all[c : c + chunk], 1, 1).astype(bf16)
            whole = base[at, c : c + chunk].astype(f32) + side.astype(f32)
            out[at, c : c + chunk] = whole.astype(bf16)

def spread(low, label, k, columns):
    rows = low.shape[1]
    ids = lax.div(iota((columns, rows), 0), ADAPTER_RANK) + k * TEN_DEV
    tall = jnp.concatenate([low] * (columns // ADAPTER_RANK), axis=0)
    return jnp.where(ids == label, tall, 0.0).astype(bf16)

def grads_kernel(shards, owners, parity, own_rows, ready, *refs):
    boths, (label, acts, scaled) = refs[:shards], refs[shards : shards + 3]
    refs = refs[shards + 3 :]
    arrived = refs[0] if parity == 0 else None
    outs, held = refs[parity == 0 : -1], refs[-1]
    rows, features = acts.shape
    keys = scaled.shape[1]
    columns = outs[0].shape[-2]
    count = owners // 2
    up = adapter_scale * ADAPTER_RANK ** (-0.5)
    down = adapter_scale * MODEL_WIDTH ** (-0.5)
    step = min(ROW_STEP, rows)
    second = None
    line = iota((count * own_rows, step), 0)
    ids = second_ids(count, own_rows, step)
    ids = ids + (lax.div(line, own_rows) + parity) * TEN_DEV
    for r in range(0, rows, step):
        at = slice(r, r + step)
        held[...] = total(boths, MID, at)
        if own_rows >= ADAPTER_RANK:
            low = jnp.concatenate([held[...]] * (count * own_rows // ADAPTER_RANK), axis=0)
        else:
            first = lax.rem(lax.axis_index("fsdp") * own_rows, ADAPTER_RANK)
            low = held[pl.ds(pl.multiple_of(first, own_rows), own_rows)]
            low = jnp.concatenate([low] * count, axis=0)
        low = jnp.where(ids == label[0:1, at], low, 0.0).astype(bf16)
        term = up * dot(low, scaled[at])
        second = term if second is None else second + term
    low = total(boths, BACK, slice(None))
    for n in range(count):
        out = outs[0].at[n] if parity else outs[n]
        k = 2 * n + parity
        grad = down * dot(spread(low, label[0:1], k, columns), acts[...])
        if parity == 0:
            grad = grad + arrived[n, :, :features].astype(f32)
        out[:, :features] = grad.astype(bf16)
        for q in range(keys // LANES):
            lines = slice(q * own_rows, (q + 1) * own_rows)
            part = second[n * own_rows : (n + 1) * own_rows, q * LANES : (q + 1) * LANES]
            if parity == 0:
                part = part + arrived[n, lines, features:].astype(f32)
            out[lines, features:] = part.astype(bf16)
        used = keys // LANES * own_rows
        if used < columns:
            out[used:, features:] = jnp.zeros((columns - used, LANES), bf16)


def adam_kernel(count, own_rows, *refs):
    grads, ends, refs = refs[:count], refs[count : 2 * count], refs[2 * count :]
    firsts, seconds, outs = refs[:3], refs[3:6], refs[6:]

    def summed(parts):
        value = parts[0][...].astype(f32)
        for part in parts[1:]:
            value = value + part[...].astype(f32)
        return value

    new = adam_step(*[x[...] for x in firsts], jnp.transpose(summed(grads)))
    for out, value in zip(outs[:3], new):
        out[...] = value

    @pl.when(pl.program_id(0) == 0)
    def _():
        grad = summed(ends)
        keys = seconds[0].shape[1]
        for q in range(keys // LANES):
            at = slice(q * LANES, (q + 1) * LANES)
            part = grad[q * own_rows : (q + 1) * own_rows]
            for out, value in zip(outs[3:], adam_step(*[x[:, at] for x in seconds], part)):
                out[:, at] = value


def lay_kernel(ready, blocks, out):
    ready()
    shards, _, width = blocks.shape
    for j in range(shards):
        out[:, j * width : (j + 1) * width] = blocks[j]


def swap(block, axis, bits):
    size = lax.axis_size(axis)
    return lax.ppermute(block, axis, [(i, i ^ bits) for i in range(size)])


def exchange(blocks, axis, groups=None):
    return lax.all_to_all(
        blocks, axis, split_axis=0, concat_axis=0, tiled=True, axis_index_groups=groups
    )

def per_device(
    acts,
    cotangent,
    tenant,
    advantage,
    base_weight,
    a_param,
    a_moment,
    a_second,
    b_param,
    b_moment,
    b_second,
):
    owners = lax.axis_size("dp")
    shards = lax.axis_size("fsdp")
    row_count, keys = cotangent.shape
    features, columns = a_param.shape
    own_rows = b_param.shape[0]
    rows = row_count * shards

    unit = min(features, keys)
    b_lines = own_rows * keys // columns
    lines = (features + keys) // unit * row_count + LABEL_ROWS

    packed, low = call(
        prep_kernel,
        [shape((shards, lines, unit)), shape((features + b_lines, columns))],
        (acts, cotangent, tenant[None], advantage[None], a_param, b_param),
        "h" * 6,
        "hh",
        vmem=FULL,
    )
    packed = exchange(packed, "fsdp")
    chips = [low] + [swap(low, "dp", k) for k in range(2, owners, 2)]
    blocks = []
    for block in chips:
        blocks += [block, swap(block, "dp", 1)]

    step = min(ROW_STEP, rows)
    factors = pltpu.VMEM((features, owners * columns), bf16)
    acts_part, scaled, label, both = call(
        functools.partial(open_kernel, owners, own_rows),
        [
            shape((rows, features)),
            shape((rows, keys)),
            shape((8, rows), jnp.int32),
            shape((2 * ADAPTER_RANK, rows)),
        ],
        (packed, *blocks),
        "v" + "r" * owners,
        "vvvv",
        [
            pltpu.VMEM((owners * own_rows, keys), bf16),
            factors,
            DMA((owners, keys // columns)),
            DMA((owners,)),
        ],
    )
    boths = [both] + [swap(both, "fsdp", j) for j in range(1, shards)]
    base = call(base_kernel, shape((rows, features)), (scaled, base_weight), "vv", "v")

    def grads(parity, outs, *more):
        return call(
            functools.partial(grads_kernel, shards, owners, parity, own_rows),
            outs,
            (*boths, label, acts_part, scaled, *more),
            "v" * (shards + 3 + len(more)),
            "v" * (1 if parity else owners // 2),
            [pltpu.VMEM((ADAPTER_RANK, step), f32)],
        )

    odd = grads(1, shape((owners // 2, columns, features + LANES)))
    base, odd = lax.optimization_barrier((base, odd))
    grad_part = call(
        functools.partial(side_kernel, shards, owners),
        shape((rows, features)),
        (*boths, *blocks, label, base),
        "v" * shards + "r" * owners + "vv",
        "v",
        [factors, pltpu.VMEM((step, owners * columns), bf16), DMA((owners,))],
    )
    returned = exchange(grad_part.reshape(shards, row_count, features), "fsdp")
    grad_input = call(
        lay_kernel, shape((row_count, shards * features)), (returned,), "h", "h", vmem=FULL
    )

    even = grads(0, [shape((columns, features + LANES))] * (owners // 2), swap(odd, "dp", 1))
    sums = [even[0]] + [swap(even[n], "dp", 2 * n) for n in range(1, owners // 2)]

    block = min(256, features)
    wide = pl.BlockSpec((columns, block), lambda i: (0, i))
    end = pl.BlockSpec((columns, LANES), lambda i: (0, features // LANES))
    tall = pl.BlockSpec((block, columns), lambda i: (i, 0))
    flat = pl.BlockSpec((own_rows, keys), lambda i: (0, 0))
    new = pl.pallas_call(
        functools.partial(adam_kernel, owners // 2, own_rows),
        grid=(features // block,),
        out_shape=[shape(a_param.shape, f32)] * 3 + [shape(b_param.shape, f32)] * 3,
        in_specs=[wide] * (owners // 2) + [end] * (owners // 2) + [tall] * 3 + [flat] * 3,
        out_specs=[tall] * 3 + [flat] * 3,
        compiler_params=pltpu.CompilerParams(vmem_limit_bytes=FULL << 20),
    )(*sums, *sums, a_param, a_moment, a_second, b_param, b_moment, b_second)
    return (grad_input, *new)


def solution(mesh):
    rows = P(("dp", "fsdp"), None)
    labels = P(("dp", "fsdp"))
    first = P("fsdp", "dp")
    return jax.shard_map(
        per_device,
        mesh=mesh,
        in_specs=(rows, rows, labels, labels, P("fsdp", None), first, first, first, rows, rows, rows),
        out_specs=(rows, first, first, first, rows, rows, rows),
        check_vma=False,
    )
```

time: 162 us -> 125 us (0.77)
  blocking collectives: 34.9 us -> 0 us
  local copies, waits for them, and re-layouts: 3.29 us -> 12.3 us
  waiting for transfers between devices: 63.5 us -> 55.5 us
  starting transfers between devices: 25.4 us -> 22.5 us
    all_to_all x2 -> x0, blocking collectives: 34.9 us -> none  [exchange(): lax.all_to_all(blocks, axis, split_axis=0, concat_axis=0, tiled=True, axi...]
    ppermute x14, waiting for transfers between devices: 42.1 us -> 30.8 us  [swap(): return lax.ppermute(block, axis, [(i, i ^ bits) for i in range(size)])]
    unnamed x42, local copies, waits for them, and re-layouts: 3.29 us -> 12.3 us
    all_to_all x3 -> x2, waiting for transfers between devices: 21.4 us -> 24.7 us  [exchange(): lax.all_to_all(blocks, axis, split_axis=0, concat_axis=0, tiled=True, axi...]
    all_to_all x3 -> x2, starting transfers between devices: 12.4 us -> 10.7 us  [exchange(): lax.all_to_all(blocks, axis, split_axis=0, concat_axis=0, tiled=True, axi...]
    pallas_call x10 -> x7, Pallas kernels: 28 us -> 27.1 us  [call(): pl.pallas_call(kernel, out_shape=outs, in_specs=[VMEM if kind == 'v' else...]
  transfers between devices with their start and end apart: 17 -> 16, of which waited for: 8 -> 7; matrix products, arithmetic and copies ran while one was open for 0% -> 0% of each run, Pallas kernels for 14% -> 10%
where the time goes in v7:
time: 125 us; the launch traced here: 124 us
  waiting for transfers between devices  55.5 us (44%)
  Pallas kernels  32.8 us (26%)
  starting transfers between devices  22.5 us (18%)
  local copies, waits for them, and re-layouts  12.3 us (10%)
    ppermute x14, waiting for transfers between devices, swap(): return lax.ppermute(block, axis, [(i, i ^ bits) for i in range(size)])  30.8 us
    pallas_call x7, Pallas kernels, call(): pl.pallas_call(kernel, out_shape=outs, in_specs=[VMEM if kind == 'v' else...  27.1 us
    all_to_all x2, waiting for transfers between devices, exchange(): lax.all_to_all(blocks, axis, split_axis=0, concat_axis=0, tiled=True, axi...  24.7 us
    unnamed x42, local copies, waits for them, and re-layouts  12.3 us
    ppermute x14, starting transfers between devices, swap(): return lax.ppermute(block, axis, [(i, i ^ bits) for i in range(size)])  11.8 us
    all_to_all x2, starting transfers between devices, exchange(): lax.all_to_all(blocks, axis, split_axis=0, concat_axis=0, tiled=True, axi...  10.7 us
    pallas_call x1, Pallas kernels, per_device(): pl.pallas_call(functools.partial(adam_kernel, owners // 2, own_rows), gri...  5.69 us
  transfers between devices with their start and end apart: 16, of which 7 were waited for; matrix products, arithmetic and copies ran while one was open for 0% of the time, Pallas kernels for 10%

profile of v7, /device:TPU:0, one launch (start us, length us, event | category | flops | bytes accessed | tf_op | source)
XLA Modules:
  0.0 123.9 jit_solution(16831046553288201628)
XLA Ops:
  0.6 3.2 %shard_map.162 = (bf16[4,400,512]{2,1,0:T(8,128)(2,1)}, bf16[1152,256]{1,0:T(8,128)(2,1)}) custom-call(bf16[128,4096]{1,0:T(8,128)(2,1)} %refs_0_.1, bf16[128,512]{1,0:T(8,128)(2,1)} %refs_1_.2, s32[1,128]{1,0:T(1,128)} %bitcast.3, s32[1,128]{1,0:T(1,128)} %bitcast.4, f32[1024,256]{1,0:T(8,128)} %refs_8_.1, f32[64,512]{1,0:T(8,128)} %refs_11_.1), custom_call_target="tpu_custom_call" | custom-call | tf_op jit(solution)/shard_map/pallas_call | solution.py:74
  3.8 0.0 copy-start.2
  3.8 6.5 %all-to-all-start = ((bf16[4,400,512]{2,1,0:T(8,128)(2,1)}), bf16[4,400,512]{2,1,0:T(8,128)(2,1)}, u32[]{:S(2)}, u32[]{:S(2)}) async-start(bf16[4,400,512]{2,1,0:T(8,128)(2,1)} %get-tuple-element.25), calls=%async_computation | async-start | bytes 3276800 | tf_op jit(solution)/shard_map/all_to_all | solution.py:359
  10.3 0.0 copy-done.2
  10.3 2.4 %collective-permute-start.5 = (bf16[1152,256]{1,0:T(8,128)(2,1)S(1)}, bf16[1152,256]{1,0:T(8,128)(2,1)S(1)}, u32[]{:S(2)}, u32[]{:S(2)}) collective-permute-start(bf16[1152,256]{1,0:T(8,128)(2,1)S(1)} %copy-done.2), channel_id=1, source_target_pairs={{0,24},{4,28},{8,16},{12,20},{16,8},{20,12},{24,0},{28,4},{1,25},{... | collective-permute-start | bytes 1769480 | tf_op jit(solution)/shard_map/ppermute | solution.py:355
  12.7 0.5 collective-permute-start.3
  13.2 0.5 collective-permute-start.1
  13.8 0.0 collective-permute-start
  13.8 13.7 %collective-permute-done.5.refs_7_.refs_10_ = bf16[1152,256]{1,0:T(8,128)(2,1)S(1)} collective-permute-done((bf16[1152,256]{1,0:T(8,128)(2,1)S(1)}, bf16[1152,256]{1,0:T(8,128)(2,1)S(1)}, u32[]{:S(2)}, u32[]{:S(2)}) %collective-permute-start.5) | collective-permute-done | bytes 589856 | tf_op jit(solution)/shard_map/ppermute | solution.py:355
  27.5 0.0 collective-permute-start.6
  27.5 11.1 %collective-permute-done.3.refs_5_.refs_8_ = bf16[1152,256]{1,0:T(8,128)(2,1)S(1)} collective-permute-done((bf16[1152,256]{1,0:T(8,128)(2,1)S(1)}, bf16[1152,256]{1,0:T(8,128)(2,1)S(1)}, u32[]{:S(2)}, u32[]{:S(2)}) %collective-permute-start.3) | collective-permute-done | bytes 589856 | tf_op jit(solution)/shard_map/ppermute | solution.py:355
  38.6 0.0 collective-permute-start.4
  38.6 0.1 collective-permute-done.1.refs_3_.refs_6_
  38.7 0.4 collective-permute-start.2
  39.1 0.0 collective-permute-done.refs_2_.refs_5_
  39.1 0.8 copy-done.5
  39.9 0.0 collective-permute-done.6.refs_8_.refs_11_
  39.9 0.8 copy-done.8
  40.8 0.0 collective-permute-done.4.refs_6_.refs_9_
  40.8 0.9 copy-done.11
  41.6 0.0 collective-permute-done.2.refs_4_.refs_7_
  41.7 0.8 copy-done.14
  42.5 6.3 %all-to-all-done.refs_0_ = bf16[4,400,512]{2,1,0:T(8,128)(2,1)} async-done(((bf16[4,400,512]{2,1,0:T(8,128)(2,1)}), bf16[4,400,512]{2,1,0:T(8,128)(2,1)}, u32[]{:S(2)}, u32[]{:S(2)}) %all-to-all-start) | async-done | bytes 1638432 | tf_op jit(solution)/shard_map/all_to_all | solution.py:359
  48.8 1.1 copy-done.6
  49.8 1.1 copy-done.9
  50.9 1.1 copy-done.12
  51.9 1.1 copy-done.15
  53.0 8.8 %shard_map.163 = (bf16[512,1024]{1,0:T(8,128)(2,1)}, bf16[512,512]{1,0:T(8,128)(2,1)S(1)}, s32[8,512]{1,0:T(8,128)S(1)}, bf16[64,512]{1,0:T(8,128)(2,1)S(1)}) custom-call(bf16[4,400,512]{2,1,0:T(8,128)(2,1)} %all-to-all-done.refs_0_, bf16[1152,256]{1,0:T(8,128)(2,1)S(1)} %copy-done.2, bf16[1152,256]{1,0:T(8,128)(2,1)S(1)} %copy-done.6, ...), custom_call_target="tpu_custom_call" | custom-call | tf_op jit(solution)/shard_map/pallas_call | solution.py:74
  61.8 0.0 copy-start.3
  61.8 0.8 copy-done.3
  62.7 1.5 %collective-permute-start.9 = (bf16[64,512]{1,0:T(8,128)(2,1)S(1)}, bf16[64,512]{1,0:T(8,128)(2,1)S(1)}, u32[]{:S(2)}, u32[]{:S(2)}) collective-permute-start(bf16[64,512]{1,0:T(8,128)(2,1)S(1)} %get-tuple-element.27.refs_0_), channel_id=1, source_target_pairs={{0,3},{1,2},{2,1},{3,0},{4,7},{5,6},{6,5},{7,4},{8,11},{9,10},{10,... | collective-permute-start | bytes 196616 | tf_op jit(solution)/shard_map/ppermute | solution.py:355
  64.1 0.0 collective-permute-start.8
  64.1 2.9 %collective-permute-start.7 = (bf16[64,512]{1,0:T(8,128)(2,1)S(1)}, bf16[64,512]{1,0:T(8,128)(2,1)S(1)}, u32[]{:S(2)}, u32[]{:S(2)}) collective-permute-start(bf16[64,512]{1,0:T(8,128)(2,1)S(1)} %get-tuple-element.27.refs_0_), channel_id=1, source_target_pairs={{0,1},{1,0},{2,3},{3,2},{4,5},{5,4},{6,7},{7,6},{8,9},{9,8},{10,11... | collective-permute-start | bytes 196616 | tf_op jit(solution)/shard_map/ppermute | solution.py:355
  67.1 1.2 copy-done.18
  68.3 0.7 shard_map.164.refs_13_
  69.0 0.0 copy-start
  69.0 1.0 copy-done
  70.0 0.0 copy-start.16
  70.0 0.0 collective-permute-done.9.refs_3_
  70.0 0.3 collective-permute-done.8.refs_2_
  70.4 0.0 collective-permute-done.7.refs_1_
  70.4 0.0 copy-done.1
  70.4 2.8 %shard_map.165 = bf16[4,256,1152]{2,1,0:T(8,128)(2,1)} custom-call(bf16[64,512]{1,0:T(8,128)(2,1)S(1)} %get-tuple-element.27.refs_0_, bf16[64,512]{1,0:T(8,128)(2,1)S(1)} %collective-permute-done.7.refs_1_, bf16[64,512]{1,0:T(8,128)(2,1)S(1)} %collective-permute-done.8.refs_2_, bf16[64,512]{1,0:T(8,128)(2,1)S(1)} %collective-permute-done.9.refs_3_, ...), custom_call_target="tpu_custom_call" | custom-call | tf_op jit(solution)/shard_map/pallas_call | solution.py:74
  73.2 0.0 collective-permute-start.10
  73.2 0.0 copy-done.4
  73.2 0.0 copy-done.7
  73.2 0.0 copy-done.10
  73.2 0.0 copy-done.13
  73.3 6.1 %shard_map.166 = bf16[512,1024]{1,0:T(8,128)(2,1)} custom-call(bf16[64,512]{1,0:T(8,128)(2,1)S(1)} %get-tuple-element.27.refs_0_, bf16[64,512]{1,0:T(8,128)(2,1)S(1)} %collective-permute-done.7.refs_1_, bf16[64,512]{1,0:T(8,128)(2,1)S(1)} %collective-permute-done.8.refs_2_, bf16[64,512]{1,0:T(8,128)(2,1)S(1)} %collective-permute-done.9.refs_3_, ...), custom_call_target="tpu_custom_call" | custom-call | tf_op jit(solution)/shard_map/pallas_call | solution.py:74
  79.4 4.3 %all-to-all-start.1 = ((bf16[4,128,1024]{2,1,0:T(8,128)(2,1)}), bf16[4,128,1024]{2,1,0:T(8,128)(2,1)}, u32[]{:S(2)}, u32[]{:S(2)}) async-start(bf16[4,128,1024]{2,1,0:T(8,128)(2,1)} %bitcast.2), calls=%async_computation.1 | async-start | bytes 2097152 | tf_op jit(solution)/shard_map/all_to_all | solution.py:359
  83.7 0.0 collective-permute-done.10.refs_7_
  83.7 0.0 copy-start.20
  83.7 0.8 copy-done.20
  84.5 3.2 %shard_map.168 = (bf16[256,1152]{1,0:T(8,128)(2,1)S(1)}, bf16[256,1152]{1,0:T(8,128)(2,1)S(1)}, bf16[256,1152]{1,0:T(8,128)(2,1)S(1)}, bf16[256,1152]{1,0:T(8,128)(2,1)S(1)}) custom-call(bf16[64,512]{1,0:T(8,128)(2,1)S(1)} %get-tuple-element.27.refs_0_, bf16[64,512]{1,0:T(8,128)(2,1)S(1)} %copy-done.20, bf16[64,512]{1,0:T(8,128)(2,1)S(1)} %collective-permute-done.8.refs_2_, ...), custom_call_target="tpu_custom_call" | custom-call | tf_op jit(solution)/shard_map/pallas_call | solution.py:74
  87.7 0.8 copy-done.17
  88.5 1.5 %collective-permute-start.11 = (bf16[256,1152]{1,0:T(8,128)(2,1)S(1)}, bf16[256,1152]{1,0:T(8,128)(2,1)}, u32[]{:S(2)}, u32[]{:S(2)}) collective-permute-start(bf16[256,1152]{1,0:T(8,128)(2,1)S(1)} %get-tuple-element.34), channel_id=1, source_target_pairs={{0,8},{4,12},{8,0},{12,4},{16,24},{20,28},{24,16},{28,20},{1,9},{5... | collective-permute-start | bytes 1769480 | tf_op jit(solution)/shard_map/ppermute | solution.py:355
  90.0 1.5 %collective-permute-start.12 = (bf16[256,1152]{1,0:T(8,128)(2,1)S(1)}, bf16[256,1152]{1,0:T(8,128)(2,1)}, u32[]{:S(2)}, u32[]{:S(2)}) collective-permute-start(bf16[256,1152]{1,0:T(8,128)(2,1)S(1)} %get-tuple-element.35), channel_id=1, source_target_pairs={{0,16},{4,20},{8,24},{12,28},{16,0},{20,4},{24,8},{28,12},{1,17},{... | collective-permute-start | bytes 1769480 | tf_op jit(solution)/shard_map/ppermute | solution.py:355
  91.5 0.5 collective-permute-start.13
  92.0 18.4 %all-to-all-done.1.refs_0_ = bf16[4,128,1024]{2,1,0:T(8,128)(2,1)} async-done(((bf16[4,128,1024]{2,1,0:T(8,128)(2,1)}), bf16[4,128,1024]{2,1,0:T(8,128)(2,1)}, u32[]{:S(2)}, u32[]{:S(2)}) %all-to-all-start.1) | async-done | bytes 1048608 | tf_op jit(solution)/shard_map/all_to_all | solution.py:359
  110.4 2.3 %shard_map.167 = bf16[128,4096]{1,0:T(8,128)(2,1)} custom-call(bf16[4,128,1024]{2,1,0:T(8,128)(2,1)} %all-to-all-done.1.refs_0_), custom_call_target="tpu_custom_call" | custom-call | tf_op jit(solution)/shard_map/pallas_call | solution.py:74
  112.7 0.0 collective-permute-done.11.refs_1_.refs_5_
  112.7 5.5 %collective-permute-done.12.refs_2_.refs_6_ = bf16[256,1152]{1,0:T(8,128)(2,1)} collective-permute-done((bf16[256,1152]{1,0:T(8,128)(2,1)S(1)}, bf16[256,1152]{1,0:T(8,128)(2,1)}, u32[]{:S(2)}, u32[]{:S(2)}) %collective-permute-start.12) | collective-permute-done | bytes 589856 | tf_op jit(solution)/shard_map/ppermute | solution.py:355
  118.2 0.0 collective-permute-done.13.refs_3_.refs_7_
  118.2 5.7 %shard_map.169 = (f32[1024,256]{1,0:T(8,128)}, f32[1024,256]{1,0:T(8,128)}, f32[1024,256]{1,0:T(8,128)}, f32[64,512]{1,0:T(8,128)}, f32[64,512]{1,0:T(8,128)}, /*index=5*/f32[64,512]{1,0:T(8,128)}) custom-call(bf16[256,1152]{1,0:T(8,128)(2,1)} %copy-done.17, bf16[256,1152]{1,0:T(8,128)(2,1)} %collective-permute-done.11.refs_1_.refs_5_, ...), custom_call_target="tpu_custom_call" | custom-call | tf_op jit(solution)/shard_map/pallas_call | solution.py:457
  (18 shorter events, 0.0 us)
Async XLA Ops:
  3.8 6.5 %copy-start.2 = (bf16[1152,256]{1,0:T(8,128)(2,1)S(1)}, bf16[1152,256]{1,0:T(8,128)(2,1)}, u32[]{:S(2)}) copy-start(bf16[1152,256]{1,0:T(8,128)(2,1)} %get-tuple-element.26.refs_1_.refs_4_) | copy-start | bytes 1769476
  3.8 44.9 %all-to-all-start = ((bf16[4,400,512]{2,1,0:T(8,128)(2,1)}), bf16[4,400,512]{2,1,0:T(8,128)(2,1)}, u32[]{:S(2)}, u32[]{:S(2)}) async-start(bf16[4,400,512]{2,1,0:T(8,128)(2,1)} %get-tuple-element.25), calls=%async_computation | async-start | bytes 3276800 | tf_op jit(solution)/shard_map/all_to_all | solution.py:359
  10.3 17.2 %collective-permute-start.5 = (bf16[1152,256]{1,0:T(8,128)(2,1)S(1)}, bf16[1152,256]{1,0:T(8,128)(2,1)S(1)}, u32[]{:S(2)}, u32[]{:S(2)}) collective-permute-start(bf16[1152,256]{1,0:T(8,128)(2,1)S(1)} %copy-done.2), channel_id=1, source_target_pairs={{0,24},{4,28},{8,16},{12,20},{16,8},{20,12},{24,0},{28,4},{1,25},{... | collective-permute-start | bytes 1769480 | tf_op jit(solution)/shard_map/ppermute | solution.py:355
  12.7 25.9 %collective-permute-start.3 = (bf16[1152,256]{1,0:T(8,128)(2,1)S(1)}, bf16[1152,256]{1,0:T(8,128)(2,1)S(1)}, u32[]{:S(2)}, u32[]{:S(2)}) collective-permute-start(bf16[1152,256]{1,0:T(8,128)(2,1)S(1)} %copy-done.2), channel_id=1, source_target_pairs={{0,16},{4,20},{8,24},{12,28},{16,0},{20,4},{24,8},{28,12},{1,17},{... | collective-permute-start | bytes 1769480 | tf_op jit(solution)/shard_map/ppermute | solution.py:355
  13.2 25.5 %collective-permute-start.1 = (bf16[1152,256]{1,0:T(8,128)(2,1)S(1)}, bf16[1152,256]{1,0:T(8,128)(2,1)S(1)}, u32[]{:S(2)}, u32[]{:S(2)}) collective-permute-start(bf16[1152,256]{1,0:T(8,128)(2,1)S(1)} %copy-done.2), channel_id=1, source_target_pairs={{0,8},{4,12},{8,0},{12,4},{16,24},{20,28},{24,16},{28,20},{1,9},{5... | collective-permute-start | bytes 1769480 | tf_op jit(solution)/shard_map/ppermute | solution.py:355
  13.8 25.4 %collective-permute-start = (bf16[1152,256]{1,0:T(8,128)(2,1)S(1)}, bf16[1152,256]{1,0:T(8,128)(2,1)S(1)}, u32[]{:S(2)}, u32[]{:S(2)}) collective-permute-start(bf16[1152,256]{1,0:T(8,128)(2,1)S(1)} %copy-done.2), channel_id=1, source_target_pairs={{0,4},{4,0},{8,12},{12,8},{16,20},{20,16},{24,28},{28,24},{1,5},{5... | collective-permute-start | bytes 1769480 | tf_op jit(solution)/shard_map/ppermute | solution.py:355
  27.5 12.5 %collective-permute-start.6 = (bf16[1152,256]{1,0:T(8,128)(2,1)S(1)}, bf16[1152,256]{1,0:T(8,128)(2,1)S(1)}, u32[]{:S(2)}, u32[]{:S(2)}) collective-permute-start(bf16[1152,256]{1,0:T(8,128)(2,1)S(1)} %collective-permute-done.5.refs_7_.refs_10_), channel_id=1, source_target_pairs={{0,4},{4,0},{8,12},{12,8},{16,20},{20,16},{24,28},{28,24},{1,5},{5... | collective-permute-start | bytes 1769480 | tf_op jit(solution)/shard_map/ppermute | solution.py:355
  38.6 2.2 %collective-permute-start.4 = (bf16[1152,256]{1,0:T(8,128)(2,1)S(1)}, bf16[1152,256]{1,0:T(8,128)(2,1)S(1)}, u32[]{:S(2)}, u32[]{:S(2)}) collective-permute-start(bf16[1152,256]{1,0:T(8,128)(2,1)S(1)} %collective-permute-done.3.refs_5_.refs_8_), channel_id=1, source_target_pairs={{0,4},{4,0},{8,12},{12,8},{16,20},{20,16},{24,28},{28,24},{1,5},{5... | collective-permute-start | bytes 1769480 | tf_op jit(solution)/shard_map/ppermute | solution.py:355
  38.7 2.9 %collective-permute-start.2 = (bf16[1152,256]{1,0:T(8,128)(2,1)S(1)}, bf16[1152,256]{1,0:T(8,128)(2,1)S(1)}, u32[]{:S(2)}, u32[]{:S(2)}) collective-permute-start(bf16[1152,256]{1,0:T(8,128)(2,1)S(1)} %collective-permute-done.1.refs_3_.refs_6_), channel_id=1, source_target_pairs={{0,4},{4,0},{8,12},{12,8},{16,20},{20,16},{24,28},{28,24},{1,5},{5... | collective-permute-start | bytes 1769480 | tf_op jit(solution)/shard_map/ppermute | solution.py:355
  39.1 0.8 copy-start.5
  39.9 0.8 copy-start.8
  40.8 0.9 copy-start.11
  41.6 0.8 copy-start.14
  48.7 1.1 copy-start.6
  49.8 1.1 copy-start.9
  50.9 1.1 copy-start.12
  51.9 1.1 copy-start.15
  61.8 0.8 copy-start.3
  62.7 7.7 %copy-start.1 = (bf16[512,1024]{1,0:T(8,128)(2,1)S(1)}, bf16[512,1024]{1,0:T(8,128)(2,1)}, u32[]{:S(2)}) copy-start(bf16[512,1024]{1,0:T(8,128)(2,1)} %get-tuple-element.30.refs_5_) | copy-start | bytes 3145732
  62.7 7.4 %collective-permute-start.9 = (bf16[64,512]{1,0:T(8,128)(2,1)S(1)}, bf16[64,512]{1,0:T(8,128)(2,1)S(1)}, u32[]{:S(2)}, u32[]{:S(2)}) collective-permute-start(bf16[64,512]{1,0:T(8,128)(2,1)S(1)} %get-tuple-element.27.refs_0_), channel_id=1, source_target_pairs={{0,3},{1,2},{2,1},{3,0},{4,7},{5,6},{6,5},{7,4},{8,11},{9,10},{10,... | collective-permute-start | bytes 196616 | tf_op jit(solution)/shard_map/ppermute | solution.py:355
  64.1 6.2 %collective-permute-start.8 = (bf16[64,512]{1,0:T(8,128)(2,1)S(1)}, bf16[64,512]{1,0:T(8,128)(2,1)S(1)}, u32[]{:S(2)}, u32[]{:S(2)}) collective-permute-start(bf16[64,512]{1,0:T(8,128)(2,1)S(1)} %get-tuple-element.27.refs_0_), channel_id=1, source_target_pairs={{0,2},{1,3},{2,0},{3,1},{4,6},{5,7},{6,4},{7,5},{8,10},{9,11},{10,... | collective-permute-start | bytes 196616 | tf_op jit(solution)/shard_map/ppermute | solution.py:355
  64.1 6.2 %collective-permute-start.7 = (bf16[64,512]{1,0:T(8,128)(2,1)S(1)}, bf16[64,512]{1,0:T(8,128)(2,1)S(1)}, u32[]{:S(2)}, u32[]{:S(2)}) collective-permute-start(bf16[64,512]{1,0:T(8,128)(2,1)S(1)} %get-tuple-element.27.refs_0_), channel_id=1, source_target_pairs={{0,1},{1,0},{2,3},{3,2},{4,5},{5,4},{6,7},{7,6},{8,9},{9,8},{10,11... | collective-permute-start | bytes 196616 | tf_op jit(solution)/shard_map/ppermute | solution.py:355
  67.0 1.2 copy-start.18
  69.0 1.0 copy-start
  70.0 3.2 %copy-start.4 = (bf16[1152,256]{1,0:T(8,128)(2,1)S(1)}, bf16[1152,256]{1,0:T(8,128)(2,1)}, u32[]{:S(2)}) copy-start(bf16[1152,256]{1,0:T(8,128)(2,1)} %copy-done.3) | copy-start | bytes 1769476
  70.0 3.2 %copy-start.7 = (bf16[1152,256]{1,0:T(8,128)(2,1)S(1)}, bf16[1152,256]{1,0:T(8,128)(2,1)}, u32[]{:S(2)}) copy-start(bf16[1152,256]{1,0:T(8,128)(2,1)} %copy-done.5) | copy-start | bytes 1769476
  70.0 3.2 %copy-start.10 = (bf16[1152,256]{1,0:T(8,128)(2,1)S(1)}, bf16[1152,256]{1,0:T(8,128)(2,1)}, u32[]{:S(2)}) copy-start(bf16[1152,256]{1,0:T(8,128)(2,1)} %copy-done.8) | copy-start | bytes 1769476
  70.0 3.2 %copy-start.13 = (bf16[1152,256]{1,0:T(8,128)(2,1)S(1)}, bf16[1152,256]{1,0:T(8,128)(2,1)}, u32[]{:S(2)}) copy-start(bf16[1152,256]{1,0:T(8,128)(2,1)} %copy-done.11) | copy-start | bytes 1769476
  70.0 3.3 %copy-start.16 = (bf16[1152,256]{1,0:T(8,128)(2,1)S(1)}, bf16[1152,256]{1,0:T(8,128)(2,1)}, u32[]{:S(2)}) copy-start(bf16[1152,256]{1,0:T(8,128)(2,1)} %copy-done.14) | copy-start | bytes 1769476
  70.4 9.0 %copy-start.19 = (bf16[64,512]{1,0:T(8,128)(2,1)}, bf16[64,512]{1,0:T(8,128)(2,1)S(1)}, u32[]{:S(2)}) copy-start(bf16[64,512]{1,0:T(8,128)(2,1)S(1)} %collective-permute-done.7.refs_1_) | copy-start | bytes 196612
  73.2 10.4 %collective-permute-start.10 = (bf16[4,256,1152]{2,1,0:T(8,128)(2,1)}, bf16[4,256,1152]{2,1,0:T(8,128)(2,1)}, u32[]{:S(2)}, u32[]{:S(2)}) collective-permute-start(bf16[4,256,1152]{2,1,0:T(8,128)(2,1)} %shard_map.165), channel_id=1, source_target_pairs={{0,4},{4,0},{8,12},{12,8},{16,20},{20,16},{24,28},{28,24},{1,5},{5... | collective-permute-start | bytes 7077896 | tf_op jit(solution)/shard_map/ppermute | solution.py:355
  79.4 31.0 %all-to-all-start.1 = ((bf16[4,128,1024]{2,1,0:T(8,128)(2,1)}), bf16[4,128,1024]{2,1,0:T(8,128)(2,1)}, u32[]{:S(2)}, u32[]{:S(2)}) async-start(bf16[4,128,1024]{2,1,0:T(8,128)(2,1)} %bitcast.2), calls=%async_computation.1 | async-start | bytes 2097152 | tf_op jit(solution)/shard_map/all_to_all | solution.py:359
  83.7 0.8 copy-start.20
  87.7 0.8 copy-start.17
  88.5 24.2 %collective-permute-start.11 = (bf16[256,1152]{1,0:T(8,128)(2,1)S(1)}, bf16[256,1152]{1,0:T(8,128)(2,1)}, u32[]{:S(2)}, u32[]{:S(2)}) collective-permute-start(bf16[256,1152]{1,0:T(8,128)(2,1)S(1)} %get-tuple-element.34), channel_id=1, source_target_pairs={{0,8},{4,12},{8,0},{12,4},{16,24},{20,28},{24,16},{28,20},{1,9},{5... | collective-permute-start | bytes 1769480 | tf_op jit(solution)/shard_map/ppermute | solution.py:355
  90.0 28.2 %collective-permute-start.12 = (bf16[256,1152]{1,0:T(8,128)(2,1)S(1)}, bf16[256,1152]{1,0:T(8,128)(2,1)}, u32[]{:S(2)}, u32[]{:S(2)}) collective-permute-start(bf16[256,1152]{1,0:T(8,128)(2,1)S(1)} %get-tuple-element.35), channel_id=1, source_target_pairs={{0,16},{4,20},{8,24},{12,28},{16,0},{20,4},{24,8},{28,12},{1,17},{... | collective-permute-start | bytes 1769480 | tf_op jit(solution)/shard_map/ppermute | solution.py:355
  91.5 26.7 %collective-permute-start.13 = (bf16[256,1152]{1,0:T(8,128)(2,1)S(1)}, bf16[256,1152]{1,0:T(8,128)(2,1)}, u32[]{:S(2)}, u32[]{:S(2)}) collective-permute-start(bf16[256,1152]{1,0:T(8,128)(2,1)S(1)} %get-tuple-element.36), channel_id=1, source_target_pairs={{0,24},{4,28},{8,16},{12,20},{16,8},{20,12},{24,0},{28,4},{1,25},{... | collective-permute-start | bytes 1769480 | tf_op jit(solution)/shard_map/ppermute | solution.py:355

commit v8 on v7

--- a/solution.py
+++ b/solution.py
@@ -13,8 +13,7 @@
 LANES = 128
 ROW_STEP = 512
 LABEL_ROWS = 16
-ROOMY = 48
-FULL = 62
+FULL = (64 << 20) - (64 << 10)
 
 adapter_scale = 2.0
 learn_rate = 0.02
@@ -26,14 +25,33 @@
 
 f32 = jnp.float32
 bf16 = jnp.bfloat16
-VMEM = pl.BlockSpec(memory_space=pltpu.VMEM)
 HBM = pl.BlockSpec(memory_space=pltpu.HBM)
 DMA = pltpu.SemaphoreType.DMA
 
 def shape(dims, kind=bf16):
     return jax.ShapeDtypeStruct(tuple(dims), kind)
 
-def call(body, outs, ins, kinds, out_kinds, scratch=(), vmem=ROOMY, work=0):
+class Staging:
+    def __init__(self, loads, stores):
+        self.loads, self.stores, self.gone = loads, stores, set()
+
+    def ready(self):
+        for copy in self.loads:
+            copy.wait()
+
+    def store(self, n):
+        self.stores[n].start()
+        self.gone.add(n)
+
+    def finish(self):
+        for n in self.stores:
+            if n not in self.gone:
+                self.store(n)
+        for copy in self.stores.values():
+            copy.wait()
+
+
+def call(body, outs, ins, kinds, out_kinds, scratch=()):
     single = not isinstance(outs, (list, tuple))
     outs = [outs] if single else list(outs)
     staged = [x for x, kind in zip(ins, kinds) if kind == "h"]
@@ -45,9 +63,8 @@
         refs = list(refs)
         given, made = refs[: len(ins)], refs[len(ins) : len(ins) + len(outs)]
         rest = refs[len(ins) + len(outs) :]
-        held, own = rest[:count], rest[count : len(rest) - bool(count)]
-        sems = rest[-1] if count else None
-        loads, stores = [], []
+        held, own, sems = rest[:count], rest[count:-1], rest[-1]
+        loads, stores = [], {}
         for n, kind in enumerate(kinds):
             if kind == "h":
                 at = len(loads)
@@ -56,31 +73,25 @@
         for n, kind in enumerate(out_kinds):
             if kind == "h":
                 at = len(loads) + len(stores)
-                stores.append(pltpu.make_async_copy(held[at], made[n], sems.at[at]))
+                stores[n] = pltpu.make_async_copy(held[at], made[n], sems.at[at])
                 made[n] = held[at]
         for copy in loads:
             copy.start()
-
-        def ready():
-            for copy in loads:
-                copy.wait()
-
-        body(ready, *given, *made, *own)
-        for copy in stores:
-            copy.start()
-        for copy in stores:
-            copy.wait()
+        io = Staging(loads, stores)
+        body(io, *given, *made, *own)
+        io.finish()
 
     result = pl.pallas_call(
         kernel,
         out_shape=outs,
-        in_specs=[VMEM if kind == "v" else HBM for kind in kinds],
-        out_specs=[VMEM if kind == "v" else HBM for kind in out_kinds],
-        scratch_shapes=buffers + list(scratch) + ([DMA((count,))] if count else []),
-        compiler_params=pltpu.CompilerParams(vmem_limit_bytes=vmem << 20),
-        cost_estimate=pl.CostEstimate(flops=work, bytes_accessed=0, transcendentals=0),
+        in_specs=[HBM] * len(ins),
+        out_specs=[HBM] * len(outs),
+        scratch_shapes=buffers + list(scratch) + [DMA((count,))],
+        compiler_params=pltpu.CompilerParams(vmem_limit_bytes=FULL),
+        cost_estimate=pl.CostEstimate(flops=0, bytes_accessed=0, transcendentals=0),
     )(*ins)
     return result[0] if single else result
+
 
 def adam_step(param, moment, second, gradient):
     moment = beta_one * moment + (1.0 - beta_one) * gradient
@@ -102,8 +113,8 @@
     wide = jnp.broadcast_to(row.astype(f32), (lanes, n))
     return jnp.transpose(wide)
 
-def prep_kernel(ready, acts, cot, tenant, advantage, a_param, b_param, packed, low):
-    ready()
+def prep_kernel(io, acts, cot, tenant, advantage, a_param, b_param, packed, low):
+    io.ready()
     rows, keys = cot.shape
     shards, _, unit = packed.shape
     features, columns = a_param.shape
@@ -126,6 +137,7 @@
         first += keys // unit * rows
         packed[j, first:, :rows] = labels
         packed[j, first:, rows:] = jnp.zeros((LABEL_ROWS, unit - rows), bf16)
+    io.store(0)
     low[:features] = (a_param[...] * MODEL_WIDTH ** (-0.5)).astype(bf16)
     own_rows = b_param.shape[0]
     for q in range(keys // columns):
@@ -137,13 +149,6 @@
     line = iota((count * own_rows, rows), 0)
     inner = lax.rem(line, own_rows) + lax.axis_index("fsdp") * own_rows
     return lax.div(line, own_rows) * TEN_DEV + lax.div(inner, ADAPTER_RANK)
-
-
-def base_kernel(ready, scaled, weight, base):
-    rows = scaled.shape[0]
-    step = min(ROW_STEP, rows)
-    for r in range(0, rows, step):
-        base[r : r + step] = dot(scaled[r : r + step], weight[...], 1, 1).astype(bf16)
 
 
 def load_factors(a_blocks, a_all, sems):
@@ -161,7 +166,7 @@
     return copies
 
 
-def open_kernel(owners, own_rows, ready, packed, *refs):
+def open_kernel(owners, own_rows, io, packed, *refs):
     blocks = refs[:owners]
     acts, scaled, label, both, b_all, a_all, b_sems, sems = refs[owners:]
     rows, features = acts.shape
@@ -182,6 +187,7 @@
     for copy in b_copies:
         copy.start()
     copies = load_factors(blocks, a_all, sems)
+    io.ready()
     me = lax.axis_index("dp")
     for j in range(shards):
         at = slice(j * rd, (j + 1) * rd)
@@ -195,6 +201,8 @@
         ids = packed[j, first:, :rd].astype(f32).astype(jnp.int32)
         tid = (ids[0:1] ^ me) * TEN_DEV + ids[1:2]
         label[:, at] = jnp.broadcast_to(tid, (8, rd))
+    for n in range(3):
+        io.store(n)
     step = min(ROW_STEP, rows)
     ids = second_ids(owners, own_rows, step)
     for copy in b_copies:
@@ -238,50 +246,15 @@
 MID = slice(ADAPTER_RANK, 2 * ADAPTER_RANK)
 
 
-def side_kernel(shards, owners, ready, *refs):
-    backs, a_blocks = refs[:shards], refs[shards : shards + owners]
-    label, base, out, a_all, back_wide, sems = refs[shards + owners :]
-    copies = load_factors(a_blocks, a_all, sems)
-    ready()
-    rows, features = out.shape
-    step = min(ROW_STEP, rows)
-    width = a_all.shape[1]
-    for r in range(0, rows, step):
-        at = slice(r, r + step)
-        low = adapter_scale * jnp.transpose(total(backs, BACK, at))
-        low = jnp.concatenate([low] * (LANES // ADAPTER_RANK), axis=1)
-        where = column_of(label[0:1, at]).astype(jnp.int32) - lax.div(
-            iota((step, LANES), 1), ADAPTER_RANK
-        )
-        for q in range(width // LANES):
-            hit = where == q * (LANES // ADAPTER_RANK)
-            back_wide[:, q * LANES : (q + 1) * LANES] = jnp.where(hit, low, 0.0).astype(bf16)
-        if r == 0:
-            for copy in copies:
-                copy.wait()
-        chunk = min(256, features)
-        for c in range(0, features, chunk):
-            side = dot(back_wide[...], a_all[c : c + chunk], 1, 1).astype(bf16)
-            whole = base[at, c : c + chunk].astype(f32) + side.astype(f32)
-            out[at, c : c + chunk] = whole.astype(bf16)
-
 def spread(low, label, k, columns):
     rows = low.shape[1]
     ids = lax.div(iota((columns, rows), 0), ADAPTER_RANK) + k * TEN_DEV
     tall = jnp.concatenate([low] * (columns // ADAPTER_RANK), axis=0)
     return jnp.where(ids == label, tall, 0.0).astype(bf16)
 
-def grads_kernel(shards, owners, parity, own_rows, ready, *refs):
-    boths, (label, acts, scaled) = refs[:shards], refs[shards : shards + 3]
-    refs = refs[shards + 3 :]
-    arrived = refs[0] if parity == 0 else None
-    outs, held = refs[parity == 0 : -1], refs[-1]
-    rows, features = acts.shape
-    keys = scaled.shape[1]
-    columns = outs[0].shape[-2]
+def second_grads(owners, parity, own_rows, boths, label, scaled, held):
+    rows = scaled.shape[0]
     count = owners // 2
-    up = adapter_scale * ADAPTER_RANK ** (-0.5)
-    down = adapter_scale * MODEL_WIDTH ** (-0.5)
     step = min(ROW_STEP, rows)
     second = None
     line = iota((count * own_rows, step), 0)
@@ -297,25 +270,86 @@
             low = held[pl.ds(pl.multiple_of(first, own_rows), own_rows)]
             low = jnp.concatenate([low] * count, axis=0)
         low = jnp.where(ids == label[0:1, at], low, 0.0).astype(bf16)
-        term = up * dot(low, scaled[at])
+        term = dot(low, scaled[at])
         second = term if second is None else second + term
+    return adapter_scale * ADAPTER_RANK ** (-0.5) * second
+
+
+def grads_step(owners, parity, own_rows, boths, label, acts, scaled, held, out, arrived, send):
+    features = acts.shape[1]
+    keys = scaled.shape[1]
+    columns = out.shape[1]
+    down = adapter_scale * MODEL_WIDTH ** (-0.5)
+    second = second_grads(owners, parity, own_rows, boths, label, scaled, held)
     low = total(boths, BACK, slice(None))
-    for n in range(count):
-        out = outs[0].at[n] if parity else outs[n]
-        k = 2 * n + parity
-        grad = down * dot(spread(low, label[0:1], k, columns), acts[...])
-        if parity == 0:
+    for n in range(owners // 2):
+        grad = down * dot(spread(low, label[0:1], 2 * n + parity, columns), acts[...])
+        if arrived is not None:
             grad = grad + arrived[n, :, :features].astype(f32)
-        out[:, :features] = grad.astype(bf16)
+        out[n, :, :features] = grad.astype(bf16)
         for q in range(keys // LANES):
             lines = slice(q * own_rows, (q + 1) * own_rows)
             part = second[n * own_rows : (n + 1) * own_rows, q * LANES : (q + 1) * LANES]
-            if parity == 0:
+            if arrived is not None:
                 part = part + arrived[n, lines, features:].astype(f32)
-            out[lines, features:] = part.astype(bf16)
+            out[n, lines, features:] = part.astype(bf16)
         used = keys // LANES * own_rows
         if used < columns:
-            out[used:, features:] = jnp.zeros((columns - used, LANES), bf16)
+            out[n, used:, features:] = jnp.zeros((columns - used, LANES), bf16)
+        send[n].start()
+
+
+def even_kernel(shards, owners, own_rows, io, *refs):
+    boths, (label, acts, scaled, arrived) = refs[:shards], refs[shards : shards + 4]
+    outs = refs[shards + 4 : shards + 4 + owners // 2]
+    held, made, sems = refs[shards + 4 + owners // 2 :]
+    send = [pltpu.make_async_copy(made.at[n], outs[n], sems.at[n]) for n in range(owners // 2)]
+    io.ready()
+    grads_step(owners, 0, own_rows, boths, label, acts, scaled, held, made, arrived, send)
+    for copy in send:
+        copy.wait()
+
+
+def main_kernel(shards, owners, own_rows, io, *refs):
+    boths, (label, acts, scaled, weight) = refs[:shards], refs[shards : shards + 4]
+    a_blocks = refs[shards + 4 : shards + 4 + owners]
+    odd, out, held, made, part, a_all, back_wide, sems, odd_sems, part_sems = refs[
+        shards + 4 + owners :
+    ]
+    copies = load_factors(a_blocks, a_all, sems)
+    send = [pltpu.make_async_copy(made.at[n], odd.at[n], odd_sems.at[n]) for n in range(owners // 2)]
+    io.ready()
+    grads_step(owners, 1, own_rows, boths, label, acts, scaled, held, made, None, send)
+    rows, features = part.shape
+    step = min(ROW_STEP, rows)
+    width = a_all.shape[1]
+    chunk = min(256, features)
+    for r in range(0, rows, step):
+        at = slice(r, r + step)
+        low = adapter_scale * jnp.transpose(total(boths, BACK, at))
+        low = jnp.concatenate([low] * (LANES // ADAPTER_RANK), axis=1)
+        where = column_of(label[0:1, at]).astype(jnp.int32) - lax.div(
+            iota((step, LANES), 1), ADAPTER_RANK
+        )
+        for q in range(width // LANES):
+            hit = where == q * (LANES // ADAPTER_RANK)
+            back_wide[:, q * LANES : (q + 1) * LANES] = jnp.where(hit, low, 0.0).astype(bf16)
+        if r == 0:
+            for copy in copies:
+                copy.wait()
+        for c in range(0, features, chunk):
+            base = dot(scaled[at], weight[c : c + chunk], 1, 1).astype(bf16)
+            side = dot(back_wide[...], a_all[c : c + chunk], 1, 1).astype(bf16)
+            part[at, c : c + chunk] = (base.astype(f32) + side.astype(f32)).astype(bf16)
+            copy = pltpu.make_async_copy(
+                part.at[pl.ds(r, step), pl.ds(c, chunk)],
+                out.at[pl.ds(r, step), pl.ds(c, chunk)],
+                part_sems.at[r // step, c // chunk],
+            )
+            copy.start()
+            send.append(copy)
+    for copy in send:
+        copy.wait()
 
 
 def adam_kernel(count, own_rows, *refs):
@@ -343,8 +377,8 @@
                 out[:, at] = value
 
 
-def lay_kernel(ready, blocks, out):
-    ready()
+def lay_kernel(io, blocks, out):
+    io.ready()
     shards, _, width = blocks.shape
     for j in range(shards):
         out[:, j * width : (j + 1) * width] = blocks[j]
@@ -390,7 +424,6 @@
         (acts, cotangent, tenant[None], advantage[None], a_param, b_param),
         "h" * 6,
         "hh",
-        vmem=FULL,
     )
     packed = exchange(packed, "fsdp")
     chips = [low] + [swap(low, "dp", k) for k in range(2, owners, 2)]
@@ -409,8 +442,8 @@
             shape((2 * ADAPTER_RANK, rows)),
         ],
         (packed, *blocks),
-        "v" + "r" * owners,
-        "vvvv",
+        "h" + "r" * owners,
+        "hhhh",
         [
             pltpu.VMEM((owners * own_rows, keys), bf16),
             factors,
@@ -419,37 +452,40 @@
         ],
     )
     boths = [both] + [swap(both, "fsdp", j) for j in range(1, shards)]
-    base = call(base_kernel, shape((rows, features)), (scaled, base_weight), "vv", "v")
-
-    def grads(parity, outs, *more):
-        return call(
-            functools.partial(grads_kernel, shards, owners, parity, own_rows),
-            outs,
-            (*boths, label, acts_part, scaled, *more),
-            "v" * (shards + 3 + len(more)),
-            "v" * (1 if parity else owners // 2),
-            [pltpu.VMEM((ADAPTER_RANK, step), f32)],
-        )
-
-    odd = grads(1, shape((owners // 2, columns, features + LANES)))
-    base, odd = lax.optimization_barrier((base, odd))
-    grad_part = call(
-        functools.partial(side_kernel, shards, owners),
-        shape((rows, features)),
-        (*boths, *blocks, label, base),
-        "v" * shards + "r" * owners + "vv",
-        "v",
-        [factors, pltpu.VMEM((step, owners * columns), bf16), DMA((owners,))],
+
+    grads = shape((owners // 2, columns, features + LANES))
+    held = [pltpu.VMEM((ADAPTER_RANK, step), f32), pltpu.VMEM(grads.shape, bf16)]
+    odd, grad_part = call(
+        functools.partial(main_kernel, shards, owners, own_rows),
+        [grads, shape((rows, features))],
+        (*boths, label, acts_part, scaled, base_weight, *blocks),
+        "h" * (shards + 4) + "r" * owners,
+        "rr",
+        held
+        + [
+            pltpu.VMEM((rows, features), bf16),
+            factors,
+            pltpu.VMEM((step, owners * columns), bf16),
+            DMA((owners,)),
+            DMA((owners // 2,)),
+            DMA((rows // step, features // min(256, features))),
+        ],
     )
     returned = exchange(grad_part.reshape(shards, row_count, features), "fsdp")
     grad_input = call(
-        lay_kernel, shape((row_count, shards * features)), (returned,), "h", "h", vmem=FULL
-    )
-
-    even = grads(0, [shape((columns, features + LANES))] * (owners // 2), swap(odd, "dp", 1))
+        lay_kernel, shape((row_count, shards * features)), (returned,), "h", "h"
+    )
+    even = call(
+        functools.partial(even_kernel, shards, owners, own_rows),
+        [shape((columns, features + LANES))] * (owners // 2),
+        (*boths, label, acts_part, scaled, swap(odd, "dp", 1)),
+        "h" * (shards + 4),
+        "r" * (owners // 2),
+        held + [DMA((owners // 2,))],
+    )
     sums = [even[0]] + [swap(even[n], "dp", 2 * n) for n in range(1, owners // 2)]
 
-    block = min(256, features)
+    block = LANES
     wide = pl.BlockSpec((columns, block), lambda i: (0, i))
     end = pl.BlockSpec((columns, LANES), lambda i: (0, features // LANES))
     tall = pl.BlockSpec((block, columns), lambda i: (i, 0))
@@ -460,7 +496,7 @@
         out_shape=[shape(a_param.shape, f32)] * 3 + [shape(b_param.shape, f32)] * 3,
         in_specs=[wide] * (owners // 2) + [end] * (owners // 2) + [tall] * 3 + [flat] * 3,
         out_specs=[tall] * 3 + [flat] * 3,
-        compiler_params=pltpu.CompilerParams(vmem_limit_bytes=FULL << 20),
+        compiler_params=pltpu.CompilerParams(vmem_limit_bytes=FULL),
     )(*sums, *sums, a_param, a_moment, a_second, b_param, b_moment, b_second)
     return (grad_input, *new)
 

time: 125 us -> 123 us (0.984)
  local copies, waits for them, and re-layouts: 12.3 us -> 1.12 us
  waiting for transfers between devices: 55.5 us -> 61.4 us
  Pallas kernels: 32.8 us -> 36.9 us
    unnamed x42 -> x14, local copies, waits for them, and re-layouts: 12.3 us -> 1.12 us
    ppermute x14, waiting for transfers between devices: 30.8 us -> 36.5 us  [swap(): return lax.ppermute(block, axis, [(i, i ^ bits) for i in range(size)])]
    pallas_call x1, Pallas kernels: 5.69 us -> 7.77 us  [per_device(): pl.pallas_call(functools.partial(adam_kernel, owners // 2, own_rows), gri...]
    pallas_call x7 -> x5, Pallas kernels: 27.1 us -> 29.1 us  [call(): pl.pallas_call(kernel, out_shape=outs, in_specs=[HBM] * len(ins), out_spe...]
  transfers between devices with their start and end apart: 16 -> 16, of which waited for: 7 -> 11; matrix products, arithmetic and copies ran while one was open for 0% -> 0% of each run, Pallas kernels for 10% -> 6%
where the time goes in v8:
time: 123 us
  waiting for transfers between devices  61.4 us (50%)
  Pallas kernels  36.9 us (30%)
  starting transfers between devices  22.7 us (18%)
    ppermute x14, waiting for transfers between devices, swap(): return lax.ppermute(block, axis, [(i, i ^ bits) for i in range(size)])  36.5 us
    pallas_call x5, Pallas kernels, call(): pl.pallas_call(kernel, out_shape=outs, in_specs=[HBM] * len(ins), out_spe...  29.1 us
    all_to_all x2, waiting for transfers between devices, exchange(): lax.all_to_all(blocks, axis, split_axis=0, concat_axis=0, tiled=True, axi...  24.9 us
    ppermute x14, starting transfers between devices, swap(): return lax.ppermute(block, axis, [(i, i ^ bits) for i in range(size)])  12 us
    all_to_all x2, starting transfers between devices, exchange(): lax.all_to_all(blocks, axis, split_axis=0, concat_axis=0, tiled=True, axi...  10.7 us
    pallas_call x1, Pallas kernels, per_device(): pl.pallas_call(functools.partial(adam_kernel, owners // 2, own_rows), gri...  7.77 us
  transfers between devices with their start and end apart: 16, of which 11 were waited for; matrix products, arithmetic and copies ran while one was open for 0% of the time, Pallas kernels for 6%

profile of v8, /device:TPU:0, one launch (start us, length us, event | category | flops | bytes accessed | tf_op | source)
XLA Modules:
  0.0 122.8 jit_solution(7208378505977977091)
XLA Ops:
  0.6 3.2 %shard_map.162 = (bf16[4,400,512]{2,1,0:T(8,128)(2,1)}, bf16[1152,256]{1,0:T(8,128)(2,1)}) custom-call(bf16[128,4096]{1,0:T(8,128)(2,1)} %refs_0_.1, bf16[128,512]{1,0:T(8,128)(2,1)} %refs_1_.1, s32[1,128]{1,0:T(1,128)} %bitcast.4, s32[1,128]{1,0:T(1,128)} %bitcast.5, f32[1024,256]{1,0:T(8,128)} %refs_8_.1, f32[64,512]{1,0:T(8,128)} %refs_11_.1), custom_call_target="tpu_custom_call" | custom-call | tf_op jit(solution)/shard_map/pallas_call | solution.py:84
  3.8 0.0 copy-start
  3.8 6.5 %all-to-all-start = ((bf16[4,400,512]{2,1,0:T(8,128)(2,1)}), bf16[4,400,512]{2,1,0:T(8,128)(2,1)}, u32[]{:S(2)}, u32[]{:S(2)}) async-start(bf16[4,400,512]{2,1,0:T(8,128)(2,1)} %get-tuple-element.25), calls=%async_computation | async-start | bytes 3276800 | tf_op jit(solution)/shard_map/all_to_all | solution.py:393
  10.3 0.0 copy-done
  10.3 2.4 %collective-permute-start.5 = (bf16[1152,256]{1,0:T(8,128)(2,1)S(1)}, bf16[1152,256]{1,0:T(8,128)(2,1)S(1)}, u32[]{:S(2)}, u32[]{:S(2)}) collective-permute-start(bf16[1152,256]{1,0:T(8,128)(2,1)S(1)} %copy-done), channel_id=1, source_target_pairs={{0,24},{4,28},{8,16},{12,20},{16,8},{20,12},{24,0},{28,4},{1,25},{... | collective-permute-start | bytes 1769480 | tf_op jit(solution)/shard_map/ppermute | solution.py:389
  12.7 0.5 collective-permute-start.3
  13.2 0.5 collective-permute-start.1
  13.8 0.0 collective-permute-start
  13.8 13.7 %collective-permute-done.5.refs_7_.refs_14_ = bf16[1152,256]{1,0:T(8,128)(2,1)S(1)} collective-permute-done((bf16[1152,256]{1,0:T(8,128)(2,1)S(1)}, bf16[1152,256]{1,0:T(8,128)(2,1)S(1)}, u32[]{:S(2)}, u32[]{:S(2)}) %collective-permute-start.5) | collective-permute-done | bytes 589856 | tf_op jit(solution)/shard_map/ppermute | solution.py:389
  27.5 0.0 copy-start.1
  27.5 0.0 collective-permute-start.6
  27.5 11.1 %collective-permute-done.3.refs_5_.refs_12_ = bf16[1152,256]{1,0:T(8,128)(2,1)S(1)} collective-permute-done((bf16[1152,256]{1,0:T(8,128)(2,1)S(1)}, bf16[1152,256]{1,0:T(8,128)(2,1)S(1)}, u32[]{:S(2)}, u32[]{:S(2)}) %collective-permute-start.3) | collective-permute-done | bytes 589856 | tf_op jit(solution)/shard_map/ppermute | solution.py:389
  38.6 0.0 copy-start.2
  38.6 0.0 collective-permute-start.4
  38.6 0.1 collective-permute-done.1.refs_3_.refs_10_
  38.7 0.0 copy-start.3
  38.7 0.4 collective-permute-start.2
  39.1 0.0 collective-permute-done.refs_2_.refs_9_
  39.1 0.0 copy-done.1
  39.1 0.0 copy-start.4
  39.1 0.0 collective-permute-done.6.refs_8_.refs_15_
  39.1 0.3 copy-done.2
  39.4 0.0 copy-start.5
  39.4 1.2 collective-permute-done.4.refs_6_.refs_13_
  40.6 0.0 copy-done.3
  40.6 0.0 copy-done.4
  40.6 0.0 copy-done.5
  40.6 0.0 copy-start.6
  40.6 0.8 copy-done.6
  41.4 0.1 collective-permute-done.2.refs_4_.refs_11_
  41.6 7.2 %all-to-all-done.refs_0_ = bf16[4,400,512]{2,1,0:T(8,128)(2,1)} async-done(((bf16[4,400,512]{2,1,0:T(8,128)(2,1)}), bf16[4,400,512]{2,1,0:T(8,128)(2,1)}, u32[]{:S(2)}, u32[]{:S(2)}) %all-to-all-start) | async-done | bytes 1638432 | tf_op jit(solution)/shard_map/all_to_all | solution.py:393
  48.7 10.0 %shard_map.163 = (bf16[512,1024]{1,0:T(8,128)(2,1)}, bf16[512,512]{1,0:T(8,128)(2,1)}, s32[8,512]{1,0:T(8,128)}, bf16[64,512]{1,0:T(8,128)(2,1)}) custom-call(bf16[4,400,512]{2,1,0:T(8,128)(2,1)} %all-to-all-done.refs_0_, bf16[1152,256]{1,0:T(8,128)(2,1)} %get-tuple-element.26.refs_1_.refs_8_, bf16[1152,256]{1,0:T(8,128)(2,1)} %copy-done.4, ...), custom_call_target="tpu_custom_call" | custom-call | tf_op jit(solution)/shard_map/pallas_call | solution.py:84
  58.7 1.5 %collective-permute-start.9 = (bf16[64,512]{1,0:T(8,128)(2,1)}, bf16[64,512]{1,0:T(8,128)(2,1)}, u32[]{:S(2)}, u32[]{:S(2)}) collective-permute-start(bf16[64,512]{1,0:T(8,128)(2,1)} %get-tuple-element.27.refs_0_), channel_id=1, source_target_pairs={{0,3},{1,2},{2,1},{3,0},{4,7},{5,6},{6,5},{7,4},{8,11},{9,10},{10,... | collective-permute-start | bytes 196616 | tf_op jit(solution)/shard_map/ppermute | solution.py:389
  60.3 0.0 collective-permute-start.8
  60.3 2.9 %collective-permute-start.7 = (bf16[64,512]{1,0:T(8,128)(2,1)}, bf16[64,512]{1,0:T(8,128)(2,1)}, u32[]{:S(2)}, u32[]{:S(2)}) collective-permute-start(bf16[64,512]{1,0:T(8,128)(2,1)} %get-tuple-element.27.refs_0_), channel_id=1, source_target_pairs={{0,1},{1,0},{2,3},{3,2},{4,5},{5,4},{6,7},{7,6},{8,9},{9,8},{10,11... | collective-permute-start | bytes 196616 | tf_op jit(solution)/shard_map/ppermute | solution.py:389
  63.2 2.3 %collective-permute-done.9.refs_3_ = bf16[64,512]{1,0:T(8,128)(2,1)} collective-permute-done((bf16[64,512]{1,0:T(8,128)(2,1)}, bf16[64,512]{1,0:T(8,128)(2,1)}, u32[]{:S(2)}, u32[]{:S(2)}) %collective-permute-start.9) | collective-permute-done | bytes 65568 | tf_op jit(solution)/shard_map/ppermute | solution.py:389
  65.5 1.3 %collective-permute-done.8.refs_2_ = bf16[64,512]{1,0:T(8,128)(2,1)} collective-permute-done((bf16[64,512]{1,0:T(8,128)(2,1)}, bf16[64,512]{1,0:T(8,128)(2,1)}, u32[]{:S(2)}, u32[]{:S(2)}) %collective-permute-start.8) | collective-permute-done | bytes 65568 | tf_op jit(solution)/shard_map/ppermute | solution.py:389
  66.8 0.0 collective-permute-done.7.refs_1_
  66.8 8.8 %shard_map.164 = (bf16[4,256,1152]{2,1,0:T(8,128)(2,1)}, bf16[512,1024]{1,0:T(8,128)(2,1)}) custom-call(bf16[64,512]{1,0:T(8,128)(2,1)} %get-tuple-element.27.refs_0_, bf16[64,512]{1,0:T(8,128)(2,1)} %collective-permute-done.7.refs_1_, bf16[64,512]{1,0:T(8,128)(2,1)} %collective-permute-done.8.refs_2_, bf16[64,512]{1,0:T(8,128)(2,1)} %collective-permute-done.9.refs_3_, ...), custom_call_target="tpu_custom_call" | custom-call | tf_op jit(solution)/shard_map/pallas_call | solution.py:84
  75.7 0.1 collective-permute-start.10
  75.8 4.3 %all-to-all-start.1 = ((bf16[4,128,1024]{2,1,0:T(8,128)(2,1)}), bf16[4,128,1024]{2,1,0:T(8,128)(2,1)}, u32[]{:S(2)}, u32[]{:S(2)}) async-start(bf16[4,128,1024]{2,1,0:T(8,128)(2,1)} %bitcast.3), calls=%async_computation.1 | async-start | bytes 2097152 | tf_op jit(solution)/shard_map/all_to_all | solution.py:393
  80.0 0.6 collective-permute-done.10.refs_7_
  80.6 4.8 %shard_map.166 = (bf16[256,1152]{1,0:T(8,128)(2,1)}, bf16[256,1152]{1,0:T(8,128)(2,1)}, bf16[256,1152]{1,0:T(8,128)(2,1)}, bf16[256,1152]{1,0:T(8,128)(2,1)}) custom-call(bf16[64,512]{1,0:T(8,128)(2,1)} %get-tuple-element.27.refs_0_, bf16[64,512]{1,0:T(8,128)(2,1)} %collective-permute-done.7.refs_1_, bf16[64,512]{1,0:T(8,128)(2,1)} %collective-permute-done.8.refs_2_, ...), custom_call_target="tpu_custom_call" | custom-call | tf_op jit(solution)/shard_map/pallas_call | solution.py:84
  85.5 1.6 %collective-permute-start.11 = (bf16[256,1152]{1,0:T(8,128)(2,1)}, bf16[256,1152]{1,0:T(8,128)(2,1)}, u32[]{:S(2)}, u32[]{:S(2)}) collective-permute-start(bf16[256,1152]{1,0:T(8,128)(2,1)} %get-tuple-element.34), channel_id=1, source_target_pairs={{0,8},{4,12},{8,0},{12,4},{16,24},{20,28},{24,16},{28,20},{1,9},{5... | collective-permute-start | bytes 1769480 | tf_op jit(solution)/shard_map/ppermute | solution.py:389
  87.0 1.5 %collective-permute-start.12 = (bf16[256,1152]{1,0:T(8,128)(2,1)}, bf16[256,1152]{1,0:T(8,128)(2,1)}, u32[]{:S(2)}, u32[]{:S(2)}) collective-permute-start(bf16[256,1152]{1,0:T(8,128)(2,1)} %get-tuple-element.35), channel_id=1, source_target_pairs={{0,16},{4,20},{8,24},{12,28},{16,0},{20,4},{24,8},{28,12},{1,17},{... | collective-permute-start | bytes 1769480 | tf_op jit(solution)/shard_map/ppermute | solution.py:389
  88.5 0.5 collective-permute-start.13
  89.0 17.7 %all-to-all-done.1.refs_0_ = bf16[4,128,1024]{2,1,0:T(8,128)(2,1)} async-done(((bf16[4,128,1024]{2,1,0:T(8,128)(2,1)}), bf16[4,128,1024]{2,1,0:T(8,128)(2,1)}, u32[]{:S(2)}, u32[]{:S(2)}) %all-to-all-start.1) | async-done | bytes 1048608 | tf_op jit(solution)/shard_map/all_to_all | solution.py:393
  106.8 2.3 %shard_map.165 = bf16[128,4096]{1,0:T(8,128)(2,1)} custom-call(bf16[4,128,1024]{2,1,0:T(8,128)(2,1)} %all-to-all-done.1.refs_0_), custom_call_target="tpu_custom_call" | custom-call | tf_op jit(solution)/shard_map/pallas_call | solution.py:84
  109.0 0.0 collective-permute-done.11.refs_1_.refs_5_
  109.1 6.0 %collective-permute-done.12.refs_2_.refs_6_ = bf16[256,1152]{1,0:T(8,128)(2,1)} collective-permute-done((bf16[256,1152]{1,0:T(8,128)(2,1)}, bf16[256,1152]{1,0:T(8,128)(2,1)}, u32[]{:S(2)}, u32[]{:S(2)}) %collective-permute-start.12) | collective-permute-done | bytes 589856 | tf_op jit(solution)/shard_map/ppermute | solution.py:389
  115.1 0.0 collective-permute-done.13.refs_3_.refs_7_
  115.1 7.8 %shard_map.167 = (f32[1024,256]{1,0:T(8,128)}, f32[1024,256]{1,0:T(8,128)}, f32[1024,256]{1,0:T(8,128)}, f32[64,512]{1,0:T(8,128)}, f32[64,512]{1,0:T(8,128)}, /*index=5*/f32[64,512]{1,0:T(8,128)}) custom-call(bf16[256,1152]{1,0:T(8,128)(2,1)} %get-tuple-element.33.refs_0_.refs_4_, bf16[256,1152]{1,0:T(8,128)(2,1)} %collective-permute-done.11.refs_1_.refs_5_, ...), custom_call_target="tpu_custom_call" | custom-call | tf_op jit(solution)/shard_map/pallas_call | solution.py:493
Async XLA Ops:
  3.8 6.5 %copy-start = (bf16[1152,256]{1,0:T(8,128)(2,1)S(1)}, bf16[1152,256]{1,0:T(8,128)(2,1)}, u32[]{:S(2)}) copy-start(bf16[1152,256]{1,0:T(8,128)(2,1)} %get-tuple-element.26.refs_1_.refs_8_) | copy-start | bytes 1769476
  3.8 44.9 %all-to-all-start = ((bf16[4,400,512]{2,1,0:T(8,128)(2,1)}), bf16[4,400,512]{2,1,0:T(8,128)(2,1)}, u32[]{:S(2)}, u32[]{:S(2)}) async-start(bf16[4,400,512]{2,1,0:T(8,128)(2,1)} %get-tuple-element.25), calls=%async_computation | async-start | bytes 3276800 | tf_op jit(solution)/shard_map/all_to_all | solution.py:393
  10.3 17.2 %collective-permute-start.5 = (bf16[1152,256]{1,0:T(8,128)(2,1)S(1)}, bf16[1152,256]{1,0:T(8,128)(2,1)S(1)}, u32[]{:S(2)}, u32[]{:S(2)}) collective-permute-start(bf16[1152,256]{1,0:T(8,128)(2,1)S(1)} %copy-done), channel_id=1, source_target_pairs={{0,24},{4,28},{8,16},{12,20},{16,8},{20,12},{24,0},{28,4},{1,25},{... | collective-permute-start | bytes 1769480 | tf_op jit(solution)/shard_map/ppermute | solution.py:389
  12.7 25.9 %collective-permute-start.3 = (bf16[1152,256]{1,0:T(8,128)(2,1)S(1)}, bf16[1152,256]{1,0:T(8,128)(2,1)S(1)}, u32[]{:S(2)}, u32[]{:S(2)}) collective-permute-start(bf16[1152,256]{1,0:T(8,128)(2,1)S(1)} %copy-done), channel_id=1, source_target_pairs={{0,16},{4,20},{8,24},{12,28},{16,0},{20,4},{24,8},{28,12},{1,17},{... | collective-permute-start | bytes 1769480 | tf_op jit(solution)/shard_map/ppermute | solution.py:389
  13.2 25.5 %collective-permute-start.1 = (bf16[1152,256]{1,0:T(8,128)(2,1)S(1)}, bf16[1152,256]{1,0:T(8,128)(2,1)S(1)}, u32[]{:S(2)}, u32[]{:S(2)}) collective-permute-start(bf16[1152,256]{1,0:T(8,128)(2,1)S(1)} %copy-done), channel_id=1, source_target_pairs={{0,8},{4,12},{8,0},{12,4},{16,24},{20,28},{24,16},{28,20},{1,9},{5... | collective-permute-start | bytes 1769480 | tf_op jit(solution)/shard_map/ppermute | solution.py:389
  13.8 25.4 %collective-permute-start = (bf16[1152,256]{1,0:T(8,128)(2,1)S(1)}, bf16[1152,256]{1,0:T(8,128)(2,1)S(1)}, u32[]{:S(2)}, u32[]{:S(2)}) collective-permute-start(bf16[1152,256]{1,0:T(8,128)(2,1)S(1)} %copy-done), channel_id=1, source_target_pairs={{0,4},{4,0},{8,12},{12,8},{16,20},{20,16},{24,28},{28,24},{1,5},{5... | collective-permute-start | bytes 1769480 | tf_op jit(solution)/shard_map/ppermute | solution.py:389
  27.5 11.7 %copy-start.1 = (bf16[1152,256]{1,0:T(8,128)(2,1)}, bf16[1152,256]{1,0:T(8,128)(2,1)S(1)}, u32[]{:S(2)}) copy-start(bf16[1152,256]{1,0:T(8,128)(2,1)S(1)} %collective-permute-done.5.refs_7_.refs_14_) | copy-start | bytes 1769476
  27.5 11.7 %collective-permute-start.6 = (bf16[1152,256]{1,0:T(8,128)(2,1)S(1)}, bf16[1152,256]{1,0:T(8,128)(2,1)S(1)}, u32[]{:S(2)}, u32[]{:S(2)}) collective-permute-start(bf16[1152,256]{1,0:T(8,128)(2,1)S(1)} %collective-permute-done.5.refs_7_.refs_14_), channel_id=1, source_target_pairs={{0,4},{4,0},{8,12},{12,8},{16,20},{20,16},{24,28},{28,24},{1,5},{5... | collective-permute-start | bytes 1769480 | tf_op jit(solution)/shard_map/ppermute | solution.py:389
  38.6 0.8 copy-start.2
  38.6 2.0 %collective-permute-start.4 = (bf16[1152,256]{1,0:T(8,128)(2,1)S(1)}, bf16[1152,256]{1,0:T(8,128)(2,1)S(1)}, u32[]{:S(2)}, u32[]{:S(2)}) collective-permute-start(bf16[1152,256]{1,0:T(8,128)(2,1)S(1)} %collective-permute-done.3.refs_5_.refs_12_), channel_id=1, source_target_pairs={{0,4},{4,0},{8,12},{12,8},{16,20},{20,16},{24,28},{28,24},{1,5},{5... | collective-permute-start | bytes 1769480 | tf_op jit(solution)/shard_map/ppermute | solution.py:389
  38.7 1.9 %copy-start.3 = (bf16[1152,256]{1,0:T(8,128)(2,1)}, bf16[1152,256]{1,0:T(8,128)(2,1)S(1)}, u32[]{:S(2)}) copy-start(bf16[1152,256]{1,0:T(8,128)(2,1)S(1)} %collective-permute-done.1.refs_3_.refs_10_) | copy-start | bytes 1769476
  38.7 2.9 %collective-permute-start.2 = (bf16[1152,256]{1,0:T(8,128)(2,1)S(1)}, bf16[1152,256]{1,0:T(8,128)(2,1)}, u32[]{:S(2)}, u32[]{:S(2)}) collective-permute-start(bf16[1152,256]{1,0:T(8,128)(2,1)S(1)} %collective-permute-done.1.refs_3_.refs_10_), channel_id=1, source_target_pairs={{0,4},{4,0},{8,12},{12,8},{16,20},{20,16},{24,28},{28,24},{1,5},{5... | collective-permute-start | bytes 1769480 | tf_op jit(solution)/shard_map/ppermute | solution.py:389
  39.1 1.5 %copy-start.4 = (bf16[1152,256]{1,0:T(8,128)(2,1)}, bf16[1152,256]{1,0:T(8,128)(2,1)S(1)}, u32[]{:S(2)}) copy-start(bf16[1152,256]{1,0:T(8,128)(2,1)S(1)} %collective-permute-done.refs_2_.refs_9_) | copy-start | bytes 1769476
  39.4 1.2 copy-start.5
  40.6 0.8 copy-start.6
  58.7 6.8 %collective-permute-start.9 = (bf16[64,512]{1,0:T(8,128)(2,1)}, bf16[64,512]{1,0:T(8,128)(2,1)}, u32[]{:S(2)}, u32[]{:S(2)}) collective-permute-start(bf16[64,512]{1,0:T(8,128)(2,1)} %get-tuple-element.27.refs_0_), channel_id=1, source_target_pairs={{0,3},{1,2},{2,1},{3,0},{4,7},{5,6},{6,5},{7,4},{8,11},{9,10},{10,... | collective-permute-start | bytes 196616 | tf_op jit(solution)/shard_map/ppermute | solution.py:389
  60.3 6.6 %collective-permute-start.8 = (bf16[64,512]{1,0:T(8,128)(2,1)}, bf16[64,512]{1,0:T(8,128)(2,1)}, u32[]{:S(2)}, u32[]{:S(2)}) collective-permute-start(bf16[64,512]{1,0:T(8,128)(2,1)} %get-tuple-element.27.refs_0_), channel_id=1, source_target_pairs={{0,2},{1,3},{2,0},{3,1},{4,6},{5,7},{6,4},{7,5},{8,10},{9,11},{10,... | collective-permute-start | bytes 196616 | tf_op jit(solution)/shard_map/ppermute | solution.py:389
  60.3 6.6 %collective-permute-start.7 = (bf16[64,512]{1,0:T(8,128)(2,1)}, bf16[64,512]{1,0:T(8,128)(2,1)}, u32[]{:S(2)}, u32[]{:S(2)}) collective-permute-start(bf16[64,512]{1,0:T(8,128)(2,1)} %get-tuple-element.27.refs_0_), channel_id=1, source_target_pairs={{0,1},{1,0},{2,3},{3,2},{4,5},{5,4},{6,7},{7,6},{8,9},{9,8},{10,11... | collective-permute-start | bytes 196616 | tf_op jit(solution)/shard_map/ppermute | solution.py:389
  75.7 4.9 %collective-permute-start.10 = (bf16[4,256,1152]{2,1,0:T(8,128)(2,1)}, bf16[4,256,1152]{2,1,0:T(8,128)(2,1)}, u32[]{:S(2)}, u32[]{:S(2)}) collective-permute-start(bf16[4,256,1152]{2,1,0:T(8,128)(2,1)} %get-tuple-element.32), channel_id=1, source_target_pairs={{0,4},{4,0},{8,12},{12,8},{16,20},{20,16},{24,28},{28,24},{1,5},{5... | collective-permute-start | bytes 7077896 | tf_op jit(solution)/shard_map/ppermute | solution.py:389
  75.8 31.0 %all-to-all-start.1 = ((bf16[4,128,1024]{2,1,0:T(8,128)(2,1)}), bf16[4,128,1024]{2,1,0:T(8,128)(2,1)}, u32[]{:S(2)}, u32[]{:S(2)}) async-start(bf16[4,128,1024]{2,1,0:T(8,128)(2,1)} %bitcast.3), calls=%async_computation.1 | async-start | bytes 2097152 | tf_op jit(solution)/shard_map/all_to_all | solution.py:393
  85.5 23.6 %collective-permute-start.11 = (bf16[256,1152]{1,0:T(8,128)(2,1)}, bf16[256,1152]{1,0:T(8,128)(2,1)}, u32[]{:S(2)}, u32[]{:S(2)}) collective-permute-start(bf16[256,1152]{1,0:T(8,128)(2,1)} %get-tuple-element.34), channel_id=1, source_target_pairs={{0,8},{4,12},{8,0},{12,4},{16,24},{20,28},{24,16},{28,20},{1,9},{5... | collective-permute-start | bytes 1769480 | tf_op jit(solution)/shard_map/ppermute | solution.py:389
  87.0 28.0 %collective-permute-start.12 = (bf16[256,1152]{1,0:T(8,128)(2,1)}, bf16[256,1152]{1,0:T(8,128)(2,1)}, u32[]{:S(2)}, u32[]{:S(2)}) collective-permute-start(bf16[256,1152]{1,0:T(8,128)(2,1)} %get-tuple-element.35), channel_id=1, source_target_pairs={{0,16},{4,20},{8,24},{12,28},{16,0},{20,4},{24,8},{28,12},{1,17},{... | collective-permute-start | bytes 1769480 | tf_op jit(solution)/shard_map/ppermute | solution.py:389
  88.5 26.5 %collective-permute-start.13 = (bf16[256,1152]{1,0:T(8,128)(2,1)}, bf16[256,1152]{1,0:T(8,128)(2,1)}, u32[]{:S(2)}, u32[]{:S(2)}) collective-permute-start(bf16[256,1152]{1,0:T(8,128)(2,1)} %get-tuple-element.36), channel_id=1, source_target_pairs={{0,24},{4,28},{8,16},{12,20},{16,8},{20,12},{24,0},{28,4},{1,25},{... | collective-permute-start | bytes 1769480 | tf_op jit(solution)/shard_map/ppermute | solution.py:389

commit v9 on v8

--- a/solution.py
+++ b/solution.py
@@ -12,6 +12,7 @@
 TEN_DEV = 8
 LANES = 128
 ROW_STEP = 512
+MID_STEP = 256
 LABEL_ROWS = 16
 FULL = (64 << 20) - (64 << 10)
 
@@ -220,6 +221,9 @@
             place = lax.rem(lax.axis_index("fsdp"), ADAPTER_RANK // own_rows)
             low = jnp.where(part == place, low, 0.0)
         both[:ADAPTER_RANK, at] = low.astype(bf16)
+    step = min(MID_STEP, rows)
+    for r in range(0, rows, step):
+        at = slice(r, r + step)
         where = column_of(label[0:1, at]).astype(jnp.int32) - lax.div(
             iota((step, LANES), 1), ADAPTER_RANK
         )
@@ -299,27 +303,28 @@
         send[n].start()
 
 
-def even_kernel(shards, owners, own_rows, io, *refs):
-    boths, (label, acts, scaled, arrived) = refs[:shards], refs[shards : shards + 4]
-    outs = refs[shards + 4 : shards + 4 + owners // 2]
-    held, made, sems = refs[shards + 4 + owners // 2 :]
-    send = [pltpu.make_async_copy(made.at[n], outs[n], sems.at[n]) for n in range(owners // 2)]
+def grads_kernel(shards, owners, own_rows, parity, io, *refs):
+    boths, (label, acts, scaled) = refs[:shards], refs[shards : shards + 3]
+    refs = refs[shards + 3 :]
+    arrived = refs[0] if parity == 0 else None
+    outs, (held, made, sems) = refs[parity == 0 : -3], refs[-3:]
+    send = []
+    for n in range(owners // 2):
+        out = outs[0].at[n] if parity else outs[n]
+        send.append(pltpu.make_async_copy(made.at[n], out, sems.at[n]))
     io.ready()
-    grads_step(owners, 0, own_rows, boths, label, acts, scaled, held, made, arrived, send)
+    grads_step(owners, parity, own_rows, boths, label, acts, scaled, held, made, arrived, send)
     for copy in send:
         copy.wait()
 
 
-def main_kernel(shards, owners, own_rows, io, *refs):
-    boths, (label, acts, scaled, weight) = refs[:shards], refs[shards : shards + 4]
-    a_blocks = refs[shards + 4 : shards + 4 + owners]
-    odd, out, held, made, part, a_all, back_wide, sems, odd_sems, part_sems = refs[
-        shards + 4 + owners :
-    ]
+def side_kernel(shards, owners, io, *refs):
+    boths, (label, scaled, weight) = refs[:shards], refs[shards : shards + 3]
+    a_blocks = refs[shards + 3 : shards + 3 + owners]
+    out, part, a_all, back_wide, sems, part_sems = refs[shards + 3 + owners :]
     copies = load_factors(a_blocks, a_all, sems)
-    send = [pltpu.make_async_copy(made.at[n], odd.at[n], odd_sems.at[n]) for n in range(owners // 2)]
+    send = []
     io.ready()
-    grads_step(owners, 1, own_rows, boths, label, acts, scaled, held, made, None, send)
     rows, features = part.shape
     step = min(ROW_STEP, rows)
     width = a_all.shape[1]
@@ -352,29 +357,40 @@
         copy.wait()
 
 
-def adam_kernel(count, own_rows, *refs):
-    grads, ends, refs = refs[:count], refs[count : 2 * count], refs[2 * count :]
-    firsts, seconds, outs = refs[:3], refs[3:6], refs[6:]
-
-    def summed(parts):
-        value = parts[0][...].astype(f32)
-        for part in parts[1:]:
-            value = value + part[...].astype(f32)
+def adam_kernel(count, own_rows, io, *refs):
+    grads, firsts = refs[:count], refs[count : count + 3]
+    seconds, outs = refs[count + 3 : count + 6], refs[count + 6 : count + 12]
+    made, sems = refs[count + 12 : count + 15], refs[count + 15]
+    features, _ = firsts[0].shape
+    keys = seconds[0].shape[1]
+    io.ready()
+
+    def summed(at):
+        value = grads[0][:, at].astype(f32)
+        for part in grads[1:]:
+            value = value + part[:, at].astype(f32)
         return value
 
-    new = adam_step(*[x[...] for x in firsts], jnp.transpose(summed(grads)))
-    for out, value in zip(outs[:3], new):
-        out[...] = value
-
-    @pl.when(pl.program_id(0) == 0)
-    def _():
-        grad = summed(ends)
-        keys = seconds[0].shape[1]
-        for q in range(keys // LANES):
-            at = slice(q * LANES, (q + 1) * LANES)
-            part = grad[q * own_rows : (q + 1) * own_rows]
-            for out, value in zip(outs[3:], adam_step(*[x[:, at] for x in seconds], part)):
-                out[:, at] = value
+    copies = []
+    block = min(256, features)
+    for n, c in enumerate(range(0, features, block)):
+        at = slice(c, c + block)
+        grad = jnp.transpose(summed(at))
+        for m, value in enumerate(adam_step(*[x[at] for x in firsts], grad)):
+            made[m][at] = value
+            rows = pl.ds(c, block)
+            copies.append(
+                pltpu.make_async_copy(made[m].at[rows], outs[m].at[rows], sems.at[m, n])
+            )
+            copies[-1].start()
+    grad = summed(slice(features, features + LANES))
+    for q in range(keys // LANES):
+        at = slice(q * LANES, (q + 1) * LANES)
+        part = grad[q * own_rows : (q + 1) * own_rows]
+        for out, value in zip(outs[3:], adam_step(*[x[:, at] for x in seconds], part)):
+            out[:, at] = value
+    for copy in copies:
+        copy.wait()
 
 
 def lay_kernel(io, blocks, out):
@@ -454,50 +470,53 @@
     boths = [both] + [swap(both, "fsdp", j) for j in range(1, shards)]
 
     grads = shape((owners // 2, columns, features + LANES))
-    held = [pltpu.VMEM((ADAPTER_RANK, step), f32), pltpu.VMEM(grads.shape, bf16)]
-    odd, grad_part = call(
-        functools.partial(main_kernel, shards, owners, own_rows),
-        [grads, shape((rows, features))],
-        (*boths, label, acts_part, scaled, base_weight, *blocks),
-        "h" * (shards + 4) + "r" * owners,
-        "rr",
-        held
-        + [
+
+    def gradients(parity, outs, *more):
+        return call(
+            functools.partial(grads_kernel, shards, owners, own_rows, parity),
+            outs,
+            (*boths, label, acts_part, scaled, *more),
+            "h" * (shards + 3 + len(more)),
+            "r" * (1 if parity else owners // 2),
+            [
+                pltpu.VMEM((ADAPTER_RANK, step), f32),
+                pltpu.VMEM(grads.shape, bf16),
+                DMA((owners // 2,)),
+            ],
+        )
+
+    odd = gradients(1, grads)
+    odd, *own = lax.optimization_barrier((odd, *boths))
+    grad_part = call(
+        functools.partial(side_kernel, shards, owners),
+        shape((rows, features)),
+        (*own, label, scaled, base_weight, *blocks),
+        "h" * (shards + 3) + "r" * owners,
+        "r",
+        [
             pltpu.VMEM((rows, features), bf16),
             factors,
             pltpu.VMEM((step, owners * columns), bf16),
             DMA((owners,)),
-            DMA((owners // 2,)),
             DMA((rows // step, features // min(256, features))),
         ],
     )
+    even = gradients(0, [shape(grads.shape[1:])] * (owners // 2), swap(odd, "dp", 1))
+    grad_part, *even = lax.optimization_barrier((grad_part, *even))
+    sums = [even[0]] + [swap(even[n], "dp", 2 * n) for n in range(1, owners // 2)]
     returned = exchange(grad_part.reshape(shards, row_count, features), "fsdp")
     grad_input = call(
         lay_kernel, shape((row_count, shards * features)), (returned,), "h", "h"
     )
-    even = call(
-        functools.partial(even_kernel, shards, owners, own_rows),
-        [shape((columns, features + LANES))] * (owners // 2),
-        (*boths, label, acts_part, scaled, swap(odd, "dp", 1)),
-        "h" * (shards + 4),
-        "r" * (owners // 2),
-        held + [DMA((owners // 2,))],
-    )
-    sums = [even[0]] + [swap(even[n], "dp", 2 * n) for n in range(1, owners // 2)]
-
-    block = LANES
-    wide = pl.BlockSpec((columns, block), lambda i: (0, i))
-    end = pl.BlockSpec((columns, LANES), lambda i: (0, features // LANES))
-    tall = pl.BlockSpec((block, columns), lambda i: (i, 0))
-    flat = pl.BlockSpec((own_rows, keys), lambda i: (0, 0))
-    new = pl.pallas_call(
+
+    new = call(
         functools.partial(adam_kernel, owners // 2, own_rows),
-        grid=(features // block,),
-        out_shape=[shape(a_param.shape, f32)] * 3 + [shape(b_param.shape, f32)] * 3,
-        in_specs=[wide] * (owners // 2) + [end] * (owners // 2) + [tall] * 3 + [flat] * 3,
-        out_specs=[tall] * 3 + [flat] * 3,
-        compiler_params=pltpu.CompilerParams(vmem_limit_bytes=FULL),
-    )(*sums, *sums, a_param, a_moment, a_second, b_param, b_moment, b_second)
+        [shape(a_param.shape, f32)] * 3 + [shape(b_param.shape, f32)] * 3,
+        (*sums, a_param, a_moment, a_second, b_param, b_moment, b_second),
+        "h" * (owners // 2 + 6),
+        "rrrhhh",
+        [pltpu.VMEM(a_param.shape, f32)] * 3 + [DMA((3, features // min(256, features)))],
+    )
     return (grad_input, *new)
 
 

time: 123 us -> 125 us (1.016)
  waiting for transfers between devices: 61.4 us -> 63.5 us
    ppermute x14, waiting for transfers between devices: 36.5 us -> 56.3 us  [swap(): return lax.ppermute(block, axis, [(i, i ^ bits) for i in range(size)])]
    all_to_all x2, waiting for transfers between devices: 24.9 us -> 7.16 us  [exchange(): lax.all_to_all(blocks, axis, split_axis=0, concat_axis=0, tiled=True, axi...]
    pallas_call x1 -> x0, Pallas kernels: 7.77 us -> none  [per_device(): pl.pallas_call(functools.partial(adam_kernel, owners // 2, own_rows), gri...]
    pallas_call x5 -> x7, Pallas kernels: 29.1 us -> 36.1 us  [call(): pl.pallas_call(kernel, out_shape=outs, in_specs=[HBM] * len(ins), out_spe...]
  transfers between devices with their start and end apart: 16 -> 16, of which waited for: 11 -> 10; matrix products, arithmetic and copies ran while one was open for 0% -> 0% of each run, Pallas kernels for 6% -> 10%
where the time goes in v9:
time: 125 us; the launch traced here: 124 us
  waiting for transfers between devices  63.5 us (51%)
  Pallas kernels  36.1 us (29%)
  starting transfers between devices  22.7 us (18%)
    ppermute x14, waiting for transfers between devices, swap(): return lax.ppermute(block, axis, [(i, i ^ bits) for i in range(size)])  56.3 us
    pallas_call x7, Pallas kernels, call(): pl.pallas_call(kernel, out_shape=outs, in_specs=[HBM] * len(ins), out_spe...  36.1 us
    ppermute x14, starting transfers between devices, swap(): return lax.ppermute(block, axis, [(i, i ^ bits) for i in range(size)])  12 us
    all_to_all x2, starting transfers between devices, exchange(): lax.all_to_all(blocks, axis, split_axis=0, concat_axis=0, tiled=True, axi...  10.7 us
    all_to_all x2, waiting for transfers between devices, exchange(): lax.all_to_all(blocks, axis, split_axis=0, concat_axis=0, tiled=True, axi...  7.16 us
  transfers between devices with their start and end apart: 16, of which 10 were waited for; matrix products, arithmetic and copies ran while one was open for 0% of the time, Pallas kernels for 10%

profile of v9, /device:TPU:0, one launch (start us, length us, event | category | flops | bytes accessed | tf_op | source)
XLA Modules:
  0.0 124.2 jit_solution(16854590553838717580)
XLA Ops:
  0.6 3.2 %shard_map.162 = (bf16[4,400,512]{2,1,0:T(8,128)(2,1)}, bf16[1152,256]{1,0:T(8,128)(2,1)}) custom-call(bf16[128,4096]{1,0:T(8,128)(2,1)} %refs_0_.1, bf16[128,512]{1,0:T(8,128)(2,1)} %refs_1_.1, s32[1,128]{1,0:T(1,128)} %bitcast.4, s32[1,128]{1,0:T(1,128)} %bitcast.5, f32[1024,256]{1,0:T(8,128)} %refs_4_.3, f32[64,512]{1,0:T(8,128)} %refs_7_.1), custom_call_target="tpu_custom_call" | custom-call | tf_op jit(solution)/shard_map/pallas_call | solution.py:85
  3.8 0.0 copy-start
  3.8 6.5 %all-to-all-start = ((bf16[4,400,512]{2,1,0:T(8,128)(2,1)}), bf16[4,400,512]{2,1,0:T(8,128)(2,1)}, u32[]{:S(2)}, u32[]{:S(2)}) async-start(bf16[4,400,512]{2,1,0:T(8,128)(2,1)} %get-tuple-element.33), calls=%async_computation | async-start | bytes 3276800 | tf_op jit(solution)/shard_map/all_to_all | solution.py:409
  10.3 0.0 copy-done
  10.3 2.4 %collective-permute-start.5 = (bf16[1152,256]{1,0:T(8,128)(2,1)S(1)}, bf16[1152,256]{1,0:T(8,128)(2,1)S(1)}, u32[]{:S(2)}, u32[]{:S(2)}) collective-permute-start(bf16[1152,256]{1,0:T(8,128)(2,1)S(1)} %copy-done), channel_id=1, source_target_pairs={{0,24},{4,28},{8,16},{12,20},{16,8},{20,12},{24,0},{28,4},{1,25},{... | collective-permute-start | bytes 1769480 | tf_op jit(solution)/shard_map/ppermute | solution.py:405
  12.7 0.5 collective-permute-start.3
  13.2 0.5 collective-permute-start.1
  13.8 0.0 collective-permute-start
  13.8 13.7 %collective-permute-done.5.refs_7_.refs_13_ = bf16[1152,256]{1,0:T(8,128)(2,1)S(1)} collective-permute-done((bf16[1152,256]{1,0:T(8,128)(2,1)S(1)}, bf16[1152,256]{1,0:T(8,128)(2,1)S(1)}, u32[]{:S(2)}, u32[]{:S(2)}) %collective-permute-start.5) | collective-permute-done | bytes 589856 | tf_op jit(solution)/shard_map/ppermute | solution.py:405
  27.5 0.0 copy-start.1
  27.5 0.0 collective-permute-start.6
  27.5 11.1 %collective-permute-done.3.refs_5_.refs_11_ = bf16[1152,256]{1,0:T(8,128)(2,1)S(1)} collective-permute-done((bf16[1152,256]{1,0:T(8,128)(2,1)S(1)}, bf16[1152,256]{1,0:T(8,128)(2,1)S(1)}, u32[]{:S(2)}, u32[]{:S(2)}) %collective-permute-start.3) | collective-permute-done | bytes 589856 | tf_op jit(solution)/shard_map/ppermute | solution.py:405
  38.6 0.0 copy-start.2
  38.6 0.0 collective-permute-start.4
  38.6 0.1 collective-permute-done.1.refs_3_.refs_9_
  38.7 0.0 copy-start.3
  38.7 0.4 collective-permute-start.2
  39.1 0.0 collective-permute-done.refs_2_.refs_8_
  39.1 0.0 copy-done.1
  39.1 0.0 copy-start.4
  39.1 0.0 collective-permute-done.6.refs_8_.refs_14_
  39.1 0.3 copy-done.2
  39.4 0.0 copy-start.5
  39.4 1.2 collective-permute-done.4.refs_6_.refs_12_
  40.6 0.0 copy-done.3
  40.6 0.0 copy-done.4
  40.6 0.0 copy-done.5
  40.6 0.0 copy-start.6
  40.6 0.8 copy-done.6
  41.4 0.1 collective-permute-done.2.refs_4_.refs_10_
  41.6 7.2 %all-to-all-done.refs_0_ = bf16[4,400,512]{2,1,0:T(8,128)(2,1)} async-done(((bf16[4,400,512]{2,1,0:T(8,128)(2,1)}), bf16[4,400,512]{2,1,0:T(8,128)(2,1)}, u32[]{:S(2)}, u32[]{:S(2)}) %all-to-all-start) | async-done | bytes 1638432 | tf_op jit(solution)/shard_map/all_to_all | solution.py:409
  48.7 8.9 %shard_map.163 = (bf16[512,1024]{1,0:T(8,128)(2,1)}, bf16[512,512]{1,0:T(8,128)(2,1)}, s32[8,512]{1,0:T(8,128)}, bf16[64,512]{1,0:T(8,128)(2,1)}) custom-call(bf16[4,400,512]{2,1,0:T(8,128)(2,1)} %all-to-all-done.refs_0_, bf16[1152,256]{1,0:T(8,128)(2,1)} %get-tuple-element.34.refs_1_.refs_7_, bf16[1152,256]{1,0:T(8,128)(2,1)} %copy-done.4, ...), custom_call_target="tpu_custom_call" | custom-call | tf_op jit(solution)/shard_map/pallas_call | solution.py:85
  57.7 1.5 %collective-permute-start.9 = (bf16[64,512]{1,0:T(8,128)(2,1)}, bf16[64,512]{1,0:T(8,128)(2,1)}, u32[]{:S(2)}, u32[]{:S(2)}) collective-permute-start(bf16[64,512]{1,0:T(8,128)(2,1)} %get-tuple-element.39.refs_0_), channel_id=1, source_target_pairs={{0,3},{1,2},{2,1},{3,0},{4,7},{5,6},{6,5},{7,4},{8,11},{9,10},{10,... | collective-permute-start | bytes 196616 | tf_op jit(solution)/shard_map/ppermute | solution.py:405
  59.2 0.0 collective-permute-start.8
  59.2 2.9 %collective-permute-start.7 = (bf16[64,512]{1,0:T(8,128)(2,1)}, bf16[64,512]{1,0:T(8,128)(2,1)}, u32[]{:S(2)}, u32[]{:S(2)}) collective-permute-start(bf16[64,512]{1,0:T(8,128)(2,1)} %get-tuple-element.39.refs_0_), channel_id=1, source_target_pairs={{0,1},{1,0},{2,3},{3,2},{4,5},{5,4},{6,7},{7,6},{8,9},{9,8},{10,11... | collective-permute-start | bytes 196616 | tf_op jit(solution)/shard_map/ppermute | solution.py:405
  62.1 2.3 %collective-permute-done.9.refs_3_ = bf16[64,512]{1,0:T(8,128)(2,1)} collective-permute-done((bf16[64,512]{1,0:T(8,128)(2,1)}, bf16[64,512]{1,0:T(8,128)(2,1)}, u32[]{:S(2)}, u32[]{:S(2)}) %collective-permute-start.9) | collective-permute-done | bytes 65568 | tf_op jit(solution)/shard_map/ppermute | solution.py:405
  64.4 1.3 %collective-permute-done.8.refs_2_ = bf16[64,512]{1,0:T(8,128)(2,1)} collective-permute-done((bf16[64,512]{1,0:T(8,128)(2,1)}, bf16[64,512]{1,0:T(8,128)(2,1)}, u32[]{:S(2)}, u32[]{:S(2)}) %collective-permute-start.8) | collective-permute-done | bytes 65568 | tf_op jit(solution)/shard_map/ppermute | solution.py:405
  65.8 0.0 collective-permute-done.7.refs_1_
  65.8 3.9 %shard_map.164 = bf16[4,256,1152]{2,1,0:T(8,128)(2,1)} custom-call(bf16[64,512]{1,0:T(8,128)(2,1)} %get-tuple-element.39.refs_0_, bf16[64,512]{1,0:T(8,128)(2,1)} %collective-permute-done.7.refs_1_, bf16[64,512]{1,0:T(8,128)(2,1)} %collective-permute-done.8.refs_2_, bf16[64,512]{1,0:T(8,128)(2,1)} %collective-permute-done.9.refs_3_, ...), custom_call_target="tpu_custom_call" | custom-call | tf_op jit(solution)/shard_map/pallas_call | solution.py:85
  69.7 0.1 collective-permute-start.10
  69.8 7.4 %shard_map.165 = bf16[512,1024]{1,0:T(8,128)(2,1)} custom-call(bf16[64,512]{1,0:T(8,128)(2,1)} %get-tuple-element.39.refs_0_, bf16[64,512]{1,0:T(8,128)(2,1)} %collective-permute-done.7.refs_1_, bf16[64,512]{1,0:T(8,128)(2,1)} %collective-permute-done.8.refs_2_, bf16[64,512]{1,0:T(8,128)(2,1)} %collective-permute-done.9.refs_3_, ...), custom_call_target="tpu_custom_call" | custom-call | tf_op jit(solution)/shard_map/pallas_call | solution.py:85
  77.1 0.0 collective-permute-done.10.refs_7_
  77.1 4.8 %shard_map.166 = (bf16[256,1152]{1,0:T(8,128)(2,1)}, bf16[256,1152]{1,0:T(8,128)(2,1)}, bf16[256,1152]{1,0:T(8,128)(2,1)}, bf16[256,1152]{1,0:T(8,128)(2,1)}) custom-call(bf16[64,512]{1,0:T(8,128)(2,1)} %get-tuple-element.39.refs_0_, bf16[64,512]{1,0:T(8,128)(2,1)} %collective-permute-done.7.refs_1_, bf16[64,512]{1,0:T(8,128)(2,1)} %collective-permute-done.8.refs_2_, ...), custom_call_target="tpu_custom_call" | custom-call | tf_op jit(solution)/shard_map/pallas_call | solution.py:85
  82.0 4.3 %all-to-all-start.1 = ((bf16[4,128,1024]{2,1,0:T(8,128)(2,1)}), bf16[4,128,1024]{2,1,0:T(8,128)(2,1)}, u32[]{:S(2)}, u32[]{:S(2)}) async-start(bf16[4,128,1024]{2,1,0:T(8,128)(2,1)} %bitcast.3), calls=%async_computation.1 | async-start | bytes 2097152 | tf_op jit(solution)/shard_map/all_to_all | solution.py:409
  86.3 1.6 %collective-permute-start.11 = (bf16[256,1152]{1,0:T(8,128)(2,1)}, bf16[256,1152]{1,0:T(8,128)(2,1)}, u32[]{:S(2)}, u32[]{:S(2)}) collective-permute-start(bf16[256,1152]{1,0:T(8,128)(2,1)} %get-tuple-element.50), channel_id=1, source_target_pairs={{0,8},{4,12},{8,0},{12,4},{16,24},{20,28},{24,16},{28,20},{1,9},{5... | collective-permute-start | bytes 1769480 | tf_op jit(solution)/shard_map/ppermute | solution.py:405
  87.8 1.5 %collective-permute-start.12 = (bf16[256,1152]{1,0:T(8,128)(2,1)}, bf16[256,1152]{1,0:T(8,128)(2,1)}, u32[]{:S(2)}, u32[]{:S(2)}) collective-permute-start(bf16[256,1152]{1,0:T(8,128)(2,1)} %get-tuple-element.51), channel_id=1, source_target_pairs={{0,16},{4,20},{8,24},{12,28},{16,0},{20,4},{24,8},{28,12},{1,17},{... | collective-permute-start | bytes 1769480 | tf_op jit(solution)/shard_map/ppermute | solution.py:405
  89.3 0.5 collective-permute-start.13
  89.8 13.0 %collective-permute-done.11.refs_1_ = bf16[256,1152]{1,0:T(8,128)(2,1)} collective-permute-done((bf16[256,1152]{1,0:T(8,128)(2,1)}, bf16[256,1152]{1,0:T(8,128)(2,1)}, u32[]{:S(2)}, u32[]{:S(2)}) %collective-permute-start.11) | collective-permute-done | bytes 589856 | tf_op jit(solution)/shard_map/ppermute | solution.py:405
  102.8 13.5 %collective-permute-done.12.refs_2_ = bf16[256,1152]{1,0:T(8,128)(2,1)} collective-permute-done((bf16[256,1152]{1,0:T(8,128)(2,1)}, bf16[256,1152]{1,0:T(8,128)(2,1)}, u32[]{:S(2)}, u32[]{:S(2)}) %collective-permute-start.12) | collective-permute-done | bytes 589856 | tf_op jit(solution)/shard_map/ppermute | solution.py:405
  116.2 0.0 collective-permute-done.13.refs_3_
  116.2 5.7 %shard_map.168 = (f32[1024,256]{1,0:T(8,128)}, f32[1024,256]{1,0:T(8,128)}, f32[1024,256]{1,0:T(8,128)}, f32[64,512]{1,0:T(8,128)}, f32[64,512]{1,0:T(8,128)}, /*index=5*/f32[64,512]{1,0:T(8,128)}) custom-call(bf16[256,1152]{1,0:T(8,128)(2,1)} %get-tuple-element.49.refs_0_, bf16[256,1152]{1,0:T(8,128)(2,1)} %collective-permute-done.11.refs_1_, ...), custom_call_target="tpu_custom_call" | custom-call | tf_op jit(solution)/shard_map/pallas_call | solution.py:85
  121.9 0.0 all-to-all-done.1.refs_0_
  121.9 2.3 %shard_map.167 = bf16[128,4096]{1,0:T(8,128)(2,1)} custom-call(bf16[4,128,1024]{2,1,0:T(8,128)(2,1)} %all-to-all-done.1.refs_0_), custom_call_target="tpu_custom_call" | custom-call | tf_op jit(solution)/shard_map/pallas_call | solution.py:85
Async XLA Ops:
  3.8 6.5 %copy-start = (bf16[1152,256]{1,0:T(8,128)(2,1)S(1)}, bf16[1152,256]{1,0:T(8,128)(2,1)}, u32[]{:S(2)}) copy-start(bf16[1152,256]{1,0:T(8,128)(2,1)} %get-tuple-element.34.refs_1_.refs_7_) | copy-start | bytes 1769476
  3.8 44.9 %all-to-all-start = ((bf16[4,400,512]{2,1,0:T(8,128)(2,1)}), bf16[4,400,512]{2,1,0:T(8,128)(2,1)}, u32[]{:S(2)}, u32[]{:S(2)}) async-start(bf16[4,400,512]{2,1,0:T(8,128)(2,1)} %get-tuple-element.33), calls=%async_computation | async-start | bytes 3276800 | tf_op jit(solution)/shard_map/all_to_all | solution.py:409
  10.3 17.2 %collective-permute-start.5 = (bf16[1152,256]{1,0:T(8,128)(2,1)S(1)}, bf16[1152,256]{1,0:T(8,128)(2,1)S(1)}, u32[]{:S(2)}, u32[]{:S(2)}) collective-permute-start(bf16[1152,256]{1,0:T(8,128)(2,1)S(1)} %copy-done), channel_id=1, source_target_pairs={{0,24},{4,28},{8,16},{12,20},{16,8},{20,12},{24,0},{28,4},{1,25},{... | collective-permute-start | bytes 1769480 | tf_op jit(solution)/shard_map/ppermute | solution.py:405
  12.7 25.9 %collective-permute-start.3 = (bf16[1152,256]{1,0:T(8,128)(2,1)S(1)}, bf16[1152,256]{1,0:T(8,128)(2,1)S(1)}, u32[]{:S(2)}, u32[]{:S(2)}) collective-permute-start(bf16[1152,256]{1,0:T(8,128)(2,1)S(1)} %copy-done), channel_id=1, source_target_pairs={{0,16},{4,20},{8,24},{12,28},{16,0},{20,4},{24,8},{28,12},{1,17},{... | collective-permute-start | bytes 1769480 | tf_op jit(solution)/shard_map/ppermute | solution.py:405
  13.2 25.5 %collective-permute-start.1 = (bf16[1152,256]{1,0:T(8,128)(2,1)S(1)}, bf16[1152,256]{1,0:T(8,128)(2,1)S(1)}, u32[]{:S(2)}, u32[]{:S(2)}) collective-permute-start(bf16[1152,256]{1,0:T(8,128)(2,1)S(1)} %copy-done), channel_id=1, source_target_pairs={{0,8},{4,12},{8,0},{12,4},{16,24},{20,28},{24,16},{28,20},{1,9},{5... | collective-permute-start | bytes 1769480 | tf_op jit(solution)/shard_map/ppermute | solution.py:405
  13.8 25.4 %collective-permute-start = (bf16[1152,256]{1,0:T(8,128)(2,1)S(1)}, bf16[1152,256]{1,0:T(8,128)(2,1)S(1)}, u32[]{:S(2)}, u32[]{:S(2)}) collective-permute-start(bf16[1152,256]{1,0:T(8,128)(2,1)S(1)} %copy-done), channel_id=1, source_target_pairs={{0,4},{4,0},{8,12},{12,8},{16,20},{20,16},{24,28},{28,24},{1,5},{5... | collective-permute-start | bytes 1769480 | tf_op jit(solution)/shard_map/ppermute | solution.py:405
  27.5 11.7 %copy-start.1 = (bf16[1152,256]{1,0:T(8,128)(2,1)}, bf16[1152,256]{1,0:T(8,128)(2,1)S(1)}, u32[]{:S(2)}) copy-start(bf16[1152,256]{1,0:T(8,128)(2,1)S(1)} %collective-permute-done.5.refs_7_.refs_13_) | copy-start | bytes 1769476
  27.5 11.7 %collective-permute-start.6 = (bf16[1152,256]{1,0:T(8,128)(2,1)S(1)}, bf16[1152,256]{1,0:T(8,128)(2,1)S(1)}, u32[]{:S(2)}, u32[]{:S(2)}) collective-permute-start(bf16[1152,256]{1,0:T(8,128)(2,1)S(1)} %collective-permute-done.5.refs_7_.refs_13_), channel_id=1, source_target_pairs={{0,4},{4,0},{8,12},{12,8},{16,20},{20,16},{24,28},{28,24},{1,5},{5... | collective-permute-start | bytes 1769480 | tf_op jit(solution)/shard_map/ppermute | solution.py:405
  38.6 0.8 copy-start.2
  38.6 2.0 %collective-permute-start.4 = (bf16[1152,256]{1,0:T(8,128)(2,1)S(1)}, bf16[1152,256]{1,0:T(8,128)(2,1)S(1)}, u32[]{:S(2)}, u32[]{:S(2)}) collective-permute-start(bf16[1152,256]{1,0:T(8,128)(2,1)S(1)} %collective-permute-done.3.refs_5_.refs_11_), channel_id=1, source_target_pairs={{0,4},{4,0},{8,12},{12,8},{16,20},{20,16},{24,28},{28,24},{1,5},{5... | collective-permute-start | bytes 1769480 | tf_op jit(solution)/shard_map/ppermute | solution.py:405
  38.7 1.9 %copy-start.3 = (bf16[1152,256]{1,0:T(8,128)(2,1)}, bf16[1152,256]{1,0:T(8,128)(2,1)S(1)}, u32[]{:S(2)}) copy-start(bf16[1152,256]{1,0:T(8,128)(2,1)S(1)} %collective-permute-done.1.refs_3_.refs_9_) | copy-start | bytes 1769476
  38.7 2.9 %collective-permute-start.2 = (bf16[1152,256]{1,0:T(8,128)(2,1)S(1)}, bf16[1152,256]{1,0:T(8,128)(2,1)}, u32[]{:S(2)}, u32[]{:S(2)}) collective-permute-start(bf16[1152,256]{1,0:T(8,128)(2,1)S(1)} %collective-permute-done.1.refs_3_.refs_9_), channel_id=1, source_target_pairs={{0,4},{4,0},{8,12},{12,8},{16,20},{20,16},{24,28},{28,24},{1,5},{5... | collective-permute-start | bytes 1769480 | tf_op jit(solution)/shard_map/ppermute | solution.py:405
  39.1 1.5 %copy-start.4 = (bf16[1152,256]{1,0:T(8,128)(2,1)}, bf16[1152,256]{1,0:T(8,128)(2,1)S(1)}, u32[]{:S(2)}) copy-start(bf16[1152,256]{1,0:T(8,128)(2,1)S(1)} %collective-permute-done.refs_2_.refs_8_) | copy-start | bytes 1769476
  39.4 1.2 copy-start.5
  40.6 0.8 copy-start.6
  57.7 6.8 %collective-permute-start.9 = (bf16[64,512]{1,0:T(8,128)(2,1)}, bf16[64,512]{1,0:T(8,128)(2,1)}, u32[]{:S(2)}, u32[]{:S(2)}) collective-permute-start(bf16[64,512]{1,0:T(8,128)(2,1)} %get-tuple-element.39.refs_0_), channel_id=1, source_target_pairs={{0,3},{1,2},{2,1},{3,0},{4,7},{5,6},{6,5},{7,4},{8,11},{9,10},{10,... | collective-permute-start | bytes 196616 | tf_op jit(solution)/shard_map/ppermute | solution.py:405
  59.2 6.6 %collective-permute-start.8 = (bf16[64,512]{1,0:T(8,128)(2,1)}, bf16[64,512]{1,0:T(8,128)(2,1)}, u32[]{:S(2)}, u32[]{:S(2)}) collective-permute-start(bf16[64,512]{1,0:T(8,128)(2,1)} %get-tuple-element.39.refs_0_), channel_id=1, source_target_pairs={{0,2},{1,3},{2,0},{3,1},{4,6},{5,7},{6,4},{7,5},{8,10},{9,11},{10,... | collective-permute-start | bytes 196616 | tf_op jit(solution)/shard_map/ppermute | solution.py:405
  59.2 6.6 %collective-permute-start.7 = (bf16[64,512]{1,0:T(8,128)(2,1)}, bf16[64,512]{1,0:T(8,128)(2,1)}, u32[]{:S(2)}, u32[]{:S(2)}) collective-permute-start(bf16[64,512]{1,0:T(8,128)(2,1)} %get-tuple-element.39.refs_0_), channel_id=1, source_target_pairs={{0,1},{1,0},{2,3},{3,2},{4,5},{5,4},{6,7},{7,6},{8,9},{9,8},{10,11... | collective-permute-start | bytes 196616 | tf_op jit(solution)/shard_map/ppermute | solution.py:405
  69.7 7.4 %collective-permute-start.10 = (bf16[4,256,1152]{2,1,0:T(8,128)(2,1)}, bf16[4,256,1152]{2,1,0:T(8,128)(2,1)}, u32[]{:S(2)}, u32[]{:S(2)}) collective-permute-start(bf16[4,256,1152]{2,1,0:T(8,128)(2,1)} %shard_map.164), channel_id=1, source_target_pairs={{0,4},{4,0},{8,12},{12,8},{16,20},{20,16},{24,28},{28,24},{1,5},{5... | collective-permute-start | bytes 7077896 | tf_op jit(solution)/shard_map/ppermute | solution.py:405
  82.0 39.9 %all-to-all-start.1 = ((bf16[4,128,1024]{2,1,0:T(8,128)(2,1)}), bf16[4,128,1024]{2,1,0:T(8,128)(2,1)}, u32[]{:S(2)}, u32[]{:S(2)}) async-start(bf16[4,128,1024]{2,1,0:T(8,128)(2,1)} %bitcast.3), calls=%async_computation.1 | async-start | bytes 2097152 | tf_op jit(solution)/shard_map/all_to_all | solution.py:409
  86.3 16.5 %collective-permute-start.11 = (bf16[256,1152]{1,0:T(8,128)(2,1)}, bf16[256,1152]{1,0:T(8,128)(2,1)}, u32[]{:S(2)}, u32[]{:S(2)}) collective-permute-start(bf16[256,1152]{1,0:T(8,128)(2,1)} %get-tuple-element.50), channel_id=1, source_target_pairs={{0,8},{4,12},{8,0},{12,4},{16,24},{20,28},{24,16},{28,20},{1,9},{5... | collective-permute-start | bytes 1769480 | tf_op jit(solution)/shard_map/ppermute | solution.py:405
  87.8 28.4 %collective-permute-start.12 = (bf16[256,1152]{1,0:T(8,128)(2,1)}, bf16[256,1152]{1,0:T(8,128)(2,1)}, u32[]{:S(2)}, u32[]{:S(2)}) collective-permute-start(bf16[256,1152]{1,0:T(8,128)(2,1)} %get-tuple-element.51), channel_id=1, source_target_pairs={{0,16},{4,20},{8,24},{12,28},{16,0},{20,4},{24,8},{28,12},{1,17},{... | collective-permute-start | bytes 1769480 | tf_op jit(solution)/shard_map/ppermute | solution.py:405
  89.3 26.9 %collective-permute-start.13 = (bf16[256,1152]{1,0:T(8,128)(2,1)}, bf16[256,1152]{1,0:T(8,128)(2,1)}, u32[]{:S(2)}, u32[]{:S(2)}) collective-permute-start(bf16[256,1152]{1,0:T(8,128)(2,1)} %get-tuple-element.52), channel_id=1, source_target_pairs={{0,24},{4,28},{8,16},{12,20},{16,8},{20,12},{24,0},{28,4},{1,25},{... | collective-permute-start | bytes 1769480 | tf_op jit(solution)/shard_map/ppermute | solution.py:405

commit v10 on v9

--- a/solution.py
+++ b/solution.py
@@ -105,6 +105,18 @@
     return lax.dot_general(
         left, right, (((left_dim,), (right_dim,)), ((), ())), preferred_element_type=f32
     )
+
+def halvings(n):
+    return n.bit_length() - 1
+
+
+def over(x, n):
+    return lax.shift_right_logical(x, jnp.full(x.shape, halvings(n), jnp.int32))
+
+
+def past(x, n):
+    return x & (n - 1)
+
 
 def iota(dims, axis):
     return lax.broadcasted_iota(jnp.int32, dims, axis)
@@ -148,8 +160,8 @@
 
 def second_ids(count, own_rows, rows):
     line = iota((count * own_rows, rows), 0)
-    inner = lax.rem(line, own_rows) + lax.axis_index("fsdp") * own_rows
-    return lax.div(line, own_rows) * TEN_DEV + lax.div(inner, ADAPTER_RANK)
+    inner = past(line, own_rows) + lax.axis_index("fsdp") * own_rows
+    return over(line, own_rows) * TEN_DEV + over(inner, ADAPTER_RANK)
 
 
 def load_factors(a_blocks, a_all, sems):
@@ -169,13 +181,30 @@
 
 def open_kernel(owners, own_rows, io, packed, *refs):
     blocks = refs[:owners]
-    acts, scaled, label, both, b_all, a_all, b_sems, sems = refs[owners:]
+    acts, scaled, label, both, marks, b_all, a_all, in_sems, b_sems, sems = refs[owners:]
     rows, features = acts.shape
     keys = scaled.shape[1]
     columns = blocks[0].shape[1]
     shards, _, unit = packed.shape
     rd = rows // shards
-    b_copies = []
+    first = (features + keys) // unit * rd
+    act_copies, row_copies, b_copies = [], [], []
+    for j in range(shards):
+        at = pl.ds(j * rd, rd)
+        for q in range((features + keys) // unit):
+            piece = packed.at[j, pl.ds(q * rd, rd)]
+            c = q * unit
+            if c < features:
+                copy = pltpu.make_async_copy(piece, acts.at[at, pl.ds(c, unit)], in_sems.at[j, q])
+                act_copies.append(copy)
+            else:
+                to = scaled.at[at, pl.ds(c - features, unit)]
+                row_copies.append(pltpu.make_async_copy(piece, to, in_sems.at[j, q]))
+        row_copies.append(
+            pltpu.make_async_copy(
+                packed.at[j, pl.ds(first, LABEL_ROWS)], marks.at[j], in_sems.at[j, first // rd]
+            )
+        )
     for k in range(owners):
         for q in range(keys // columns):
             b_copies.append(
@@ -185,25 +214,18 @@
                     b_sems.at[k, q],
                 )
             )
-    for copy in b_copies:
+    for copy in row_copies + b_copies + act_copies:
         copy.start()
     copies = load_factors(blocks, a_all, sems)
-    io.ready()
     me = lax.axis_index("dp")
+    for copy in row_copies:
+        copy.wait()
     for j in range(shards):
-        at = slice(j * rd, (j + 1) * rd)
-        for q in range(features // unit):
-            acts[at, q * unit : (q + 1) * unit] = packed[j, q * rd : (q + 1) * rd]
-        first = features // unit * rd
-        for q in range(keys // unit):
-            part = packed[j, first + q * rd : first + (q + 1) * rd]
-            scaled[at, q * unit : (q + 1) * unit] = part
-        first += keys // unit * rd
-        ids = packed[j, first:, :rd].astype(f32).astype(jnp.int32)
+        ids = marks[j, :, :rd].astype(f32).astype(jnp.int32)
         tid = (ids[0:1] ^ me) * TEN_DEV + ids[1:2]
-        label[:, at] = jnp.broadcast_to(tid, (8, rd))
-    for n in range(3):
-        io.store(n)
+        label[:, j * rd : (j + 1) * rd] = jnp.broadcast_to(tid, (8, rd))
+    io.store(1)
+    io.store(2)
     step = min(ROW_STEP, rows)
     ids = second_ids(owners, own_rows, step)
     for copy in b_copies:
@@ -217,14 +239,17 @@
         else:
             low = jnp.sum(wide.reshape(-1, own_rows, step), axis=0)
             low = jnp.concatenate([low] * (ADAPTER_RANK // own_rows), axis=0)
-            part = lax.div(iota(low.shape, 0), own_rows)
+            part = over(iota(low.shape, 0), own_rows)
             place = lax.rem(lax.axis_index("fsdp"), ADAPTER_RANK // own_rows)
             low = jnp.where(part == place, low, 0.0)
         both[:ADAPTER_RANK, at] = low.astype(bf16)
+    for copy in act_copies:
+        copy.wait()
+    io.store(0)
     step = min(MID_STEP, rows)
     for r in range(0, rows, step):
         at = slice(r, r + step)
-        where = column_of(label[0:1, at]).astype(jnp.int32) - lax.div(
+        where = column_of(label[0:1, at]).astype(jnp.int32) - over(
             iota((step, LANES), 1), ADAPTER_RANK
         )
         low = jnp.zeros((step, LANES), f32)
@@ -250,11 +275,9 @@
 MID = slice(ADAPTER_RANK, 2 * ADAPTER_RANK)
 
 
-def spread(low, label, k, columns):
-    rows = low.shape[1]
-    ids = lax.div(iota((columns, rows), 0), ADAPTER_RANK) + k * TEN_DEV
-    tall = jnp.concatenate([low] * (columns // ADAPTER_RANK), axis=0)
-    return jnp.where(ids == label, tall, 0.0).astype(bf16)
+def spread(tall, ids, label, k):
+    return jnp.where(ids == label - k * TEN_DEV, tall, 0.0).astype(bf16)
+
 
 def second_grads(owners, parity, own_rows, boths, label, scaled, held):
     rows = scaled.shape[0]
@@ -263,7 +286,7 @@
     second = None
     line = iota((count * own_rows, step), 0)
     ids = second_ids(count, own_rows, step)
-    ids = ids + (lax.div(line, own_rows) + parity) * TEN_DEV
+    ids = ids + (over(line, own_rows) + parity) * TEN_DEV
     for r in range(0, rows, step):
         at = slice(r, r + step)
         held[...] = total(boths, MID, at)
@@ -279,15 +302,19 @@
     return adapter_scale * ADAPTER_RANK ** (-0.5) * second
 
 
-def grads_step(owners, parity, own_rows, boths, label, acts, scaled, held, out, arrived, send):
+def grads_step(owners, parity, own_rows, boths, label, acts, scaled, held, out, arrived, send, wait=None):
     features = acts.shape[1]
     keys = scaled.shape[1]
     columns = out.shape[1]
     down = adapter_scale * MODEL_WIDTH ** (-0.5)
     second = second_grads(owners, parity, own_rows, boths, label, scaled, held)
-    low = total(boths, BACK, slice(None))
+    tall = down * total(boths, BACK, slice(None))
+    ids = over(iota((columns, tall.shape[1]), 0), ADAPTER_RANK)
+    tall = jnp.concatenate([tall] * (columns // ADAPTER_RANK), axis=0)
     for n in range(owners // 2):
-        grad = down * dot(spread(low, label[0:1], 2 * n + parity, columns), acts[...])
+        grad = dot(spread(tall, ids, label[0:1], 2 * n + parity), acts[...])
+        if n == 0 and wait is not None:
+            wait()
         if arrived is not None:
             grad = grad + arrived[n, :, :features].astype(f32)
         out[n, :, :features] = grad.astype(bf16)
@@ -303,28 +330,31 @@
         send[n].start()
 
 
-def grads_kernel(shards, owners, own_rows, parity, io, *refs):
-    boths, (label, acts, scaled) = refs[:shards], refs[shards : shards + 3]
-    refs = refs[shards + 3 :]
-    arrived = refs[0] if parity == 0 else None
-    outs, (held, made, sems) = refs[parity == 0 : -3], refs[-3:]
-    send = []
-    for n in range(owners // 2):
-        out = outs[0].at[n] if parity else outs[n]
-        send.append(pltpu.make_async_copy(made.at[n], out, sems.at[n]))
+def even_kernel(shards, owners, own_rows, io, *refs):
+    boths, (label, acts, scaled, arrived) = refs[:shards], refs[shards : shards + 4]
+    outs = refs[shards + 4 : shards + 4 + owners // 2]
+    held, made, got, sems, got_sem = refs[shards + 4 + owners // 2 :]
+    late = pltpu.make_async_copy(arrived, got, got_sem)
+    late.start()
+    send = [pltpu.make_async_copy(made.at[n], outs[n], sems.at[n]) for n in range(owners // 2)]
     io.ready()
-    grads_step(owners, parity, own_rows, boths, label, acts, scaled, held, made, arrived, send)
+    grads_step(
+        owners, 0, own_rows, boths, label, acts, scaled, held, made, got, send, late.wait
+    )
     for copy in send:
         copy.wait()
 
 
-def side_kernel(shards, owners, io, *refs):
-    boths, (label, scaled, weight) = refs[:shards], refs[shards : shards + 3]
-    a_blocks = refs[shards + 3 : shards + 3 + owners]
-    out, part, a_all, back_wide, sems, part_sems = refs[shards + 3 + owners :]
+def main_kernel(shards, owners, own_rows, io, *refs):
+    boths, (label, acts, scaled, weight) = refs[:shards], refs[shards : shards + 4]
+    a_blocks = refs[shards + 4 : shards + 4 + owners]
+    odd, out, held, made, part, a_all, back_wide, sems, odd_sems, part_sems = refs[
+        shards + 4 + owners :
+    ]
     copies = load_factors(a_blocks, a_all, sems)
-    send = []
+    send = [pltpu.make_async_copy(made.at[n], odd.at[n], odd_sems.at[n]) for n in range(owners // 2)]
     io.ready()
+    grads_step(owners, 1, own_rows, boths, label, acts, scaled, held, made, None, send)
     rows, features = part.shape
     step = min(ROW_STEP, rows)
     width = a_all.shape[1]
@@ -333,7 +363,7 @@
         at = slice(r, r + step)
         low = adapter_scale * jnp.transpose(total(boths, BACK, at))
         low = jnp.concatenate([low] * (LANES // ADAPTER_RANK), axis=1)
-        where = column_of(label[0:1, at]).astype(jnp.int32) - lax.div(
+        where = column_of(label[0:1, at]).astype(jnp.int32) - over(
             iota((step, LANES), 1), ADAPTER_RANK
         )
         for q in range(width // LANES):
@@ -458,11 +488,13 @@
             shape((2 * ADAPTER_RANK, rows)),
         ],
         (packed, *blocks),
-        "h" + "r" * owners,
+        "r" + "r" * owners,
         "hhhh",
         [
+            pltpu.VMEM((shards, LABEL_ROWS, unit), bf16),
             pltpu.VMEM((owners * own_rows, keys), bf16),
             factors,
+            DMA((shards, (features + keys) // unit + 1)),
             DMA((owners, keys // columns)),
             DMA((owners,)),
         ],
@@ -470,44 +502,36 @@
     boths = [both] + [swap(both, "fsdp", j) for j in range(1, shards)]
 
     grads = shape((owners // 2, columns, features + LANES))
-
-    def gradients(parity, outs, *more):
-        return call(
-            functools.partial(grads_kernel, shards, owners, own_rows, parity),
-            outs,
-            (*boths, label, acts_part, scaled, *more),
-            "h" * (shards + 3 + len(more)),
-            "r" * (1 if parity else owners // 2),
-            [
-                pltpu.VMEM((ADAPTER_RANK, step), f32),
-                pltpu.VMEM(grads.shape, bf16),
-                DMA((owners // 2,)),
-            ],
-        )
-
-    odd = gradients(1, grads)
-    odd, *own = lax.optimization_barrier((odd, *boths))
-    grad_part = call(
-        functools.partial(side_kernel, shards, owners),
-        shape((rows, features)),
-        (*own, label, scaled, base_weight, *blocks),
-        "h" * (shards + 3) + "r" * owners,
-        "r",
-        [
+    held = [pltpu.VMEM((ADAPTER_RANK, step), f32), pltpu.VMEM(grads.shape, bf16)]
+    odd, grad_part = call(
+        functools.partial(main_kernel, shards, owners, own_rows),
+        [grads, shape((rows, features))],
+        (*boths, label, acts_part, scaled, base_weight, *blocks),
+        "h" * (shards + 4) + "r" * owners,
+        "rr",
+        held
+        + [
             pltpu.VMEM((rows, features), bf16),
             factors,
             pltpu.VMEM((step, owners * columns), bf16),
             DMA((owners,)),
+            DMA((owners // 2,)),
             DMA((rows // step, features // min(256, features))),
         ],
     )
-    even = gradients(0, [shape(grads.shape[1:])] * (owners // 2), swap(odd, "dp", 1))
-    grad_part, *even = lax.optimization_barrier((grad_part, *even))
-    sums = [even[0]] + [swap(even[n], "dp", 2 * n) for n in range(1, owners // 2)]
     returned = exchange(grad_part.reshape(shards, row_count, features), "fsdp")
     grad_input = call(
         lay_kernel, shape((row_count, shards * features)), (returned,), "h", "h"
     )
+    even = call(
+        functools.partial(even_kernel, shards, owners, own_rows),
+        [shape((columns, features + LANES))] * (owners // 2),
+        (*boths, label, acts_part, scaled, swap(odd, "dp", 1)),
+        "h" * (shards + 3) + "r",
+        "r" * (owners // 2),
+        held + [pltpu.VMEM(grads.shape, bf16), DMA((owners // 2,)), DMA],
+    )
+    sums = [even[0]] + [swap(even[n], "dp", 2 * n) for n in range(1, owners // 2)]
 
     new = call(
         functools.partial(adam_kernel, owners // 2, own_rows),

time: 125 us -> 120 us (0.960)
  Pallas kernels: 36.1 us -> 33.3 us
  waiting for transfers between devices: 63.5 us -> 61.2 us
    ppermute x14, waiting for transfers between devices: 56.3 us -> 36 us  [swap(): return lax.ppermute(block, axis, [(i, i ^ bits) for i in range(size)])]
    all_to_all x2, waiting for transfers between devices: 7.16 us -> 25.2 us  [exchange(): lax.all_to_all(blocks, axis, split_axis=0, concat_axis=0, tiled=True, axi...]
    pallas_call x7 -> x6, Pallas kernels: 36.1 us -> 33.3 us  [call(): pl.pallas_call(kernel, out_shape=outs, in_specs=[HBM] * len(ins), out_spe...]
  transfers between devices with their start and end apart: 16 -> 16, of which waited for: 10 -> 11; matrix products, arithmetic and copies ran while one was open for 0% -> 0% of each run, Pallas kernels for 10% -> 6%
where the time goes in v10:
time: 120 us; the launch traced here: 119 us
  waiting for transfers between devices  61.2 us (51%)
  Pallas kernels  33.3 us (28%)
  starting transfers between devices  22.9 us (19%)
    ppermute x14, waiting for transfers between devices, swap(): return lax.ppermute(block, axis, [(i, i ^ bits) for i in range(size)])  36 us
    pallas_call x6, Pallas kernels, call(): pl.pallas_call(kernel, out_shape=outs, in_specs=[HBM] * len(ins), out_spe...  33.3 us
    all_to_all x2, waiting for transfers between devices, exchange(): lax.all_to_all(blocks, axis, split_axis=0, concat_axis=0, tiled=True, axi...  25.2 us
    ppermute x14, starting transfers between devices, swap(): return lax.ppermute(block, axis, [(i, i ^ bits) for i in range(size)])  12 us
    all_to_all x2, starting transfers between devices, exchange(): lax.all_to_all(blocks, axis, split_axis=0, concat_axis=0, tiled=True, axi...  10.9 us
  transfers between devices with their start and end apart: 16, of which 11 were waited for; matrix products, arithmetic and copies ran while one was open for 0% of the time, Pallas kernels for 6%

profile of v10, /device:TPU:0, one launch (start us, length us, event | category | flops | bytes accessed | tf_op | source)
XLA Modules:
  0.0 119.5 jit_solution(1718773486072258720)
XLA Ops:
  0.6 3.2 %shard_map.162 = (bf16[4,400,512]{2,1,0:T(8,128)(2,1)}, bf16[1152,256]{1,0:T(8,128)(2,1)}) custom-call(bf16[128,4096]{1,0:T(8,128)(2,1)} %refs_0_.1, bf16[128,512]{1,0:T(8,128)(2,1)} %refs_1_.1, s32[1,128]{1,0:T(1,128)} %bitcast.4, s32[1,128]{1,0:T(1,128)} %bitcast.5, f32[1024,256]{1,0:T(8,128)} %refs_4_.3, f32[64,512]{1,0:T(8,128)} %refs_7_.3), custom_call_target="tpu_custom_call" | custom-call | tf_op jit(solution)/shard_map/pallas_call | solution.py:85
  3.8 0.0 copy-start
  3.8 6.5 %all-to-all-start = ((bf16[4,400,512]{2,1,0:T(8,128)(2,1)}), bf16[4,400,512]{2,1,0:T(8,128)(2,1)}, u32[]{:S(2)}, u32[]{:S(2)}) async-start(bf16[4,400,512]{2,1,0:T(8,128)(2,1)} %get-tuple-element.25), calls=%async_computation | async-start | bytes 3276800 | tf_op jit(solution)/shard_map/all_to_all | solution.py:439
  10.3 0.0 copy-done
  10.3 2.4 %collective-permute-start.5 = (bf16[1152,256]{1,0:T(8,128)(2,1)S(1)}, bf16[1152,256]{1,0:T(8,128)(2,1)S(1)}, u32[]{:S(2)}, u32[]{:S(2)}) collective-permute-start(bf16[1152,256]{1,0:T(8,128)(2,1)S(1)} %copy-done), channel_id=1, source_target_pairs={{0,24},{4,28},{8,16},{12,20},{16,8},{20,12},{24,0},{28,4},{1,25},{... | collective-permute-start | bytes 1769480 | tf_op jit(solution)/shard_map/ppermute | solution.py:435
  12.7 0.5 collective-permute-start.3
  13.2 0.5 collective-permute-start.1
  13.8 0.0 collective-permute-start
  13.8 13.7 %collective-permute-done.5.refs_7_.refs_14_ = bf16[1152,256]{1,0:T(8,128)(2,1)S(1)} collective-permute-done((bf16[1152,256]{1,0:T(8,128)(2,1)S(1)}, bf16[1152,256]{1,0:T(8,128)(2,1)S(1)}, u32[]{:S(2)}, u32[]{:S(2)}) %collective-permute-start.5) | collective-permute-done | bytes 589856 | tf_op jit(solution)/shard_map/ppermute | solution.py:435
  27.5 0.0 copy-start.1
  27.5 0.0 collective-permute-start.6
  27.5 11.1 %collective-permute-done.3.refs_5_.refs_12_ = bf16[1152,256]{1,0:T(8,128)(2,1)S(1)} collective-permute-done((bf16[1152,256]{1,0:T(8,128)(2,1)S(1)}, bf16[1152,256]{1,0:T(8,128)(2,1)S(1)}, u32[]{:S(2)}, u32[]{:S(2)}) %collective-permute-start.3) | collective-permute-done | bytes 589856 | tf_op jit(solution)/shard_map/ppermute | solution.py:435
  38.6 0.0 copy-start.2
  38.6 0.0 collective-permute-start.4
  38.6 0.1 collective-permute-done.1.refs_3_.refs_10_
  38.7 0.0 copy-start.3
  38.7 0.4 collective-permute-start.2
  39.1 0.0 collective-permute-done.refs_2_.refs_9_
  39.1 0.0 copy-done.1
  39.1 0.0 copy-start.4
  39.1 0.0 collective-permute-done.6.refs_8_.refs_15_
  39.1 0.3 copy-done.2
  39.4 0.0 copy-start.5
  39.4 1.2 collective-permute-done.4.refs_6_.refs_13_
  40.6 0.0 copy-done.3
  40.6 0.0 copy-done.4
  40.6 0.0 copy-done.5
  40.6 0.0 copy-start.6
  40.6 0.8 copy-done.6
  41.4 0.1 collective-permute-done.2.refs_4_.refs_11_
  41.6 7.2 %all-to-all-done.refs_0_ = bf16[4,400,512]{2,1,0:T(8,128)(2,1)} async-done(((bf16[4,400,512]{2,1,0:T(8,128)(2,1)}), bf16[4,400,512]{2,1,0:T(8,128)(2,1)}, u32[]{:S(2)}, u32[]{:S(2)}) %all-to-all-start) | async-done | bytes 1638432 | tf_op jit(solution)/shard_map/all_to_all | solution.py:439
  48.7 8.9 %shard_map.163 = (bf16[512,1024]{1,0:T(8,128)(2,1)}, bf16[512,512]{1,0:T(8,128)(2,1)}, s32[8,512]{1,0:T(8,128)}, bf16[64,512]{1,0:T(8,128)(2,1)}) custom-call(bf16[4,400,512]{2,1,0:T(8,128)(2,1)} %all-to-all-done.refs_0_, bf16[1152,256]{1,0:T(8,128)(2,1)} %get-tuple-element.26.refs_1_.refs_8_, bf16[1152,256]{1,0:T(8,128)(2,1)} %copy-done.4, ...), custom_call_target="tpu_custom_call" | custom-call | tf_op jit(solution)/shard_map/pallas_call | solution.py:85
  57.7 1.5 %collective-permute-start.9 = (bf16[64,512]{1,0:T(8,128)(2,1)}, bf16[64,512]{1,0:T(8,128)(2,1)}, u32[]{:S(2)}, u32[]{:S(2)}) collective-permute-start(bf16[64,512]{1,0:T(8,128)(2,1)} %get-tuple-element.27.refs_0_), channel_id=1, source_target_pairs={{0,3},{1,2},{2,1},{3,0},{4,7},{5,6},{6,5},{7,4},{8,11},{9,10},{10,... | collective-permute-start | bytes 196616 | tf_op jit(solution)/shard_map/ppermute | solution.py:435
  59.2 0.0 collective-permute-start.8
  59.2 2.9 %collective-permute-start.7 = (bf16[64,512]{1,0:T(8,128)(2,1)}, bf16[64,512]{1,0:T(8,128)(2,1)}, u32[]{:S(2)}, u32[]{:S(2)}) collective-permute-start(bf16[64,512]{1,0:T(8,128)(2,1)} %get-tuple-element.27.refs_0_), channel_id=1, source_target_pairs={{0,1},{1,0},{2,3},{3,2},{4,5},{5,4},{6,7},{7,6},{8,9},{9,8},{10,11... | collective-permute-start | bytes 196616 | tf_op jit(solution)/shard_map/ppermute | solution.py:435
  62.1 2.3 %collective-permute-done.9.refs_3_ = bf16[64,512]{1,0:T(8,128)(2,1)} collective-permute-done((bf16[64,512]{1,0:T(8,128)(2,1)}, bf16[64,512]{1,0:T(8,128)(2,1)}, u32[]{:S(2)}, u32[]{:S(2)}) %collective-permute-start.9) | collective-permute-done | bytes 65568 | tf_op jit(solution)/shard_map/ppermute | solution.py:435
  64.5 1.3 %collective-permute-done.8.refs_2_ = bf16[64,512]{1,0:T(8,128)(2,1)} collective-permute-done((bf16[64,512]{1,0:T(8,128)(2,1)}, bf16[64,512]{1,0:T(8,128)(2,1)}, u32[]{:S(2)}, u32[]{:S(2)}) %collective-permute-start.8) | collective-permute-done | bytes 65568 | tf_op jit(solution)/shard_map/ppermute | solution.py:435
  65.8 0.0 collective-permute-done.7.refs_1_
  65.8 8.8 %shard_map.164 = (bf16[4,256,1152]{2,1,0:T(8,128)(2,1)}, bf16[512,1024]{1,0:T(8,128)(2,1)}) custom-call(bf16[64,512]{1,0:T(8,128)(2,1)} %get-tuple-element.27.refs_0_, bf16[64,512]{1,0:T(8,128)(2,1)} %collective-permute-done.7.refs_1_, bf16[64,512]{1,0:T(8,128)(2,1)} %collective-permute-done.8.refs_2_, bf16[64,512]{1,0:T(8,128)(2,1)} %collective-permute-done.9.refs_3_, ...), custom_call_target="tpu_custom_call" | custom-call | tf_op jit(solution)/shard_map/pallas_call | solution.py:85
  74.6 0.1 collective-permute-start.10
  74.6 4.4 %all-to-all-start.1 = ((bf16[4,128,1024]{2,1,0:T(8,128)(2,1)}), bf16[4,128,1024]{2,1,0:T(8,128)(2,1)}, u32[]{:S(2)}, u32[]{:S(2)}) async-start(bf16[4,128,1024]{2,1,0:T(8,128)(2,1)} %bitcast.3), calls=%async_computation.1 | async-start | bytes 2097152 | tf_op jit(solution)/shard_map/all_to_all | solution.py:439
  79.1 0.4 collective-permute-done.10.refs_7_
  79.5 4.5 %shard_map.166 = (bf16[256,1152]{1,0:T(8,128)(2,1)}, bf16[256,1152]{1,0:T(8,128)(2,1)}, bf16[256,1152]{1,0:T(8,128)(2,1)}, bf16[256,1152]{1,0:T(8,128)(2,1)}) custom-call(bf16[64,512]{1,0:T(8,128)(2,1)} %get-tuple-element.27.refs_0_, bf16[64,512]{1,0:T(8,128)(2,1)} %collective-permute-done.7.refs_1_, bf16[64,512]{1,0:T(8,128)(2,1)} %collective-permute-done.8.refs_2_, ...), custom_call_target="tpu_custom_call" | custom-call | tf_op jit(solution)/shard_map/pallas_call | solution.py:85
  84.0 1.6 %collective-permute-start.11 = (bf16[256,1152]{1,0:T(8,128)(2,1)}, bf16[256,1152]{1,0:T(8,128)(2,1)}, u32[]{:S(2)}, u32[]{:S(2)}) collective-permute-start(bf16[256,1152]{1,0:T(8,128)(2,1)} %get-tuple-element.34), channel_id=1, source_target_pairs={{0,8},{4,12},{8,0},{12,4},{16,24},{20,28},{24,16},{28,20},{1,9},{5... | collective-permute-start | bytes 1769480 | tf_op jit(solution)/shard_map/ppermute | solution.py:435
  85.6 1.5 %collective-permute-start.12 = (bf16[256,1152]{1,0:T(8,128)(2,1)}, bf16[256,1152]{1,0:T(8,128)(2,1)}, u32[]{:S(2)}, u32[]{:S(2)}) collective-permute-start(bf16[256,1152]{1,0:T(8,128)(2,1)} %get-tuple-element.35), channel_id=1, source_target_pairs={{0,16},{4,20},{8,24},{12,28},{16,0},{20,4},{24,8},{28,12},{1,17},{... | collective-permute-start | bytes 1769480 | tf_op jit(solution)/shard_map/ppermute | solution.py:435
  87.1 0.5 collective-permute-start.13
  87.6 18.1 %all-to-all-done.1.refs_0_ = bf16[4,128,1024]{2,1,0:T(8,128)(2,1)} async-done(((bf16[4,128,1024]{2,1,0:T(8,128)(2,1)}), bf16[4,128,1024]{2,1,0:T(8,128)(2,1)}, u32[]{:S(2)}, u32[]{:S(2)}) %all-to-all-start.1) | async-done | bytes 1048608 | tf_op jit(solution)/shard_map/all_to_all | solution.py:439
  105.6 2.3 %shard_map.165 = bf16[128,4096]{1,0:T(8,128)(2,1)} custom-call(bf16[4,128,1024]{2,1,0:T(8,128)(2,1)} %all-to-all-done.1.refs_0_), custom_call_target="tpu_custom_call" | custom-call | tf_op jit(solution)/shard_map/pallas_call | solution.py:85
  107.9 0.0 collective-permute-done.11.refs_1_
  107.9 5.7 %collective-permute-done.12.refs_2_ = bf16[256,1152]{1,0:T(8,128)(2,1)} collective-permute-done((bf16[256,1152]{1,0:T(8,128)(2,1)}, bf16[256,1152]{1,0:T(8,128)(2,1)}, u32[]{:S(2)}, u32[]{:S(2)}) %collective-permute-start.12) | collective-permute-done | bytes 589856 | tf_op jit(solution)/shard_map/ppermute | solution.py:435
  113.6 0.0 collective-permute-done.13.refs_3_
  113.6 5.7 %shard_map.167 = (f32[1024,256]{1,0:T(8,128)}, f32[1024,256]{1,0:T(8,128)}, f32[1024,256]{1,0:T(8,128)}, f32[64,512]{1,0:T(8,128)}, f32[64,512]{1,0:T(8,128)}, /*index=5*/f32[64,512]{1,0:T(8,128)}) custom-call(bf16[256,1152]{1,0:T(8,128)(2,1)} %get-tuple-element.33.refs_0_, bf16[256,1152]{1,0:T(8,128)(2,1)} %collective-permute-done.11.refs_1_, ...), custom_call_target="tpu_custom_call" | custom-call | tf_op jit(solution)/shard_map/pallas_call | solution.py:85
Async XLA Ops:
  3.8 6.5 %copy-start = (bf16[1152,256]{1,0:T(8,128)(2,1)S(1)}, bf16[1152,256]{1,0:T(8,128)(2,1)}, u32[]{:S(2)}) copy-start(bf16[1152,256]{1,0:T(8,128)(2,1)} %get-tuple-element.26.refs_1_.refs_8_) | copy-start | bytes 1769476
  3.8 44.9 %all-to-all-start = ((bf16[4,400,512]{2,1,0:T(8,128)(2,1)}), bf16[4,400,512]{2,1,0:T(8,128)(2,1)}, u32[]{:S(2)}, u32[]{:S(2)}) async-start(bf16[4,400,512]{2,1,0:T(8,128)(2,1)} %get-tuple-element.25), calls=%async_computation | async-start | bytes 3276800 | tf_op jit(solution)/shard_map/all_to_all | solution.py:439
  10.3 17.2 %collective-permute-start.5 = (bf16[1152,256]{1,0:T(8,128)(2,1)S(1)}, bf16[1152,256]{1,0:T(8,128)(2,1)S(1)}, u32[]{:S(2)}, u32[]{:S(2)}) collective-permute-start(bf16[1152,256]{1,0:T(8,128)(2,1)S(1)} %copy-done), channel_id=1, source_target_pairs={{0,24},{4,28},{8,16},{12,20},{16,8},{20,12},{24,0},{28,4},{1,25},{... | collective-permute-start | bytes 1769480 | tf_op jit(solution)/shard_map/ppermute | solution.py:435
  12.7 25.9 %collective-permute-start.3 = (bf16[1152,256]{1,0:T(8,128)(2,1)S(1)}, bf16[1152,256]{1,0:T(8,128)(2,1)S(1)}, u32[]{:S(2)}, u32[]{:S(2)}) collective-permute-start(bf16[1152,256]{1,0:T(8,128)(2,1)S(1)} %copy-done), channel_id=1, source_target_pairs={{0,16},{4,20},{8,24},{12,28},{16,0},{20,4},{24,8},{28,12},{1,17},{... | collective-permute-start | bytes 1769480 | tf_op jit(solution)/shard_map/ppermute | solution.py:435
  13.2 25.5 %collective-permute-start.1 = (bf16[1152,256]{1,0:T(8,128)(2,1)S(1)}, bf16[1152,256]{1,0:T(8,128)(2,1)S(1)}, u32[]{:S(2)}, u32[]{:S(2)}) collective-permute-start(bf16[1152,256]{1,0:T(8,128)(2,1)S(1)} %copy-done), channel_id=1, source_target_pairs={{0,8},{4,12},{8,0},{12,4},{16,24},{20,28},{24,16},{28,20},{1,9},{5... | collective-permute-start | bytes 1769480 | tf_op jit(solution)/shard_map/ppermute | solution.py:435
  13.8 25.4 %collective-permute-start = (bf16[1152,256]{1,0:T(8,128)(2,1)S(1)}, bf16[1152,256]{1,0:T(8,128)(2,1)S(1)}, u32[]{:S(2)}, u32[]{:S(2)}) collective-permute-start(bf16[1152,256]{1,0:T(8,128)(2,1)S(1)} %copy-done), channel_id=1, source_target_pairs={{0,4},{4,0},{8,12},{12,8},{16,20},{20,16},{24,28},{28,24},{1,5},{5... | collective-permute-start | bytes 1769480 | tf_op jit(solution)/shard_map/ppermute | solution.py:435
  27.5 11.7 %copy-start.1 = (bf16[1152,256]{1,0:T(8,128)(2,1)}, bf16[1152,256]{1,0:T(8,128)(2,1)S(1)}, u32[]{:S(2)}) copy-start(bf16[1152,256]{1,0:T(8,128)(2,1)S(1)} %collective-permute-done.5.refs_7_.refs_14_) | copy-start | bytes 1769476
  27.5 11.7 %collective-permute-start.6 = (bf16[1152,256]{1,0:T(8,128)(2,1)S(1)}, bf16[1152,256]{1,0:T(8,128)(2,1)S(1)}, u32[]{:S(2)}, u32[]{:S(2)}) collective-permute-start(bf16[1152,256]{1,0:T(8,128)(2,1)S(1)} %collective-permute-done.5.refs_7_.refs_14_), channel_id=1, source_target_pairs={{0,4},{4,0},{8,12},{12,8},{16,20},{20,16},{24,28},{28,24},{1,5},{5... | collective-permute-start | bytes 1769480 | tf_op jit(solution)/shard_map/ppermute | solution.py:435
  38.6 0.8 copy-start.2
  38.6 2.0 %collective-permute-start.4 = (bf16[1152,256]{1,0:T(8,128)(2,1)S(1)}, bf16[1152,256]{1,0:T(8,128)(2,1)S(1)}, u32[]{:S(2)}, u32[]{:S(2)}) collective-permute-start(bf16[1152,256]{1,0:T(8,128)(2,1)S(1)} %collective-permute-done.3.refs_5_.refs_12_), channel_id=1, source_target_pairs={{0,4},{4,0},{8,12},{12,8},{16,20},{20,16},{24,28},{28,24},{1,5},{5... | collective-permute-start | bytes 1769480 | tf_op jit(solution)/shard_map/ppermute | solution.py:435
  38.7 1.9 %copy-start.3 = (bf16[1152,256]{1,0:T(8,128)(2,1)}, bf16[1152,256]{1,0:T(8,128)(2,1)S(1)}, u32[]{:S(2)}) copy-start(bf16[1152,256]{1,0:T(8,128)(2,1)S(1)} %collective-permute-done.1.refs_3_.refs_10_) | copy-start | bytes 1769476
  38.7 2.9 %collective-permute-start.2 = (bf16[1152,256]{1,0:T(8,128)(2,1)S(1)}, bf16[1152,256]{1,0:T(8,128)(2,1)}, u32[]{:S(2)}, u32[]{:S(2)}) collective-permute-start(bf16[1152,256]{1,0:T(8,128)(2,1)S(1)} %collective-permute-done.1.refs_3_.refs_10_), channel_id=1, source_target_pairs={{0,4},{4,0},{8,12},{12,8},{16,20},{20,16},{24,28},{28,24},{1,5},{5... | collective-permute-start | bytes 1769480 | tf_op jit(solution)/shard_map/ppermute | solution.py:435
  39.1 1.5 %copy-start.4 = (bf16[1152,256]{1,0:T(8,128)(2,1)}, bf16[1152,256]{1,0:T(8,128)(2,1)S(1)}, u32[]{:S(2)}) copy-start(bf16[1152,256]{1,0:T(8,128)(2,1)S(1)} %collective-permute-done.refs_2_.refs_9_) | copy-start | bytes 1769476
  39.4 1.2 %copy-start.5 = (bf16[1152,256]{1,0:T(8,128)(2,1)}, bf16[1152,256]{1,0:T(8,128)(2,1)S(1)}, u32[]{:S(2)}) copy-start(bf16[1152,256]{1,0:T(8,128)(2,1)S(1)} %collective-permute-done.6.refs_8_.refs_15_) | copy-start | bytes 1769476
  40.6 0.8 copy-start.6
  57.7 6.8 %collective-permute-start.9 = (bf16[64,512]{1,0:T(8,128)(2,1)}, bf16[64,512]{1,0:T(8,128)(2,1)}, u32[]{:S(2)}, u32[]{:S(2)}) collective-permute-start(bf16[64,512]{1,0:T(8,128)(2,1)} %get-tuple-element.27.refs_0_), channel_id=1, source_target_pairs={{0,3},{1,2},{2,1},{3,0},{4,7},{5,6},{6,5},{7,4},{8,11},{9,10},{10,... | collective-permute-start | bytes 196616 | tf_op jit(solution)/shard_map/ppermute | solution.py:435
  59.2 6.6 %collective-permute-start.8 = (bf16[64,512]{1,0:T(8,128)(2,1)}, bf16[64,512]{1,0:T(8,128)(2,1)}, u32[]{:S(2)}, u32[]{:S(2)}) collective-permute-start(bf16[64,512]{1,0:T(8,128)(2,1)} %get-tuple-element.27.refs_0_), channel_id=1, source_target_pairs={{0,2},{1,3},{2,0},{3,1},{4,6},{5,7},{6,4},{7,5},{8,10},{9,11},{10,... | collective-permute-start | bytes 196616 | tf_op jit(solution)/shard_map/ppermute | solution.py:435
  59.2 6.6 %collective-permute-start.7 = (bf16[64,512]{1,0:T(8,128)(2,1)}, bf16[64,512]{1,0:T(8,128)(2,1)}, u32[]{:S(2)}, u32[]{:S(2)}) collective-permute-start(bf16[64,512]{1,0:T(8,128)(2,1)} %get-tuple-element.27.refs_0_), channel_id=1, source_target_pairs={{0,1},{1,0},{2,3},{3,2},{4,5},{5,4},{6,7},{7,6},{8,9},{9,8},{10,11... | collective-permute-start | bytes 196616 | tf_op jit(solution)/shard_map/ppermute | solution.py:435
  74.6 4.9 %collective-permute-start.10 = (bf16[4,256,1152]{2,1,0:T(8,128)(2,1)}, bf16[4,256,1152]{2,1,0:T(8,128)(2,1)}, u32[]{:S(2)}, u32[]{:S(2)}) collective-permute-start(bf16[4,256,1152]{2,1,0:T(8,128)(2,1)} %get-tuple-element.32), channel_id=1, source_target_pairs={{0,4},{4,0},{8,12},{12,8},{16,20},{20,16},{24,28},{28,24},{1,5},{5... | collective-permute-start | bytes 7077896 | tf_op jit(solution)/shard_map/ppermute | solution.py:435
  74.6 31.0 %all-to-all-start.1 = ((bf16[4,128,1024]{2,1,0:T(8,128)(2,1)}), bf16[4,128,1024]{2,1,0:T(8,128)(2,1)}, u32[]{:S(2)}, u32[]{:S(2)}) async-start(bf16[4,128,1024]{2,1,0:T(8,128)(2,1)} %bitcast.3), calls=%async_computation.1 | async-start | bytes 2097152 | tf_op jit(solution)/shard_map/all_to_all | solution.py:439
  84.0 23.9 %collective-permute-start.11 = (bf16[256,1152]{1,0:T(8,128)(2,1)}, bf16[256,1152]{1,0:T(8,128)(2,1)}, u32[]{:S(2)}, u32[]{:S(2)}) collective-permute-start(bf16[256,1152]{1,0:T(8,128)(2,1)} %get-tuple-element.34), channel_id=1, source_target_pairs={{0,8},{4,12},{8,0},{12,4},{16,24},{20,28},{24,16},{28,20},{1,9},{5... | collective-permute-start | bytes 1769480 | tf_op jit(solution)/shard_map/ppermute | solution.py:435
  85.6 28.0 %collective-permute-start.12 = (bf16[256,1152]{1,0:T(8,128)(2,1)}, bf16[256,1152]{1,0:T(8,128)(2,1)}, u32[]{:S(2)}, u32[]{:S(2)}) collective-permute-start(bf16[256,1152]{1,0:T(8,128)(2,1)} %get-tuple-element.35), channel_id=1, source_target_pairs={{0,16},{4,20},{8,24},{12,28},{16,0},{20,4},{24,8},{28,12},{1,17},{... | collective-permute-start | bytes 1769480 | tf_op jit(solution)/shard_map/ppermute | solution.py:435
  87.1 26.5 %collective-permute-start.13 = (bf16[256,1152]{1,0:T(8,128)(2,1)}, bf16[256,1152]{1,0:T(8,128)(2,1)}, u32[]{:S(2)}, u32[]{:S(2)}) collective-permute-start(bf16[256,1152]{1,0:T(8,128)(2,1)} %get-tuple-element.36), channel_id=1, source_target_pairs={{0,24},{4,28},{8,16},{12,20},{16,8},{20,12},{24,0},{28,4},{1,25},{... | collective-permute-start | bytes 1769480 | tf_op jit(solution)/shard_map/ppermute | solution.py:435

commit v11 on v10

--- a/solution.py
+++ b/solution.py
@@ -165,13 +165,8 @@
 
 
 def load_factors(a_blocks, a_all, sems):
-    columns = a_blocks[0].shape[1]
     copies = [
-        pltpu.make_async_copy(
-            block.at[pl.ds(0, a_all.shape[0])],
-            a_all.at[:, pl.ds(k * columns, columns)],
-            sems.at[k],
-        )
+        pltpu.make_async_copy(block.at[pl.ds(0, a_all.shape[1])], a_all.at[k], sems.at[k])
         for k, block in enumerate(a_blocks)
     ]
     for copy in copies:
@@ -256,7 +251,7 @@
         for k in range(owners):
             if r == 0:
                 copies[k].wait()
-            wide = dot(acts[at], a_all[:, k * columns : (k + 1) * columns])
+            wide = dot(acts[at], a_all[k])
             for q in range(columns // LANES):
                 hit = where == k * TEN_DEV + q * (LANES // ADAPTER_RANK)
                 low = low + jnp.where(hit, wide[:, q * LANES : (q + 1) * LANES], 0.0)
@@ -357,7 +352,7 @@
     grads_step(owners, 1, own_rows, boths, label, acts, scaled, held, made, None, send)
     rows, features = part.shape
     step = min(ROW_STEP, rows)
-    width = a_all.shape[1]
+    width = back_wide.shape[1]
     chunk = min(256, features)
     for r in range(0, rows, step):
         at = slice(r, r + step)
@@ -374,7 +369,8 @@
                 copy.wait()
         for c in range(0, features, chunk):
             base = dot(scaled[at], weight[c : c + chunk], 1, 1).astype(bf16)
-            side = dot(back_wide[...], a_all[c : c + chunk], 1, 1).astype(bf16)
+            factor = [a_all[k, c : c + chunk] for k in range(owners)]
+            side = dot(back_wide[...], jnp.concatenate(factor, axis=1), 1, 1).astype(bf16)
             part[at, c : c + chunk] = (base.astype(f32) + side.astype(f32)).astype(bf16)
             copy = pltpu.make_async_copy(
                 part.at[pl.ds(r, step), pl.ds(c, chunk)],
@@ -388,31 +384,48 @@
 
 
 def adam_kernel(count, own_rows, io, *refs):
-    grads, firsts = refs[:count], refs[count : count + 3]
+    given, firsts = refs[:count], refs[count : count + 3]
     seconds, outs = refs[count + 3 : count + 6], refs[count + 6 : count + 12]
-    made, sems = refs[count + 12 : count + 15], refs[count + 15]
+    grads, (held, made, grad_sems, in_sems, sems) = refs[count + 12], refs[count + 13 :]
     features, _ = firsts[0].shape
     keys = seconds[0].shape[1]
-    io.ready()
+    block = min(256, features)
+    starts = list(range(0, features, block))
+    grad_loads = [
+        pltpu.make_async_copy(given[n], grads.at[n], grad_sems.at[n]) for n in range(count)
+    ]
+    loads = [
+        pltpu.make_async_copy(
+            firsts[m].at[pl.ds(c, block)], held.at[m, pl.ds(c, block)], in_sems.at[m, n]
+        )
+        for n, c in enumerate(starts)
+        for m in range(3)
+    ]
+    for copy in grad_loads + loads:
+        copy.start()
 
     def summed(at):
-        value = grads[0][:, at].astype(f32)
-        for part in grads[1:]:
-            value = value + part[:, at].astype(f32)
+        value = grads[0, :, at].astype(f32)
+        for n in range(1, count):
+            value = value + grads[n, :, at].astype(f32)
         return value
 
+    for copy in grad_loads:
+        copy.wait()
     copies = []
-    block = min(256, features)
-    for n, c in enumerate(range(0, features, block)):
+    for n, c in enumerate(starts):
         at = slice(c, c + block)
         grad = jnp.transpose(summed(at))
-        for m, value in enumerate(adam_step(*[x[at] for x in firsts], grad)):
-            made[m][at] = value
+        for m in range(3):
+            loads[3 * n + m].wait()
+        for m, value in enumerate(adam_step(*[held[m, at] for m in range(3)], grad)):
+            made[m, at] = value
             rows = pl.ds(c, block)
             copies.append(
-                pltpu.make_async_copy(made[m].at[rows], outs[m].at[rows], sems.at[m, n])
+                pltpu.make_async_copy(made.at[m, rows], outs[m].at[rows], sems.at[m, n])
             )
             copies[-1].start()
+    io.ready()
     grad = summed(slice(features, features + LANES))
     for q in range(keys // LANES):
         at = slice(q * LANES, (q + 1) * LANES)
@@ -478,7 +491,7 @@
         blocks += [block, swap(block, "dp", 1)]
 
     step = min(ROW_STEP, rows)
-    factors = pltpu.VMEM((features, owners * columns), bf16)
+    factors = pltpu.VMEM((owners, features, columns), bf16)
     acts_part, scaled, label, both = call(
         functools.partial(open_kernel, owners, own_rows),
         [
@@ -533,13 +546,21 @@
     )
     sums = [even[0]] + [swap(even[n], "dp", 2 * n) for n in range(1, owners // 2)]
 
+    pieces = features // min(256, features)
     new = call(
         functools.partial(adam_kernel, owners // 2, own_rows),
         [shape(a_param.shape, f32)] * 3 + [shape(b_param.shape, f32)] * 3,
         (*sums, a_param, a_moment, a_second, b_param, b_moment, b_second),
-        "h" * (owners // 2 + 6),
+        "r" * (owners // 2 + 3) + "hhh",
         "rrrhhh",
-        [pltpu.VMEM(a_param.shape, f32)] * 3 + [DMA((3, features // min(256, features)))],
+        [
+            pltpu.VMEM(grads.shape, bf16),
+            pltpu.VMEM((3, features, columns), f32),
+            pltpu.VMEM((3, features, columns), f32),
+            DMA((owners // 2,)),
+            DMA((3, pieces)),
+            DMA((3, pieces)),
+        ],
     )
     return (grad_input, *new)
 

time: 120 us -> 120 us (level)
  no operation moved by 1% of the time
where the time goes in v11:
time: 120 us
  waiting for transfers between devices  61.2 us (51%)
  Pallas kernels  33.7 us (28%)
  starting transfers between devices  22.9 us (19%)
    ppermute x14, waiting for transfers between devices, swap(): return lax.ppermute(block, axis, [(i, i ^ bits) for i in range(size)])  36 us
    pallas_call x6, Pallas kernels, call(): pl.pallas_call(kernel, out_shape=outs, in_specs=[HBM] * len(ins), out_spe...  33.7 us
    all_to_all x2, waiting for transfers between devices, exchange(): lax.all_to_all(blocks, axis, split_axis=0, concat_axis=0, tiled=True, axi...  25.2 us
    ppermute x14, starting transfers between devices, swap(): return lax.ppermute(block, axis, [(i, i ^ bits) for i in range(size)])  12 us
    all_to_all x2, starting transfers between devices, exchange(): lax.all_to_all(blocks, axis, split_axis=0, concat_axis=0, tiled=True, axi...  10.9 us
  transfers between devices with their start and end apart: 16, of which 11 were waited for; matrix products, arithmetic and copies ran while one was open for 0% of the time, Pallas kernels for 6%

profile of v11, /device:TPU:0, one launch (start us, length us, event | category | flops | bytes accessed | tf_op | source)
XLA Modules:
  0.0 119.9 jit_solution(3303806467876183887)
XLA Ops:
  0.6 3.2 %shard_map.162 = (bf16[4,400,512]{2,1,0:T(8,128)(2,1)}, bf16[1152,256]{1,0:T(8,128)(2,1)}) custom-call(bf16[128,4096]{1,0:T(8,128)(2,1)} %refs_0_.1, bf16[128,512]{1,0:T(8,128)(2,1)} %refs_1_.1, s32[1,128]{1,0:T(1,128)} %bitcast.4, s32[1,128]{1,0:T(1,128)} %bitcast.5, f32[1024,256]{1,0:T(8,128)} %refs_4_.3, f32[64,512]{1,0:T(8,128)} %refs_7_.3), custom_call_target="tpu_custom_call" | custom-call | tf_op jit(solution)/shard_map/pallas_call | solution.py:85
  3.8 0.0 copy-start
  3.8 6.5 %all-to-all-start = ((bf16[4,400,512]{2,1,0:T(8,128)(2,1)}), bf16[4,400,512]{2,1,0:T(8,128)(2,1)}, u32[]{:S(2)}, u32[]{:S(2)}) async-start(bf16[4,400,512]{2,1,0:T(8,128)(2,1)} %get-tuple-element.25), calls=%async_computation | async-start | bytes 3276800 | tf_op jit(solution)/shard_map/all_to_all | solution.py:452
  10.3 0.0 copy-done
  10.3 2.4 %collective-permute-start.5 = (bf16[1152,256]{1,0:T(8,128)(2,1)S(1)}, bf16[1152,256]{1,0:T(8,128)(2,1)S(1)}, u32[]{:S(2)}, u32[]{:S(2)}) collective-permute-start(bf16[1152,256]{1,0:T(8,128)(2,1)S(1)} %copy-done), channel_id=1, source_target_pairs={{0,24},{4,28},{8,16},{12,20},{16,8},{20,12},{24,0},{28,4},{1,25},{... | collective-permute-start | bytes 1769480 | tf_op jit(solution)/shard_map/ppermute | solution.py:448
  12.7 0.5 collective-permute-start.3
  13.2 0.5 collective-permute-start.1
  13.8 0.0 collective-permute-start
  13.8 13.7 %collective-permute-done.5.refs_7_.refs_14_ = bf16[1152,256]{1,0:T(8,128)(2,1)S(1)} collective-permute-done((bf16[1152,256]{1,0:T(8,128)(2,1)S(1)}, bf16[1152,256]{1,0:T(8,128)(2,1)S(1)}, u32[]{:S(2)}, u32[]{:S(2)}) %collective-permute-start.5) | collective-permute-done | bytes 589856 | tf_op jit(solution)/shard_map/ppermute | solution.py:448
  27.5 0.0 copy-start.1
  27.5 0.0 collective-permute-start.6
  27.5 11.1 %collective-permute-done.3.refs_5_.refs_12_ = bf16[1152,256]{1,0:T(8,128)(2,1)S(1)} collective-permute-done((bf16[1152,256]{1,0:T(8,128)(2,1)S(1)}, bf16[1152,256]{1,0:T(8,128)(2,1)S(1)}, u32[]{:S(2)}, u32[]{:S(2)}) %collective-permute-start.3) | collective-permute-done | bytes 589856 | tf_op jit(solution)/shard_map/ppermute | solution.py:448
  38.6 0.0 copy-start.2
  38.6 0.0 collective-permute-start.4
  38.6 0.1 collective-permute-done.1.refs_3_.refs_10_
  38.7 0.0 copy-start.3
  38.7 0.4 collective-permute-start.2
  39.1 0.0 collective-permute-done.refs_2_.refs_9_
  39.1 0.0 copy-done.1
  39.1 0.0 copy-start.4
  39.1 0.0 collective-permute-done.6.refs_8_.refs_15_
  39.1 0.3 copy-done.2
  39.4 0.0 copy-start.5
  39.4 1.2 collective-permute-done.4.refs_6_.refs_13_
  40.6 0.0 copy-done.3
  40.6 0.0 copy-done.4
  40.6 0.0 copy-done.5
  40.6 0.0 copy-start.6
  40.6 0.8 copy-done.6
  41.4 0.1 collective-permute-done.2.refs_4_.refs_11_
  41.6 7.2 %all-to-all-done.refs_0_ = bf16[4,400,512]{2,1,0:T(8,128)(2,1)} async-done(((bf16[4,400,512]{2,1,0:T(8,128)(2,1)}), bf16[4,400,512]{2,1,0:T(8,128)(2,1)}, u32[]{:S(2)}, u32[]{:S(2)}) %all-to-all-start) | async-done | bytes 1638432 | tf_op jit(solution)/shard_map/all_to_all | solution.py:452
  48.7 8.9 %shard_map.163 = (bf16[512,1024]{1,0:T(8,128)(2,1)}, bf16[512,512]{1,0:T(8,128)(2,1)}, s32[8,512]{1,0:T(8,128)}, bf16[64,512]{1,0:T(8,128)(2,1)}) custom-call(bf16[4,400,512]{2,1,0:T(8,128)(2,1)} %all-to-all-done.refs_0_, bf16[1152,256]{1,0:T(8,128)(2,1)} %get-tuple-element.26.refs_1_.refs_8_, bf16[1152,256]{1,0:T(8,128)(2,1)} %copy-done.4, ...), custom_call_target="tpu_custom_call" | custom-call | tf_op jit(solution)/shard_map/pallas_call | solution.py:85
  57.7 1.5 %collective-permute-start.9 = (bf16[64,512]{1,0:T(8,128)(2,1)}, bf16[64,512]{1,0:T(8,128)(2,1)}, u32[]{:S(2)}, u32[]{:S(2)}) collective-permute-start(bf16[64,512]{1,0:T(8,128)(2,1)} %get-tuple-element.27.refs_0_), channel_id=1, source_target_pairs={{0,3},{1,2},{2,1},{3,0},{4,7},{5,6},{6,5},{7,4},{8,11},{9,10},{10,... | collective-permute-start | bytes 196616 | tf_op jit(solution)/shard_map/ppermute | solution.py:448
  59.2 0.0 collective-permute-start.8
  59.2 2.9 %collective-permute-start.7 = (bf16[64,512]{1,0:T(8,128)(2,1)}, bf16[64,512]{1,0:T(8,128)(2,1)}, u32[]{:S(2)}, u32[]{:S(2)}) collective-permute-start(bf16[64,512]{1,0:T(8,128)(2,1)} %get-tuple-element.27.refs_0_), channel_id=1, source_target_pairs={{0,1},{1,0},{2,3},{3,2},{4,5},{5,4},{6,7},{7,6},{8,9},{9,8},{10,11... | collective-permute-start | bytes 196616 | tf_op jit(solution)/shard_map/ppermute | solution.py:448
  62.1 2.3 %collective-permute-done.9.refs_3_ = bf16[64,512]{1,0:T(8,128)(2,1)} collective-permute-done((bf16[64,512]{1,0:T(8,128)(2,1)}, bf16[64,512]{1,0:T(8,128)(2,1)}, u32[]{:S(2)}, u32[]{:S(2)}) %collective-permute-start.9) | collective-permute-done | bytes 65568 | tf_op jit(solution)/shard_map/ppermute | solution.py:448
  64.4 1.3 %collective-permute-done.8.refs_2_ = bf16[64,512]{1,0:T(8,128)(2,1)} collective-permute-done((bf16[64,512]{1,0:T(8,128)(2,1)}, bf16[64,512]{1,0:T(8,128)(2,1)}, u32[]{:S(2)}, u32[]{:S(2)}) %collective-permute-start.8) | collective-permute-done | bytes 65568 | tf_op jit(solution)/shard_map/ppermute | solution.py:448
  65.8 0.0 collective-permute-done.7.refs_1_
  65.8 8.8 %shard_map.164 = (bf16[4,256,1152]{2,1,0:T(8,128)(2,1)}, bf16[512,1024]{1,0:T(8,128)(2,1)}) custom-call(bf16[64,512]{1,0:T(8,128)(2,1)} %get-tuple-element.27.refs_0_, bf16[64,512]{1,0:T(8,128)(2,1)} %collective-permute-done.7.refs_1_, bf16[64,512]{1,0:T(8,128)(2,1)} %collective-permute-done.8.refs_2_, bf16[64,512]{1,0:T(8,128)(2,1)} %collective-permute-done.9.refs_3_, ...), custom_call_target="tpu_custom_call" | custom-call | tf_op jit(solution)/shard_map/pallas_call | solution.py:85
  74.5 0.1 collective-permute-start.10
  74.6 4.4 %all-to-all-start.1 = ((bf16[4,128,1024]{2,1,0:T(8,128)(2,1)}), bf16[4,128,1024]{2,1,0:T(8,128)(2,1)}, u32[]{:S(2)}, u32[]{:S(2)}) async-start(bf16[4,128,1024]{2,1,0:T(8,128)(2,1)} %bitcast.3), calls=%async_computation.1 | async-start | bytes 2097152 | tf_op jit(solution)/shard_map/all_to_all | solution.py:452
  79.1 0.4 collective-permute-done.10.refs_7_
  79.5 4.5 %shard_map.166 = (bf16[256,1152]{1,0:T(8,128)(2,1)}, bf16[256,1152]{1,0:T(8,128)(2,1)}, bf16[256,1152]{1,0:T(8,128)(2,1)}, bf16[256,1152]{1,0:T(8,128)(2,1)}) custom-call(bf16[64,512]{1,0:T(8,128)(2,1)} %get-tuple-element.27.refs_0_, bf16[64,512]{1,0:T(8,128)(2,1)} %collective-permute-done.7.refs_1_, bf16[64,512]{1,0:T(8,128)(2,1)} %collective-permute-done.8.refs_2_, ...), custom_call_target="tpu_custom_call" | custom-call | tf_op jit(solution)/shard_map/pallas_call | solution.py:85
  84.0 1.6 %collective-permute-start.11 = (bf16[256,1152]{1,0:T(8,128)(2,1)}, bf16[256,1152]{1,0:T(8,128)(2,1)}, u32[]{:S(2)}, u32[]{:S(2)}) collective-permute-start(bf16[256,1152]{1,0:T(8,128)(2,1)} %get-tuple-element.34), channel_id=1, source_target_pairs={{0,8},{4,12},{8,0},{12,4},{16,24},{20,28},{24,16},{28,20},{1,9},{5... | collective-permute-start | bytes 1769480 | tf_op jit(solution)/shard_map/ppermute | solution.py:448
  85.6 1.5 %collective-permute-start.12 = (bf16[256,1152]{1,0:T(8,128)(2,1)}, bf16[256,1152]{1,0:T(8,128)(2,1)}, u32[]{:S(2)}, u32[]{:S(2)}) collective-permute-start(bf16[256,1152]{1,0:T(8,128)(2,1)} %get-tuple-element.35), channel_id=1, source_target_pairs={{0,16},{4,20},{8,24},{12,28},{16,0},{20,4},{24,8},{28,12},{1,17},{... | collective-permute-start | bytes 1769480 | tf_op jit(solution)/shard_map/ppermute | solution.py:448
  87.1 0.5 collective-permute-start.13
  87.6 18.1 %all-to-all-done.1.refs_0_ = bf16[4,128,1024]{2,1,0:T(8,128)(2,1)} async-done(((bf16[4,128,1024]{2,1,0:T(8,128)(2,1)}), bf16[4,128,1024]{2,1,0:T(8,128)(2,1)}, u32[]{:S(2)}, u32[]{:S(2)}) %all-to-all-start.1) | async-done | bytes 1048608 | tf_op jit(solution)/shard_map/all_to_all | solution.py:452
  105.6 2.3 %shard_map.165 = bf16[128,4096]{1,0:T(8,128)(2,1)} custom-call(bf16[4,128,1024]{2,1,0:T(8,128)(2,1)} %all-to-all-done.1.refs_0_), custom_call_target="tpu_custom_call" | custom-call | tf_op jit(solution)/shard_map/pallas_call | solution.py:85
  107.9 0.0 collective-permute-done.11.refs_1_
  107.9 5.7 %collective-permute-done.12.refs_2_ = bf16[256,1152]{1,0:T(8,128)(2,1)} collective-permute-done((bf16[256,1152]{1,0:T(8,128)(2,1)}, bf16[256,1152]{1,0:T(8,128)(2,1)}, u32[]{:S(2)}, u32[]{:S(2)}) %collective-permute-start.12) | collective-permute-done | bytes 589856 | tf_op jit(solution)/shard_map/ppermute | solution.py:448
  113.6 0.0 collective-permute-done.13.refs_3_
  113.6 6.1 %shard_map.167 = (f32[1024,256]{1,0:T(8,128)}, f32[1024,256]{1,0:T(8,128)}, f32[1024,256]{1,0:T(8,128)}, f32[64,512]{1,0:T(8,128)}, f32[64,512]{1,0:T(8,128)}, /*index=5*/f32[64,512]{1,0:T(8,128)}) custom-call(bf16[256,1152]{1,0:T(8,128)(2,1)} %get-tuple-element.33.refs_0_, bf16[256,1152]{1,0:T(8,128)(2,1)} %collective-permute-done.11.refs_1_, ...), custom_call_target="tpu_custom_call" | custom-call | tf_op jit(solution)/shard_map/pallas_call | solution.py:85
Async XLA Ops:
  3.8 6.5 %copy-start = (bf16[1152,256]{1,0:T(8,128)(2,1)S(1)}, bf16[1152,256]{1,0:T(8,128)(2,1)}, u32[]{:S(2)}) copy-start(bf16[1152,256]{1,0:T(8,128)(2,1)} %get-tuple-element.26.refs_1_.refs_8_) | copy-start | bytes 1769476
  3.8 44.9 %all-to-all-start = ((bf16[4,400,512]{2,1,0:T(8,128)(2,1)}), bf16[4,400,512]{2,1,0:T(8,128)(2,1)}, u32[]{:S(2)}, u32[]{:S(2)}) async-start(bf16[4,400,512]{2,1,0:T(8,128)(2,1)} %get-tuple-element.25), calls=%async_computation | async-start | bytes 3276800 | tf_op jit(solution)/shard_map/all_to_all | solution.py:452
  10.3 17.2 %collective-permute-start.5 = (bf16[1152,256]{1,0:T(8,128)(2,1)S(1)}, bf16[1152,256]{1,0:T(8,128)(2,1)S(1)}, u32[]{:S(2)}, u32[]{:S(2)}) collective-permute-start(bf16[1152,256]{1,0:T(8,128)(2,1)S(1)} %copy-done), channel_id=1, source_target_pairs={{0,24},{4,28},{8,16},{12,20},{16,8},{20,12},{24,0},{28,4},{1,25},{... | collective-permute-start | bytes 1769480 | tf_op jit(solution)/shard_map/ppermute | solution.py:448
  12.7 25.9 %collective-permute-start.3 = (bf16[1152,256]{1,0:T(8,128)(2,1)S(1)}, bf16[1152,256]{1,0:T(8,128)(2,1)S(1)}, u32[]{:S(2)}, u32[]{:S(2)}) collective-permute-start(bf16[1152,256]{1,0:T(8,128)(2,1)S(1)} %copy-done), channel_id=1, source_target_pairs={{0,16},{4,20},{8,24},{12,28},{16,0},{20,4},{24,8},{28,12},{1,17},{... | collective-permute-start | bytes 1769480 | tf_op jit(solution)/shard_map/ppermute | solution.py:448
  13.2 25.5 %collective-permute-start.1 = (bf16[1152,256]{1,0:T(8,128)(2,1)S(1)}, bf16[1152,256]{1,0:T(8,128)(2,1)S(1)}, u32[]{:S(2)}, u32[]{:S(2)}) collective-permute-start(bf16[1152,256]{1,0:T(8,128)(2,1)S(1)} %copy-done), channel_id=1, source_target_pairs={{0,8},{4,12},{8,0},{12,4},{16,24},{20,28},{24,16},{28,20},{1,9},{5... | collective-permute-start | bytes 1769480 | tf_op jit(solution)/shard_map/ppermute | solution.py:448
  13.8 25.4 %collective-permute-start = (bf16[1152,256]{1,0:T(8,128)(2,1)S(1)}, bf16[1152,256]{1,0:T(8,128)(2,1)S(1)}, u32[]{:S(2)}, u32[]{:S(2)}) collective-permute-start(bf16[1152,256]{1,0:T(8,128)(2,1)S(1)} %copy-done), channel_id=1, source_target_pairs={{0,4},{4,0},{8,12},{12,8},{16,20},{20,16},{24,28},{28,24},{1,5},{5... | collective-permute-start | bytes 1769480 | tf_op jit(solution)/shard_map/ppermute | solution.py:448
  27.5 11.7 %copy-start.1 = (bf16[1152,256]{1,0:T(8,128)(2,1)}, bf16[1152,256]{1,0:T(8,128)(2,1)S(1)}, u32[]{:S(2)}) copy-start(bf16[1152,256]{1,0:T(8,128)(2,1)S(1)} %collective-permute-done.5.refs_7_.refs_14_) | copy-start | bytes 1769476
  27.5 11.7 %collective-permute-start.6 = (bf16[1152,256]{1,0:T(8,128)(2,1)S(1)}, bf16[1152,256]{1,0:T(8,128)(2,1)S(1)}, u32[]{:S(2)}, u32[]{:S(2)}) collective-permute-start(bf16[1152,256]{1,0:T(8,128)(2,1)S(1)} %collective-permute-done.5.refs_7_.refs_14_), channel_id=1, source_target_pairs={{0,4},{4,0},{8,12},{12,8},{16,20},{20,16},{24,28},{28,24},{1,5},{5... | collective-permute-start | bytes 1769480 | tf_op jit(solution)/shard_map/ppermute | solution.py:448
  38.6 0.8 copy-start.2
  38.6 2.0 %collective-permute-start.4 = (bf16[1152,256]{1,0:T(8,128)(2,1)S(1)}, bf16[1152,256]{1,0:T(8,128)(2,1)S(1)}, u32[]{:S(2)}, u32[]{:S(2)}) collective-permute-start(bf16[1152,256]{1,0:T(8,128)(2,1)S(1)} %collective-permute-done.3.refs_5_.refs_12_), channel_id=1, source_target_pairs={{0,4},{4,0},{8,12},{12,8},{16,20},{20,16},{24,28},{28,24},{1,5},{5... | collective-permute-start | bytes 1769480 | tf_op jit(solution)/shard_map/ppermute | solution.py:448
  38.7 1.9 %copy-start.3 = (bf16[1152,256]{1,0:T(8,128)(2,1)}, bf16[1152,256]{1,0:T(8,128)(2,1)S(1)}, u32[]{:S(2)}) copy-start(bf16[1152,256]{1,0:T(8,128)(2,1)S(1)} %collective-permute-done.1.refs_3_.refs_10_) | copy-start | bytes 1769476
  38.7 2.9 %collective-permute-start.2 = (bf16[1152,256]{1,0:T(8,128)(2,1)S(1)}, bf16[1152,256]{1,0:T(8,128)(2,1)}, u32[]{:S(2)}, u32[]{:S(2)}) collective-permute-start(bf16[1152,256]{1,0:T(8,128)(2,1)S(1)} %collective-permute-done.1.refs_3_.refs_10_), channel_id=1, source_target_pairs={{0,4},{4,0},{8,12},{12,8},{16,20},{20,16},{24,28},{28,24},{1,5},{5... | collective-permute-start | bytes 1769480 | tf_op jit(solution)/shard_map/ppermute | solution.py:448
  39.1 1.5 %copy-start.4 = (bf16[1152,256]{1,0:T(8,128)(2,1)}, bf16[1152,256]{1,0:T(8,128)(2,1)S(1)}, u32[]{:S(2)}) copy-start(bf16[1152,256]{1,0:T(8,128)(2,1)S(1)} %collective-permute-done.refs_2_.refs_9_) | copy-start | bytes 1769476
  39.4 1.2 copy-start.5
  40.6 0.8 copy-start.6
  57.7 6.8 %collective-permute-start.9 = (bf16[64,512]{1,0:T(8,128)(2,1)}, bf16[64,512]{1,0:T(8,128)(2,1)}, u32[]{:S(2)}, u32[]{:S(2)}) collective-permute-start(bf16[64,512]{1,0:T(8,128)(2,1)} %get-tuple-element.27.refs_0_), channel_id=1, source_target_pairs={{0,3},{1,2},{2,1},{3,0},{4,7},{5,6},{6,5},{7,4},{8,11},{9,10},{10,... | collective-permute-start | bytes 196616 | tf_op jit(solution)/shard_map/ppermute | solution.py:448
  59.2 6.6 %collective-permute-start.8 = (bf16[64,512]{1,0:T(8,128)(2,1)}, bf16[64,512]{1,0:T(8,128)(2,1)}, u32[]{:S(2)}, u32[]{:S(2)}) collective-permute-start(bf16[64,512]{1,0:T(8,128)(2,1)} %get-tuple-element.27.refs_0_), channel_id=1, source_target_pairs={{0,2},{1,3},{2,0},{3,1},{4,6},{5,7},{6,4},{7,5},{8,10},{9,11},{10,... | collective-permute-start | bytes 196616 | tf_op jit(solution)/shard_map/ppermute | solution.py:448
  59.2 6.6 %collective-permute-start.7 = (bf16[64,512]{1,0:T(8,128)(2,1)}, bf16[64,512]{1,0:T(8,128)(2,1)}, u32[]{:S(2)}, u32[]{:S(2)}) collective-permute-start(bf16[64,512]{1,0:T(8,128)(2,1)} %get-tuple-element.27.refs_0_), channel_id=1, source_target_pairs={{0,1},{1,0},{2,3},{3,2},{4,5},{5,4},{6,7},{7,6},{8,9},{9,8},{10,11... | collective-permute-start | bytes 196616 | tf_op jit(solution)/shard_map/ppermute | solution.py:448
  74.5 4.9 %collective-permute-start.10 = (bf16[4,256,1152]{2,1,0:T(8,128)(2,1)}, bf16[4,256,1152]{2,1,0:T(8,128)(2,1)}, u32[]{:S(2)}, u32[]{:S(2)}) collective-permute-start(bf16[4,256,1152]{2,1,0:T(8,128)(2,1)} %get-tuple-element.32), channel_id=1, source_target_pairs={{0,4},{4,0},{8,12},{12,8},{16,20},{20,16},{24,28},{28,24},{1,5},{5... | collective-permute-start | bytes 7077896 | tf_op jit(solution)/shard_map/ppermute | solution.py:448
  74.6 31.0 %all-to-all-start.1 = ((bf16[4,128,1024]{2,1,0:T(8,128)(2,1)}), bf16[4,128,1024]{2,1,0:T(8,128)(2,1)}, u32[]{:S(2)}, u32[]{:S(2)}) async-start(bf16[4,128,1024]{2,1,0:T(8,128)(2,1)} %bitcast.3), calls=%async_computation.1 | async-start | bytes 2097152 | tf_op jit(solution)/shard_map/all_to_all | solution.py:452
  84.0 23.9 %collective-permute-start.11 = (bf16[256,1152]{1,0:T(8,128)(2,1)}, bf16[256,1152]{1,0:T(8,128)(2,1)}, u32[]{:S(2)}, u32[]{:S(2)}) collective-permute-start(bf16[256,1152]{1,0:T(8,128)(2,1)} %get-tuple-element.34), channel_id=1, source_target_pairs={{0,8},{4,12},{8,0},{12,4},{16,24},{20,28},{24,16},{28,20},{1,9},{5... | collective-permute-start | bytes 1769480 | tf_op jit(solution)/shard_map/ppermute | solution.py:448
  85.6 28.0 %collective-permute-start.12 = (bf16[256,1152]{1,0:T(8,128)(2,1)}, bf16[256,1152]{1,0:T(8,128)(2,1)}, u32[]{:S(2)}, u32[]{:S(2)}) collective-permute-start(bf16[256,1152]{1,0:T(8,128)(2,1)} %get-tuple-element.35), channel_id=1, source_target_pairs={{0,16},{4,20},{8,24},{12,28},{16,0},{20,4},{24,8},{28,12},{1,17},{... | collective-permute-start | bytes 1769480 | tf_op jit(solution)/shard_map/ppermute | solution.py:448
  87.1 26.5 %collective-permute-start.13 = (bf16[256,1152]{1,0:T(8,128)(2,1)}, bf16[256,1152]{1,0:T(8,128)(2,1)}, u32[]{:S(2)}, u32[]{:S(2)}) collective-permute-start(bf16[256,1152]{1,0:T(8,128)(2,1)} %get-tuple-element.36), channel_id=1, source_target_pairs={{0,24},{4,28},{8,16},{12,20},{16,8},{20,12},{24,0},{28,4},{1,25},{... | collective-permute-start | bytes 1769480 | tf_op jit(solution)/shard_map/ppermute | solution.py:448

commit v12 on v10

--- a/solution.py
+++ b/solution.py
@@ -52,7 +52,7 @@
             copy.wait()
 
 
-def call(body, outs, ins, kinds, out_kinds, scratch=()):
+def call(body, outs, ins, kinds, out_kinds, scratch=(), aliases={}):
     single = not isinstance(outs, (list, tuple))
     outs = [outs] if single else list(outs)
     staged = [x for x, kind in zip(ins, kinds) if kind == "h"]
@@ -88,6 +88,7 @@
         in_specs=[HBM] * len(ins),
         out_specs=[HBM] * len(outs),
         scratch_shapes=buffers + list(scratch) + [DMA((count,))],
+        input_output_aliases=aliases,
         compiler_params=pltpu.CompilerParams(vmem_limit_bytes=FULL),
         cost_estimate=pl.CostEstimate(flops=0, bytes_accessed=0, transcendentals=0),
     )(*ins)
@@ -165,13 +166,8 @@
 
 
 def load_factors(a_blocks, a_all, sems):
-    columns = a_blocks[0].shape[1]
     copies = [
-        pltpu.make_async_copy(
-            block.at[pl.ds(0, a_all.shape[0])],
-            a_all.at[:, pl.ds(k * columns, columns)],
-            sems.at[k],
-        )
+        pltpu.make_async_copy(block.at[pl.ds(0, a_all.shape[1])], a_all.at[k], sems.at[k])
         for k, block in enumerate(a_blocks)
     ]
     for copy in copies:
@@ -256,7 +252,7 @@
         for k in range(owners):
             if r == 0:
                 copies[k].wait()
-            wide = dot(acts[at], a_all[:, k * columns : (k + 1) * columns])
+            wide = dot(acts[at], a_all[k])
             for q in range(columns // LANES):
                 hit = where == k * TEN_DEV + q * (LANES // ADAPTER_RANK)
                 low = low + jnp.where(hit, wide[:, q * LANES : (q + 1) * LANES], 0.0)
@@ -302,44 +298,51 @@
     return adapter_scale * ADAPTER_RANK ** (-0.5) * second
 
 
-def grads_step(owners, parity, own_rows, boths, label, acts, scaled, held, out, arrived, send, wait=None):
-    features = acts.shape[1]
+def grads_step(
+    owners, parity, own_rows, boths, label, acts, scaled, held, out, arrived, send, span, wait=None
+):
+    width = span[1] - span[0]
     keys = scaled.shape[1]
     columns = out.shape[1]
     down = adapter_scale * MODEL_WIDTH ** (-0.5)
-    second = second_grads(owners, parity, own_rows, boths, label, scaled, held)
+    ends = out.shape[2] > width
+    if ends:
+        second = second_grads(owners, parity, own_rows, boths, label, scaled, held)
     tall = down * total(boths, BACK, slice(None))
     ids = over(iota((columns, tall.shape[1]), 0), ADAPTER_RANK)
     tall = jnp.concatenate([tall] * (columns // ADAPTER_RANK), axis=0)
     for n in range(owners // 2):
-        grad = dot(spread(tall, ids, label[0:1], 2 * n + parity), acts[...])
+        rows = spread(tall, ids, label[0:1], 2 * n + parity)
+        grad = dot(rows, acts[:, span[0] : span[1]])
         if n == 0 and wait is not None:
             wait()
         if arrived is not None:
-            grad = grad + arrived[n, :, :features].astype(f32)
-        out[n, :, :features] = grad.astype(bf16)
-        for q in range(keys // LANES):
-            lines = slice(q * own_rows, (q + 1) * own_rows)
-            part = second[n * own_rows : (n + 1) * own_rows, q * LANES : (q + 1) * LANES]
-            if arrived is not None:
-                part = part + arrived[n, lines, features:].astype(f32)
-            out[n, lines, features:] = part.astype(bf16)
-        used = keys // LANES * own_rows
-        if used < columns:
-            out[n, used:, features:] = jnp.zeros((columns - used, LANES), bf16)
+            grad = grad + arrived[n, :, :width].astype(f32)
+        out[n, :, :width] = grad.astype(bf16)
+        if ends:
+            for q in range(keys // LANES):
+                lines = slice(q * own_rows, (q + 1) * own_rows)
+                part = second[n * own_rows : (n + 1) * own_rows, q * LANES : (q + 1) * LANES]
+                if arrived is not None:
+                    part = part + arrived[n, lines, width:].astype(f32)
+                out[n, lines, width:] = part.astype(bf16)
+            used = keys // LANES * own_rows
+            if used < columns:
+                out[n, used:, width:] = jnp.zeros((columns - used, LANES), bf16)
         send[n].start()
 
 
-def even_kernel(shards, owners, own_rows, io, *refs):
+def even_kernel(shards, owners, own_rows, span, io, *refs):
     boths, (label, acts, scaled, arrived) = refs[:shards], refs[shards : shards + 4]
     outs = refs[shards + 4 : shards + 4 + owners // 2]
     held, made, got, sems, got_sem = refs[shards + 4 + owners // 2 :]
-    late = pltpu.make_async_copy(arrived, got, got_sem)
+    lanes = pl.ds(span[0], got.shape[2])
+    late = pltpu.make_async_copy(arrived.at[:, :, lanes], got, got_sem)
     late.start()
     send = [pltpu.make_async_copy(made.at[n], outs[n], sems.at[n]) for n in range(owners // 2)]
     io.ready()
     grads_step(
-        owners, 0, own_rows, boths, label, acts, scaled, held, made, got, send, late.wait
+        owners, 0, own_rows, boths, label, acts, scaled, held, made, got, send, span, late.wait
     )
     for copy in send:
         copy.wait()
@@ -354,10 +357,11 @@
     copies = load_factors(a_blocks, a_all, sems)
     send = [pltpu.make_async_copy(made.at[n], odd.at[n], odd_sems.at[n]) for n in range(owners // 2)]
     io.ready()
-    grads_step(owners, 1, own_rows, boths, label, acts, scaled, held, made, None, send)
+    span = (0, acts.shape[1])
+    grads_step(owners, 1, own_rows, boths, label, acts, scaled, held, made, None, send, span)
     rows, features = part.shape
     step = min(ROW_STEP, rows)
-    width = a_all.shape[1]
+    width = back_wide.shape[1]
     chunk = min(256, features)
     for r in range(0, rows, step):
         at = slice(r, r + step)
@@ -374,7 +378,8 @@
                 copy.wait()
         for c in range(0, features, chunk):
             base = dot(scaled[at], weight[c : c + chunk], 1, 1).astype(bf16)
-            side = dot(back_wide[...], a_all[c : c + chunk], 1, 1).astype(bf16)
+            factor = [a_all[k, c : c + chunk] for k in range(owners)]
+            side = dot(back_wide[...], jnp.concatenate(factor, axis=1), 1, 1).astype(bf16)
             part[at, c : c + chunk] = (base.astype(f32) + side.astype(f32)).astype(bf16)
             copy = pltpu.make_async_copy(
                 part.at[pl.ds(r, step), pl.ds(c, chunk)],
@@ -387,38 +392,51 @@
         copy.wait()
 
 
-def adam_kernel(count, own_rows, io, *refs):
-    grads, firsts = refs[:count], refs[count : count + 3]
-    seconds, outs = refs[count + 3 : count + 6], refs[count + 6 : count + 12]
-    made, sems = refs[count + 12 : count + 15], refs[count + 15]
-    features, _ = firsts[0].shape
-    keys = seconds[0].shape[1]
+def adam_kernel(count, own_rows, span, io, *refs):
+    grads, firsts, refs = refs[:count], refs[count : count + 3], refs[count + 3 :]
+    held, made, in_sems, sems = refs[-4:]
+    width = span[1] - span[0]
+    ends = grads[0].shape[1] > width
+    at = pl.ds(span[0], width)
+    seconds = refs[:3] if ends else ()
+    outs = refs[:-4][-6:] if ends else refs[:-4]
+    loads = [
+        pltpu.make_async_copy(firsts[m].at[at], held.at[m], in_sems.at[m]) for m in range(3)
+    ]
+    for copy in loads:
+        copy.start()
+
+    def summed(lanes):
+        value = grads[0][:, lanes].astype(f32)
+        for part in grads[1:]:
+            value = value + part[:, lanes].astype(f32)
+        return value
+
     io.ready()
-
-    def summed(at):
-        value = grads[0][:, at].astype(f32)
-        for part in grads[1:]:
-            value = value + part[:, at].astype(f32)
-        return value
-
+    for copy in loads:
+        copy.wait()
     copies = []
-    block = min(256, features)
-    for n, c in enumerate(range(0, features, block)):
-        at = slice(c, c + block)
-        grad = jnp.transpose(summed(at))
-        for m, value in enumerate(adam_step(*[x[at] for x in firsts], grad)):
-            made[m][at] = value
-            rows = pl.ds(c, block)
+    block = min(256, width)
+    for n, c in enumerate(range(0, width, block)):
+        rows = slice(c, c + block)
+        grad = jnp.transpose(summed(rows))
+        for m, value in enumerate(adam_step(*[held[m, rows] for m in range(3)], grad)):
+            made[m, rows] = value
             copies.append(
-                pltpu.make_async_copy(made[m].at[rows], outs[m].at[rows], sems.at[m, n])
+                pltpu.make_async_copy(
+                    made.at[m, pl.ds(c, block)],
+                    outs[m].at[pl.ds(span[0] + c, block)],
+                    sems.at[m, n],
+                )
             )
             copies[-1].start()
-    grad = summed(slice(features, features + LANES))
-    for q in range(keys // LANES):
-        at = slice(q * LANES, (q + 1) * LANES)
-        part = grad[q * own_rows : (q + 1) * own_rows]
-        for out, value in zip(outs[3:], adam_step(*[x[:, at] for x in seconds], part)):
-            out[:, at] = value
+    if ends:
+        grad = summed(slice(width, width + LANES))
+        for q in range(seconds[0].shape[1] // LANES):
+            lanes = slice(q * LANES, (q + 1) * LANES)
+            part = grad[q * own_rows : (q + 1) * own_rows]
+            for out, value in zip(outs[3:], adam_step(*[x[:, lanes] for x in seconds], part)):
+                out[:, lanes] = value
     for copy in copies:
         copy.wait()
 
@@ -478,7 +496,7 @@
         blocks += [block, swap(block, "dp", 1)]
 
     step = min(ROW_STEP, rows)
-    factors = pltpu.VMEM((features, owners * columns), bf16)
+    factors = pltpu.VMEM((owners, features, columns), bf16)
     acts_part, scaled, label, both = call(
         functools.partial(open_kernel, owners, own_rows),
         [
@@ -523,23 +541,53 @@
     grad_input = call(
         lay_kernel, shape((row_count, shards * features)), (returned,), "h", "h"
     )
-    even = call(
-        functools.partial(even_kernel, shards, owners, own_rows),
-        [shape((columns, features + LANES))] * (owners // 2),
-        (*boths, label, acts_part, scaled, swap(odd, "dp", 1)),
-        "h" * (shards + 3) + "r",
-        "r" * (owners // 2),
-        held + [pltpu.VMEM(grads.shape, bf16), DMA((owners // 2,)), DMA],
-    )
-    sums = [even[0]] + [swap(even[n], "dp", 2 * n) for n in range(1, owners // 2)]
-
+    arrived = swap(odd, "dp", 1)
+    count = owners // 2
+    half = features // 2
+    sums = []
+    for first in (0, half):
+        lanes = half if first == 0 else half + LANES
+        even = call(
+            functools.partial(even_kernel, shards, owners, own_rows, (first, first + half)),
+            [shape((columns, lanes))] * count,
+            (*boths, label, acts_part, scaled, arrived),
+            "h" * (shards + 3) + "r",
+            "r" * count,
+            [
+                held[0],
+                pltpu.VMEM((count, columns, lanes), bf16),
+                pltpu.VMEM((count, columns, lanes), bf16),
+                DMA((count,)),
+                DMA,
+            ],
+        )
+        if first == 0:
+            arrived, *even = lax.optimization_barrier((arrived, *even))
+        sums.append([even[0]] + [swap(even[n], "dp", 2 * n) for n in range(1, count)])
+
+    firsts = (a_param, a_moment, a_second)
+    space = [
+        pltpu.VMEM((3, half, columns), f32),
+        pltpu.VMEM((3, half, columns), f32),
+        DMA((3,)),
+        DMA((3, half // min(256, half))),
+    ]
+    begun = call(
+        functools.partial(adam_kernel, count, own_rows, (0, half)),
+        [shape(a_param.shape, f32)] * 3,
+        (*sums[0], *firsts),
+        "h" * count + "rrr",
+        "rrr",
+        space,
+    )
     new = call(
-        functools.partial(adam_kernel, owners // 2, own_rows),
+        functools.partial(adam_kernel, count, own_rows, (half, features)),
         [shape(a_param.shape, f32)] * 3 + [shape(b_param.shape, f32)] * 3,
-        (*sums, a_param, a_moment, a_second, b_param, b_moment, b_second),
-        "h" * (owners // 2 + 6),
+        (*sums[1], *firsts, b_param, b_moment, b_second, *begun),
+        "h" * count + "rrr" + "hhh" + "rrr",
         "rrrhhh",
-        [pltpu.VMEM(a_param.shape, f32)] * 3 + [DMA((3, features // min(256, features)))],
+        space,
+        {count + 6 + m: m for m in range(3)},
     )
     return (grad_input, *new)
 

time: 120 us -> 125 us (1.042)
  starting transfers between devices: 22.9 us -> 27.8 us
  waiting for transfers between devices: 61.2 us -> 56.6 us
  Pallas kernels: 33.3 us -> 37.6 us
    all_to_all x2, waiting for transfers between devices: 25.2 us -> 17.9 us  [exchange(): lax.all_to_all(blocks, axis, split_axis=0, concat_axis=0, tiled=True, axi...]
    ppermute x14 -> x17, starting transfers between devices: 12 us -> 16.9 us  [swap(): return lax.ppermute(block, axis, [(i, i ^ bits) for i in range(size)])]
    pallas_call x6 -> x8, Pallas kernels: 33.3 us -> 37.6 us  [call(): pl.pallas_call(kernel, out_shape=outs, in_specs=[HBM] * len(ins), out_spe...]
    ppermute x14 -> x17, waiting for transfers between devices: 36 us -> 38.7 us  [swap(): return lax.ppermute(block, axis, [(i, i ^ bits) for i in range(size)])]
  transfers between devices with their start and end apart: 16 -> 19, of which waited for: 11 -> 11; matrix products, arithmetic and copies ran while one was open for 0% -> 0% of each run, Pallas kernels for 6% -> 10%
where the time goes in v12:
time: 125 us; the launch traced here: 124 us
  waiting for transfers between devices  56.6 us (45%)
  Pallas kernels  37.6 us (30%)
  starting transfers between devices  27.8 us (22%)
    ppermute x17, waiting for transfers between devices, swap(): return lax.ppermute(block, axis, [(i, i ^ bits) for i in range(size)])  38.7 us
    pallas_call x8, Pallas kernels, call(): pl.pallas_call(kernel, out_shape=outs, in_specs=[HBM] * len(ins), out_spe...  37.6 us
    all_to_all x2, waiting for transfers between devices, exchange(): lax.all_to_all(blocks, axis, split_axis=0, concat_axis=0, tiled=True, axi...  17.9 us
    ppermute x17, starting transfers between devices, swap(): return lax.ppermute(block, axis, [(i, i ^ bits) for i in range(size)])  16.9 us
    all_to_all x2, starting transfers between devices, exchange(): lax.all_to_all(blocks, axis, split_axis=0, concat_axis=0, tiled=True, axi...  10.9 us
  transfers between devices with their start and end apart: 19, of which 11 were waited for; matrix products, arithmetic and copies ran while one was open for 0% of the time, Pallas kernels for 10%

profile of v12, /device:TPU:0, one launch (start us, length us, event | category | flops | bytes accessed | tf_op | source)
XLA Modules:
  0.0 124.1 jit_solution(2568360770925706033)
XLA Ops:
  0.6 3.2 %shard_map.162 = (bf16[4,400,512]{2,1,0:T(8,128)(2,1)}, bf16[1152,256]{1,0:T(8,128)(2,1)}) custom-call(bf16[128,4096]{1,0:T(8,128)(2,1)} %refs_0_.1, bf16[128,512]{1,0:T(8,128)(2,1)} %refs_1_.1, s32[1,128]{1,0:T(1,128)} %bitcast.4, s32[1,128]{1,0:T(1,128)} %bitcast.5, f32[1024,256]{1,0:T(8,128)} %refs_4_.5, f32[64,512]{1,0:T(8,128)} %refs_7_.3), custom_call_target="tpu_custom_call" | custom-call | tf_op jit(solution)/shard_map/pallas_call | solution.py:85
  3.8 0.0 copy-start
  3.8 6.5 %all-to-all-start = ((bf16[4,400,512]{2,1,0:T(8,128)(2,1)}), bf16[4,400,512]{2,1,0:T(8,128)(2,1)}, u32[]{:S(2)}, u32[]{:S(2)}) async-start(bf16[4,400,512]{2,1,0:T(8,128)(2,1)} %get-tuple-element.37), calls=%async_computation | async-start | bytes 3276800 | tf_op jit(solution)/shard_map/all_to_all | solution.py:457
  10.3 0.0 copy-done
  10.3 2.4 %collective-permute-start.5 = (bf16[1152,256]{1,0:T(8,128)(2,1)S(1)}, bf16[1152,256]{1,0:T(8,128)(2,1)S(1)}, u32[]{:S(2)}, u32[]{:S(2)}) collective-permute-start(bf16[1152,256]{1,0:T(8,128)(2,1)S(1)} %copy-done), channel_id=1, source_target_pairs={{0,24},{4,28},{8,16},{12,20},{16,8},{20,12},{24,0},{28,4},{1,25},{... | collective-permute-start | bytes 1769480 | tf_op jit(solution)/shard_map/ppermute | solution.py:453
  12.7 0.5 collective-permute-start.3
  13.2 0.5 collective-permute-start.1
  13.8 0.0 collective-permute-start
  13.8 13.7 %collective-permute-done.5.refs_7_.refs_14_ = bf16[1152,256]{1,0:T(8,128)(2,1)S(1)} collective-permute-done((bf16[1152,256]{1,0:T(8,128)(2,1)S(1)}, bf16[1152,256]{1,0:T(8,128)(2,1)S(1)}, u32[]{:S(2)}, u32[]{:S(2)}) %collective-permute-start.5) | collective-permute-done | bytes 589856 | tf_op jit(solution)/shard_map/ppermute | solution.py:453
  27.5 0.0 copy-start.1
  27.5 0.0 collective-permute-start.6
  27.5 11.1 %collective-permute-done.3.refs_5_.refs_12_ = bf16[1152,256]{1,0:T(8,128)(2,1)S(1)} collective-permute-done((bf16[1152,256]{1,0:T(8,128)(2,1)S(1)}, bf16[1152,256]{1,0:T(8,128)(2,1)S(1)}, u32[]{:S(2)}, u32[]{:S(2)}) %collective-permute-start.3) | collective-permute-done | bytes 589856 | tf_op jit(solution)/shard_map/ppermute | solution.py:453
  38.6 0.0 copy-start.2
  38.6 0.0 collective-permute-start.4
  38.6 0.1 collective-permute-done.1.refs_3_.refs_10_
  38.7 0.0 copy-start.3
  38.7 0.4 collective-permute-start.2
  39.1 0.0 collective-permute-done.refs_2_.refs_9_
  39.1 0.0 copy-done.1
  39.1 0.0 copy-start.4
  39.1 0.0 collective-permute-done.6.refs_8_.refs_15_
  39.1 0.3 copy-done.2
  39.4 0.0 copy-start.5
  39.4 1.2 collective-permute-done.4.refs_6_.refs_13_
  40.6 0.0 copy-done.3
  40.6 0.0 copy-done.4
  40.6 0.0 copy-done.5
  40.6 0.0 copy-start.6
  40.6 0.8 copy-done.6
  41.4 0.1 collective-permute-done.2.refs_4_.refs_11_
  41.6 7.2 %all-to-all-done.refs_0_ = bf16[4,400,512]{2,1,0:T(8,128)(2,1)} async-done(((bf16[4,400,512]{2,1,0:T(8,128)(2,1)}), bf16[4,400,512]{2,1,0:T(8,128)(2,1)}, u32[]{:S(2)}, u32[]{:S(2)}) %all-to-all-start) | async-done | bytes 1638432 | tf_op jit(solution)/shard_map/all_to_all | solution.py:457
  48.7 8.9 %shard_map.163 = (bf16[512,1024]{1,0:T(8,128)(2,1)}, bf16[512,512]{1,0:T(8,128)(2,1)}, s32[8,512]{1,0:T(8,128)}, bf16[64,512]{1,0:T(8,128)(2,1)}) custom-call(bf16[4,400,512]{2,1,0:T(8,128)(2,1)} %all-to-all-done.refs_0_, bf16[1152,256]{1,0:T(8,128)(2,1)} %get-tuple-element.38.refs_1_.refs_8_, bf16[1152,256]{1,0:T(8,128)(2,1)} %copy-done.4, ...), custom_call_target="tpu_custom_call" | custom-call | tf_op jit(solution)/shard_map/pallas_call | solution.py:85
  57.7 1.5 %collective-permute-start.9 = (bf16[64,512]{1,0:T(8,128)(2,1)}, bf16[64,512]{1,0:T(8,128)(2,1)}, u32[]{:S(2)}, u32[]{:S(2)}) collective-permute-start(bf16[64,512]{1,0:T(8,128)(2,1)} %get-tuple-element.39.refs_0_), channel_id=1, source_target_pairs={{0,3},{1,2},{2,1},{3,0},{4,7},{5,6},{6,5},{7,4},{8,11},{9,10},{10,... | collective-permute-start | bytes 196616 | tf_op jit(solution)/shard_map/ppermute | solution.py:453
  59.2 0.0 collective-permute-start.8
  59.2 2.9 %collective-permute-start.7 = (bf16[64,512]{1,0:T(8,128)(2,1)}, bf16[64,512]{1,0:T(8,128)(2,1)}, u32[]{:S(2)}, u32[]{:S(2)}) collective-permute-start(bf16[64,512]{1,0:T(8,128)(2,1)} %get-tuple-element.39.refs_0_), channel_id=1, source_target_pairs={{0,1},{1,0},{2,3},{3,2},{4,5},{5,4},{6,7},{7,6},{8,9},{9,8},{10,11... | collective-permute-start | bytes 196616 | tf_op jit(solution)/shard_map/ppermute | solution.py:453
  62.1 2.3 %collective-permute-done.9.refs_3_ = bf16[64,512]{1,0:T(8,128)(2,1)} collective-permute-done((bf16[64,512]{1,0:T(8,128)(2,1)}, bf16[64,512]{1,0:T(8,128)(2,1)}, u32[]{:S(2)}, u32[]{:S(2)}) %collective-permute-start.9) | collective-permute-done | bytes 65568 | tf_op jit(solution)/shard_map/ppermute | solution.py:453
  64.4 1.3 %collective-permute-done.8.refs_2_ = bf16[64,512]{1,0:T(8,128)(2,1)} collective-permute-done((bf16[64,512]{1,0:T(8,128)(2,1)}, bf16[64,512]{1,0:T(8,128)(2,1)}, u32[]{:S(2)}, u32[]{:S(2)}) %collective-permute-start.8) | collective-permute-done | bytes 65568 | tf_op jit(solution)/shard_map/ppermute | solution.py:453
  65.8 0.0 collective-permute-done.7.refs_1_
  65.8 8.8 %shard_map.164 = (bf16[4,256,1152]{2,1,0:T(8,128)(2,1)}, bf16[512,1024]{1,0:T(8,128)(2,1)}) custom-call(bf16[64,512]{1,0:T(8,128)(2,1)} %get-tuple-element.39.refs_0_, bf16[64,512]{1,0:T(8,128)(2,1)} %collective-permute-done.7.refs_1_, bf16[64,512]{1,0:T(8,128)(2,1)} %collective-permute-done.8.refs_2_, bf16[64,512]{1,0:T(8,128)(2,1)} %collective-permute-done.9.refs_3_, ...), custom_call_target="tpu_custom_call" | custom-call | tf_op jit(solution)/shard_map/pallas_call | solution.py:85
  74.5 0.1 collective-permute-start.10
  74.6 4.4 %all-to-all-start.1 = ((bf16[4,128,1024]{2,1,0:T(8,128)(2,1)}), bf16[4,128,1024]{2,1,0:T(8,128)(2,1)}, u32[]{:S(2)}, u32[]{:S(2)}) async-start(bf16[4,128,1024]{2,1,0:T(8,128)(2,1)} %bitcast.3), calls=%async_computation.1 | async-start | bytes 2097152 | tf_op jit(solution)/shard_map/all_to_all | solution.py:457
  79.1 0.4 collective-permute-done.10.refs_7_
  79.5 3.4 %shard_map.166 = (bf16[256,512]{1,0:T(8,128)(2,1)}, bf16[256,512]{1,0:T(8,128)(2,1)}, bf16[256,512]{1,0:T(8,128)(2,1)}, bf16[256,512]{1,0:T(8,128)(2,1)}) custom-call(bf16[64,512]{1,0:T(8,128)(2,1)} %get-tuple-element.39.refs_0_, bf16[64,512]{1,0:T(8,128)(2,1)} %collective-permute-done.7.refs_1_, bf16[64,512]{1,0:T(8,128)(2,1)} %collective-permute-done.8.refs_2_, ...), custom_call_target="tpu_custom_call" | custom-call | tf_op jit(solution)/shard_map/pallas_call | solution.py:85
  82.9 1.6 %collective-permute-start.14 = (bf16[256,512]{1,0:T(8,128)(2,1)}, bf16[256,512]{1,0:T(8,128)(2,1)}, u32[]{:S(2)}, u32[]{:S(2)}) collective-permute-start(bf16[256,512]{1,0:T(8,128)(2,1)} %get-tuple-element.55), channel_id=1, source_target_pairs={{0,8},{4,12},{8,0},{12,4},{16,24},{20,28},{24,16},{28,20},{1,9},{5... | collective-permute-start | bytes 786440 | tf_op jit(solution)/shard_map/ppermute | solution.py:453
  84.4 3.5 %shard_map.167 = (bf16[256,640]{1,0:T(8,128)(2,1)}, bf16[256,640]{1,0:T(8,128)(2,1)}, bf16[256,640]{1,0:T(8,128)(2,1)}, bf16[256,640]{1,0:T(8,128)(2,1)}) custom-call(bf16[64,512]{1,0:T(8,128)(2,1)} %get-tuple-element.39.refs_0_, bf16[64,512]{1,0:T(8,128)(2,1)} %collective-permute-done.7.refs_1_, bf16[64,512]{1,0:T(8,128)(2,1)} %collective-permute-done.8.refs_2_, ...), custom_call_target="tpu_custom_call" | custom-call | tf_op jit(solution)/shard_map/pallas_call | solution.py:85
  87.9 0.6 collective-permute-start.11
  88.5 1.5 %collective-permute-start.12 = (bf16[256,640]{1,0:T(8,128)(2,1)}, bf16[256,640]{1,0:T(8,128)(2,1)}, u32[]{:S(2)}, u32[]{:S(2)}) collective-permute-start(bf16[256,640]{1,0:T(8,128)(2,1)} %get-tuple-element.52), channel_id=1, source_target_pairs={{0,16},{4,20},{8,24},{12,28},{16,0},{20,4},{24,8},{28,12},{1,17},{... | collective-permute-start | bytes 983048 | tf_op jit(solution)/shard_map/ppermute | solution.py:453
  90.0 1.5 %collective-permute-start.13 = (bf16[256,640]{1,0:T(8,128)(2,1)}, bf16[256,640]{1,0:T(8,128)(2,1)}, u32[]{:S(2)}, u32[]{:S(2)}) collective-permute-start(bf16[256,640]{1,0:T(8,128)(2,1)} %get-tuple-element.53), channel_id=1, source_target_pairs={{0,24},{4,28},{8,16},{12,20},{16,8},{20,12},{24,0},{28,4},{1,25},{... | collective-permute-start | bytes 983048 | tf_op jit(solution)/shard_map/ppermute | solution.py:453
  91.5 1.5 %collective-permute-start.15 = (bf16[256,512]{1,0:T(8,128)(2,1)}, bf16[256,512]{1,0:T(8,128)(2,1)}, u32[]{:S(2)}, u32[]{:S(2)}) collective-permute-start(bf16[256,512]{1,0:T(8,128)(2,1)} %get-tuple-element.56), channel_id=1, source_target_pairs={{0,16},{4,20},{8,24},{12,28},{16,0},{20,4},{24,8},{28,12},{1,17},{... | collective-permute-start | bytes 786440 | tf_op jit(solution)/shard_map/ppermute | solution.py:453
  93.0 0.0 collective-permute-done.14.refs_1_
  93.0 1.8 %collective-permute-start.16 = (bf16[256,512]{1,0:T(8,128)(2,1)}, bf16[256,512]{1,0:T(8,128)(2,1)}, u32[]{:S(2)}, u32[]{:S(2)}) collective-permute-start(bf16[256,512]{1,0:T(8,128)(2,1)} %get-tuple-element.57), channel_id=1, source_target_pairs={{0,24},{4,28},{8,16},{12,20},{16,8},{20,12},{24,0},{28,4},{1,25},{... | collective-permute-start | bytes 786440 | tf_op jit(solution)/shard_map/ppermute | solution.py:453
  94.8 10.8 %all-to-all-done.1.refs_0_ = bf16[4,128,1024]{2,1,0:T(8,128)(2,1)} async-done(((bf16[4,128,1024]{2,1,0:T(8,128)(2,1)}), bf16[4,128,1024]{2,1,0:T(8,128)(2,1)}, u32[]{:S(2)}, u32[]{:S(2)}) %all-to-all-start.1) | async-done | bytes 1048608 | tf_op jit(solution)/shard_map/all_to_all | solution.py:457
  105.6 2.3 %shard_map.165 = bf16[128,4096]{1,0:T(8,128)(2,1)} custom-call(bf16[4,128,1024]{2,1,0:T(8,128)(2,1)} %all-to-all-done.1.refs_0_), custom_call_target="tpu_custom_call" | custom-call | tf_op jit(solution)/shard_map/pallas_call | solution.py:85
  107.9 8.4 %collective-permute-done.15.refs_2_ = bf16[256,512]{1,0:T(8,128)(2,1)} collective-permute-done((bf16[256,512]{1,0:T(8,128)(2,1)}, bf16[256,512]{1,0:T(8,128)(2,1)}, u32[]{:S(2)}, u32[]{:S(2)}) %collective-permute-start.15) | collective-permute-done | bytes 262176 | tf_op jit(solution)/shard_map/ppermute | solution.py:453
  116.3 0.0 collective-permute-done.16.refs_3_
  116.3 3.3 %shard_map.168 = (f32[1024,256]{1,0:T(8,128)}, f32[1024,256]{1,0:T(8,128)}, f32[1024,256]{1,0:T(8,128)}) custom-call(bf16[256,512]{1,0:T(8,128)(2,1)} %get-tuple-element.54.refs_0_, bf16[256,512]{1,0:T(8,128)(2,1)} %collective-permute-done.14.refs_1_, bf16[256,512]{1,0:T(8,128)(2,1)} %collective-permute-done.15.refs_2_, ...), custom_call_target="tpu_custom_call" | custom-call | tf_op jit(solution)/shard_map/pallas_call | solution.py:85
  119.6 0.0 collective-permute-done.11.refs_1_
  119.6 0.0 collective-permute-done.12.refs_2_
  119.6 0.0 collective-permute-done.13.refs_3_
  119.6 4.4 %shard_map.169 = (f32[1024,256]{1,0:T(8,128)}, f32[1024,256]{1,0:T(8,128)}, f32[1024,256]{1,0:T(8,128)}, f32[64,512]{1,0:T(8,128)}, f32[64,512]{1,0:T(8,128)}, /*index=5*/f32[64,512]{1,0:T(8,128)}) custom-call(bf16[256,640]{1,0:T(8,128)(2,1)} %get-tuple-element.50.refs_0_, ...), custom_call_target="tpu_custom_call", output_to_operand_aliasing={{0}: (10, {}), {1}: (11, {}), {2}: (12, {})} | custom-call | tf_op jit(solution)/shard_map/pallas_call | solution.py:85
Async XLA Ops:
  3.8 6.5 %copy-start = (bf16[1152,256]{1,0:T(8,128)(2,1)S(1)}, bf16[1152,256]{1,0:T(8,128)(2,1)}, u32[]{:S(2)}) copy-start(bf16[1152,256]{1,0:T(8,128)(2,1)} %get-tuple-element.38.refs_1_.refs_8_) | copy-start | bytes 1769476
  3.8 44.9 %all-to-all-start = ((bf16[4,400,512]{2,1,0:T(8,128)(2,1)}), bf16[4,400,512]{2,1,0:T(8,128)(2,1)}, u32[]{:S(2)}, u32[]{:S(2)}) async-start(bf16[4,400,512]{2,1,0:T(8,128)(2,1)} %get-tuple-element.37), calls=%async_computation | async-start | bytes 3276800 | tf_op jit(solution)/shard_map/all_to_all | solution.py:457
  10.3 17.2 %collective-permute-start.5 = (bf16[1152,256]{1,0:T(8,128)(2,1)S(1)}, bf16[1152,256]{1,0:T(8,128)(2,1)S(1)}, u32[]{:S(2)}, u32[]{:S(2)}) collective-permute-start(bf16[1152,256]{1,0:T(8,128)(2,1)S(1)} %copy-done), channel_id=1, source_target_pairs={{0,24},{4,28},{8,16},{12,20},{16,8},{20,12},{24,0},{28,4},{1,25},{... | collective-permute-start | bytes 1769480 | tf_op jit(solution)/shard_map/ppermute | solution.py:453
  12.7 25.9 %collective-permute-start.3 = (bf16[1152,256]{1,0:T(8,128)(2,1)S(1)}, bf16[1152,256]{1,0:T(8,128)(2,1)S(1)}, u32[]{:S(2)}, u32[]{:S(2)}) collective-permute-start(bf16[1152,256]{1,0:T(8,128)(2,1)S(1)} %copy-done), channel_id=1, source_target_pairs={{0,16},{4,20},{8,24},{12,28},{16,0},{20,4},{24,8},{28,12},{1,17},{... | collective-permute-start | bytes 1769480 | tf_op jit(solution)/shard_map/ppermute | solution.py:453
  13.2 25.5 %collective-permute-start.1 = (bf16[1152,256]{1,0:T(8,128)(2,1)S(1)}, bf16[1152,256]{1,0:T(8,128)(2,1)S(1)}, u32[]{:S(2)}, u32[]{:S(2)}) collective-permute-start(bf16[1152,256]{1,0:T(8,128)(2,1)S(1)} %copy-done), channel_id=1, source_target_pairs={{0,8},{4,12},{8,0},{12,4},{16,24},{20,28},{24,16},{28,20},{1,9},{5... | collective-permute-start | bytes 1769480 | tf_op jit(solution)/shard_map/ppermute | solution.py:453
  13.8 25.4 %collective-permute-start = (bf16[1152,256]{1,0:T(8,128)(2,1)S(1)}, bf16[1152,256]{1,0:T(8,128)(2,1)S(1)}, u32[]{:S(2)}, u32[]{:S(2)}) collective-permute-start(bf16[1152,256]{1,0:T(8,128)(2,1)S(1)} %copy-done), channel_id=1, source_target_pairs={{0,4},{4,0},{8,12},{12,8},{16,20},{20,16},{24,28},{28,24},{1,5},{5... | collective-permute-start | bytes 1769480 | tf_op jit(solution)/shard_map/ppermute | solution.py:453
  27.5 11.7 %copy-start.1 = (bf16[1152,256]{1,0:T(8,128)(2,1)}, bf16[1152,256]{1,0:T(8,128)(2,1)S(1)}, u32[]{:S(2)}) copy-start(bf16[1152,256]{1,0:T(8,128)(2,1)S(1)} %collective-permute-done.5.refs_7_.refs_14_) | copy-start | bytes 1769476
  27.5 11.7 %collective-permute-start.6 = (bf16[1152,256]{1,0:T(8,128)(2,1)S(1)}, bf16[1152,256]{1,0:T(8,128)(2,1)S(1)}, u32[]{:S(2)}, u32[]{:S(2)}) collective-permute-start(bf16[1152,256]{1,0:T(8,128)(2,1)S(1)} %collective-permute-done.5.refs_7_.refs_14_), channel_id=1, source_target_pairs={{0,4},{4,0},{8,12},{12,8},{16,20},{20,16},{24,28},{28,24},{1,5},{5... | collective-permute-start | bytes 1769480 | tf_op jit(solution)/shard_map/ppermute | solution.py:453
  38.6 0.8 copy-start.2
  38.6 2.0 %collective-permute-start.4 = (bf16[1152,256]{1,0:T(8,128)(2,1)S(1)}, bf16[1152,256]{1,0:T(8,128)(2,1)S(1)}, u32[]{:S(2)}, u32[]{:S(2)}) collective-permute-start(bf16[1152,256]{1,0:T(8,128)(2,1)S(1)} %collective-permute-done.3.refs_5_.refs_12_), channel_id=1, source_target_pairs={{0,4},{4,0},{8,12},{12,8},{16,20},{20,16},{24,28},{28,24},{1,5},{5... | collective-permute-start | bytes 1769480 | tf_op jit(solution)/shard_map/ppermute | solution.py:453
  38.7 1.9 %copy-start.3 = (bf16[1152,256]{1,0:T(8,128)(2,1)}, bf16[1152,256]{1,0:T(8,128)(2,1)S(1)}, u32[]{:S(2)}) copy-start(bf16[1152,256]{1,0:T(8,128)(2,1)S(1)} %collective-permute-done.1.refs_3_.refs_10_) | copy-start | bytes 1769476
  38.7 2.9 %collective-permute-start.2 = (bf16[1152,256]{1,0:T(8,128)(2,1)S(1)}, bf16[1152,256]{1,0:T(8,128)(2,1)}, u32[]{:S(2)}, u32[]{:S(2)}) collective-permute-start(bf16[1152,256]{1,0:T(8,128)(2,1)S(1)} %collective-permute-done.1.refs_3_.refs_10_), channel_id=1, source_target_pairs={{0,4},{4,0},{8,12},{12,8},{16,20},{20,16},{24,28},{28,24},{1,5},{5... | collective-permute-start | bytes 1769480 | tf_op jit(solution)/shard_map/ppermute | solution.py:453
  39.1 1.5 %copy-start.4 = (bf16[1152,256]{1,0:T(8,128)(2,1)}, bf16[1152,256]{1,0:T(8,128)(2,1)S(1)}, u32[]{:S(2)}) copy-start(bf16[1152,256]{1,0:T(8,128)(2,1)S(1)} %collective-permute-done.refs_2_.refs_9_) | copy-start | bytes 1769476
  39.4 1.2 copy-start.5
  40.6 0.8 copy-start.6
  57.7 6.8 %collective-permute-start.9 = (bf16[64,512]{1,0:T(8,128)(2,1)}, bf16[64,512]{1,0:T(8,128)(2,1)}, u32[]{:S(2)}, u32[]{:S(2)}) collective-permute-start(bf16[64,512]{1,0:T(8,128)(2,1)} %get-tuple-element.39.refs_0_), channel_id=1, source_target_pairs={{0,3},{1,2},{2,1},{3,0},{4,7},{5,6},{6,5},{7,4},{8,11},{9,10},{10,... | collective-permute-start | bytes 196616 | tf_op jit(solution)/shard_map/ppermute | solution.py:453
  59.2 6.6 %collective-permute-start.8 = (bf16[64,512]{1,0:T(8,128)(2,1)}, bf16[64,512]{1,0:T(8,128)(2,1)}, u32[]{:S(2)}, u32[]{:S(2)}) collective-permute-start(bf16[64,512]{1,0:T(8,128)(2,1)} %get-tuple-element.39.refs_0_), channel_id=1, source_target_pairs={{0,2},{1,3},{2,0},{3,1},{4,6},{5,7},{6,4},{7,5},{8,10},{9,11},{10,... | collective-permute-start | bytes 196616 | tf_op jit(solution)/shard_map/ppermute | solution.py:453
  59.2 6.6 %collective-permute-start.7 = (bf16[64,512]{1,0:T(8,128)(2,1)}, bf16[64,512]{1,0:T(8,128)(2,1)}, u32[]{:S(2)}, u32[]{:S(2)}) collective-permute-start(bf16[64,512]{1,0:T(8,128)(2,1)} %get-tuple-element.39.refs_0_), channel_id=1, source_target_pairs={{0,1},{1,0},{2,3},{3,2},{4,5},{5,4},{6,7},{7,6},{8,9},{9,8},{10,11... | collective-permute-start | bytes 196616 | tf_op jit(solution)/shard_map/ppermute | solution.py:453
  74.5 4.9 %collective-permute-start.10 = (bf16[4,256,1152]{2,1,0:T(8,128)(2,1)}, bf16[4,256,1152]{2,1,0:T(8,128)(2,1)}, u32[]{:S(2)}, u32[]{:S(2)}) collective-permute-start(bf16[4,256,1152]{2,1,0:T(8,128)(2,1)} %get-tuple-element.44), channel_id=1, source_target_pairs={{0,4},{4,0},{8,12},{12,8},{16,20},{20,16},{24,28},{28,24},{1,5},{5... | collective-permute-start | bytes 7077896 | tf_op jit(solution)/shard_map/ppermute | solution.py:453
  74.6 31.0 %all-to-all-start.1 = ((bf16[4,128,1024]{2,1,0:T(8,128)(2,1)}), bf16[4,128,1024]{2,1,0:T(8,128)(2,1)}, u32[]{:S(2)}, u32[]{:S(2)}) async-start(bf16[4,128,1024]{2,1,0:T(8,128)(2,1)} %bitcast.3), calls=%async_computation.1 | async-start | bytes 2097152 | tf_op jit(solution)/shard_map/all_to_all | solution.py:457
  82.9 10.2 %collective-permute-start.14 = (bf16[256,512]{1,0:T(8,128)(2,1)}, bf16[256,512]{1,0:T(8,128)(2,1)}, u32[]{:S(2)}, u32[]{:S(2)}) collective-permute-start(bf16[256,512]{1,0:T(8,128)(2,1)} %get-tuple-element.55), channel_id=1, source_target_pairs={{0,8},{4,12},{8,0},{12,4},{16,24},{20,28},{24,16},{28,20},{1,9},{5... | collective-permute-start | bytes 786440 | tf_op jit(solution)/shard_map/ppermute | solution.py:453
  87.9 31.6 %collective-permute-start.11 = (bf16[256,640]{1,0:T(8,128)(2,1)}, bf16[256,640]{1,0:T(8,128)(2,1)}, u32[]{:S(2)}, u32[]{:S(2)}) collective-permute-start(bf16[256,640]{1,0:T(8,128)(2,1)} %get-tuple-element.51), channel_id=1, source_target_pairs={{0,8},{4,12},{8,0},{12,4},{16,24},{20,28},{24,16},{28,20},{1,9},{5... | collective-permute-start | bytes 983048 | tf_op jit(solution)/shard_map/ppermute | solution.py:453
  88.5 31.0 %collective-permute-start.12 = (bf16[256,640]{1,0:T(8,128)(2,1)}, bf16[256,640]{1,0:T(8,128)(2,1)}, u32[]{:S(2)}, u32[]{:S(2)}) collective-permute-start(bf16[256,640]{1,0:T(8,128)(2,1)} %get-tuple-element.52), channel_id=1, source_target_pairs={{0,16},{4,20},{8,24},{12,28},{16,0},{20,4},{24,8},{28,12},{1,17},{... | collective-permute-start | bytes 983048 | tf_op jit(solution)/shard_map/ppermute | solution.py:453
  90.0 29.5 %collective-permute-start.13 = (bf16[256,640]{1,0:T(8,128)(2,1)}, bf16[256,640]{1,0:T(8,128)(2,1)}, u32[]{:S(2)}, u32[]{:S(2)}) collective-permute-start(bf16[256,640]{1,0:T(8,128)(2,1)} %get-tuple-element.53), channel_id=1, source_target_pairs={{0,24},{4,28},{8,16},{12,20},{16,8},{20,12},{24,0},{28,4},{1,25},{... | collective-permute-start | bytes 983048 | tf_op jit(solution)/shard_map/ppermute | solution.py:453
  91.5 24.8 %collective-permute-start.15 = (bf16[256,512]{1,0:T(8,128)(2,1)}, bf16[256,512]{1,0:T(8,128)(2,1)}, u32[]{:S(2)}, u32[]{:S(2)}) collective-permute-start(bf16[256,512]{1,0:T(8,128)(2,1)} %get-tuple-element.56), channel_id=1, source_target_pairs={{0,16},{4,20},{8,24},{12,28},{16,0},{20,4},{24,8},{28,12},{1,17},{... | collective-permute-start | bytes 786440 | tf_op jit(solution)/shard_map/ppermute | solution.py:453
  93.0 23.3 %collective-permute-start.16 = (bf16[256,512]{1,0:T(8,128)(2,1)}, bf16[256,512]{1,0:T(8,128)(2,1)}, u32[]{:S(2)}, u32[]{:S(2)}) collective-permute-start(bf16[256,512]{1,0:T(8,128)(2,1)} %get-tuple-element.57), channel_id=1, source_target_pairs={{0,24},{4,28},{8,16},{12,20},{16,8},{20,12},{24,0},{28,4},{1,25},{... | collective-permute-start | bytes 786440 | tf_op jit(solution)/shard_map/ppermute | solution.py:453

commit v13 on v10

--- a/solution.py
+++ b/solution.py
@@ -13,6 +13,7 @@
 LANES = 128
 ROW_STEP = 512
 MID_STEP = 256
+PIECE = 256
 LABEL_ROWS = 16
 FULL = (64 << 20) - (64 << 10)
 
@@ -312,12 +313,15 @@
     ids = over(iota((columns, tall.shape[1]), 0), ADAPTER_RANK)
     tall = jnp.concatenate([tall] * (columns // ADAPTER_RANK), axis=0)
     for n in range(owners // 2):
-        grad = dot(spread(tall, ids, label[0:1], 2 * n + parity), acts[...])
-        if n == 0 and wait is not None:
-            wait()
-        if arrived is not None:
-            grad = grad + arrived[n, :, :features].astype(f32)
-        out[n, :, :features] = grad.astype(bf16)
+        spread_rows = spread(tall, ids, label[0:1], 2 * n + parity)
+        for c in range(0, features, PIECE):
+            at = slice(c, min(c + PIECE, features))
+            grad = dot(spread_rows, acts[:, at])
+            if n == 0 and c == 0 and wait is not None:
+                wait()
+            if arrived is not None:
+                grad = grad + arrived[n, :, at].astype(f32)
+            out[n, :, at] = grad.astype(bf16)
         for q in range(keys // LANES):
             lines = slice(q * own_rows, (q + 1) * own_rows)
             part = second[n * own_rows : (n + 1) * own_rows, q * LANES : (q + 1) * LANES]
@@ -373,9 +377,13 @@
             for copy in copies:
                 copy.wait()
         for c in range(0, features, chunk):
-            base = dot(scaled[at], weight[c : c + chunk], 1, 1).astype(bf16)
-            side = dot(back_wide[...], a_all[c : c + chunk], 1, 1).astype(bf16)
-            part[at, c : c + chunk] = (base.astype(f32) + side.astype(f32)).astype(bf16)
+            for h in range(0, step, PIECE):
+                rows_at = slice(r + h, r + min(h + PIECE, step))
+                base = dot(scaled[rows_at], weight[c : c + chunk], 1, 1).astype(bf16)
+                wide = back_wide[h : min(h + PIECE, step)]
+                side = dot(wide, a_all[c : c + chunk], 1, 1).astype(bf16)
+                whole = base.astype(f32) + side.astype(f32)
+                part[rows_at, c : c + chunk] = whole.astype(bf16)
             copy = pltpu.make_async_copy(
                 part.at[pl.ds(r, step), pl.ds(c, chunk)],
                 out.at[pl.ds(r, step), pl.ds(c, chunk)],

time: 120 us -> 120 us (level)
  no operation moved by 1% of the time
where the time goes in v13:
time: 120 us
  waiting for transfers between devices  61.2 us (51%)
  Pallas kernels  33.4 us (28%)
  starting transfers between devices  22.9 us (19%)
    ppermute x14, waiting for transfers between devices, swap(): return lax.ppermute(block, axis, [(i, i ^ bits) for i in range(size)])  36 us
    pallas_call x6, Pallas kernels, call(): pl.pallas_call(kernel, out_shape=outs, in_specs=[HBM] * len(ins), out_spe...  33.4 us
    all_to_all x2, waiting for transfers between devices, exchange(): lax.all_to_all(blocks, axis, split_axis=0, concat_axis=0, tiled=True, axi...  25.2 us
    ppermute x14, starting transfers between devices, swap(): return lax.ppermute(block, axis, [(i, i ^ bits) for i in range(size)])  12 us
    all_to_all x2, starting transfers between devices, exchange(): lax.all_to_all(blocks, axis, split_axis=0, concat_axis=0, tiled=True, axi...  10.9 us
  transfers between devices with their start and end apart: 16, of which 11 were waited for; matrix products, arithmetic and copies ran while one was open for 0% of the time, Pallas kernels for 6%

profile of v13, /device:TPU:0, one launch (start us, length us, event | category | flops | bytes accessed | tf_op | source)
XLA Modules:
  0.0 119.6 jit_solution(16579047493706657734)
XLA Ops:
  0.6 3.2 %shard_map.162 = (bf16[4,400,512]{2,1,0:T(8,128)(2,1)}, bf16[1152,256]{1,0:T(8,128)(2,1)}) custom-call(bf16[128,4096]{1,0:T(8,128)(2,1)} %refs_0_.1, bf16[128,512]{1,0:T(8,128)(2,1)} %refs_1_.1, s32[1,128]{1,0:T(1,128)} %bitcast.4, s32[1,128]{1,0:T(1,128)} %bitcast.5, f32[1024,256]{1,0:T(8,128)} %refs_4_.3, f32[64,512]{1,0:T(8,128)} %refs_7_.3), custom_call_target="tpu_custom_call" | custom-call | tf_op jit(solution)/shard_map/pallas_call | solution.py:86
  3.8 0.0 copy-start
  3.8 6.5 %all-to-all-start = ((bf16[4,400,512]{2,1,0:T(8,128)(2,1)}), bf16[4,400,512]{2,1,0:T(8,128)(2,1)}, u32[]{:S(2)}, u32[]{:S(2)}) async-start(bf16[4,400,512]{2,1,0:T(8,128)(2,1)} %get-tuple-element.25), calls=%async_computation | async-start | bytes 3276800 | tf_op jit(solution)/shard_map/all_to_all | solution.py:447
  10.3 0.0 copy-done
  10.3 2.4 %collective-permute-start.5 = (bf16[1152,256]{1,0:T(8,128)(2,1)S(1)}, bf16[1152,256]{1,0:T(8,128)(2,1)S(1)}, u32[]{:S(2)}, u32[]{:S(2)}) collective-permute-start(bf16[1152,256]{1,0:T(8,128)(2,1)S(1)} %copy-done), channel_id=1, source_target_pairs={{0,24},{4,28},{8,16},{12,20},{16,8},{20,12},{24,0},{28,4},{1,25},{... | collective-permute-start | bytes 1769480 | tf_op jit(solution)/shard_map/ppermute | solution.py:443
  12.7 0.5 collective-permute-start.3
  13.2 0.5 collective-permute-start.1
  13.8 0.0 collective-permute-start
  13.8 13.7 %collective-permute-done.5.refs_7_.refs_14_ = bf16[1152,256]{1,0:T(8,128)(2,1)S(1)} collective-permute-done((bf16[1152,256]{1,0:T(8,128)(2,1)S(1)}, bf16[1152,256]{1,0:T(8,128)(2,1)S(1)}, u32[]{:S(2)}, u32[]{:S(2)}) %collective-permute-start.5) | collective-permute-done | bytes 589856 | tf_op jit(solution)/shard_map/ppermute | solution.py:443
  27.5 0.0 copy-start.1
  27.5 0.0 collective-permute-start.6
  27.5 11.1 %collective-permute-done.3.refs_5_.refs_12_ = bf16[1152,256]{1,0:T(8,128)(2,1)S(1)} collective-permute-done((bf16[1152,256]{1,0:T(8,128)(2,1)S(1)}, bf16[1152,256]{1,0:T(8,128)(2,1)S(1)}, u32[]{:S(2)}, u32[]{:S(2)}) %collective-permute-start.3) | collective-permute-done | bytes 589856 | tf_op jit(solution)/shard_map/ppermute | solution.py:443
  38.6 0.0 copy-start.2
  38.6 0.0 collective-permute-start.4
  38.6 0.1 collective-permute-done.1.refs_3_.refs_10_
  38.7 0.0 copy-start.3
  38.7 0.4 collective-permute-start.2
  39.1 0.0 collective-permute-done.refs_2_.refs_9_
  39.1 0.0 copy-done.1
  39.1 0.0 copy-start.4
  39.1 0.0 collective-permute-done.6.refs_8_.refs_15_
  39.1 0.3 copy-done.2
  39.4 0.0 copy-start.5
  39.4 1.2 collective-permute-done.4.refs_6_.refs_13_
  40.6 0.0 copy-done.3
  40.6 0.0 copy-done.4
  40.6 0.0 copy-done.5
  40.6 0.0 copy-start.6
  40.6 0.8 copy-done.6
  41.4 0.1 collective-permute-done.2.refs_4_.refs_11_
  41.6 7.2 %all-to-all-done.refs_0_ = bf16[4,400,512]{2,1,0:T(8,128)(2,1)} async-done(((bf16[4,400,512]{2,1,0:T(8,128)(2,1)}), bf16[4,400,512]{2,1,0:T(8,128)(2,1)}, u32[]{:S(2)}, u32[]{:S(2)}) %all-to-all-start) | async-done | bytes 1638432 | tf_op jit(solution)/shard_map/all_to_all | solution.py:447
  48.7 8.9 %shard_map.163 = (bf16[512,1024]{1,0:T(8,128)(2,1)}, bf16[512,512]{1,0:T(8,128)(2,1)}, s32[8,512]{1,0:T(8,128)}, bf16[64,512]{1,0:T(8,128)(2,1)}) custom-call(bf16[4,400,512]{2,1,0:T(8,128)(2,1)} %all-to-all-done.refs_0_, bf16[1152,256]{1,0:T(8,128)(2,1)} %get-tuple-element.26.refs_1_.refs_8_, bf16[1152,256]{1,0:T(8,128)(2,1)} %copy-done.4, ...), custom_call_target="tpu_custom_call" | custom-call | tf_op jit(solution)/shard_map/pallas_call | solution.py:86
  57.7 1.5 %collective-permute-start.9 = (bf16[64,512]{1,0:T(8,128)(2,1)}, bf16[64,512]{1,0:T(8,128)(2,1)}, u32[]{:S(2)}, u32[]{:S(2)}) collective-permute-start(bf16[64,512]{1,0:T(8,128)(2,1)} %get-tuple-element.27.refs_0_), channel_id=1, source_target_pairs={{0,3},{1,2},{2,1},{3,0},{4,7},{5,6},{6,5},{7,4},{8,11},{9,10},{10,... | collective-permute-start | bytes 196616 | tf_op jit(solution)/shard_map/ppermute | solution.py:443
  59.2 0.0 collective-permute-start.8
  59.2 2.9 %collective-permute-start.7 = (bf16[64,512]{1,0:T(8,128)(2,1)}, bf16[64,512]{1,0:T(8,128)(2,1)}, u32[]{:S(2)}, u32[]{:S(2)}) collective-permute-start(bf16[64,512]{1,0:T(8,128)(2,1)} %get-tuple-element.27.refs_0_), channel_id=1, source_target_pairs={{0,1},{1,0},{2,3},{3,2},{4,5},{5,4},{6,7},{7,6},{8,9},{9,8},{10,11... | collective-permute-start | bytes 196616 | tf_op jit(solution)/shard_map/ppermute | solution.py:443
  62.1 2.3 %collective-permute-done.9.refs_3_ = bf16[64,512]{1,0:T(8,128)(2,1)} collective-permute-done((bf16[64,512]{1,0:T(8,128)(2,1)}, bf16[64,512]{1,0:T(8,128)(2,1)}, u32[]{:S(2)}, u32[]{:S(2)}) %collective-permute-start.9) | collective-permute-done | bytes 65568 | tf_op jit(solution)/shard_map/ppermute | solution.py:443
  64.5 1.3 %collective-permute-done.8.refs_2_ = bf16[64,512]{1,0:T(8,128)(2,1)} collective-permute-done((bf16[64,512]{1,0:T(8,128)(2,1)}, bf16[64,512]{1,0:T(8,128)(2,1)}, u32[]{:S(2)}, u32[]{:S(2)}) %collective-permute-start.8) | collective-permute-done | bytes 65568 | tf_op jit(solution)/shard_map/ppermute | solution.py:443
  65.8 0.0 collective-permute-done.7.refs_1_
  65.8 8.9 %shard_map.164 = (bf16[4,256,1152]{2,1,0:T(8,128)(2,1)}, bf16[512,1024]{1,0:T(8,128)(2,1)}) custom-call(bf16[64,512]{1,0:T(8,128)(2,1)} %get-tuple-element.27.refs_0_, bf16[64,512]{1,0:T(8,128)(2,1)} %collective-permute-done.7.refs_1_, bf16[64,512]{1,0:T(8,128)(2,1)} %collective-permute-done.8.refs_2_, bf16[64,512]{1,0:T(8,128)(2,1)} %collective-permute-done.9.refs_3_, ...), custom_call_target="tpu_custom_call" | custom-call | tf_op jit(solution)/shard_map/pallas_call | solution.py:86
  74.7 0.1 collective-permute-start.10
  74.7 4.4 %all-to-all-start.1 = ((bf16[4,128,1024]{2,1,0:T(8,128)(2,1)}), bf16[4,128,1024]{2,1,0:T(8,128)(2,1)}, u32[]{:S(2)}, u32[]{:S(2)}) async-start(bf16[4,128,1024]{2,1,0:T(8,128)(2,1)} %bitcast.3), calls=%async_computation.1 | async-start | bytes 2097152 | tf_op jit(solution)/shard_map/all_to_all | solution.py:447
  79.2 0.4 collective-permute-done.10.refs_7_
  79.6 4.5 %shard_map.166 = (bf16[256,1152]{1,0:T(8,128)(2,1)}, bf16[256,1152]{1,0:T(8,128)(2,1)}, bf16[256,1152]{1,0:T(8,128)(2,1)}, bf16[256,1152]{1,0:T(8,128)(2,1)}) custom-call(bf16[64,512]{1,0:T(8,128)(2,1)} %get-tuple-element.27.refs_0_, bf16[64,512]{1,0:T(8,128)(2,1)} %collective-permute-done.7.refs_1_, bf16[64,512]{1,0:T(8,128)(2,1)} %collective-permute-done.8.refs_2_, ...), custom_call_target="tpu_custom_call" | custom-call | tf_op jit(solution)/shard_map/pallas_call | solution.py:86
  84.1 1.6 %collective-permute-start.11 = (bf16[256,1152]{1,0:T(8,128)(2,1)}, bf16[256,1152]{1,0:T(8,128)(2,1)}, u32[]{:S(2)}, u32[]{:S(2)}) collective-permute-start(bf16[256,1152]{1,0:T(8,128)(2,1)} %get-tuple-element.34), channel_id=1, source_target_pairs={{0,8},{4,12},{8,0},{12,4},{16,24},{20,28},{24,16},{28,20},{1,9},{5... | collective-permute-start | bytes 1769480 | tf_op jit(solution)/shard_map/ppermute | solution.py:443
  85.7 1.5 %collective-permute-start.12 = (bf16[256,1152]{1,0:T(8,128)(2,1)}, bf16[256,1152]{1,0:T(8,128)(2,1)}, u32[]{:S(2)}, u32[]{:S(2)}) collective-permute-start(bf16[256,1152]{1,0:T(8,128)(2,1)} %get-tuple-element.35), channel_id=1, source_target_pairs={{0,16},{4,20},{8,24},{12,28},{16,0},{20,4},{24,8},{28,12},{1,17},{... | collective-permute-start | bytes 1769480 | tf_op jit(solution)/shard_map/ppermute | solution.py:443
  87.2 0.5 collective-permute-start.13
  87.7 18.0 %all-to-all-done.1.refs_0_ = bf16[4,128,1024]{2,1,0:T(8,128)(2,1)} async-done(((bf16[4,128,1024]{2,1,0:T(8,128)(2,1)}), bf16[4,128,1024]{2,1,0:T(8,128)(2,1)}, u32[]{:S(2)}, u32[]{:S(2)}) %all-to-all-start.1) | async-done | bytes 1048608 | tf_op jit(solution)/shard_map/all_to_all | solution.py:447
  105.7 2.3 %shard_map.165 = bf16[128,4096]{1,0:T(8,128)(2,1)} custom-call(bf16[4,128,1024]{2,1,0:T(8,128)(2,1)} %all-to-all-done.1.refs_0_), custom_call_target="tpu_custom_call" | custom-call | tf_op jit(solution)/shard_map/pallas_call | solution.py:86
  108.0 0.0 collective-permute-done.11.refs_1_
  108.0 5.7 %collective-permute-done.12.refs_2_ = bf16[256,1152]{1,0:T(8,128)(2,1)} collective-permute-done((bf16[256,1152]{1,0:T(8,128)(2,1)}, bf16[256,1152]{1,0:T(8,128)(2,1)}, u32[]{:S(2)}, u32[]{:S(2)}) %collective-permute-start.12) | collective-permute-done | bytes 589856 | tf_op jit(solution)/shard_map/ppermute | solution.py:443
  113.7 0.0 collective-permute-done.13.refs_3_
  113.7 5.7 %shard_map.167 = (f32[1024,256]{1,0:T(8,128)}, f32[1024,256]{1,0:T(8,128)}, f32[1024,256]{1,0:T(8,128)}, f32[64,512]{1,0:T(8,128)}, f32[64,512]{1,0:T(8,128)}, /*index=5*/f32[64,512]{1,0:T(8,128)}) custom-call(bf16[256,1152]{1,0:T(8,128)(2,1)} %get-tuple-element.33.refs_0_, bf16[256,1152]{1,0:T(8,128)(2,1)} %collective-permute-done.11.refs_1_, ...), custom_call_target="tpu_custom_call" | custom-call | tf_op jit(solution)/shard_map/pallas_call | solution.py:86
Async XLA Ops:
  3.8 6.5 %copy-start = (bf16[1152,256]{1,0:T(8,128)(2,1)S(1)}, bf16[1152,256]{1,0:T(8,128)(2,1)}, u32[]{:S(2)}) copy-start(bf16[1152,256]{1,0:T(8,128)(2,1)} %get-tuple-element.26.refs_1_.refs_8_) | copy-start | bytes 1769476
  3.8 44.9 %all-to-all-start = ((bf16[4,400,512]{2,1,0:T(8,128)(2,1)}), bf16[4,400,512]{2,1,0:T(8,128)(2,1)}, u32[]{:S(2)}, u32[]{:S(2)}) async-start(bf16[4,400,512]{2,1,0:T(8,128)(2,1)} %get-tuple-element.25), calls=%async_computation | async-start | bytes 3276800 | tf_op jit(solution)/shard_map/all_to_all | solution.py:447
  10.3 17.2 %collective-permute-start.5 = (bf16[1152,256]{1,0:T(8,128)(2,1)S(1)}, bf16[1152,256]{1,0:T(8,128)(2,1)S(1)}, u32[]{:S(2)}, u32[]{:S(2)}) collective-permute-start(bf16[1152,256]{1,0:T(8,128)(2,1)S(1)} %copy-done), channel_id=1, source_target_pairs={{0,24},{4,28},{8,16},{12,20},{16,8},{20,12},{24,0},{28,4},{1,25},{... | collective-permute-start | bytes 1769480 | tf_op jit(solution)/shard_map/ppermute | solution.py:443
  12.7 25.9 %collective-permute-start.3 = (bf16[1152,256]{1,0:T(8,128)(2,1)S(1)}, bf16[1152,256]{1,0:T(8,128)(2,1)S(1)}, u32[]{:S(2)}, u32[]{:S(2)}) collective-permute-start(bf16[1152,256]{1,0:T(8,128)(2,1)S(1)} %copy-done), channel_id=1, source_target_pairs={{0,16},{4,20},{8,24},{12,28},{16,0},{20,4},{24,8},{28,12},{1,17},{... | collective-permute-start | bytes 1769480 | tf_op jit(solution)/shard_map/ppermute | solution.py:443
  13.2 25.5 %collective-permute-start.1 = (bf16[1152,256]{1,0:T(8,128)(2,1)S(1)}, bf16[1152,256]{1,0:T(8,128)(2,1)S(1)}, u32[]{:S(2)}, u32[]{:S(2)}) collective-permute-start(bf16[1152,256]{1,0:T(8,128)(2,1)S(1)} %copy-done), channel_id=1, source_target_pairs={{0,8},{4,12},{8,0},{12,4},{16,24},{20,28},{24,16},{28,20},{1,9},{5... | collective-permute-start | bytes 1769480 | tf_op jit(solution)/shard_map/ppermute | solution.py:443
  13.8 25.4 %collective-permute-start = (bf16[1152,256]{1,0:T(8,128)(2,1)S(1)}, bf16[1152,256]{1,0:T(8,128)(2,1)S(1)}, u32[]{:S(2)}, u32[]{:S(2)}) collective-permute-start(bf16[1152,256]{1,0:T(8,128)(2,1)S(1)} %copy-done), channel_id=1, source_target_pairs={{0,4},{4,0},{8,12},{12,8},{16,20},{20,16},{24,28},{28,24},{1,5},{5... | collective-permute-start | bytes 1769480 | tf_op jit(solution)/shard_map/ppermute | solution.py:443
  27.5 11.7 %copy-start.1 = (bf16[1152,256]{1,0:T(8,128)(2,1)}, bf16[1152,256]{1,0:T(8,128)(2,1)S(1)}, u32[]{:S(2)}) copy-start(bf16[1152,256]{1,0:T(8,128)(2,1)S(1)} %collective-permute-done.5.refs_7_.refs_14_) | copy-start | bytes 1769476
  27.5 11.7 %collective-permute-start.6 = (bf16[1152,256]{1,0:T(8,128)(2,1)S(1)}, bf16[1152,256]{1,0:T(8,128)(2,1)S(1)}, u32[]{:S(2)}, u32[]{:S(2)}) collective-permute-start(bf16[1152,256]{1,0:T(8,128)(2,1)S(1)} %collective-permute-done.5.refs_7_.refs_14_), channel_id=1, source_target_pairs={{0,4},{4,0},{8,12},{12,8},{16,20},{20,16},{24,28},{28,24},{1,5},{5... | collective-permute-start | bytes 1769480 | tf_op jit(solution)/shard_map/ppermute | solution.py:443
  38.6 0.8 copy-start.2
  38.6 2.0 %collective-permute-start.4 = (bf16[1152,256]{1,0:T(8,128)(2,1)S(1)}, bf16[1152,256]{1,0:T(8,128)(2,1)S(1)}, u32[]{:S(2)}, u32[]{:S(2)}) collective-permute-start(bf16[1152,256]{1,0:T(8,128)(2,1)S(1)} %collective-permute-done.3.refs_5_.refs_12_), channel_id=1, source_target_pairs={{0,4},{4,0},{8,12},{12,8},{16,20},{20,16},{24,28},{28,24},{1,5},{5... | collective-permute-start | bytes 1769480 | tf_op jit(solution)/shard_map/ppermute | solution.py:443
  38.7 1.9 %copy-start.3 = (bf16[1152,256]{1,0:T(8,128)(2,1)}, bf16[1152,256]{1,0:T(8,128)(2,1)S(1)}, u32[]{:S(2)}) copy-start(bf16[1152,256]{1,0:T(8,128)(2,1)S(1)} %collective-permute-done.1.refs_3_.refs_10_) | copy-start | bytes 1769476
  38.7 2.9 %collective-permute-start.2 = (bf16[1152,256]{1,0:T(8,128)(2,1)S(1)}, bf16[1152,256]{1,0:T(8,128)(2,1)}, u32[]{:S(2)}, u32[]{:S(2)}) collective-permute-start(bf16[1152,256]{1,0:T(8,128)(2,1)S(1)} %collective-permute-done.1.refs_3_.refs_10_), channel_id=1, source_target_pairs={{0,4},{4,0},{8,12},{12,8},{16,20},{20,16},{24,28},{28,24},{1,5},{5... | collective-permute-start | bytes 1769480 | tf_op jit(solution)/shard_map/ppermute | solution.py:443
  39.1 1.5 %copy-start.4 = (bf16[1152,256]{1,0:T(8,128)(2,1)}, bf16[1152,256]{1,0:T(8,128)(2,1)S(1)}, u32[]{:S(2)}) copy-start(bf16[1152,256]{1,0:T(8,128)(2,1)S(1)} %collective-permute-done.refs_2_.refs_9_) | copy-start | bytes 1769476
  39.4 1.2 %copy-start.5 = (bf16[1152,256]{1,0:T(8,128)(2,1)}, bf16[1152,256]{1,0:T(8,128)(2,1)S(1)}, u32[]{:S(2)}) copy-start(bf16[1152,256]{1,0:T(8,128)(2,1)S(1)} %collective-permute-done.6.refs_8_.refs_15_) | copy-start | bytes 1769476
  40.6 0.8 copy-start.6
  57.7 6.8 %collective-permute-start.9 = (bf16[64,512]{1,0:T(8,128)(2,1)}, bf16[64,512]{1,0:T(8,128)(2,1)}, u32[]{:S(2)}, u32[]{:S(2)}) collective-permute-start(bf16[64,512]{1,0:T(8,128)(2,1)} %get-tuple-element.27.refs_0_), channel_id=1, source_target_pairs={{0,3},{1,2},{2,1},{3,0},{4,7},{5,6},{6,5},{7,4},{8,11},{9,10},{10,... | collective-permute-start | bytes 196616 | tf_op jit(solution)/shard_map/ppermute | solution.py:443
  59.2 6.6 %collective-permute-start.8 = (bf16[64,512]{1,0:T(8,128)(2,1)}, bf16[64,512]{1,0:T(8,128)(2,1)}, u32[]{:S(2)}, u32[]{:S(2)}) collective-permute-start(bf16[64,512]{1,0:T(8,128)(2,1)} %get-tuple-element.27.refs_0_), channel_id=1, source_target_pairs={{0,2},{1,3},{2,0},{3,1},{4,6},{5,7},{6,4},{7,5},{8,10},{9,11},{10,... | collective-permute-start | bytes 196616 | tf_op jit(solution)/shard_map/ppermute | solution.py:443
  59.2 6.6 %collective-permute-start.7 = (bf16[64,512]{1,0:T(8,128)(2,1)}, bf16[64,512]{1,0:T(8,128)(2,1)}, u32[]{:S(2)}, u32[]{:S(2)}) collective-permute-start(bf16[64,512]{1,0:T(8,128)(2,1)} %get-tuple-element.27.refs_0_), channel_id=1, source_target_pairs={{0,1},{1,0},{2,3},{3,2},{4,5},{5,4},{6,7},{7,6},{8,9},{9,8},{10,11... | collective-permute-start | bytes 196616 | tf_op jit(solution)/shard_map/ppermute | solution.py:443
  74.7 4.9 %collective-permute-start.10 = (bf16[4,256,1152]{2,1,0:T(8,128)(2,1)}, bf16[4,256,1152]{2,1,0:T(8,128)(2,1)}, u32[]{:S(2)}, u32[]{:S(2)}) collective-permute-start(bf16[4,256,1152]{2,1,0:T(8,128)(2,1)} %get-tuple-element.32), channel_id=1, source_target_pairs={{0,4},{4,0},{8,12},{12,8},{16,20},{20,16},{24,28},{28,24},{1,5},{5... | collective-permute-start | bytes 7077896 | tf_op jit(solution)/shard_map/ppermute | solution.py:443
  74.7 31.0 %all-to-all-start.1 = ((bf16[4,128,1024]{2,1,0:T(8,128)(2,1)}), bf16[4,128,1024]{2,1,0:T(8,128)(2,1)}, u32[]{:S(2)}, u32[]{:S(2)}) async-start(bf16[4,128,1024]{2,1,0:T(8,128)(2,1)} %bitcast.3), calls=%async_computation.1 | async-start | bytes 2097152 | tf_op jit(solution)/shard_map/all_to_all | solution.py:447
  84.1 23.9 %collective-permute-start.11 = (bf16[256,1152]{1,0:T(8,128)(2,1)}, bf16[256,1152]{1,0:T(8,128)(2,1)}, u32[]{:S(2)}, u32[]{:S(2)}) collective-permute-start(bf16[256,1152]{1,0:T(8,128)(2,1)} %get-tuple-element.34), channel_id=1, source_target_pairs={{0,8},{4,12},{8,0},{12,4},{16,24},{20,28},{24,16},{28,20},{1,9},{5... | collective-permute-start | bytes 1769480 | tf_op jit(solution)/shard_map/ppermute | solution.py:443
  85.7 28.0 %collective-permute-start.12 = (bf16[256,1152]{1,0:T(8,128)(2,1)}, bf16[256,1152]{1,0:T(8,128)(2,1)}, u32[]{:S(2)}, u32[]{:S(2)}) collective-permute-start(bf16[256,1152]{1,0:T(8,128)(2,1)} %get-tuple-element.35), channel_id=1, source_target_pairs={{0,16},{4,20},{8,24},{12,28},{16,0},{20,4},{24,8},{28,12},{1,17},{... | collective-permute-start | bytes 1769480 | tf_op jit(solution)/shard_map/ppermute | solution.py:443
  87.2 26.5 %collective-permute-start.13 = (bf16[256,1152]{1,0:T(8,128)(2,1)}, bf16[256,1152]{1,0:T(8,128)(2,1)}, u32[]{:S(2)}, u32[]{:S(2)}) collective-permute-start(bf16[256,1152]{1,0:T(8,128)(2,1)} %get-tuple-element.36), channel_id=1, source_target_pairs={{0,24},{4,28},{8,16},{12,20},{16,8},{20,12},{24,0},{28,4},{1,25},{... | collective-permute-start | bytes 1769480 | tf_op jit(solution)/shard_map/ppermute | solution.py:443

commit v14 on v10

--- a/solution.py
+++ b/solution.py
@@ -24,9 +24,12 @@
 bias_one = 1.0 - 0.9**10
 bias_two = 1.0 - 0.999**10
 
+SOME = 16 << 20
+
 f32 = jnp.float32
 bf16 = jnp.bfloat16
 HBM = pl.BlockSpec(memory_space=pltpu.HBM)
+VMEM = pl.BlockSpec(memory_space=pltpu.VMEM)
 DMA = pltpu.SemaphoreType.DMA
 
 def shape(dims, kind=bf16):
@@ -52,7 +55,7 @@
             copy.wait()
 
 
-def call(body, outs, ins, kinds, out_kinds, scratch=()):
+def call(body, outs, ins, kinds, out_kinds, scratch=(), room=FULL):
     single = not isinstance(outs, (list, tuple))
     outs = [outs] if single else list(outs)
     staged = [x for x, kind in zip(ins, kinds) if kind == "h"]
@@ -85,10 +88,10 @@
     result = pl.pallas_call(
         kernel,
         out_shape=outs,
-        in_specs=[HBM] * len(ins),
+        in_specs=[VMEM if kind == "v" else HBM for kind in kinds],
         out_specs=[HBM] * len(outs),
         scratch_shapes=buffers + list(scratch) + [DMA((count,))],
-        compiler_params=pltpu.CompilerParams(vmem_limit_bytes=FULL),
+        compiler_params=pltpu.CompilerParams(vmem_limit_bytes=room),
         cost_estimate=pl.CostEstimate(flops=0, bytes_accessed=0, transcendentals=0),
     )(*ins)
     return result[0] if single else result
@@ -521,7 +524,7 @@
     )
     returned = exchange(grad_part.reshape(shards, row_count, features), "fsdp")
     grad_input = call(
-        lay_kernel, shape((row_count, shards * features)), (returned,), "h", "h"
+        lay_kernel, shape((row_count, shards * features)), (returned,), "h", "h", room=SOME
     )
     even = call(
         functools.partial(even_kernel, shards, owners, own_rows),
@@ -537,9 +540,10 @@
         functools.partial(adam_kernel, owners // 2, own_rows),
         [shape(a_param.shape, f32)] * 3 + [shape(b_param.shape, f32)] * 3,
         (*sums, a_param, a_moment, a_second, b_param, b_moment, b_second),
-        "h" * (owners // 2 + 6),
+        "v" * (owners // 2 + 6),
         "rrrhhh",
         [pltpu.VMEM(a_param.shape, f32)] * 3 + [DMA((3, features // min(256, features)))],
+        room=SOME,
     )
     return (grad_input, *new)
 

time: 120 us -> 123 us (1.025)
  local copies, waits for them, and re-layouts: 1.12 us -> 6.14 us
  Pallas kernels: 33.3 us -> 31.7 us
    unnamed x14 -> x28, local copies, waits for them, and re-layouts: 1.12 us -> 6.14 us
    pallas_call x6, Pallas kernels: 33.3 us -> 31.7 us  [call(): pl.pallas_call(kernel, out_shape=outs, in_specs=[VMEM if kind == 'v' else...]
where the time goes in v14:
time: 123 us
  waiting for transfers between devices  61.1 us (50%)
  Pallas kernels  31.7 us (26%)
  starting transfers between devices  22.9 us (19%)
  local copies, waits for them, and re-layouts  6.14 us (5%)
    ppermute x14, waiting for transfers between devices, swap(): return lax.ppermute(block, axis, [(i, i ^ bits) for i in range(size)])  35.9 us
    pallas_call x6, Pallas kernels, call(): pl.pallas_call(kernel, out_shape=outs, in_specs=[VMEM if kind == 'v' else...  31.7 us
    all_to_all x2, waiting for transfers between devices, exchange(): lax.all_to_all(blocks, axis, split_axis=0, concat_axis=0, tiled=True, axi...  25.2 us
    ppermute x14, starting transfers between devices, swap(): return lax.ppermute(block, axis, [(i, i ^ bits) for i in range(size)])  12 us
    all_to_all x2, starting transfers between devices, exchange(): lax.all_to_all(blocks, axis, split_axis=0, concat_axis=0, tiled=True, axi...  10.9 us
    unnamed x28, local copies, waits for them, and re-layouts  6.14 us
  transfers between devices with their start and end apart: 16, of which 11 were waited for; matrix products, arithmetic and copies ran while one was open for 0% of the time, Pallas kernels for 6%

profile of v14, /device:TPU:0, one launch (start us, length us, event | category | flops | bytes accessed | tf_op | source)
XLA Modules:
  0.0 122.7 jit_solution(2365684093520667676)
XLA Ops:
  0.6 3.2 %shard_map.162 = (bf16[4,400,512]{2,1,0:T(8,128)(2,1)}, bf16[1152,256]{1,0:T(8,128)(2,1)}) custom-call(bf16[128,4096]{1,0:T(8,128)(2,1)} %refs_0_.1, bf16[128,512]{1,0:T(8,128)(2,1)} %refs_1_.1, s32[1,128]{1,0:T(1,128)} %bitcast.4, s32[1,128]{1,0:T(1,128)} %bitcast.5, f32[1024,256]{1,0:T(8,128)} %refs_4_.3, f32[64,512]{1,0:T(8,128)} %refs_7_.3), custom_call_target="tpu_custom_call" | custom-call | tf_op jit(solution)/shard_map/pallas_call | solution.py:88
  3.8 0.0 copy-start.7
  3.8 6.5 %all-to-all-start = ((bf16[4,400,512]{2,1,0:T(8,128)(2,1)}), bf16[4,400,512]{2,1,0:T(8,128)(2,1)}, u32[]{:S(2)}, u32[]{:S(2)}) async-start(bf16[4,400,512]{2,1,0:T(8,128)(2,1)} %get-tuple-element.25), calls=%async_computation | async-start | bytes 3276800 | tf_op jit(solution)/shard_map/all_to_all | solution.py:442
  10.3 0.0 copy-done.7
  10.3 2.4 %collective-permute-start.5 = (bf16[1152,256]{1,0:T(8,128)(2,1)S(1)}, bf16[1152,256]{1,0:T(8,128)(2,1)S(1)}, u32[]{:S(2)}, u32[]{:S(2)}) collective-permute-start(bf16[1152,256]{1,0:T(8,128)(2,1)S(1)} %copy-done.7), channel_id=1, source_target_pairs={{0,24},{4,28},{8,16},{12,20},{16,8},{20,12},{24,0},{28,4},{1,25},{... | collective-permute-start | bytes 1769480 | tf_op jit(solution)/shard_map/ppermute | solution.py:438
  12.7 0.5 collective-permute-start.3
  13.2 0.5 collective-permute-start.1
  13.8 0.0 collective-permute-start
  13.8 13.7 %collective-permute-done.5.refs_7_.refs_14_ = bf16[1152,256]{1,0:T(8,128)(2,1)S(1)} collective-permute-done((bf16[1152,256]{1,0:T(8,128)(2,1)S(1)}, bf16[1152,256]{1,0:T(8,128)(2,1)S(1)}, u32[]{:S(2)}, u32[]{:S(2)}) %collective-permute-start.5) | collective-permute-done | bytes 589856 | tf_op jit(solution)/shard_map/ppermute | solution.py:438
  27.5 0.0 copy-start.8
  27.5 0.0 collective-permute-start.6
  27.5 11.1 %collective-permute-done.3.refs_5_.refs_12_ = bf16[1152,256]{1,0:T(8,128)(2,1)S(1)} collective-permute-done((bf16[1152,256]{1,0:T(8,128)(2,1)S(1)}, bf16[1152,256]{1,0:T(8,128)(2,1)S(1)}, u32[]{:S(2)}, u32[]{:S(2)}) %collective-permute-start.3) | collective-permute-done | bytes 589856 | tf_op jit(solution)/shard_map/ppermute | solution.py:438
  38.6 0.0 copy-start.9
  38.6 0.0 collective-permute-start.4
  38.6 0.1 collective-permute-done.1.refs_3_.refs_10_
  38.7 0.0 copy-start.10
  38.7 0.4 collective-permute-start.2
  39.1 0.0 collective-permute-done.refs_2_.refs_9_
  39.1 0.0 copy-done.8
  39.1 0.0 collective-permute-done.6.refs_8_.refs_15_
  39.1 0.3 copy-done.9
  39.4 0.0 copy-start.12
  39.4 1.2 collective-permute-done.4.refs_6_.refs_13_
  40.6 0.0 copy-done.10
  40.6 0.0 copy-done.11
  40.6 0.0 copy-done.12
  40.6 0.0 copy-start.13
  40.6 0.8 copy-done.13
  41.5 0.1 collective-permute-done.2.refs_4_.refs_11_
  41.6 7.2 %all-to-all-done.refs_0_ = bf16[4,400,512]{2,1,0:T(8,128)(2,1)} async-done(((bf16[4,400,512]{2,1,0:T(8,128)(2,1)}), bf16[4,400,512]{2,1,0:T(8,128)(2,1)}, u32[]{:S(2)}, u32[]{:S(2)}) %all-to-all-start) | async-done | bytes 1638432 | tf_op jit(solution)/shard_map/all_to_all | solution.py:442
  48.7 8.9 %shard_map.163 = (bf16[512,1024]{1,0:T(8,128)(2,1)}, bf16[512,512]{1,0:T(8,128)(2,1)}, s32[8,512]{1,0:T(8,128)}, bf16[64,512]{1,0:T(8,128)(2,1)}) custom-call(bf16[4,400,512]{2,1,0:T(8,128)(2,1)} %all-to-all-done.refs_0_, bf16[1152,256]{1,0:T(8,128)(2,1)} %get-tuple-element.26.refs_1_.refs_8_, bf16[1152,256]{1,0:T(8,128)(2,1)} %copy-done.11, ...), custom_call_target="tpu_custom_call" | custom-call | tf_op jit(solution)/shard_map/pallas_call | solution.py:88
  57.7 1.5 %collective-permute-start.9 = (bf16[64,512]{1,0:T(8,128)(2,1)}, bf16[64,512]{1,0:T(8,128)(2,1)}, u32[]{:S(2)}, u32[]{:S(2)}) collective-permute-start(bf16[64,512]{1,0:T(8,128)(2,1)} %get-tuple-element.27.refs_0_), channel_id=1, source_target_pairs={{0,3},{1,2},{2,1},{3,0},{4,7},{5,6},{6,5},{7,4},{8,11},{9,10},{10,... | collective-permute-start | bytes 196616 | tf_op jit(solution)/shard_map/ppermute | solution.py:438
  59.2 0.0 collective-permute-start.8
  59.2 2.9 %collective-permute-start.7 = (bf16[64,512]{1,0:T(8,128)(2,1)}, bf16[64,512]{1,0:T(8,128)(2,1)}, u32[]{:S(2)}, u32[]{:S(2)}) collective-permute-start(bf16[64,512]{1,0:T(8,128)(2,1)} %get-tuple-element.27.refs_0_), channel_id=1, source_target_pairs={{0,1},{1,0},{2,3},{3,2},{4,5},{5,4},{6,7},{7,6},{8,9},{9,8},{10,11... | collective-permute-start | bytes 196616 | tf_op jit(solution)/shard_map/ppermute | solution.py:438
  62.1 2.3 %collective-permute-done.9.refs_3_ = bf16[64,512]{1,0:T(8,128)(2,1)} collective-permute-done((bf16[64,512]{1,0:T(8,128)(2,1)}, bf16[64,512]{1,0:T(8,128)(2,1)}, u32[]{:S(2)}, u32[]{:S(2)}) %collective-permute-start.9) | collective-permute-done | bytes 65568 | tf_op jit(solution)/shard_map/ppermute | solution.py:438
  64.5 1.3 %collective-permute-done.8.refs_2_ = bf16[64,512]{1,0:T(8,128)(2,1)} collective-permute-done((bf16[64,512]{1,0:T(8,128)(2,1)}, bf16[64,512]{1,0:T(8,128)(2,1)}, u32[]{:S(2)}, u32[]{:S(2)}) %collective-permute-start.8) | collective-permute-done | bytes 65568 | tf_op jit(solution)/shard_map/ppermute | solution.py:438
  65.8 0.0 collective-permute-done.7.refs_1_
  65.8 8.8 %shard_map.164 = (bf16[4,256,1152]{2,1,0:T(8,128)(2,1)}, bf16[512,1024]{1,0:T(8,128)(2,1)}) custom-call(bf16[64,512]{1,0:T(8,128)(2,1)} %get-tuple-element.27.refs_0_, bf16[64,512]{1,0:T(8,128)(2,1)} %collective-permute-done.7.refs_1_, bf16[64,512]{1,0:T(8,128)(2,1)} %collective-permute-done.8.refs_2_, bf16[64,512]{1,0:T(8,128)(2,1)} %collective-permute-done.9.refs_3_, ...), custom_call_target="tpu_custom_call" | custom-call | tf_op jit(solution)/shard_map/pallas_call | solution.py:88
  74.6 0.1 collective-permute-start.10
  74.6 4.5 %all-to-all-start.1 = ((bf16[4,128,1024]{2,1,0:T(8,128)(2,1)}), bf16[4,128,1024]{2,1,0:T(8,128)(2,1)}, u32[]{:S(2)}, u32[]{:S(2)}) async-start(bf16[4,128,1024]{2,1,0:T(8,128)(2,1)} %bitcast.3), calls=%async_computation.1 | async-start | bytes 2097152 | tf_op jit(solution)/shard_map/all_to_all | solution.py:442
  79.1 0.4 collective-permute-done.10.refs_7_
  79.5 4.5 %shard_map.166 = (bf16[256,1152]{1,0:T(8,128)(2,1)}, bf16[256,1152]{1,0:T(8,128)(2,1)}, bf16[256,1152]{1,0:T(8,128)(2,1)}, bf16[256,1152]{1,0:T(8,128)(2,1)}) custom-call(bf16[64,512]{1,0:T(8,128)(2,1)} %get-tuple-element.27.refs_0_, bf16[64,512]{1,0:T(8,128)(2,1)} %collective-permute-done.7.refs_1_, bf16[64,512]{1,0:T(8,128)(2,1)} %collective-permute-done.8.refs_2_, ...), custom_call_target="tpu_custom_call" | custom-call | tf_op jit(solution)/shard_map/pallas_call | solution.py:88
  84.0 0.0 copy-start
  84.0 0.0 copy-start.1
  84.0 1.6 %collective-permute-start.11 = (bf16[256,1152]{1,0:T(8,128)(2,1)}, bf16[256,1152]{1,0:T(8,128)(2,1)S(1)}, u32[]{:S(2)}, u32[]{:S(2)}) collective-permute-start(bf16[256,1152]{1,0:T(8,128)(2,1)} %get-tuple-element.34), channel_id=1, source_target_pairs={{0,8},{4,12},{8,0},{12,4},{16,24},{20,28},{24,16},{28,20},{1,9},{5... | collective-permute-start | bytes 1769480 | tf_op jit(solution)/shard_map/ppermute | solution.py:438
  85.6 1.5 %collective-permute-start.12 = (bf16[256,1152]{1,0:T(8,128)(2,1)}, bf16[256,1152]{1,0:T(8,128)(2,1)S(1)}, u32[]{:S(2)}, u32[]{:S(2)}) collective-permute-start(bf16[256,1152]{1,0:T(8,128)(2,1)} %get-tuple-element.35), channel_id=1, source_target_pairs={{0,16},{4,20},{8,24},{12,28},{16,0},{20,4},{24,8},{28,12},{1,17},{... | collective-permute-start | bytes 1769480 | tf_op jit(solution)/shard_map/ppermute | solution.py:438
  87.1 0.5 collective-permute-start.13
  87.6 18.0 %all-to-all-done.1.refs_0_ = bf16[4,128,1024]{2,1,0:T(8,128)(2,1)} async-done(((bf16[4,128,1024]{2,1,0:T(8,128)(2,1)}), bf16[4,128,1024]{2,1,0:T(8,128)(2,1)}, u32[]{:S(2)}, u32[]{:S(2)}) %all-to-all-start.1) | async-done | bytes 1048608 | tf_op jit(solution)/shard_map/all_to_all | solution.py:442
  105.6 2.3 %shard_map.165 = bf16[128,4096]{1,0:T(8,128)(2,1)} custom-call(bf16[4,128,1024]{2,1,0:T(8,128)(2,1)} %all-to-all-done.1.refs_0_), custom_call_target="tpu_custom_call" | custom-call | tf_op jit(solution)/shard_map/pallas_call | solution.py:88
  107.9 0.0 collective-permute-done.11.refs_1_
  107.9 5.6 %collective-permute-done.12.refs_2_ = bf16[256,1152]{1,0:T(8,128)(2,1)S(1)} collective-permute-done((bf16[256,1152]{1,0:T(8,128)(2,1)}, bf16[256,1152]{1,0:T(8,128)(2,1)S(1)}, u32[]{:S(2)}, u32[]{:S(2)}) %collective-permute-start.12) | collective-permute-done | bytes 589856 | tf_op jit(solution)/shard_map/ppermute | solution.py:438
  113.5 0.0 collective-permute-done.13.refs_3_
  113.5 0.0 copy-done
  113.5 0.0 copy-done.1
  113.6 0.0 copy-start.2
  113.6 1.2 copy-done.2
  114.8 0.0 copy-start.3
  114.8 1.1 copy-done.3
  115.8 0.0 copy-start.4
  115.9 0.9 copy-done.4
  116.8 0.0 copy-start.5
  116.8 0.9 copy-done.5
  117.7 0.9 copy-done.6
  118.6 4.0 %shard_map.167 = (f32[1024,256]{1,0:T(8,128)}, f32[1024,256]{1,0:T(8,128)}, f32[1024,256]{1,0:T(8,128)}, f32[64,512]{1,0:T(8,128)}, f32[64,512]{1,0:T(8,128)}, /*index=5*/f32[64,512]{1,0:T(8,128)}) custom-call(bf16[256,1152]{1,0:T(8,128)(2,1)S(1)} %copy-done.3, bf16[256,1152]{1,0:T(8,128)(2,1)S(1)} %collective-permute-done.11.refs_1_, ...), custom_call_target="tpu_custom_call" | custom-call | tf_op jit(solution)/shard_map/pallas_call | solution.py:88
  (2 shorter events, 0.0 us)
Async XLA Ops:
  3.8 6.5 %copy-start.7 = (bf16[1152,256]{1,0:T(8,128)(2,1)S(1)}, bf16[1152,256]{1,0:T(8,128)(2,1)}, u32[]{:S(2)}) copy-start(bf16[1152,256]{1,0:T(8,128)(2,1)} %get-tuple-element.26.refs_1_.refs_8_) | copy-start | bytes 1769476
  3.8 44.9 %all-to-all-start = ((bf16[4,400,512]{2,1,0:T(8,128)(2,1)}), bf16[4,400,512]{2,1,0:T(8,128)(2,1)}, u32[]{:S(2)}, u32[]{:S(2)}) async-start(bf16[4,400,512]{2,1,0:T(8,128)(2,1)} %get-tuple-element.25), calls=%async_computation | async-start | bytes 3276800 | tf_op jit(solution)/shard_map/all_to_all | solution.py:442
  10.3 17.2 %collective-permute-start.5 = (bf16[1152,256]{1,0:T(8,128)(2,1)S(1)}, bf16[1152,256]{1,0:T(8,128)(2,1)S(1)}, u32[]{:S(2)}, u32[]{:S(2)}) collective-permute-start(bf16[1152,256]{1,0:T(8,128)(2,1)S(1)} %copy-done.7), channel_id=1, source_target_pairs={{0,24},{4,28},{8,16},{12,20},{16,8},{20,12},{24,0},{28,4},{1,25},{... | collective-permute-start | bytes 1769480 | tf_op jit(solution)/shard_map/ppermute | solution.py:438
  12.7 25.9 %collective-permute-start.3 = (bf16[1152,256]{1,0:T(8,128)(2,1)S(1)}, bf16[1152,256]{1,0:T(8,128)(2,1)S(1)}, u32[]{:S(2)}, u32[]{:S(2)}) collective-permute-start(bf16[1152,256]{1,0:T(8,128)(2,1)S(1)} %copy-done.7), channel_id=1, source_target_pairs={{0,16},{4,20},{8,24},{12,28},{16,0},{20,4},{24,8},{28,12},{1,17},{... | collective-permute-start | bytes 1769480 | tf_op jit(solution)/shard_map/ppermute | solution.py:438
  13.2 25.5 %collective-permute-start.1 = (bf16[1152,256]{1,0:T(8,128)(2,1)S(1)}, bf16[1152,256]{1,0:T(8,128)(2,1)S(1)}, u32[]{:S(2)}, u32[]{:S(2)}) collective-permute-start(bf16[1152,256]{1,0:T(8,128)(2,1)S(1)} %copy-done.7), channel_id=1, source_target_pairs={{0,8},{4,12},{8,0},{12,4},{16,24},{20,28},{24,16},{28,20},{1,9},{5... | collective-permute-start | bytes 1769480 | tf_op jit(solution)/shard_map/ppermute | solution.py:438
  13.8 25.4 %collective-permute-start = (bf16[1152,256]{1,0:T(8,128)(2,1)S(1)}, bf16[1152,256]{1,0:T(8,128)(2,1)S(1)}, u32[]{:S(2)}, u32[]{:S(2)}) collective-permute-start(bf16[1152,256]{1,0:T(8,128)(2,1)S(1)} %copy-done.7), channel_id=1, source_target_pairs={{0,4},{4,0},{8,12},{12,8},{16,20},{20,16},{24,28},{28,24},{1,5},{5... | collective-permute-start | bytes 1769480 | tf_op jit(solution)/shard_map/ppermute | solution.py:438
  27.5 11.7 %copy-start.8 = (bf16[1152,256]{1,0:T(8,128)(2,1)}, bf16[1152,256]{1,0:T(8,128)(2,1)S(1)}, u32[]{:S(2)}) copy-start(bf16[1152,256]{1,0:T(8,128)(2,1)S(1)} %collective-permute-done.5.refs_7_.refs_14_) | copy-start | bytes 1769476
  27.5 11.7 %collective-permute-start.6 = (bf16[1152,256]{1,0:T(8,128)(2,1)S(1)}, bf16[1152,256]{1,0:T(8,128)(2,1)S(1)}, u32[]{:S(2)}, u32[]{:S(2)}) collective-permute-start(bf16[1152,256]{1,0:T(8,128)(2,1)S(1)} %collective-permute-done.5.refs_7_.refs_14_), channel_id=1, source_target_pairs={{0,4},{4,0},{8,12},{12,8},{16,20},{20,16},{24,28},{28,24},{1,5},{5... | collective-permute-start | bytes 1769480 | tf_op jit(solution)/shard_map/ppermute | solution.py:438
  38.6 0.8 copy-start.9
  38.6 2.0 %collective-permute-start.4 = (bf16[1152,256]{1,0:T(8,128)(2,1)S(1)}, bf16[1152,256]{1,0:T(8,128)(2,1)S(1)}, u32[]{:S(2)}, u32[]{:S(2)}) collective-permute-start(bf16[1152,256]{1,0:T(8,128)(2,1)S(1)} %collective-permute-done.3.refs_5_.refs_12_), channel_id=1, source_target_pairs={{0,4},{4,0},{8,12},{12,8},{16,20},{20,16},{24,28},{28,24},{1,5},{5... | collective-permute-start | bytes 1769480 | tf_op jit(solution)/shard_map/ppermute | solution.py:438
  38.7 1.9 %copy-start.10 = (bf16[1152,256]{1,0:T(8,128)(2,1)}, bf16[1152,256]{1,0:T(8,128)(2,1)S(1)}, u32[]{:S(2)}) copy-start(bf16[1152,256]{1,0:T(8,128)(2,1)S(1)} %collective-permute-done.1.refs_3_.refs_10_) | copy-start | bytes 1769476
  38.7 2.9 %collective-permute-start.2 = (bf16[1152,256]{1,0:T(8,128)(2,1)S(1)}, bf16[1152,256]{1,0:T(8,128)(2,1)}, u32[]{:S(2)}, u32[]{:S(2)}) collective-permute-start(bf16[1152,256]{1,0:T(8,128)(2,1)S(1)} %collective-permute-done.1.refs_3_.refs_10_), channel_id=1, source_target_pairs={{0,4},{4,0},{8,12},{12,8},{16,20},{20,16},{24,28},{28,24},{1,5},{5... | collective-permute-start | bytes 1769480 | tf_op jit(solution)/shard_map/ppermute | solution.py:438
  39.1 1.5 %copy-start.11 = (bf16[1152,256]{1,0:T(8,128)(2,1)}, bf16[1152,256]{1,0:T(8,128)(2,1)S(1)}, u32[]{:S(2)}) copy-start(bf16[1152,256]{1,0:T(8,128)(2,1)S(1)} %collective-permute-done.refs_2_.refs_9_) | copy-start | bytes 1769476
  39.4 1.2 copy-start.12
  40.6 0.8 copy-start.13
  57.7 6.8 %collective-permute-start.9 = (bf16[64,512]{1,0:T(8,128)(2,1)}, bf16[64,512]{1,0:T(8,128)(2,1)}, u32[]{:S(2)}, u32[]{:S(2)}) collective-permute-start(bf16[64,512]{1,0:T(8,128)(2,1)} %get-tuple-element.27.refs_0_), channel_id=1, source_target_pairs={{0,3},{1,2},{2,1},{3,0},{4,7},{5,6},{6,5},{7,4},{8,11},{9,10},{10,... | collective-permute-start | bytes 196616 | tf_op jit(solution)/shard_map/ppermute | solution.py:438
  59.2 6.6 %collective-permute-start.8 = (bf16[64,512]{1,0:T(8,128)(2,1)}, bf16[64,512]{1,0:T(8,128)(2,1)}, u32[]{:S(2)}, u32[]{:S(2)}) collective-permute-start(bf16[64,512]{1,0:T(8,128)(2,1)} %get-tuple-element.27.refs_0_), channel_id=1, source_target_pairs={{0,2},{1,3},{2,0},{3,1},{4,6},{5,7},{6,4},{7,5},{8,10},{9,11},{10,... | collective-permute-start | bytes 196616 | tf_op jit(solution)/shard_map/ppermute | solution.py:438
  59.2 6.6 %collective-permute-start.7 = (bf16[64,512]{1,0:T(8,128)(2,1)}, bf16[64,512]{1,0:T(8,128)(2,1)}, u32[]{:S(2)}, u32[]{:S(2)}) collective-permute-start(bf16[64,512]{1,0:T(8,128)(2,1)} %get-tuple-element.27.refs_0_), channel_id=1, source_target_pairs={{0,1},{1,0},{2,3},{3,2},{4,5},{5,4},{6,7},{7,6},{8,9},{9,8},{10,11... | collective-permute-start | bytes 196616 | tf_op jit(solution)/shard_map/ppermute | solution.py:438
  74.6 4.9 %collective-permute-start.10 = (bf16[4,256,1152]{2,1,0:T(8,128)(2,1)}, bf16[4,256,1152]{2,1,0:T(8,128)(2,1)}, u32[]{:S(2)}, u32[]{:S(2)}) collective-permute-start(bf16[4,256,1152]{2,1,0:T(8,128)(2,1)} %get-tuple-element.32), channel_id=1, source_target_pairs={{0,4},{4,0},{8,12},{12,8},{16,20},{20,16},{24,28},{28,24},{1,5},{5... | collective-permute-start | bytes 7077896 | tf_op jit(solution)/shard_map/ppermute | solution.py:438
  74.6 31.0 %all-to-all-start.1 = ((bf16[4,128,1024]{2,1,0:T(8,128)(2,1)}), bf16[4,128,1024]{2,1,0:T(8,128)(2,1)}, u32[]{:S(2)}, u32[]{:S(2)}) async-start(bf16[4,128,1024]{2,1,0:T(8,128)(2,1)} %bitcast.3), calls=%async_computation.1 | async-start | bytes 2097152 | tf_op jit(solution)/shard_map/all_to_all | solution.py:442
  84.0 29.5 %copy-start = (f32[1024,256]{1,0:T(8,128)S(1)}, f32[1024,256]{1,0:T(8,128)}, u32[]{:S(2)}) copy-start(f32[1024,256]{1,0:T(8,128)} %refs_4_.3) | copy-start | bytes 3145732
  84.0 29.5 %copy-start.1 = (f32[1024,256]{1,0:T(8,128)S(1)}, f32[1024,256]{1,0:T(8,128)}, u32[]{:S(2)}) copy-start(f32[1024,256]{1,0:T(8,128)} %refs_5_.3) | copy-start | bytes 3145732
  84.0 23.9 %collective-permute-start.11 = (bf16[256,1152]{1,0:T(8,128)(2,1)}, bf16[256,1152]{1,0:T(8,128)(2,1)S(1)}, u32[]{:S(2)}, u32[]{:S(2)}) collective-permute-start(bf16[256,1152]{1,0:T(8,128)(2,1)} %get-tuple-element.34), channel_id=1, source_target_pairs={{0,8},{4,12},{8,0},{12,4},{16,24},{20,28},{24,16},{28,20},{1,9},{5... | collective-permute-start | bytes 1769480 | tf_op jit(solution)/shard_map/ppermute | solution.py:438
  85.6 27.9 %collective-permute-start.12 = (bf16[256,1152]{1,0:T(8,128)(2,1)}, bf16[256,1152]{1,0:T(8,128)(2,1)S(1)}, u32[]{:S(2)}, u32[]{:S(2)}) collective-permute-start(bf16[256,1152]{1,0:T(8,128)(2,1)} %get-tuple-element.35), channel_id=1, source_target_pairs={{0,16},{4,20},{8,24},{12,28},{16,0},{20,4},{24,8},{28,12},{1,17},{... | collective-permute-start | bytes 1769480 | tf_op jit(solution)/shard_map/ppermute | solution.py:438
  87.1 26.4 %collective-permute-start.13 = (bf16[256,1152]{1,0:T(8,128)(2,1)}, bf16[256,1152]{1,0:T(8,128)(2,1)}, u32[]{:S(2)}, u32[]{:S(2)}) collective-permute-start(bf16[256,1152]{1,0:T(8,128)(2,1)} %get-tuple-element.36), channel_id=1, source_target_pairs={{0,24},{4,28},{8,16},{12,20},{16,8},{20,12},{24,0},{28,4},{1,25},{... | collective-permute-start | bytes 1769480 | tf_op jit(solution)/shard_map/ppermute | solution.py:438
  113.6 1.2 %copy-start.2 = (f32[1024,256]{1,0:T(8,128)S(1)}, f32[1024,256]{1,0:T(8,128)}, u32[]{:S(2)}) copy-start(f32[1024,256]{1,0:T(8,128)} %refs_6_.1) | copy-start | bytes 3145732
  114.8 1.1 copy-start.3
  115.8 0.9 copy-start.4
  116.8 0.9 copy-start.5
  117.7 0.9 copy-start.6

commit v15 on v10

--- a/solution.py
+++ b/solution.py
@@ -126,11 +126,10 @@
     wide = jnp.broadcast_to(row.astype(f32), (lanes, n))
     return jnp.transpose(wide)
 
-def prep_kernel(io, acts, cot, tenant, advantage, a_param, b_param, packed, low):
+def prep_kernel(features, io, acts, cot, tenant, advantage, packed):
     io.ready()
     rows, keys = cot.shape
     shards, _, unit = packed.shape
-    features, columns = a_param.shape
     factor = column_of(advantage[...]) * 0.25
     factor = jnp.concatenate([factor] * (keys // LANES), axis=1)
     scaled = (cot[...].astype(f32) * factor).astype(bf16)
@@ -150,7 +149,12 @@
         first += keys // unit * rows
         packed[j, first:, :rows] = labels
         packed[j, first:, rows:] = jnp.zeros((LABEL_ROWS, unit - rows), bf16)
-    io.store(0)
+
+
+def low_kernel(io, a_param, b_param, low):
+    io.ready()
+    features, columns = a_param.shape
+    keys = b_param.shape[1]
     low[:features] = (a_param[...] * MODEL_WIDTH ** (-0.5)).astype(bf16)
     own_rows = b_param.shape[0]
     for q in range(keys // columns):
@@ -464,12 +468,16 @@
     b_lines = own_rows * keys // columns
     lines = (features + keys) // unit * row_count + LABEL_ROWS
 
-    packed, low = call(
-        prep_kernel,
-        [shape((shards, lines, unit)), shape((features + b_lines, columns))],
-        (acts, cotangent, tenant[None], advantage[None], a_param, b_param),
-        "h" * 6,
-        "hh",
+    packed = call(
+        functools.partial(prep_kernel, features),
+        shape((shards, lines, unit)),
+        (acts, cotangent, tenant[None], advantage[None]),
+        "hhhh",
+        "h",
+    )
+    packed, a_first, b_first = lax.optimization_barrier((packed, a_param, b_param))
+    low = call(
+        low_kernel, shape((features + b_lines, columns)), (a_first, b_first), "hh", "h"
     )
     packed = exchange(packed, "fsdp")
     chips = [low] + [swap(low, "dp", k) for k in range(2, owners, 2)]

time: 120 us -> 119 us (level)
  waiting for transfers between devices: 61.2 us -> 58.3 us
  Pallas kernels: 33.3 us -> 34.8 us
    all_to_all x2, waiting for transfers between devices: 25.2 us -> 22.8 us  [exchange(): lax.all_to_all(blocks, axis, split_axis=0, concat_axis=0, tiled=True, axi...]
    pallas_call x6 -> x7, Pallas kernels: 33.3 us -> 34.8 us  [call(): pl.pallas_call(kernel, out_shape=outs, in_specs=[HBM] * len(ins), out_spe...]
  transfers between devices with their start and end apart: 16 -> 16, of which waited for: 11 -> 10; matrix products, arithmetic and copies ran while one was open for 0% -> 0% of each run, Pallas kernels for 6% -> 8%
where the time goes in v15:
time: 119 us
  waiting for transfers between devices  58.3 us (49%)
  Pallas kernels  34.8 us (29%)
  starting transfers between devices  22.7 us (19%)
  local copies, waits for them, and re-layouts  1.93 us (2%)
    ppermute x14, waiting for transfers between devices, swap(): return lax.ppermute(block, axis, [(i, i ^ bits) for i in range(size)])  35.5 us
    pallas_call x7, Pallas kernels, call(): pl.pallas_call(kernel, out_shape=outs, in_specs=[HBM] * len(ins), out_spe...  34.8 us
    all_to_all x2, waiting for transfers between devices, exchange(): lax.all_to_all(blocks, axis, split_axis=0, concat_axis=0, tiled=True, axi...  22.8 us
    ppermute x14, starting transfers between devices, swap(): return lax.ppermute(block, axis, [(i, i ^ bits) for i in range(size)])  12.1 us
    all_to_all x2, starting transfers between devices, exchange(): lax.all_to_all(blocks, axis, split_axis=0, concat_axis=0, tiled=True, axi...  10.6 us
  transfers between devices with their start and end apart: 16, of which 10 were waited for; matrix products, arithmetic and copies ran while one was open for 0% of the time, Pallas kernels for 8%

profile of v15, /device:TPU:0, one launch (start us, length us, event | category | flops | bytes accessed | tf_op | source)
XLA Modules:
  0.0 118.6 jit_solution(7809769677921464313)
XLA Ops:
  0.6 2.5 %shard_map.162 = bf16[4,400,512]{2,1,0:T(8,128)(2,1)} custom-call(bf16[128,4096]{1,0:T(8,128)(2,1)} %refs_0_.1, bf16[128,512]{1,0:T(8,128)(2,1)} %refs_1_.1, s32[1,128]{1,0:T(1,128)} %bitcast.4, s32[1,128]{1,0:T(1,128)} %bitcast.5), custom_call_target="tpu_custom_call" | custom-call | tf_op jit(solution)/shard_map/pallas_call | solution.py:85
  3.2 6.3 %all-to-all-start = ((bf16[4,400,512]{2,1,0:T(8,128)(2,1)}), bf16[4,400,512]{2,1,0:T(8,128)(2,1)}, u32[]{:S(2)}, u32[]{:S(2)}) async-start(bf16[4,400,512]{2,1,0:T(8,128)(2,1)} %shard_map.162), calls=%async_computation | async-start | bytes 3276800 | tf_op jit(solution)/shard_map/all_to_all | solution.py:443
  9.5 2.1 %shard_map.163.refs_1_.refs_8_ = bf16[1152,256]{1,0:T(8,128)(2,1)} custom-call(f32[1024,256]{1,0:T(8,128)} %refs_4_.1, f32[64,512]{1,0:T(8,128)} %refs_7_.3), custom_call_target="tpu_custom_call" | custom-call | tf_op jit(solution)/shard_map/pallas_call | solution.py:85
  11.7 2.5 %collective-permute-start.5 = (bf16[1152,256]{1,0:T(8,128)(2,1)}, bf16[1152,256]{1,0:T(8,128)(2,1)S(1)}, u32[]{:S(2)}, u32[]{:S(2)}) collective-permute-start(bf16[1152,256]{1,0:T(8,128)(2,1)} %shard_map.163.refs_1_.refs_8_), channel_id=1, source_target_pairs={{0,24},{4,28},{8,16},{12,20},{16,8},{20,12},{24,0},{28,4},{1,25},{... | collective-permute-start | bytes 1769480 | tf_op jit(solution)/shard_map/ppermute | solution.py:439
  14.2 0.5 collective-permute-start.3
  14.7 0.5 collective-permute-start.1
  15.2 0.0 collective-permute-start
  15.2 13.9 %collective-permute-done.5.refs_7_.refs_14_ = bf16[1152,256]{1,0:T(8,128)(2,1)S(1)} collective-permute-done((bf16[1152,256]{1,0:T(8,128)(2,1)}, bf16[1152,256]{1,0:T(8,128)(2,1)S(1)}, u32[]{:S(2)}, u32[]{:S(2)}) %collective-permute-start.5) | collective-permute-done | bytes 589856 | tf_op jit(solution)/shard_map/ppermute | solution.py:439
  29.1 0.0 copy-start
  29.1 0.8 copy-done
  29.9 0.0 collective-permute-start.6
  30.0 10.3 %collective-permute-done.3.refs_5_.refs_12_ = bf16[1152,256]{1,0:T(8,128)(2,1)S(1)} collective-permute-done((bf16[1152,256]{1,0:T(8,128)(2,1)}, bf16[1152,256]{1,0:T(8,128)(2,1)S(1)}, u32[]{:S(2)}, u32[]{:S(2)}) %collective-permute-start.3) | collective-permute-done | bytes 589856 | tf_op jit(solution)/shard_map/ppermute | solution.py:439
  40.3 0.0 copy-start.1
  40.3 0.1 collective-permute-start.4
  40.4 0.0 collective-permute-done.1.refs_3_.refs_10_
  40.4 0.0 copy-start.2
  40.4 0.4 collective-permute-start.2
  40.8 0.0 collective-permute-done.refs_2_.refs_9_
  40.8 0.0 copy-start.3
  40.8 0.0 collective-permute-done.6.refs_8_.refs_15_
  40.8 0.3 copy-done.1
  41.1 0.0 copy-start.4
  41.1 1.2 collective-permute-done.4.refs_6_.refs_13_
  42.3 0.0 copy-done.2
  42.3 0.0 copy-done.3
  42.3 0.0 copy-done.4
  42.3 0.0 copy-start.5
  42.3 0.8 copy-done.5
  43.1 0.1 collective-permute-done.2.refs_4_.refs_11_
  43.2 4.7 %all-to-all-done.refs_0_ = bf16[4,400,512]{2,1,0:T(8,128)(2,1)} async-done(((bf16[4,400,512]{2,1,0:T(8,128)(2,1)}), bf16[4,400,512]{2,1,0:T(8,128)(2,1)}, u32[]{:S(2)}, u32[]{:S(2)}) %all-to-all-start) | async-done | bytes 1638432 | tf_op jit(solution)/shard_map/all_to_all | solution.py:443
  48.0 8.9 %shard_map.164 = (bf16[512,1024]{1,0:T(8,128)(2,1)}, bf16[512,512]{1,0:T(8,128)(2,1)}, s32[8,512]{1,0:T(8,128)}, bf16[64,512]{1,0:T(8,128)(2,1)}) custom-call(bf16[4,400,512]{2,1,0:T(8,128)(2,1)} %all-to-all-done.refs_0_, bf16[1152,256]{1,0:T(8,128)(2,1)} %shard_map.163.refs_1_.refs_8_, bf16[1152,256]{1,0:T(8,128)(2,1)} %copy-done.3, ...), custom_call_target="tpu_custom_call" | custom-call | tf_op jit(solution)/shard_map/pallas_call | solution.py:85
  56.9 1.5 %collective-permute-start.9 = (bf16[64,512]{1,0:T(8,128)(2,1)}, bf16[64,512]{1,0:T(8,128)(2,1)}, u32[]{:S(2)}, u32[]{:S(2)}) collective-permute-start(bf16[64,512]{1,0:T(8,128)(2,1)} %get-tuple-element.29.refs_0_), channel_id=1, source_target_pairs={{0,3},{1,2},{2,1},{3,0},{4,7},{5,6},{6,5},{7,4},{8,11},{9,10},{10,... | collective-permute-start | bytes 196616 | tf_op jit(solution)/shard_map/ppermute | solution.py:439
  58.5 0.0 collective-permute-start.8
  58.5 2.9 %collective-permute-start.7 = (bf16[64,512]{1,0:T(8,128)(2,1)}, bf16[64,512]{1,0:T(8,128)(2,1)}, u32[]{:S(2)}, u32[]{:S(2)}) collective-permute-start(bf16[64,512]{1,0:T(8,128)(2,1)} %get-tuple-element.29.refs_0_), channel_id=1, source_target_pairs={{0,1},{1,0},{2,3},{3,2},{4,5},{5,4},{6,7},{7,6},{8,9},{9,8},{10,11... | collective-permute-start | bytes 196616 | tf_op jit(solution)/shard_map/ppermute | solution.py:439
  61.4 2.3 %collective-permute-done.9.refs_3_ = bf16[64,512]{1,0:T(8,128)(2,1)} collective-permute-done((bf16[64,512]{1,0:T(8,128)(2,1)}, bf16[64,512]{1,0:T(8,128)(2,1)}, u32[]{:S(2)}, u32[]{:S(2)}) %collective-permute-start.9) | collective-permute-done | bytes 65568 | tf_op jit(solution)/shard_map/ppermute | solution.py:439
  63.7 1.3 %collective-permute-done.8.refs_2_ = bf16[64,512]{1,0:T(8,128)(2,1)} collective-permute-done((bf16[64,512]{1,0:T(8,128)(2,1)}, bf16[64,512]{1,0:T(8,128)(2,1)}, u32[]{:S(2)}, u32[]{:S(2)}) %collective-permute-start.8) | collective-permute-done | bytes 65568 | tf_op jit(solution)/shard_map/ppermute | solution.py:439
  65.0 0.0 collective-permute-done.7.refs_1_
  65.0 8.8 %shard_map.165 = (bf16[4,256,1152]{2,1,0:T(8,128)(2,1)}, bf16[512,1024]{1,0:T(8,128)(2,1)}) custom-call(bf16[64,512]{1,0:T(8,128)(2,1)} %get-tuple-element.29.refs_0_, bf16[64,512]{1,0:T(8,128)(2,1)} %collective-permute-done.7.refs_1_, bf16[64,512]{1,0:T(8,128)(2,1)} %collective-permute-done.8.refs_2_, bf16[64,512]{1,0:T(8,128)(2,1)} %collective-permute-done.9.refs_3_, ...), custom_call_target="tpu_custom_call" | custom-call | tf_op jit(solution)/shard_map/pallas_call | solution.py:85
  73.8 0.1 collective-permute-start.10
  73.9 4.3 %all-to-all-start.1 = ((bf16[4,128,1024]{2,1,0:T(8,128)(2,1)}), bf16[4,128,1024]{2,1,0:T(8,128)(2,1)}, u32[]{:S(2)}, u32[]{:S(2)}) async-start(bf16[4,128,1024]{2,1,0:T(8,128)(2,1)} %bitcast.3), calls=%async_computation.1 | async-start | bytes 2097152 | tf_op jit(solution)/shard_map/all_to_all | solution.py:443
  78.2 0.6 collective-permute-done.10.refs_7_
  78.7 4.5 %shard_map.167 = (bf16[256,1152]{1,0:T(8,128)(2,1)}, bf16[256,1152]{1,0:T(8,128)(2,1)}, bf16[256,1152]{1,0:T(8,128)(2,1)}, bf16[256,1152]{1,0:T(8,128)(2,1)}) custom-call(bf16[64,512]{1,0:T(8,128)(2,1)} %get-tuple-element.29.refs_0_, bf16[64,512]{1,0:T(8,128)(2,1)} %collective-permute-done.7.refs_1_, bf16[64,512]{1,0:T(8,128)(2,1)} %collective-permute-done.8.refs_2_, ...), custom_call_target="tpu_custom_call" | custom-call | tf_op jit(solution)/shard_map/pallas_call | solution.py:85
  83.3 1.6 %collective-permute-start.11 = (bf16[256,1152]{1,0:T(8,128)(2,1)}, bf16[256,1152]{1,0:T(8,128)(2,1)}, u32[]{:S(2)}, u32[]{:S(2)}) collective-permute-start(bf16[256,1152]{1,0:T(8,128)(2,1)} %get-tuple-element.36), channel_id=1, source_target_pairs={{0,8},{4,12},{8,0},{12,4},{16,24},{20,28},{24,16},{28,20},{1,9},{5... | collective-permute-start | bytes 1769480 | tf_op jit(solution)/shard_map/ppermute | solution.py:439
  84.8 1.5 %collective-permute-start.12 = (bf16[256,1152]{1,0:T(8,128)(2,1)}, bf16[256,1152]{1,0:T(8,128)(2,1)}, u32[]{:S(2)}, u32[]{:S(2)}) collective-permute-start(bf16[256,1152]{1,0:T(8,128)(2,1)} %get-tuple-element.37), channel_id=1, source_target_pairs={{0,16},{4,20},{8,24},{12,28},{16,0},{20,4},{24,8},{28,12},{1,17},{... | collective-permute-start | bytes 1769480 | tf_op jit(solution)/shard_map/ppermute | solution.py:439
  86.3 0.5 collective-permute-start.13
  86.8 18.0 %all-to-all-done.1.refs_0_ = bf16[4,128,1024]{2,1,0:T(8,128)(2,1)} async-done(((bf16[4,128,1024]{2,1,0:T(8,128)(2,1)}), bf16[4,128,1024]{2,1,0:T(8,128)(2,1)}, u32[]{:S(2)}, u32[]{:S(2)}) %all-to-all-start.1) | async-done | bytes 1048608 | tf_op jit(solution)/shard_map/all_to_all | solution.py:443
  104.9 2.3 %shard_map.166 = bf16[128,4096]{1,0:T(8,128)(2,1)} custom-call(bf16[4,128,1024]{2,1,0:T(8,128)(2,1)} %all-to-all-done.1.refs_0_), custom_call_target="tpu_custom_call" | custom-call | tf_op jit(solution)/shard_map/pallas_call | solution.py:85
  107.1 0.0 collective-permute-done.11.refs_1_
  107.2 5.7 %collective-permute-done.12.refs_2_ = bf16[256,1152]{1,0:T(8,128)(2,1)} collective-permute-done((bf16[256,1152]{1,0:T(8,128)(2,1)}, bf16[256,1152]{1,0:T(8,128)(2,1)}, u32[]{:S(2)}, u32[]{:S(2)}) %collective-permute-start.12) | collective-permute-done | bytes 589856 | tf_op jit(solution)/shard_map/ppermute | solution.py:439
  112.9 0.0 collective-permute-done.13.refs_3_
  112.9 5.7 %shard_map.168 = (f32[1024,256]{1,0:T(8,128)}, f32[1024,256]{1,0:T(8,128)}, f32[1024,256]{1,0:T(8,128)}, f32[64,512]{1,0:T(8,128)}, f32[64,512]{1,0:T(8,128)}, /*index=5*/f32[64,512]{1,0:T(8,128)}) custom-call(bf16[256,1152]{1,0:T(8,128)(2,1)} %get-tuple-element.35.refs_0_, bf16[256,1152]{1,0:T(8,128)(2,1)} %collective-permute-done.11.refs_1_, ...), custom_call_target="tpu_custom_call" | custom-call | tf_op jit(solution)/shard_map/pallas_call | solution.py:85
Async XLA Ops:
  3.2 44.8 %all-to-all-start = ((bf16[4,400,512]{2,1,0:T(8,128)(2,1)}), bf16[4,400,512]{2,1,0:T(8,128)(2,1)}, u32[]{:S(2)}, u32[]{:S(2)}) async-start(bf16[4,400,512]{2,1,0:T(8,128)(2,1)} %shard_map.162), calls=%async_computation | async-start | bytes 3276800 | tf_op jit(solution)/shard_map/all_to_all | solution.py:443
  11.7 17.5 %collective-permute-start.5 = (bf16[1152,256]{1,0:T(8,128)(2,1)}, bf16[1152,256]{1,0:T(8,128)(2,1)S(1)}, u32[]{:S(2)}, u32[]{:S(2)}) collective-permute-start(bf16[1152,256]{1,0:T(8,128)(2,1)} %shard_map.163.refs_1_.refs_8_), channel_id=1, source_target_pairs={{0,24},{4,28},{8,16},{12,20},{16,8},{20,12},{24,0},{28,4},{1,25},{... | collective-permute-start | bytes 1769480 | tf_op jit(solution)/shard_map/ppermute | solution.py:439
  14.2 26.1 %collective-permute-start.3 = (bf16[1152,256]{1,0:T(8,128)(2,1)}, bf16[1152,256]{1,0:T(8,128)(2,1)S(1)}, u32[]{:S(2)}, u32[]{:S(2)}) collective-permute-start(bf16[1152,256]{1,0:T(8,128)(2,1)} %shard_map.163.refs_1_.refs_8_), channel_id=1, source_target_pairs={{0,16},{4,20},{8,24},{12,28},{16,0},{20,4},{24,8},{28,12},{1,17},{... | collective-permute-start | bytes 1769480 | tf_op jit(solution)/shard_map/ppermute | solution.py:439
  14.7 25.7 %collective-permute-start.1 = (bf16[1152,256]{1,0:T(8,128)(2,1)}, bf16[1152,256]{1,0:T(8,128)(2,1)S(1)}, u32[]{:S(2)}, u32[]{:S(2)}) collective-permute-start(bf16[1152,256]{1,0:T(8,128)(2,1)} %shard_map.163.refs_1_.refs_8_), channel_id=1, source_target_pairs={{0,8},{4,12},{8,0},{12,4},{16,24},{20,28},{24,16},{28,20},{1,9},{5... | collective-permute-start | bytes 1769480 | tf_op jit(solution)/shard_map/ppermute | solution.py:439
  15.2 25.6 %collective-permute-start = (bf16[1152,256]{1,0:T(8,128)(2,1)}, bf16[1152,256]{1,0:T(8,128)(2,1)S(1)}, u32[]{:S(2)}, u32[]{:S(2)}) collective-permute-start(bf16[1152,256]{1,0:T(8,128)(2,1)} %shard_map.163.refs_1_.refs_8_), channel_id=1, source_target_pairs={{0,4},{4,0},{8,12},{12,8},{16,20},{20,16},{24,28},{28,24},{1,5},{5... | collective-permute-start | bytes 1769480 | tf_op jit(solution)/shard_map/ppermute | solution.py:439
  29.1 0.8 copy-start
  29.9 10.8 %collective-permute-start.6 = (bf16[1152,256]{1,0:T(8,128)(2,1)S(1)}, bf16[1152,256]{1,0:T(8,128)(2,1)S(1)}, u32[]{:S(2)}, u32[]{:S(2)}) collective-permute-start(bf16[1152,256]{1,0:T(8,128)(2,1)S(1)} %collective-permute-done.5.refs_7_.refs_14_), channel_id=1, source_target_pairs={{0,4},{4,0},{8,12},{12,8},{16,20},{20,16},{24,28},{28,24},{1,5},{5... | collective-permute-start | bytes 1769480 | tf_op jit(solution)/shard_map/ppermute | solution.py:439
  40.3 0.8 copy-start.1
  40.3 2.0 %collective-permute-start.4 = (bf16[1152,256]{1,0:T(8,128)(2,1)S(1)}, bf16[1152,256]{1,0:T(8,128)(2,1)S(1)}, u32[]{:S(2)}, u32[]{:S(2)}) collective-permute-start(bf16[1152,256]{1,0:T(8,128)(2,1)S(1)} %collective-permute-done.3.refs_5_.refs_12_), channel_id=1, source_target_pairs={{0,4},{4,0},{8,12},{12,8},{16,20},{20,16},{24,28},{28,24},{1,5},{5... | collective-permute-start | bytes 1769480 | tf_op jit(solution)/shard_map/ppermute | solution.py:439
  40.4 1.9 %copy-start.2 = (bf16[1152,256]{1,0:T(8,128)(2,1)}, bf16[1152,256]{1,0:T(8,128)(2,1)S(1)}, u32[]{:S(2)}) copy-start(bf16[1152,256]{1,0:T(8,128)(2,1)S(1)} %collective-permute-done.1.refs_3_.refs_10_) | copy-start | bytes 1769476
  40.4 2.9 %collective-permute-start.2 = (bf16[1152,256]{1,0:T(8,128)(2,1)S(1)}, bf16[1152,256]{1,0:T(8,128)(2,1)}, u32[]{:S(2)}, u32[]{:S(2)}) collective-permute-start(bf16[1152,256]{1,0:T(8,128)(2,1)S(1)} %collective-permute-done.1.refs_3_.refs_10_), channel_id=1, source_target_pairs={{0,4},{4,0},{8,12},{12,8},{16,20},{20,16},{24,28},{28,24},{1,5},{5... | collective-permute-start | bytes 1769480 | tf_op jit(solution)/shard_map/ppermute | solution.py:439
  40.8 1.5 %copy-start.3 = (bf16[1152,256]{1,0:T(8,128)(2,1)}, bf16[1152,256]{1,0:T(8,128)(2,1)S(1)}, u32[]{:S(2)}) copy-start(bf16[1152,256]{1,0:T(8,128)(2,1)S(1)} %collective-permute-done.refs_2_.refs_9_) | copy-start | bytes 1769476
  41.1 1.2 %copy-start.4 = (bf16[1152,256]{1,0:T(8,128)(2,1)}, bf16[1152,256]{1,0:T(8,128)(2,1)S(1)}, u32[]{:S(2)}) copy-start(bf16[1152,256]{1,0:T(8,128)(2,1)S(1)} %collective-permute-done.6.refs_8_.refs_15_) | copy-start | bytes 1769476
  42.3 0.8 copy-start.5
  56.9 6.8 %collective-permute-start.9 = (bf16[64,512]{1,0:T(8,128)(2,1)}, bf16[64,512]{1,0:T(8,128)(2,1)}, u32[]{:S(2)}, u32[]{:S(2)}) collective-permute-start(bf16[64,512]{1,0:T(8,128)(2,1)} %get-tuple-element.29.refs_0_), channel_id=1, source_target_pairs={{0,3},{1,2},{2,1},{3,0},{4,7},{5,6},{6,5},{7,4},{8,11},{9,10},{10,... | collective-permute-start | bytes 196616 | tf_op jit(solution)/shard_map/ppermute | solution.py:439
  58.5 6.6 %collective-permute-start.8 = (bf16[64,512]{1,0:T(8,128)(2,1)}, bf16[64,512]{1,0:T(8,128)(2,1)}, u32[]{:S(2)}, u32[]{:S(2)}) collective-permute-start(bf16[64,512]{1,0:T(8,128)(2,1)} %get-tuple-element.29.refs_0_), channel_id=1, source_target_pairs={{0,2},{1,3},{2,0},{3,1},{4,6},{5,7},{6,4},{7,5},{8,10},{9,11},{10,... | collective-permute-start | bytes 196616 | tf_op jit(solution)/shard_map/ppermute | solution.py:439
  58.5 6.6 %collective-permute-start.7 = (bf16[64,512]{1,0:T(8,128)(2,1)}, bf16[64,512]{1,0:T(8,128)(2,1)}, u32[]{:S(2)}, u32[]{:S(2)}) collective-permute-start(bf16[64,512]{1,0:T(8,128)(2,1)} %get-tuple-element.29.refs_0_), channel_id=1, source_target_pairs={{0,1},{1,0},{2,3},{3,2},{4,5},{5,4},{6,7},{7,6},{8,9},{9,8},{10,11... | collective-permute-start | bytes 196616 | tf_op jit(solution)/shard_map/ppermute | solution.py:439
  73.8 4.9 %collective-permute-start.10 = (bf16[4,256,1152]{2,1,0:T(8,128)(2,1)}, bf16[4,256,1152]{2,1,0:T(8,128)(2,1)}, u32[]{:S(2)}, u32[]{:S(2)}) collective-permute-start(bf16[4,256,1152]{2,1,0:T(8,128)(2,1)} %get-tuple-element.34), channel_id=1, source_target_pairs={{0,4},{4,0},{8,12},{12,8},{16,20},{20,16},{24,28},{28,24},{1,5},{5... | collective-permute-start | bytes 7077896 | tf_op jit(solution)/shard_map/ppermute | solution.py:439
  73.9 31.0 %all-to-all-start.1 = ((bf16[4,128,1024]{2,1,0:T(8,128)(2,1)}), bf16[4,128,1024]{2,1,0:T(8,128)(2,1)}, u32[]{:S(2)}, u32[]{:S(2)}) async-start(bf16[4,128,1024]{2,1,0:T(8,128)(2,1)} %bitcast.3), calls=%async_computation.1 | async-start | bytes 2097152 | tf_op jit(solution)/shard_map/all_to_all | solution.py:443
  83.3 23.9 %collective-permute-start.11 = (bf16[256,1152]{1,0:T(8,128)(2,1)}, bf16[256,1152]{1,0:T(8,128)(2,1)}, u32[]{:S(2)}, u32[]{:S(2)}) collective-permute-start(bf16[256,1152]{1,0:T(8,128)(2,1)} %get-tuple-element.36), channel_id=1, source_target_pairs={{0,8},{4,12},{8,0},{12,4},{16,24},{20,28},{24,16},{28,20},{1,9},{5... | collective-permute-start | bytes 1769480 | tf_op jit(solution)/shard_map/ppermute | solution.py:439
  84.8 28.0 %collective-permute-start.12 = (bf16[256,1152]{1,0:T(8,128)(2,1)}, bf16[256,1152]{1,0:T(8,128)(2,1)}, u32[]{:S(2)}, u32[]{:S(2)}) collective-permute-start(bf16[256,1152]{1,0:T(8,128)(2,1)} %get-tuple-element.37), channel_id=1, source_target_pairs={{0,16},{4,20},{8,24},{12,28},{16,0},{20,4},{24,8},{28,12},{1,17},{... | collective-permute-start | bytes 1769480 | tf_op jit(solution)/shard_map/ppermute | solution.py:439
  86.3 26.5 %collective-permute-start.13 = (bf16[256,1152]{1,0:T(8,128)(2,1)}, bf16[256,1152]{1,0:T(8,128)(2,1)}, u32[]{:S(2)}, u32[]{:S(2)}) collective-permute-start(bf16[256,1152]{1,0:T(8,128)(2,1)} %get-tuple-element.38), channel_id=1, source_target_pairs={{0,24},{4,28},{8,16},{12,20},{16,8},{20,12},{24,0},{28,4},{1,25},{... | collective-permute-start | bytes 1769480 | tf_op jit(solution)/shard_map/ppermute | solution.py:439
